TPU v7x, 256 devices: a whole 4x4x8 slice. The times are simulated.
256 devices in a mesh: gx: 16 (over z, core), gy: 16 (over x, y).
Axes of the slice: x: 4, y: 4, z: 8, core: 2. Of those that a mesh axis runs over, the one named last changes fastest.
Arguments:
- residual_in: float32 [2, 256, 256, 128], P(None, 'gx', 'gy'), may hold values from -6 to 6
- wave_sq: float32 [256, 256, 128], P('gx', 'gy'), may hold values from 0.005 to 0.08
Outputs:
- correction: float32 [2, 256, 256, 128], P(None, 'gx', 'gy')
All inputs are finite; a program needn't handle non-finite values.
Results may differ from a plain program's by a relative error of at most 0.00002.
Values sent between devices are 32-bit elements; how exact they have to be, the bound alone decides.
No kernel may reach another device: no remote copies, remote signals or barrier semaphores. Data moves between devices by JAX's collectives and lax.ppermute only.
A program may use at most 128 MiB of HBM per device.

v0:
```python
import jax
import jax.numpy as jnp
from jax import lax
from jax.sharding import PartitionSpec as P

LEVELS = 5
COARSE_SWEEPS = 6


OMEGA = 0.6
SHIFT = 0.5


def with_halo(shard, sides, width):
    for axis, dim in sides:
        count, length = (lax.axis_size(axis), shard.shape[dim])
        up = [(i, (i + 1) % count) for i in range(count - 1)]
        down = [(j, i) for i, j in up]
        last = lax.slice_in_dim(shard, length - width, length, axis=dim)
        initial = lax.slice_in_dim(shard, 0, width, axis=dim)
        before = lax.ppermute(last, axis, up)
        after = lax.ppermute(initial, axis, down)
        shard = jnp.concatenate([before, shard, after], axis=dim)
    return shard


def pad_depth(field):
    return jnp.pad(field, ((0, 0), (0, 0), (0, 0), (1, 1)))


def pad_plane(field):
    return jnp.pad(field, ((0, 0), (1, 1), (1, 1), (0, 0)))


def operator_apply(padded, wave_sq, lap_scale):
    full = pad_depth(padded)
    centre = full[:, 1:-1, 1:-1, 1:-1]
    summed = full[:, 2:, 1:-1, 1:-1] + full[:, :-2, 1:-1, 1:-1]
    summed = summed + full[:, 1:-1, 2:, 1:-1] + full[:, 1:-1, :-2, 1:-1]
    summed = summed + full[:, 1:-1, 1:-1, 2:] + full[:, 1:-1, 1:-1, :-2]
    laplace = lap_scale * (6.0 * centre - summed)
    real_part = laplace[0] - wave_sq * (centre[0] + SHIFT * centre[1])
    imag_part = laplace[1] - wave_sq * (centre[1] - SHIFT * centre[0])
    return jnp.stack([real_part, imag_part])


def inverse_diagonal(wave_sq, lap_scale):
    diag_real = 6.0 * lap_scale - wave_sq
    diag_imag = SHIFT * wave_sq
    modulus = diag_real * diag_real + diag_imag * diag_imag
    return (diag_real / modulus, -diag_imag / modulus)


def complex_mul(inv_real, inv_imag, values):
    return jnp.stack(
        [inv_real * values[0] - inv_imag * values[1], inv_real * values[1] + inv_imag * values[0]]
    )


def relax(field, padded, source, wave_sq, lap_scale, inv_real, inv_imag):
    misfit = source - operator_apply(padded, wave_sq, lap_scale)
    return field + OMEGA * complex_mul(inv_real, inv_imag, misfit)


def restrict_cells(values):
    dims_all = values.shape
    leading = dims_all[:-3]
    offset = len(leading)
    blocks = values.reshape(
        leading + (dims_all[-3] // 2, 2, dims_all[-2] // 2, 2, dims_all[-1] // 2, 2)
    )
    return jnp.mean(blocks, axis=(offset + 1, offset + 3, offset + 5))


def prolong_axis(padded, axis_dim):
    count_c = padded.shape[axis_dim] - 2
    lower_part = lax.slice_in_dim(padded, 0, count_c, axis=axis_dim)
    middle = lax.slice_in_dim(padded, 1, count_c + 1, axis=axis_dim)
    upper_part = lax.slice_in_dim(padded, 2, count_c + 2, axis=axis_dim)
    even_cells = 0.25 * lower_part + 0.75 * middle
    odd_cells = 0.75 * middle + 0.25 * upper_part
    paired = jnp.stack([even_cells, odd_cells], axis=axis_dim + 1)
    new_shape = padded.shape[:axis_dim] + (2 * count_c,) + padded.shape[axis_dim + 1 :]
    return paired.reshape(new_shape)


def prolong(padded_all):
    result = prolong_axis(padded_all, 1)
    result = prolong_axis(result, 2)
    return prolong_axis(result, 3)


def smooth_level(source, wave_sq, lap_scale, rim_of, coarse_of):
    inv_real, inv_imag = inverse_diagonal(wave_sq, lap_scale)
    field = OMEGA * complex_mul(inv_real, inv_imag, source)
    field = relax(field, rim_of(field), source, wave_sq, lap_scale, inv_real, inv_imag)
    misfit = source - operator_apply(rim_of(field), wave_sq, lap_scale)
    coarse_corr = coarse_of(restrict_cells(misfit), restrict_cells(wave_sq))
    field = field + prolong(pad_depth(coarse_corr))
    for sweep_no in range(2):
        field = relax(field, rim_of(field), source, wave_sq, lap_scale, inv_real, inv_imag)
    return field


def coarsest(source, wave_sq, lap_scale):
    inv_real, inv_imag = inverse_diagonal(wave_sq, lap_scale)
    field = OMEGA * complex_mul(inv_real, inv_imag, source)
    for sweep_no in range(COARSE_SWEEPS - 1):
        field = relax(field, pad_plane(field), source, wave_sq, lap_scale, inv_real, inv_imag)
    misfit = source - operator_apply(pad_plane(field), wave_sq, lap_scale)
    total_real = jnp.sum(misfit[0])
    total_imag = jnp.sum(misfit[1])
    factor = 1.0 / ((1.0 + SHIFT * SHIFT) * jnp.sum(wave_sq))
    shift_real = -(total_real - SHIFT * total_imag) * factor
    shift_imag = -(total_imag + SHIFT * total_real) * factor
    return field + jnp.stack([shift_real, shift_imag])[:, None, None, None]


def whole_cycle(source, wave_sq, grid_level):
    lap_scale = 0.25**grid_level
    return coarsest(source, wave_sq, lap_scale)


def field_rim(field):
    return with_halo(field, (("gx", 1), ("gy", 2)), 1)


def coarse_rim(field):
    return with_halo(field, (("gx", 1), ("gy", 2)), 1)


def agglomerate(source, wave_part, grid_level):
    pieces, waves = (
        lax.all_gather(source[None], ("gx", "gy"), axis=0, tiled=True),
        lax.all_gather(wave_part[None], ("gx", "gy"), axis=0, tiled=True),
    )
    tiles_x = lax.axis_size("gx")
    tiles_y = lax.axis_size("gy")
    rows_x, rows_y, cells_z = wave_part.shape
    whole_src = pieces.reshape(tiles_x, tiles_y, 2, rows_x, rows_y, cells_z)
    whole_src = whole_src.transpose(2, 0, 3, 1, 4, 5).reshape(
        2, tiles_x * rows_x, tiles_y * rows_y, cells_z
    )
    whole_wave = waves.reshape(tiles_x, tiles_y, rows_x, rows_y, cells_z)
    whole_wave = whole_wave.transpose(0, 2, 1, 3, 4).reshape(
        tiles_x * rows_x, tiles_y * rows_y, cells_z
    )
    solved = pad_plane(whole_cycle(whole_src, whole_wave, grid_level))
    start_x = lax.axis_index("gx") * rows_x
    start_y = lax.axis_index("gy") * rows_y
    return lax.dynamic_slice(solved, (0, start_x, start_y, 0), (2, rows_x + 2, rows_y + 2, cells_z))


def body(residual_in, wave_sq):
    split_levels = LEVELS - 1

    def vcycle(source, wave_part, grid_level):
        lap_scale = 0.25**grid_level

        def coarse_of(coarse_src, coarse_wave):
            if grid_level + 1 == split_levels:
                return agglomerate(coarse_src, coarse_wave, grid_level + 1)
            return coarse_rim(vcycle(coarse_src, coarse_wave, grid_level + 1))

        return smooth_level(source, wave_part, lap_scale, field_rim, coarse_of)

    return vcycle(residual_in, wave_sq, 0)


def solution(mesh):
    placed = (P(None, "gx", "gy", None), P("gx", "gy", None))
    return jax.shard_map(
        body, mesh=mesh, in_specs=placed, out_specs=P(None, "gx", "gy", None), check_vma=False
    )
```

profile of v0, /device:TPU:130, one launch (start us, length us, event | category | flops | bytes accessed | tf_op | source)
XLA Modules:
  0.0 604.0 jit_solution(13270884353229995754)
XLA Ops:
  5.7 3.8 collective-permute-done.1
  9.6 4.9 collective-permute-start.2
  16.5 5.8 collective-permute-done.3
  28.2 3.8 collective-permute-done.5
  34.0 3.9 collective-permute-start.7
  38.0 9.8 %reshape.409 = f32[8,2,8,2,64,2]{5,4,3,2,1,0:T(8,128)} reshape(f32[16,16,128]{2,1,0:T(8,128)S(1)} %copy-done) | data formatting | bytes 262144 | tf_op jit(solution)/shard_map/reshape | solution.py:69
  47.8 4.0 reduce_sum.113
  52.6 18.1 %reshape.410 = f32[2,8,2,8,2,64,2]{6,5,4,3,2,1,0:T(8,128)} reshape(f32[2,16,16,128]{3,2,1,0:T(8,128)S(1)} %maximum_subtract_fusion.2) | data formatting | bytes 524288 | tf_op jit(solution)/shard_map/reshape | solution.py:69
  70.7 7.0 %reduce_sum.114 = f32[2,8,8,64]{3,2,1,0:T(8,128)S(1)} reduce(f32[2,8,2,8,2,64,2]{6,5,4,3,2,1,0:T(8,128)} %reshape.410, f32[]{:T(128)} %constant.25.clone.1), dimensions={2,4,6}, to_apply=%region_1.2 | reduce | flops 57344 | bytes 294916 | tf_op jit(solution)/shard_map/reduce_sum | solution.py:72
  82.2 3.8 collective-permute-done.9
  86.0 4.0 collective-permute-start.10
  92.0 5.7 collective-permute-done.11
  108.2 3.9 collective-permute-start.15
  131.2 4.0 collective-permute-start.18
  137.3 5.6 collective-permute-done.19
  153.2 3.9 collective-permute-start.23
  171.4 3.9 collective-permute-start.27
  175.3 72.1 %all-reduce.33 = f32[2048]{0:T(1024)S(1)} all-reduce(f32[2048]{0:T(1024)S(1)} %multiply_dynamic-update-slice_fusion), channel_id=2, replica_groups=mesh['gx'=16,'gy'=16] {'gx','gy'}, use_global_device_ids=true, to_apply=%add.33 | all-reduce | flops 2048 | bytes 16384
  253.4 4.2 collective-permute-done.29
  257.6 4.7 collective-permute-start.30
  264.9 5.0 collective-permute-done.31
  270.3 99.2 %all-gather.2 = f32[256,2,8]{2,1,0:T(2,128)S(1)} all-gather(f32[1,2,8]{2,1,0:T(2,128)S(1)} %multiply_bitcast_fusion), channel_id=3, replica_groups=mesh['gx'=16,'gy'=16] {'gx','gy'}, dimensions={0}, use_global_device_ids=true | all-gather | bytes 16448 | tf_op jit(solution)/shard_map/all_gather | solution.py:134
  377.0 4.8 collective-permute-start.32
  383.7 4.2 collective-permute-done.33
  387.9 4.6 collective-permute-start.34
  394.5 5.7 collective-permute-done.35
  410.4 3.9 collective-permute-start.39
  420.2 4.9 collective-permute-start.41
  428.3 6.0 collective-permute-start.43
  441.9 4.2 collective-permute-done.45
  446.2 6.0 collective-permute-start.46
  454.1 5.7 collective-permute-done.47
  470.1 3.9 collective-permute-start.51
  480.0 4.9 collective-permute-start.53
  488.1 6.0 collective-permute-start.55
  502.1 4.2 collective-permute-done.57
  506.3 6.0 collective-permute-start.58
  514.3 5.7 collective-permute-done.59
  524.8 3.8 collective-permute-done.61
  530.5 4.1 collective-permute-start.63
  540.5 4.9 collective-permute-start.65
  548.7 6.0 collective-permute-start.67
  565.3 4.3 collective-permute-done.69
  569.7 6.0 collective-permute-start.70
  577.7 5.8 collective-permute-done.71
  588.8 3.8 collective-permute-done.73
  594.6 3.9 collective-permute-start.75
  598.6 3.8 collective-permute-done.75
  (449 shorter events, 189.5 us)
Async XLA Ops:
  3.3 6.3 %collective-permute-start.1 = (f32[2,1,16,128]{3,2,1,0:T(8,128)S(1)}, f32[2,1,16,128]{3,2,1,0:T(8,128)S(1)}, u32[]{:S(2)}, u32[]{:S(2)}) collective-permute-start(f32[2,1,16,128]{3,2,1,0:T(8,128)S(1)} %get-tuple-element.63), channel_id=1, source_target_pairs={{0,16},{16,32},{32,48},{48,64},{64,80},{80,96},{96,112},{112,128},... | collective-permute-start | bytes 49160 | tf_op jit(solution)/shard_map/ppermute | solution.py:21
  9.6 6.9 %collective-permute-start.2 = (f32[2,18,1,128]{3,0,2,1:T(2,128)S(1)}, f32[2,18,1,128]{3,0,2,1:T(2,128)S(1)}, u32[]{:S(2)}, u32[]{:S(2)}) collective-permute-start(f32[2,18,1,128]{3,0,2,1:T(2,128)S(1)} %copy.488), channel_id=1, source_target_pairs={{1,0},{2,1},{3,2},{4,3},{5,4},{6,5},{7,6},{8,7},{9,8},{10,9},{11,1... | collective-permute-start | bytes 55304 | tf_op jit(solution)/shard_map/ppermute | solution.py:22
  14.5 7.8 %collective-permute-start.3 = (f32[2,18,1,128]{3,0,2,1:T(2,128)S(1)}, f32[2,18,1,128]{3,0,2,1:T(2,128)S(1)}, u32[]{:S(2)}, u32[]{:S(2)}) collective-permute-start(f32[2,18,1,128]{3,0,2,1:T(2,128)S(1)} %copy.490), channel_id=1, source_target_pairs={{0,1},{1,2},{2,3},{3,4},{4,5},{5,6},{6,7},{7,8},{8,9},{9,10},{10,1... | collective-permute-start | bytes 55304 | tf_op jit(solution)/shard_map/ppermute | solution.py:21
  25.8 6.3 %collective-permute-start.5 = (f32[2,1,16,128]{3,2,1,0:T(8,128)S(1)}, f32[2,1,16,128]{3,2,1,0:T(8,128)S(1)}, u32[]{:S(2)}, u32[]{:S(2)}) collective-permute-start(f32[2,1,16,128]{3,2,1,0:T(8,128)S(1)} %get-tuple-element.61), channel_id=1, source_target_pairs={{0,16},{16,32},{32,48},{48,64},{64,80},{80,96},{96,112},{112,128},... | collective-permute-start | bytes 49160 | tf_op jit(solution)/shard_map/ppermute | solution.py:21
  32.1 19.7 %collective-permute-start.6 = (f32[2,18,1,128]{3,0,2,1:T(2,128)S(1)}, f32[2,18,1,128]{3,0,2,1:T(2,128)S(1)}, u32[]{:S(2)}, u32[]{:S(2)}) collective-permute-start(f32[2,18,1,128]{3,0,2,1:T(2,128)S(1)} %copy.494), channel_id=1, source_target_pairs={{1,0},{2,1},{3,2},{4,3},{5,4},{6,5},{7,6},{8,7},{9,8},{10,9},{11,1... | collective-permute-start | bytes 55304 | tf_op jit(solution)/shard_map/ppermute | solution.py:22
  34.0 17.8 %collective-permute-start.7 = (f32[2,18,1,128]{3,0,2,1:T(2,128)S(1)}, f32[2,18,1,128]{3,0,2,1:T(2,128)S(1)}, u32[]{:S(2)}, u32[]{:S(2)}) collective-permute-start(f32[2,18,1,128]{3,0,2,1:T(2,128)S(1)} %copy.496), channel_id=1, source_target_pairs={{0,1},{1,2},{2,3},{3,4},{4,5},{5,6},{6,7},{7,8},{8,9},{9,10},{10,1... | collective-permute-start | bytes 55304 | tf_op jit(solution)/shard_map/ppermute | solution.py:21
  79.8 6.2 %collective-permute-start.9 = (f32[2,1,8,64]{3,2,1,0:T(8,128)S(1)}, f32[2,1,8,64]{3,2,1,0:T(8,128)S(1)}, u32[]{:S(2)}, u32[]{:S(2)}) collective-permute-start(f32[2,1,8,64]{3,2,1,0:T(8,128)S(1)} %get-tuple-element.105), channel_id=1, source_target_pairs={{0,16},{16,32},{32,48},{48,64},{64,80},{80,96},{96,112},{112,128},... | collective-permute-start | bytes 12296 | tf_op jit(solution)/shard_map/ppermute | solution.py:21
  90.0 7.7 %collective-permute-start.11 = (f32[2,10,1,64]{3,0,2,1:T(2,128)S(1)}, f32[2,10,1,64]{3,0,2,1:T(2,128)S(1)}, u32[]{:S(2)}, u32[]{:S(2)}) collective-permute-start(f32[2,10,1,64]{3,0,2,1:T(2,128)S(1)} %copy.567), channel_id=1, source_target_pairs={{0,1},{1,2},{2,3},{3,4},{4,5},{5,6},{6,7},{7,8},{8,9},{9,10},{10,1... | collective-permute-start | bytes 15368 | tf_op jit(solution)/shard_map/ppermute | solution.py:21
  100.1 6.2 %collective-permute-start.13 = (f32[2,1,8,64]{3,2,1,0:T(8,128)S(1)}, f32[2,1,8,64]{3,2,1,0:T(8,128)S(1)}, u32[]{:S(2)}, u32[]{:S(2)}) collective-permute-start(f32[2,1,8,64]{3,2,1,0:T(8,128)S(1)} %get-tuple-element.103), channel_id=1, source_target_pairs={{0,16},{16,32},{32,48},{48,64},{64,80},{80,96},{96,112},{112,128},... | collective-permute-start | bytes 12296 | tf_op jit(solution)/shard_map/ppermute | solution.py:21
  106.3 9.3 %collective-permute-start.14 = (f32[2,10,1,64]{3,0,2,1:T(2,128)S(1)}, f32[2,10,1,64]{3,0,2,1:T(2,128)S(1)}, u32[]{:S(2)}, u32[]{:S(2)}) collective-permute-start(f32[2,10,1,64]{3,0,2,1:T(2,128)S(1)} %copy.568), channel_id=1, source_target_pairs={{1,0},{2,1},{3,2},{4,3},{5,4},{6,5},{7,6},{8,7},{9,8},{10,9},{11,1... | collective-permute-start | bytes 15368 | tf_op jit(solution)/shard_map/ppermute | solution.py:22
  108.2 7.7 %collective-permute-start.15 = (f32[2,10,1,64]{3,0,2,1:T(2,128)S(1)}, f32[2,10,1,64]{3,0,2,1:T(2,128)S(1)}, u32[]{:S(2)}, u32[]{:S(2)}) collective-permute-start(f32[2,10,1,64]{3,0,2,1:T(2,128)S(1)} %copy.569), channel_id=1, source_target_pairs={{0,1},{1,2},{2,3},{3,4},{4,5},{5,6},{6,7},{7,8},{8,9},{9,10},{10,1... | collective-permute-start | bytes 15368 | tf_op jit(solution)/shard_map/ppermute | solution.py:21
  125.1 6.1 %collective-permute-start.17 = (f32[2,1,4,32]{3,2,1,0:T(4,128)S(1)}, f32[2,1,4,32]{3,2,1,0:T(4,128)S(1)}, u32[]{:S(2)}, u32[]{:S(2)}) collective-permute-start(f32[2,1,4,32]{3,2,1,0:T(4,128)S(1)} %get-tuple-element.151), channel_id=1, source_target_pairs={{0,16},{16,32},{32,48},{48,64},{64,80},{80,96},{96,112},{112,128},... | collective-permute-start | bytes 3080 | tf_op jit(solution)/shard_map/ppermute | solution.py:21
  135.2 7.6 %collective-permute-start.19 = (f32[2,6,1,32]{3,2,1,0:T(1,128)S(1)}, f32[2,6,1,32]{3,2,1,0:T(1,128)S(1)}, u32[]{:S(2)}, u32[]{:S(2)}) collective-permute-start(f32[2,6,1,32]{3,2,1,0:T(1,128)S(1)} %get-tuple-element.133), channel_id=1, source_target_pairs={{0,1},{1,2},{2,3},{3,4},{4,5},{5,6},{6,7},{7,8},{8,9},{9,10},{10,1... | collective-permute-start | bytes 4616 | tf_op jit(solution)/shard_map/ppermute | solution.py:21
  151.2 6.3 %collective-permute-start.22 = (f32[2,6,1,32]{3,2,1,0:T(1,128)S(1)}, f32[2,6,1,32]{3,2,1,0:T(1,128)S(1)}, u32[]{:S(2)}, u32[]{:S(2)}) collective-permute-start(f32[2,6,1,32]{3,2,1,0:T(1,128)S(1)} %get-tuple-element.130), channel_id=1, source_target_pairs={{1,0},{2,1},{3,2},{4,3},{5,4},{6,5},{7,6},{8,7},{9,8},{10,9},{11,1... | collective-permute-start | bytes 4616 | tf_op jit(solution)/shard_map/ppermute | solution.py:22
  153.2 7.6 %collective-permute-start.23 = (f32[2,6,1,32]{3,2,1,0:T(1,128)S(1)}, f32[2,6,1,32]{3,2,1,0:T(1,128)S(1)}, u32[]{:S(2)}, u32[]{:S(2)}) collective-permute-start(f32[2,6,1,32]{3,2,1,0:T(1,128)S(1)} %get-tuple-element.129), channel_id=1, source_target_pairs={{0,1},{1,2},{2,3},{3,4},{4,5},{5,6},{6,7},{7,8},{8,9},{9,10},{10,1... | collective-permute-start | bytes 4616 | tf_op jit(solution)/shard_map/ppermute | solution.py:21
  169.5 78.7 %collective-permute-start.26 = (f32[2,4,1,16]{3,2,1,0:T(1,128)S(1)}, f32[2,4,1,16]{3,2,1,0:T(1,128)S(1)}, u32[]{:S(2)}, u32[]{:S(2)}) collective-permute-start(f32[2,4,1,16]{3,2,1,0:T(1,128)S(1)} %get-tuple-element.172), channel_id=1, source_target_pairs={{1,0},{2,1},{3,2},{4,3},{5,4},{6,5},{7,6},{8,7},{9,8},{10,9},{11,1... | collective-permute-start | bytes 1544 | tf_op jit(solution)/shard_map/ppermute | solution.py:22
  171.4 76.8 %collective-permute-start.27 = (f32[2,4,1,16]{3,2,1,0:T(1,128)S(1)}, f32[2,4,1,16]{3,2,1,0:T(1,128)S(1)}, u32[]{:S(2)}, u32[]{:S(2)}) collective-permute-start(f32[2,4,1,16]{3,2,1,0:T(1,128)S(1)} %get-tuple-element.171), channel_id=1, source_target_pairs={{0,1},{1,2},{2,3},{3,4},{4,5},{5,6},{6,7},{7,8},{8,9},{9,10},{10,1... | collective-permute-start | bytes 1544 | tf_op jit(solution)/shard_map/ppermute | solution.py:21
  257.6 7.2 %collective-permute-start.30 = (f32[2,4,1,16]{3,2,1,0:T(1,128)S(1)}, f32[2,4,1,16]{3,2,1,0:T(1,128)S(1)}, u32[]{:S(2)}, u32[]{:S(2)}) collective-permute-start(f32[2,4,1,16]{3,2,1,0:T(1,128)S(1)} %get-tuple-element.170), channel_id=1, source_target_pairs={{1,0},{2,1},{3,2},{4,3},{5,4},{6,5},{7,6},{8,7},{9,8},{10,9},{11,1... | collective-permute-start | bytes 1544 | tf_op jit(solution)/shard_map/ppermute | solution.py:22
  262.3 7.6 %collective-permute-start.31 = (f32[2,4,1,16]{3,2,1,0:T(1,128)S(1)}, f32[2,4,1,16]{3,2,1,0:T(1,128)S(1)}, u32[]{:S(2)}, u32[]{:S(2)}) collective-permute-start(f32[2,4,1,16]{3,2,1,0:T(1,128)S(1)} %get-tuple-element.169), channel_id=1, source_target_pairs={{0,1},{1,2},{2,3},{3,4},{4,5},{5,6},{6,7},{7,8},{8,9},{9,10},{10,1... | collective-permute-start | bytes 1544 | tf_op jit(solution)/shard_map/ppermute | solution.py:21
  377.0 6.8 %collective-permute-start.32 = (f32[2,1,2,16]{3,2,1,0:T(2,128)S(1)}, f32[2,1,2,16]{3,2,1,0:T(2,128)S(1)}, u32[]{:S(2)}, u32[]{:S(2)}) collective-permute-start(f32[2,1,2,16]{3,2,1,0:T(2,128)S(1)} %get-tuple-element.188), channel_id=1, source_target_pairs={{16,0},{32,16},{48,32},{64,48},{80,64},{96,80},{112,96},{128,112},... | collective-permute-start | bytes 776 | tf_op jit(solution)/shard_map/ppermute | solution.py:22
  387.9 6.5 %collective-permute-start.34 = (f32[2,4,1,16]{3,2,1,0:T(1,128)S(1)}, f32[2,4,1,16]{3,2,1,0:T(1,128)S(1)}, u32[]{:S(2)}, u32[]{:S(2)}) collective-permute-start(f32[2,4,1,16]{3,2,1,0:T(1,128)S(1)} %get-tuple-element.168), channel_id=1, source_target_pairs={{1,0},{2,1},{3,2},{4,3},{5,4},{6,5},{7,6},{8,7},{9,8},{10,9},{11,1... | collective-permute-start | bytes 1544 | tf_op jit(solution)/shard_map/ppermute | solution.py:22
  392.5 7.6 %collective-permute-start.35 = (f32[2,4,1,16]{3,2,1,0:T(1,128)S(1)}, f32[2,4,1,16]{3,2,1,0:T(1,128)S(1)}, u32[]{:S(2)}, u32[]{:S(2)}) collective-permute-start(f32[2,4,1,16]{3,2,1,0:T(1,128)S(1)} %get-tuple-element.167), channel_id=1, source_target_pairs={{0,1},{1,2},{2,3},{3,4},{4,5},{5,6},{6,7},{7,8},{8,9},{9,10},{10,1... | collective-permute-start | bytes 1544 | tf_op jit(solution)/shard_map/ppermute | solution.py:21
  410.4 7.6 %collective-permute-start.39 = (f32[2,4,1,16]{3,2,1,0:T(1,128)S(1)}, f32[2,4,1,16]{3,2,1,0:T(1,128)S(1)}, u32[]{:S(2)}, u32[]{:S(2)}) collective-permute-start(f32[2,4,1,16]{3,2,1,0:T(1,128)S(1)} %get-tuple-element.165), channel_id=1, source_target_pairs={{0,1},{1,2},{2,3},{3,4},{4,5},{5,6},{6,7},{7,8},{8,9},{9,10},{10,1... | collective-permute-start | bytes 1544 | tf_op jit(solution)/shard_map/ppermute | solution.py:21
  418.2 6.8 %collective-permute-start.40 = (f32[2,1,2,16]{3,2,1,0:T(2,128)S(1)}, f32[2,1,2,16]{3,2,1,0:T(2,128)S(1)}, u32[]{:S(2)}, u32[]{:S(2)}) collective-permute-start(f32[2,1,2,16]{3,2,1,0:T(2,128)S(1)} %get-tuple-element.183), channel_id=1, source_target_pairs={{0,16},{16,32},{32,48},{48,64},{64,80},{80,96},{96,112},{112,128},... | collective-permute-start | bytes 776 | tf_op jit(solution)/shard_map/ppermute | solution.py:21
  420.2 6.1 %collective-permute-start.41 = (f32[2,1,2,16]{3,2,1,0:T(2,128)S(1)}, f32[2,1,2,16]{3,2,1,0:T(2,128)S(1)}, u32[]{:S(2)}, u32[]{:S(2)}) collective-permute-start(f32[2,1,2,16]{3,2,1,0:T(2,128)S(1)} %get-tuple-element.184), channel_id=1, source_target_pairs={{16,0},{32,16},{48,32},{64,48},{80,64},{96,80},{112,96},{128,112},... | collective-permute-start | bytes 776 | tf_op jit(solution)/shard_map/ppermute | solution.py:22
  426.3 8.0 %collective-permute-start.42 = (f32[2,4,1,16]{3,2,1,0:T(1,128)S(1)}, f32[2,4,1,16]{3,2,1,0:T(1,128)S(1)}, u32[]{:S(2)}, u32[]{:S(2)}) collective-permute-start(f32[2,4,1,16]{3,2,1,0:T(1,128)S(1)} %get-tuple-element.163), channel_id=1, source_target_pairs={{0,1},{1,2},{2,3},{3,4},{4,5},{5,6},{6,7},{7,8},{8,9},{9,10},{10,1... | collective-permute-start | bytes 1544 | tf_op jit(solution)/shard_map/ppermute | solution.py:21
  428.3 7.3 %collective-permute-start.43 = (f32[2,4,1,16]{3,2,1,0:T(1,128)S(1)}, f32[2,4,1,16]{3,2,1,0:T(1,128)S(1)}, u32[]{:S(2)}, u32[]{:S(2)}) collective-permute-start(f32[2,4,1,16]{3,2,1,0:T(1,128)S(1)} %get-tuple-element.164), channel_id=1, source_target_pairs={{1,0},{2,1},{3,2},{4,3},{5,4},{6,5},{7,6},{8,7},{9,8},{10,9},{11,1... | collective-permute-start | bytes 1544 | tf_op jit(solution)/shard_map/ppermute | solution.py:22
  446.2 7.9 %collective-permute-start.46 = (f32[2,6,1,32]{3,2,1,0:T(1,128)S(1)}, f32[2,6,1,32]{3,2,1,0:T(1,128)S(1)}, u32[]{:S(2)}, u32[]{:S(2)}) collective-permute-start(f32[2,6,1,32]{3,2,1,0:T(1,128)S(1)} %get-tuple-element.128), channel_id=1, source_target_pairs={{1,0},{2,1},{3,2},{4,3},{5,4},{6,5},{7,6},{8,7},{9,8},{10,9},{11,1... | collective-permute-start | bytes 4616 | tf_op jit(solution)/shard_map/ppermute | solution.py:22
  452.2 7.6 %collective-permute-start.47 = (f32[2,6,1,32]{3,2,1,0:T(1,128)S(1)}, f32[2,6,1,32]{3,2,1,0:T(1,128)S(1)}, u32[]{:S(2)}, u32[]{:S(2)}) collective-permute-start(f32[2,6,1,32]{3,2,1,0:T(1,128)S(1)} %get-tuple-element.127), channel_id=1, source_target_pairs={{0,1},{1,2},{2,3},{3,4},{4,5},{5,6},{6,7},{7,8},{8,9},{9,10},{10,1... | collective-permute-start | bytes 4616 | tf_op jit(solution)/shard_map/ppermute | solution.py:21
  470.1 7.6 %collective-permute-start.51 = (f32[2,6,1,32]{3,2,1,0:T(1,128)S(1)}, f32[2,6,1,32]{3,2,1,0:T(1,128)S(1)}, u32[]{:S(2)}, u32[]{:S(2)}) collective-permute-start(f32[2,6,1,32]{3,2,1,0:T(1,128)S(1)} %get-tuple-element.123), channel_id=1, source_target_pairs={{0,1},{1,2},{2,3},{3,4},{4,5},{5,6},{6,7},{7,8},{8,9},{9,10},{10,1... | collective-permute-start | bytes 4616 | tf_op jit(solution)/shard_map/ppermute | solution.py:21
  478.1 6.8 %collective-permute-start.52 = (f32[2,1,4,32]{3,2,1,0:T(4,128)S(1)}, f32[2,1,4,32]{3,2,1,0:T(4,128)S(1)}, u32[]{:S(2)}, u32[]{:S(2)}) collective-permute-start(f32[2,1,4,32]{3,2,1,0:T(4,128)S(1)} %get-tuple-element.137), channel_id=1, source_target_pairs={{0,16},{16,32},{32,48},{48,64},{64,80},{80,96},{96,112},{112,128},... | collective-permute-start | bytes 3080 | tf_op jit(solution)/shard_map/ppermute | solution.py:21
  480.0 6.2 %collective-permute-start.53 = (f32[2,1,4,32]{3,2,1,0:T(4,128)S(1)}, f32[2,1,4,32]{3,2,1,0:T(4,128)S(1)}, u32[]{:S(2)}, u32[]{:S(2)}) collective-permute-start(f32[2,1,4,32]{3,2,1,0:T(4,128)S(1)} %get-tuple-element.138), channel_id=1, source_target_pairs={{16,0},{32,16},{48,32},{64,48},{80,64},{96,80},{112,96},{128,112},... | collective-permute-start | bytes 3080 | tf_op jit(solution)/shard_map/ppermute | solution.py:22
  486.2 8.0 %collective-permute-start.54 = (f32[2,6,1,32]{3,2,1,0:T(1,128)S(1)}, f32[2,6,1,32]{3,2,1,0:T(1,128)S(1)}, u32[]{:S(2)}, u32[]{:S(2)}) collective-permute-start(f32[2,6,1,32]{3,2,1,0:T(1,128)S(1)} %get-tuple-element.119), channel_id=1, source_target_pairs={{0,1},{1,2},{2,3},{3,4},{4,5},{5,6},{6,7},{7,8},{8,9},{9,10},{10,1... | collective-permute-start | bytes 4616 | tf_op jit(solution)/shard_map/ppermute | solution.py:21
  488.1 7.4 %collective-permute-start.55 = (f32[2,6,1,32]{3,2,1,0:T(1,128)S(1)}, f32[2,6,1,32]{3,2,1,0:T(1,128)S(1)}, u32[]{:S(2)}, u32[]{:S(2)}) collective-permute-start(f32[2,6,1,32]{3,2,1,0:T(1,128)S(1)} %get-tuple-element.120), channel_id=1, source_target_pairs={{1,0},{2,1},{3,2},{4,3},{5,4},{6,5},{7,6},{8,7},{9,8},{10,9},{11,1... | collective-permute-start | bytes 4616 | tf_op jit(solution)/shard_map/ppermute | solution.py:22
  500.1 6.2 %collective-permute-start.57 = (f32[2,1,8,64]{3,2,1,0:T(8,128)S(1)}, f32[2,1,8,64]{3,2,1,0:T(8,128)S(1)}, u32[]{:S(2)}, u32[]{:S(2)}) collective-permute-start(f32[2,1,8,64]{3,2,1,0:T(8,128)S(1)} %get-tuple-element.99), channel_id=1, source_target_pairs={{0,16},{16,32},{32,48},{48,64},{64,80},{80,96},{96,112},{112,128},... | collective-permute-start | bytes 12296 | tf_op jit(solution)/shard_map/ppermute | solution.py:21
  506.3 8.0 %collective-permute-start.58 = (f32[2,10,1,64]{3,0,2,1:T(2,128)S(1)}, f32[2,10,1,64]{3,0,2,1:T(2,128)S(1)}, u32[]{:S(2)}, u32[]{:S(2)}) collective-permute-start(f32[2,10,1,64]{3,0,2,1:T(2,128)S(1)} %copy.570), channel_id=1, source_target_pairs={{1,0},{2,1},{3,2},{4,3},{5,4},{6,5},{7,6},{8,7},{9,8},{10,9},{11,1... | collective-permute-start | bytes 15368 | tf_op jit(solution)/shard_map/ppermute | solution.py:22
  512.4 7.7 %collective-permute-start.59 = (f32[2,10,1,64]{3,0,2,1:T(2,128)S(1)}, f32[2,10,1,64]{3,0,2,1:T(2,128)S(1)}, u32[]{:S(2)}, u32[]{:S(2)}) collective-permute-start(f32[2,10,1,64]{3,0,2,1:T(2,128)S(1)} %copy.571), channel_id=1, source_target_pairs={{0,1},{1,2},{2,3},{3,4},{4,5},{5,6},{6,7},{7,8},{8,9},{9,10},{10,1... | collective-permute-start | bytes 15368 | tf_op jit(solution)/shard_map/ppermute | solution.py:21
  522.4 6.2 %collective-permute-start.61 = (f32[2,1,8,64]{3,2,1,0:T(8,128)S(1)}, f32[2,1,8,64]{3,2,1,0:T(8,128)S(1)}, u32[]{:S(2)}, u32[]{:S(2)}) collective-permute-start(f32[2,1,8,64]{3,2,1,0:T(8,128)S(1)} %get-tuple-element.97), channel_id=1, source_target_pairs={{0,16},{16,32},{32,48},{48,64},{64,80},{80,96},{96,112},{112,128},... | collective-permute-start | bytes 12296 | tf_op jit(solution)/shard_map/ppermute | solution.py:21
  530.5 7.7 %collective-permute-start.63 = (f32[2,10,1,64]{3,0,2,1:T(2,128)S(1)}, f32[2,10,1,64]{3,0,2,1:T(2,128)S(1)}, u32[]{:S(2)}, u32[]{:S(2)}) collective-permute-start(f32[2,10,1,64]{3,0,2,1:T(2,128)S(1)} %copy.573), channel_id=1, source_target_pairs={{0,1},{1,2},{2,3},{3,4},{4,5},{5,6},{6,7},{7,8},{8,9},{9,10},{10,1... | collective-permute-start | bytes 15368 | tf_op jit(solution)/shard_map/ppermute | solution.py:21
  538.6 6.8 %collective-permute-start.64 = (f32[2,1,8,64]{3,2,1,0:T(8,128)S(1)}, f32[2,1,8,64]{3,2,1,0:T(8,128)S(1)}, u32[]{:S(2)}, u32[]{:S(2)}) collective-permute-start(f32[2,1,8,64]{3,2,1,0:T(8,128)S(1)} %get-tuple-element.95), channel_id=1, source_target_pairs={{0,16},{16,32},{32,48},{48,64},{64,80},{80,96},{96,112},{112,128},... | collective-permute-start | bytes 12296 | tf_op jit(solution)/shard_map/ppermute | solution.py:21
  540.5 6.2 %collective-permute-start.65 = (f32[2,1,8,64]{3,2,1,0:T(8,128)S(1)}, f32[2,1,8,64]{3,2,1,0:T(8,128)S(1)}, u32[]{:S(2)}, u32[]{:S(2)}) collective-permute-start(f32[2,1,8,64]{3,2,1,0:T(8,128)S(1)} %get-tuple-element.96), channel_id=1, source_target_pairs={{16,0},{32,16},{48,32},{64,48},{80,64},{96,80},{112,96},{128,112},... | collective-permute-start | bytes 12296 | tf_op jit(solution)/shard_map/ppermute | solution.py:22
  546.8 8.0 %collective-permute-start.66 = (f32[2,10,1,64]{3,0,2,1:T(2,128)S(1)}, f32[2,10,1,64]{3,0,2,1:T(2,128)S(1)}, u32[]{:S(2)}, u32[]{:S(2)}) collective-permute-start(f32[2,10,1,64]{3,0,2,1:T(2,128)S(1)} %get-tuple-element.85), channel_id=1, source_target_pairs={{0,1},{1,2},{2,3},{3,4},{4,5},{5,6},{6,7},{7,8},{8,9},{9,10},{10,1... | collective-permute-start | bytes 15368 | tf_op jit(solution)/shard_map/ppermute | solution.py:21
  548.7 7.4 %collective-permute-start.67 = (f32[2,10,1,64]{3,0,2,1:T(2,128)S(1)}, f32[2,10,1,64]{3,0,2,1:T(2,128)S(1)}, u32[]{:S(2)}, u32[]{:S(2)}) collective-permute-start(f32[2,10,1,64]{3,0,2,1:T(2,128)S(1)} %get-tuple-element.86), channel_id=1, source_target_pairs={{1,0},{2,1},{3,2},{4,3},{5,4},{6,5},{7,6},{8,7},{9,8},{10,9},{11,1... | collective-permute-start | bytes 15368 | tf_op jit(solution)/shard_map/ppermute | solution.py:22
  563.4 6.3 %collective-permute-start.69 = (f32[2,1,16,128]{3,2,1,0:T(8,128)S(1)}, f32[2,1,16,128]{3,2,1,0:T(8,128)S(1)}, u32[]{:S(2)}, u32[]{:S(2)}) collective-permute-start(f32[2,1,16,128]{3,2,1,0:T(8,128)S(1)} %get-tuple-element.57), channel_id=1, source_target_pairs={{0,16},{16,32},{32,48},{48,64},{64,80},{80,96},{96,112},{112,128},... | collective-permute-start | bytes 49160 | tf_op jit(solution)/shard_map/ppermute | solution.py:21
  569.7 8.0 %collective-permute-start.70 = (f32[2,18,1,128]{3,0,2,1:T(2,128)S(1)}, f32[2,18,1,128]{3,0,2,1:T(2,128)S(1)}, u32[]{:S(2)}, u32[]{:S(2)}) collective-permute-start(f32[2,18,1,128]{3,0,2,1:T(2,128)S(1)} %copy.552), channel_id=1, source_target_pairs={{1,0},{2,1},{3,2},{4,3},{5,4},{6,5},{7,6},{8,7},{9,8},{10,9},{11,1... | collective-permute-start | bytes 55304 | tf_op jit(solution)/shard_map/ppermute | solution.py:22
  575.8 7.8 %collective-permute-start.71 = (f32[2,18,1,128]{3,0,2,1:T(2,128)S(1)}, f32[2,18,1,128]{3,0,2,1:T(2,128)S(1)}, u32[]{:S(2)}, u32[]{:S(2)}) collective-permute-start(f32[2,18,1,128]{3,0,2,1:T(2,128)S(1)} %copy.554), channel_id=1, source_target_pairs={{0,1},{1,2},{2,3},{3,4},{4,5},{5,6},{6,7},{7,8},{8,9},{9,10},{10,1... | collective-permute-start | bytes 55304 | tf_op jit(solution)/shard_map/ppermute | solution.py:21
  586.4 6.3 %collective-permute-start.73 = (f32[2,1,16,128]{3,2,1,0:T(8,128)S(1)}, f32[2,1,16,128]{3,2,1,0:T(8,128)S(1)}, u32[]{:S(2)}, u32[]{:S(2)}) collective-permute-start(f32[2,1,16,128]{3,2,1,0:T(8,128)S(1)} %get-tuple-element.55), channel_id=1, source_target_pairs={{0,16},{16,32},{32,48},{48,64},{64,80},{80,96},{96,112},{112,128},... | collective-permute-start | bytes 49160 | tf_op jit(solution)/shard_map/ppermute | solution.py:21
  594.6 7.8 %collective-permute-start.75 = (f32[2,18,1,128]{3,0,2,1:T(2,128)S(1)}, f32[2,18,1,128]{3,0,2,1:T(2,128)S(1)}, u32[]{:S(2)}, u32[]{:S(2)}) collective-permute-start(f32[2,18,1,128]{3,0,2,1:T(2,128)S(1)} %copy.560), channel_id=1, source_target_pairs={{0,1},{1,2},{2,3},{3,4},{4,5},{5,6},{6,7},{7,8},{8,9},{9,10},{10,1... | collective-permute-start | bytes 55304 | tf_op jit(solution)/shard_map/ppermute | solution.py:21
  (52 other events, 883.0 us)
where the time goes:
time: 607 us; the launch traced here: 604 us
  starting transfers between devices  223 us (37%)
  blocking collectives  171 us (28%)
  waiting for transfers between devices  133 us (22%)
  local copies, waits for them, and re-layouts  41.9 us (7%)
  other arithmetic  28.6 us (5%)
    ppermute x38, starting transfers between devices, with_halo(): after = lax.ppermute(initial, axis, down)  128 us
    ppermute x38, waiting for transfers between devices, with_halo(): before = lax.ppermute(last, axis, up)  125 us
    all_gather x1, blocking collectives, agglomerate(): lax.all_gather(source[None], ('gx', 'gy'), axis=0, tiled=True)  99.2 us
    ppermute x38, starting transfers between devices, with_halo(): before = lax.ppermute(last, axis, up)  94.7 us
    unnamed x1, blocking collectives  72.1 us
    reshape x2, local copies, waits for them, and re-layouts, restrict_cells(): values.reshape(leading + (dims_all[-3] // 2, 2, dims_all[-2] // 2, 2, dim...  27.9 us
    reduce_sum x10, other arithmetic, restrict_cells(): return jnp.mean(blocks, axis=(offset + 1, offset + 3, offset + 5))  13.3 us
  transfers between devices with their start and end apart: 76, of which 36 were waited for; matrix products, arithmetic and copies ran while one was open for 3% of the time, Pallas kernels for 0%

commit v1 on v0

v1 whole, which is shorter than its diff:
```python
import functools

import jax
import jax.numpy as jnp
from jax import lax
from jax.experimental import pallas as pl
from jax.experimental.pallas import tpu as pltpu
from jax.sharding import PartitionSpec as P

OMEGA = 0.6
SHIFT = 0.5
F32 = jnp.float32


def lroll(v, shift):
    return pltpu.roll(v, shift % v.shape[1], 1)


def sroll(v, shift):
    return pltpu.roll(v, shift % v.shape[0], 0)


def lanes(rows):
    return lax.broadcasted_iota(jnp.int32, (rows, 128), 1)


def sublanes(rows):
    return lax.broadcasted_iota(jnp.int32, (rows, 128), 0)


def row_mask(rows, first, count):
    place = sublanes(rows) + first
    return jnp.where((place >= 0) & (place < count), F32(1), F32(0))


def scalar_mask(place, count):
    return jnp.where((place >= 0) & (place < count), F32(1), F32(0))


def z_pair(v, lane, step):
    low = jnp.where(lane >= step, lroll(v, step), 0.0)
    high = jnp.where(lane < 128 - step, lroll(v, -step), 0.0)
    return low, high


def z_sum(v, lane, step):
    low, high = z_pair(v, lane, step)
    return low + high


def y_sum(v):
    return sroll(v, 1) + sroll(v, -1)


def inverse(w, scale, keep):
    real = 6.0 * scale - w
    imag = SHIFT * w
    factor = (OMEGA * keep) / (real * real + imag * imag)
    return real * factor, -imag * factor


def misfit(f, w, v, nb, scale):
    (fr, fi), (vr, vi), (nr, ni) = f, v, nb
    mr = fr - scale * (6.0 * vr - nr) + w * (vr + SHIFT * vi)
    mi = fi - scale * (6.0 * vi - ni) + w * (vi - SHIFT * vr)
    return mr, mi


def cmul(g, m):
    return g[0] * m[0] - g[1] * m[1], g[0] * m[1] + g[1] * m[0]


def repeat(low, high, step, unroll=1):
    def run(i, carry):
        step(i)
        return carry

    lax.fori_loop(low, high, run, 0, unroll=unroll)


class Window:
    def __init__(self, src, gain, scale, pad, neighbours):
        self.src, self.gain, self.scale, self.pad = src, gain, scale, pad
        self.neighbours = neighbours

    def start(self, row, keep, out):
        w = self.src[2, row]
        g = inverse(w, self.scale, keep)
        self.gain[0, row], self.gain[1, row] = g
        u = cmul(g, (self.src[0, row], self.src[1, row]))
        out[0, row + self.pad], out[1, row + self.pad] = u

    def misfit(self, row, field):
        at = row + self.pad
        v = (field[0, at], field[1, at])
        nb = tuple(self.neighbours(field, c, at, v[c]) for c in range(2))
        f = (self.src[0, row], self.src[1, row])
        return v, misfit(f, self.src[2, row], v, nb, self.scale)

    def relaxed(self, row, field):
        v, m = self.misfit(row, field)
        d = cmul((self.gain[0, row], self.gain[1, row]), m)
        return v[0] + d[0], v[1] + d[1]

    def relax(self, row, field, out):
        at = row + self.pad
        out[0, at], out[1, at] = self.relaxed(row, field)


def near0(lane, ref, c, at, v):
    return ref[c, at - 1] + ref[c, at + 1] + y_sum(v) + z_sum(v, lane, 1)


def near1(lane, ref, c, at, v):
    low = lroll(ref[c, at - 1] + v, -1)
    high = lroll(v + ref[c, at + 1], 1)
    return jnp.where(lane % 2 == 0, low, high) + y_sum(v) + z_sum(v, lane, 2)


def near2_sparse(lane, ref, c, at, v):
    return ref[c, at - 1] + ref[c, at + 1] + y_sum(v) + z_sum(v, lane, 4)


def near2(lane, ref, c, at, v):
    slot = lane % 4
    low = jnp.where(slot == 0, lroll(ref[c, at - 1], -3), lroll(v, 1))
    high = jnp.where(slot == 3, lroll(ref[c, at + 1], 3), lroll(v, -1))
    return low + high + y_sum(v) + z_sum(v, lane, 4)


def level0(src, gain, first, ix, iy):
    lane = lanes(24)
    win = Window(src, gain, 1.0, 0, functools.partial(near0, lane))
    inside = row_mask(24, iy * 16 - 3, 256)
    repeat(0, 22, lambda x: win.start(x, inside * scalar_mask(ix * 16 - 3 + x, 256), first), 2)
    return win, inside


def level1(src, gain, first, ix, iy):
    lane = lanes(24)
    win = Window(src, gain, 0.25, 1, functools.partial(near1, lane))
    inside = row_mask(24, iy * 8 - 8, 128)
    repeat(0, 10, lambda q: win.start(q, inside * scalar_mask(ix * 4 - 3 + q, 64), first), 2)
    return win, inside


def down0_kernel(idx, src, out, gain, ua, ub, tmp):
    ix, iy = idx[0], idx[1]
    win, _ = level0(src, gain, ua, ix, iy)
    repeat(2, 20, lambda x: win.relax(x, ua, ub), 2)
    lane = lanes(8)
    even = lane % 2 == 0

    def halve(q):
        rows = []
        for half in range(2):
            x = 4 * q + 3 + 2 * half
            _, m0 = win.misfit(x, ub)
            _, m1 = win.misfit(x + 1, ub)
            parts = (m0[0] + m1[0], m0[1] + m1[1], src[2, x] + src[2, x + 1])
            got = []
            for c in range(3):
                tmp[c, 2 * q + half] = parts[c]
                t = tmp[c, 2 * q + half, pl.ds(3, 8, 2)] + tmp[c, 2 * q + half, pl.ds(4, 8, 2)]
                got.append(0.125 * (t + lroll(t, -1)))
            rows.append(got)
        for c in range(3):
            out[c, q] = jnp.where(even, rows[0][c], lroll(rows[1][c], 1))

    repeat(0, 4, halve)


def down1_kernel(idx, src, out, gain, ua, ub, tmp, src2, gain2, va, vb):
    ix, iy = idx[0], idx[1]
    for buf in (ua, ub):
        for c in range(2):
            buf[c, 0] = jnp.zeros((24, 128), F32)
            buf[c, 11] = jnp.zeros((24, 128), F32)
    win, _ = level1(src, gain, ua, ix, iy)
    repeat(0, 10, lambda q: win.relax(q, ua, ub), 2)
    lane = lanes(8)

    def halve(q):
        _, m = win.misfit(q, ub)
        parts = (m[0], m[1], src[2, q])
        for c in range(3):
            t = parts[c] + lroll(parts[c], -1)
            tmp[c, q] = t + lroll(t, -2)
            src2[c, q - 1] = 0.125 * (tmp[c, q, pl.ds(4, 8, 2)] + tmp[c, q, pl.ds(5, 8, 2)])

    repeat(1, 9, halve)
    for buf in (va, vb):
        for c in range(2):
            buf[c, 0] = jnp.zeros((8, 128), F32)
            buf[c, 9] = jnp.zeros((8, 128), F32)
    win2 = Window(src2, gain2, 0.0625, 1, functools.partial(near2_sparse, lane))
    inside = row_mask(8, iy * 4 - 2, 64)
    for q in range(8):
        win2.start(q, inside * scalar_mask(ix * 4 - 2 + q, 64), va)
    for q in range(1, 7):
        win2.relax(q, va, vb)
    res = [win2.misfit(q, vb)[1] for q in range(2, 6)]
    for c in range(3):
        packed = jnp.where(lane % 4 == 0, src2[c, 2], 0.0)
        for j in range(1, 4):
            packed = packed + lroll(jnp.where(lane % 4 == 0, src2[c, 2 + j], 0.0), j)
        out[pl.ds(4 * c, 4), :] = packed[2:6]

    def third(low, high):
        t = low + high
        t = t + sroll(t, -1)
        t = 0.125 * (t + lroll(t, -4))
        return jnp.where(lane % 8 == 0, t, 0.0)

    def merged(values):
        return values[2:3] + lroll(values[4:5], 1)

    field = jnp.zeros((8, 128), F32)
    wave = jnp.zeros((8, 128), F32)
    for xl in range(2):
        for part in range(2):
            field = field + lroll(third(res[2 * xl][part], res[2 * xl + 1][part]), 4 * part + 2 * xl)
        t = third(src2[2, 2 + 2 * xl], src2[2, 3 + 2 * xl])
        wave = wave + lroll(t, 2 * xl) + lroll(t, 4 + 2 * xl)
    out[pl.ds(12, 1), :] = merged(field)
    out[pl.ds(13, 1), :] = merged(wave)
    out[pl.ds(14, 2), :] = jnp.zeros((2, 128), F32)


def swap(v, real):
    return jnp.where(real, lroll(v, -4), lroll(v, 4))


def up_kernel(
    idx, src0, src1, got, out,
    f3, w3, ga3, gb3, ua3, ub3, f4, w4, ga4, gb4, ua4, ub4, e3,
    src2, gain2, ua2, ub2, wide2, gain1, ua1, ub1, wide1, wide0, gain0, ua0, ub0,
):
    ix, iy = idx[0], idx[1]
    flat = got.reshape(16 * 96, 128)
    lane = lanes(16)
    real = lane // 4 % 2 == 0
    sign = jnp.where(real, F32(SHIFT), F32(-SHIFT))
    xlow = lane // 2 % 2 == 0
    ylow = lane % 2 == 0
    row = sublanes(16)
    zero16 = jnp.zeros((16, 128), F32)

    def y_pair(v):
        return jnp.where(row >= 1, sroll(v, 1), 0.0), jnp.where(row < 15, sroll(v, -1), 0.0)

    def packed_gain(w, scale):
        gr, gi = inverse(w, scale, 1.0)
        return gr, jnp.where(real, -gi, gi)

    def near3(ref, at, v):
        down, up = y_pair(v)
        xs = jnp.where(xlow, lroll(ref[at - 1] + v, -2), lroll(v + ref[at + 1], 2))
        ys = jnp.where(ylow, lroll(v + down, -1), lroll(v + up, 1))
        return xs + ys + z_sum(v, lane, 8)

    def near4(ref, at, v):
        down, up = y_pair(v)
        return ref[at - 1] + ref[at + 1] + down + up + z_sum(v, lane, 16)

    def make(f, w, ga, gb, scale, near):
        def start(x, out_ref):
            ga[x], gb[x] = packed_gain(w[x], scale)
            out_ref[x + 1] = ga[x] * f[x] + gb[x] * swap(f[x], real)

        def miss(x, ref):
            v = ref[x + 1]
            m = f[x] - scale * (6.0 * v - near(ref, x + 1, v)) + w[x] * (v + sign * swap(v, real))
            return v, m

        def relax(x, ref, out_ref):
            v, m = miss(x, ref)
            out_ref[x + 1] = v + ga[x] * m + gb[x] * swap(m, real)

        return start, miss, relax

    for buf in (ua3, ub3, ua4, ub4):
        buf[0] = zero16
        buf[17] = zero16

    for x in range(16):
        f3[x] = flat[pl.ds(2 * x, 16, 96), :]
        w3[x] = flat[pl.ds(2 * x + 1, 16, 96), :]
    start3, miss3, relax3 = make(f3, w3, ga3, gb3, 1.0 / 64, near3)
    start4, miss4, relax4 = make(f4, w4, ga4, gb4, 1.0 / 256, near4)
    repeat(0, 16, lambda x: start3(x, ua3), 4)
    repeat(0, 16, lambda x: relax3(x, ua3, ub3), 4)

    def eighth(v):
        v = v + lroll(v, -1)
        v = v + lroll(v, -2)
        return 0.125 * (v + lroll(v, -8))

    def halve3(x):
        f4[x] = eighth(miss3(x, ub3)[1])
        w4[x] = eighth(w3[x])
        start4(x, ua4)

    repeat(0, 16, halve3, 4)
    now, other = ua4, ub4
    for _ in range(5):
        repeat(0, 16, lambda x: relax4(x, now, other), 4)
        now, other = other, now
    total_m = zero16
    total_w = zero16
    for x in range(16):
        total_m = total_m + miss4(x, now)[1]
        total_w = total_w + w4[x]
    sum_r = jnp.sum(jnp.where(lane % 16 == 0, total_m, 0.0))
    sum_i = jnp.sum(jnp.where(lane % 16 == 4, total_m, 0.0))
    sum_w = jnp.sum(jnp.where(lane % 16 == 0, total_w, 0.0))
    numer = jnp.where(real, sum_r - SHIFT * sum_i, sum_i + SHIFT * sum_r)
    const = -numer / (jnp.full((16, 128), (1.0 + SHIFT * SHIFT), F32) * sum_w)

    keep4 = (lane % 16 == 0) | (lane % 16 == 4)
    zlow = lane // 8 % 2 == 0

    def spread4(x):
        t = jnp.where(keep4, now[x + 1] + const, 0.0)
        t = t + lroll(t, 1)
        t = t + lroll(t, 2)
        t = t + lroll(t, 8)
        low, high = z_pair(t, lane, 16)
        t = 0.75 * t + 0.25 * jnp.where(zlow, low, high)
        down, up = y_pair(t)
        other[x + 1] = 0.75 * t + 0.25 * jnp.where(ylow, down, up)

    repeat(0, 16, spread4, 4)

    def correct3(x):
        side = jnp.where(xlow, other[x], other[x + 2])
        ub3[x + 1] = ub3[x + 1] + 0.75 * other[x + 1] + 0.25 * side

    repeat(0, 16, correct3, 4)
    repeat(0, 16, lambda x: relax3(x, ub3, ua3), 4)
    for at in (0, 1, 2, 19, 20, 21):
        e3[at] = jnp.zeros((32, 128), F32)
    for at in range(3, 19):
        e3[at, pl.ds(0, 8), :] = jnp.zeros((8, 128), F32)
        e3[at, pl.ds(24, 8), :] = jnp.zeros((8, 128), F32)

    def finish3(x):
        relax3(x, ua3, ub3)
        e3[x + 3, pl.ds(8, 16), :] = ub3[x + 1]

    repeat(0, 16, finish3, 4)

    lane8 = lanes(8)
    lane24 = lanes(24)
    zero24 = jnp.zeros((24, 128), F32)
    for b in range(5):
        for c in range(3):
            src2[c, b] = zero24
    for g in range(5):
        other_y = lax.rem(iy + 14 + g, 16)
        for b in range(5):
            for c in range(3):
                src2[c, b, pl.ds(4 * g, 4), :] = got[other_y, pl.ds(32 + 12 * b + 4 * c, 4), :]
    for buf in (ua2, ub2):
        for c in range(2):
            buf[c, 0] = zero24
            buf[c, 6] = zero24
    win2 = Window(src2, gain2, 0.0625, 1, functools.partial(near2, lane24))
    inside2 = row_mask(24, iy * 4 - 8, 64)
    keep2 = [inside2 * scalar_mask(ix - 2 + b, 16) for b in range(5)]
    for b in range(5):
        win2.start(b, keep2[b], ua2)
    for b in range(5):
        win2.relax(b, ua2, ub2)
    near = [e3[ix + bb, pl.ds(iy + 5, 8), :] for bb in range(7)]
    xl3 = lane8 // 2 % 2
    a_low = lane8 % 2 == 0
    b_low = lane8 // 4 % 2 == 0
    for c in range(2):
        sides = []
        for yl in range(2):
            pick = (lane8 // 4 % 2 == c) & (lane8 % 2 == yl)
            cells = []
            for v in near:
                t = jnp.where(pick, v, 0.0)
                t = t + lroll(t, 1 - 2 * yl)
                t = t + lroll(t, 4 - 8 * c)
                low, high = z_pair(t, lane8, 8)
                cells.append(0.75 * t + 0.25 * jnp.where(b_low, low, high))
            blocks = []
            for b in range(1, 6):
                low = lroll(jnp.where(a_low, cells[b - 1], cells[b]), -2)
                high = lroll(jnp.where(a_low, cells[b], cells[b + 1]), 2)
                blocks.append(0.75 * cells[b] + 0.25 * jnp.where(xl3 == 0, low, high))
            sides.append(blocks)
        for b in range(5):
            t0, t1 = sides[0][b], sides[1][b]
            wide2[c, b, pl.ds(0, 8, 4), :] = 0.75 * t0 + 0.25 * sroll(t1, 1)
            wide2[c, b, pl.ds(1, 8, 4), :] = 0.75 * t0 + 0.25 * t1
            wide2[c, b, pl.ds(2, 8, 4), :] = 0.75 * t1 + 0.25 * t0
            wide2[c, b, pl.ds(3, 8, 4), :] = 0.75 * t1 + 0.25 * sroll(t0, -1)
            fix = wide2[c, b, pl.ds(4, 24), :]
            ub2[c, b + 1] = ub2[c, b + 1] + jnp.where(keep2[b] > 0, fix, 0.0)
    for b in range(5):
        win2.relax(b, ub2, ua2)
    for b in range(1, 4):
        win2.relax(b, ua2, ub2)

    for buf in (ua1, ub1):
        for c in range(2):
            buf[c, 0] = zero24
            buf[c, 11] = zero24
    win1, inside1 = level1(src1, gain1, ua1, ix, iy)
    repeat(0, 10, lambda q: win1.relax(q, ua1, ub1), 2)
    slot4 = lane24 % 4
    for c in range(2):
        cells = []
        for at in range(12):
            b, xl = 1 + at // 4, at % 4
            t = jnp.where(slot4 == xl, ub2[c, b + 1], 0.0)
            t = lroll(t, -xl) if xl else t
            t = t + lroll(t, 1)
            t = t + lroll(t, 2)
            low, high = z_pair(t, lane24, 4)
            cells.append(0.75 * t + 0.25 * jnp.where(slot4 < 2, low, high))
        for q in range(10):
            side = jnp.where(lane24 % 2 == 0, cells[q], cells[q + 2])
            t = 0.75 * cells[q + 1] + 0.25 * side
            wide1[c, q, pl.ds(0, 24, 2), :] = 0.75 * t + 0.25 * sroll(t, 1)
            wide1[c, q, pl.ds(1, 24, 2), :] = 0.75 * t + 0.25 * sroll(t, -1)
            keep = inside1 * scalar_mask(ix * 4 - 3 + q, 64)
            fix = wide1[c, q, pl.ds(8, 24), :]
            ub1[c, q + 1] = ub1[c, q + 1] + jnp.where(keep > 0, fix, 0.0)
    repeat(0, 10, lambda q: win1.relax(q, ub1, ua1), 2)
    repeat(1, 9, lambda q: win1.relax(q, ua1, ub1), 2)

    win0, inside0 = level0(src0, gain0, ua0, ix, iy)
    repeat(1, 21, lambda x: win0.relax(x, ua0, ub0), 2)
    for c in range(2):
        for x in (0, 21):
            ub0[c, x] = zero24

    def widen(q):
        for c in range(2):
            t = ub1[c, q + 1]
            even = jnp.where(lane24 % 2 == 0, t, lroll(t, 1))
            odd = jnp.where(lane24 % 2 == 0, lroll(t, -1), t)
            for p, v in ((0, even), (1, odd)):
                low, high = z_pair(v, lane24, 2)
                v = 0.75 * v + 0.25 * jnp.where(lane24 % 2 == 0, low, high)
                wide0[c, 2 * q + p, pl.ds(0, 24, 2), :] = 0.75 * v + 0.25 * sroll(v, 1)
                wide0[c, 2 * q + p, pl.ds(1, 24, 2), :] = 0.75 * v + 0.25 * sroll(v, -1)

    repeat(2, 8, widen)

    def correct0(at):
        for c in range(2):
            low = wide0[c, at - 1, pl.ds(13, 24), :]
            mid = wide0[c, at, pl.ds(13, 24), :]
            high = wide0[c, at + 1, pl.ds(13, 24), :]
            for child, side in ((0, low), (1, high)):
                x = 2 * at - 9 + child
                keep = inside0 * scalar_mask(ix * 16 - 3 + x, 256)
                fix = 0.75 * mid + 0.25 * side
                ub0[c, x] = ub0[c, x] + jnp.where(keep > 0, fix, 0.0)

    repeat(5, 15, correct0)
    repeat(2, 20, lambda x: win0.relax(x, ub0, ua0), 2)

    def finish0(x):
        ur, ui = win0.relaxed(x + 3, ua0)
        ub0[0, x + 3], ub0[1, x + 3] = ur, ui
        out[0, x] = ub0[0, x + 3, pl.ds(3, 16), :]
        out[1, x] = ub0[1, x + 3, pl.ds(3, 16), :]

    repeat(0, 16, finish0, 2)


def call(kernel, name, out_shape, scratch, *args):
    vmem = pl.BlockSpec(memory_space=pltpu.VMEM)
    return pl.pallas_call(
        kernel,
        name=name,
        out_shape=jax.ShapeDtypeStruct(out_shape, F32),
        in_specs=[pl.BlockSpec(memory_space=pltpu.SMEM)] + [vmem] * (len(args) - 1),
        out_specs=vmem,
        scratch_shapes=[pltpu.VMEM(shape, F32) for shape in scratch],
        compiler_params=pltpu.CompilerParams(vmem_limit_bytes=40 * 1024 * 1024),
    )(*args)


def send(value, axis, step):
    count = lax.axis_size(axis)
    return lax.ppermute(value, axis, [(i, (i + step) % count) for i in range(count)])


def share(value, axis):
    count = lax.axis_size(axis)
    return lax.all_to_all(jnp.broadcast_to(value[None], (count,) + value.shape), axis, 0, 0)


def body(residual_in, wave_sq):
    ix = lax.axis_index("gx")
    iy = lax.axis_index("gy")
    idx = jnp.stack([ix, iy]).astype(jnp.int32)

    own = jnp.concatenate([residual_in, wave_sq[None]], axis=0)
    low = send(own[:, 13:], "gx", 1)
    high = send(own[:, :3], "gx", -1)
    strip = jnp.concatenate([low, own, high], axis=1)
    low = send(strip[:, :, 13:].transpose(0, 2, 1, 3).reshape(9, 22, 128), "gy", 1)
    high = send(strip[:, :, :3].transpose(0, 2, 1, 3).reshape(9, 22, 128), "gy", -1)
    low = low.reshape(3, 3, 22, 128).transpose(0, 2, 1, 3)
    high = high.reshape(3, 3, 22, 128).transpose(0, 2, 1, 3)
    src0 = jnp.concatenate([low, strip, high, jnp.zeros((3, 22, 2, 128), F32)], axis=2)

    n0 = (2, 22, 24, 128)
    n1 = (2, 12, 24, 128)
    own1 = call(
        down0_kernel, "down0", (3, 4, 8, 128), [n0, n0, n0, (3, 8, 24, 128)], idx, src0
    )
    low = send(own1[:, 1:], "gx", 1)
    high = send(own1[:, :3], "gx", -1)
    strip = jnp.concatenate([low, own1, high], axis=1)
    low = send(strip, "gy", 1)
    high = send(strip, "gy", -1)
    src1 = jnp.concatenate([low, strip, high], axis=2)

    part = call(
        down1_kernel,
        "down1",
        (16, 128),
        [(2, 10, 24, 128), n1, n1, (3, 10, 24, 128)]
        + [(3, 8, 8, 128), (2, 8, 8, 128), (2, 10, 8, 128), (2, 10, 8, 128)],
        idx,
        src1,
    )
    line = share(part, "gx")
    ring = jnp.concatenate([line[14:], line, line[:2]], axis=0)
    blocks = lax.dynamic_slice(ring, (ix, 0, 0), (5, 12, 128))
    mine = jnp.concatenate(
        [line[:, 12:14].reshape(32, 128), blocks.reshape(60, 128), jnp.zeros((4, 128), F32)], axis=0
    )
    got = share(mine, "gy")

    one = (16, 16, 128)
    two = (18, 16, 128)
    return call(
        up_kernel,
        "up",
        (2, 16, 16, 128),
        [one, one, one, one, two, two, one, one, one, one, two, two, (22, 32, 128)]
        + [(3, 5, 24, 128), (2, 5, 24, 128), (2, 7, 24, 128), (2, 7, 24, 128), (2, 5, 32, 128)]
        + [(2, 10, 24, 128), n1, n1, (2, 10, 48, 128), (2, 16, 48, 128), n0, n0, n0],
        idx,
        src0,
        src1,
        got,
    )


def solution(mesh):
    placed = (P(None, "gx", "gy", None), P("gx", "gy", None))
    return jax.shard_map(
        body, mesh=mesh, in_specs=placed, out_specs=P(None, "gx", "gy", None), check_vma=False
    )
```

time: 607 us -> 99.4 us (0.16)
  the two profiles are of different devices: /device:TPU:130 before, /device:TPU:1 now
where the time goes in v1:
time: 99.4 us; the launch traced here: 99.2 us
  Pallas kernels  29.4 us (30%)
  waiting for transfers between devices  26.8 us (27%)
  starting transfers between devices  23.8 us (24%)
  blocking collectives  16.7 us (17%)
  other arithmetic  1.36 us (1%)
  local copies, waits for them, and re-layouts  1.03 us (1%)
    pallas_call x3, Pallas kernels, call(): pl.pallas_call(kernel, name=name, out_shape=jax.ShapeDtypeStruct(out_shap...  29.4 us
    ppermute x8, waiting for transfers between devices, send(): lax.ppermute(value, axis, [(i, (i + step) % count) for i in range(count)])  17.7 us
    all_to_all x1, blocking collectives, share(): lax.all_to_all(jnp.broadcast_to(value[None], (count,) + value.shape), axi...  16.7 us
    ppermute x8, starting transfers between devices, send(): lax.ppermute(value, axis, [(i, (i + step) % count) for i in range(count)])  13.3 us
    all_to_all x1, starting transfers between devices, share(): lax.all_to_all(jnp.broadcast_to(value[None], (count,) + value.shape), axi...  10.5 us
    all_to_all x1, waiting for transfers between devices, share(): lax.all_to_all(jnp.broadcast_to(value[None], (count,) + value.shape), axi...  9.09 us
  transfers between devices with their start and end apart: 9, of which 9 were waited for; matrix products, arithmetic and copies ran while one was open for 0% of the time, Pallas kernels for 0%

profile of v1, /device:TPU:1, one launch (start us, length us, event | category | flops | bytes accessed | tf_op | source)
XLA Modules:
  0.0 99.2 jit_solution(1076514264347184039)
XLA Ops:
  0.0 0.0 copy-start
  0.0 0.0 copy-start.1
  0.0 0.9 pad_maximum_fusion.6
  0.9 3.0 %collective-permute-start = (f32[3,3,16,128]{3,2,1,0:T(8,128)S(1)}, f32[3,3,16,128]{3,2,1,0:T(8,128)S(1)}, u32[]{:S(2)}, u32[]{:S(2)}) collective-permute-start(f32[3,3,16,128]{3,2,1,0:T(8,128)S(1)} %get-tuple-element.7), channel_id=1, source_target_pairs={{0,16},{16,32},{32,48},{48,64},{64,80},{80,96},{96,112},{112,128},... | collective-permute-start | bytes 221192 | tf_op jit(solution)/shard_map/ppermute | solution.py:494
  4.0 0.2 collective-permute-start.1
  4.2 0.1 pad.20.clone
  4.3 1.1 %collective-permute-done = f32[3,3,16,128]{3,2,1,0:T(8,128)S(1)} collective-permute-done((f32[3,3,16,128]{3,2,1,0:T(8,128)S(1)}, f32[3,3,16,128]{3,2,1,0:T(8,128)S(1)}, u32[]{:S(2)}, u32[]{:S(2)}) %collective-permute-start) | collective-permute-done | bytes 73760 | tf_op jit(solution)/shard_map/ppermute | solution.py:494
  5.4 2.4 %collective-permute-done.1 = f32[3,3,16,128]{3,2,1,0:T(8,128)S(1)} collective-permute-done((f32[3,3,16,128]{3,2,1,0:T(8,128)S(1)}, f32[3,3,16,128]{3,2,1,0:T(8,128)S(1)}, u32[]{:S(2)}, u32[]{:S(2)}) %collective-permute-start.1) | collective-permute-done | bytes 73760 | tf_op jit(solution)/shard_map/ppermute | solution.py:494
  7.7 0.0 copy-done
  7.7 0.0 copy-done.1
  7.8 5.0 %collective-permute-start.3 = (f32[9,22,128]{2,1,0:T(8,128)S(1)}, f32[9,22,128]{2,1,0:T(8,128)S(1)}, u32[]{:S(2)}, u32[]{:S(2)}) collective-permute-start(f32[9,22,128]{2,1,0:T(8,128)S(1)} %bitcast.25), channel_id=1, source_target_pairs={{0,15},{1,0},{2,1},{3,2},{4,3},{5,4},{6,5},{7,6},{8,7},{9,8},{10,9... | collective-permute-start | bytes 304136 | tf_op jit(solution)/shard_map/ppermute | solution.py:494
  12.8 0.0 collective-permute-start.2
  12.9 0.1 pad_add_fusion.idx
  12.9 1.7 %collective-permute-done.3 = f32[9,22,128]{2,1,0:T(8,128)S(1)} collective-permute-done((f32[9,22,128]{2,1,0:T(8,128)S(1)}, f32[9,22,128]{2,1,0:T(8,128)S(1)}, u32[]{:S(2)}, u32[]{:S(2)}) %collective-permute-start.3) | collective-permute-done | bytes 101408 | tf_op jit(solution)/shard_map/ppermute | solution.py:494
  14.6 5.1 %collective-permute-done.2 = f32[9,22,128]{2,1,0:T(8,128)S(1)} collective-permute-done((f32[9,22,128]{2,1,0:T(8,128)S(1)}, f32[9,22,128]{2,1,0:T(8,128)S(1)}, u32[]{:S(2)}, u32[]{:S(2)}) %collective-permute-start.2) | collective-permute-done | bytes 101408 | tf_op jit(solution)/shard_map/ppermute | solution.py:494
  19.8 0.2 maximum_maximum_fusion.src.src0
  20.0 2.7 %down0.1 = f32[3,4,8,128]{3,2,1,0:T(8,128)S(1)} custom-call(s32[2]{0:T(128)S(1)} %pad_add_fusion.idx, f32[3,22,24,128]{3,2,1,0:T(8,128)S(1)} %maximum_maximum_fusion.src.src0), custom_call_target="tpu_custom_call" | custom-call | tf_op jit(solution)/shard_map/down0/pallas_call | solution.py:481
  22.7 1.9 %collective-permute-start.4 = (f32[3,3,8,128]{3,2,1,0:T(8,128)S(1)}, f32[3,3,8,128]{3,2,1,0:T(8,128)S(1)}, u32[]{:S(2)}, u32[]{:S(2)}) collective-permute-start(f32[3,3,8,128]{3,2,1,0:T(8,128)S(1)} %get-tuple-element.11), channel_id=1, source_target_pairs={{0,16},{16,32},{32,48},{48,64},{64,80},{80,96},{96,112},{112,128},... | collective-permute-start | bytes 110600 | tf_op jit(solution)/shard_map/ppermute | solution.py:494
  24.6 1.6 %collective-permute-start.5 = (f32[3,3,8,128]{3,2,1,0:T(8,128)S(1)}, f32[3,3,8,128]{3,2,1,0:T(8,128)S(1)}, u32[]{:S(2)}, u32[]{:S(2)}) collective-permute-start(f32[3,3,8,128]{3,2,1,0:T(8,128)S(1)} %get-tuple-element.12), channel_id=1, source_target_pairs={{0,240},{16,0},{32,16},{48,32},{64,48},{80,64},{96,80},{112,96},{1... | collective-permute-start | bytes 110600 | tf_op jit(solution)/shard_map/ppermute | solution.py:494
  26.2 0.7 collective-permute-done.4
  26.9 1.1 %collective-permute-done.5 = f32[3,3,8,128]{3,2,1,0:T(8,128)S(1)} collective-permute-done((f32[3,3,8,128]{3,2,1,0:T(8,128)S(1)}, f32[3,3,8,128]{3,2,1,0:T(8,128)S(1)}, u32[]{:S(2)}, u32[]{:S(2)}) %collective-permute-start.5) | collective-permute-done | bytes 36896 | tf_op jit(solution)/shard_map/ppermute | solution.py:494
  28.0 0.1 collective-permute-start.7
  28.1 1.5 %collective-permute-start.6 = (f32[3,10,8,128]{3,2,1,0:T(8,128)S(1)}, f32[3,10,8,128]{3,2,1,0:T(8,128)S(1)}, u32[]{:S(2)}, u32[]{:S(2)}) collective-permute-start(f32[3,10,8,128]{3,2,1,0:T(8,128)S(1)} %pad_maximum_fusion.4), channel_id=1, source_target_pairs={{0,1},{1,2},{2,3},{3,4},{4,5},{5,6},{6,7},{7,8},{8,9},{9,10},{10,1... | collective-permute-start | bytes 368648 | tf_op jit(solution)/shard_map/ppermute | solution.py:494
  29.5 2.3 %collective-permute-done.7 = f32[3,10,8,128]{3,2,1,0:T(8,128)S(1)} collective-permute-done((f32[3,10,8,128]{3,2,1,0:T(8,128)S(1)}, f32[3,10,8,128]{3,2,1,0:T(8,128)S(1)}, u32[]{:S(2)}, u32[]{:S(2)}) %collective-permute-start.7) | collective-permute-done | bytes 122912 | tf_op jit(solution)/shard_map/ppermute | solution.py:494
  31.8 3.4 %collective-permute-done.6 = f32[3,10,8,128]{3,2,1,0:T(8,128)S(1)} collective-permute-done((f32[3,10,8,128]{3,2,1,0:T(8,128)S(1)}, f32[3,10,8,128]{3,2,1,0:T(8,128)S(1)}, u32[]{:S(2)}, u32[]{:S(2)}) %collective-permute-start.6) | collective-permute-done | bytes 122912 | tf_op jit(solution)/shard_map/ppermute | solution.py:494
  35.2 3.7 %down1.1 = f32[16,128]{1,0:T(8,128)S(1)} custom-call(s32[2]{0:T(128)S(1)} %pad_add_fusion.idx, f32[3,10,24,128]{3,2,1,0:T(8,128)S(1)} %pad_maximum_fusion.src.src1), custom_call_target="tpu_custom_call" | custom-call | tf_op jit(solution)/shard_map/down1/pallas_call | solution.py:481
  38.9 0.7 broadcast_in_dim.23
  39.6 10.5 %all-to-all-start = ((f32[16,16,128]{2,1,0:T(8,128)}), f32[16,16,128]{2,1,0:T(8,128)S(1)}, u32[]{:S(2)}, u32[]{:S(2)}) async-start(f32[16,16,128]{2,1,0:T(8,128)} %broadcast_in_dim.23), calls=%async_computation | async-start | bytes 262144 | tf_op jit(solution)/shard_map/all_to_all | solution.py:499
  50.1 0.1 pad.2.clone
  50.2 9.1 %all-to-all-done = f32[16,16,128]{2,1,0:T(8,128)S(1)} async-done(((f32[16,16,128]{2,1,0:T(8,128)}), f32[16,16,128]{2,1,0:T(8,128)S(1)}, u32[]{:S(2)}, u32[]{:S(2)}) %all-to-all-start) | async-done | bytes 131104 | tf_op jit(solution)/shard_map/all_to_all | solution.py:499
  59.3 0.1 maximum_maximum_fusion.1
  59.4 0.1 broadcast_in_dim.25
  59.5 16.7 %all_to_all.10.got = f32[16,96,128]{2,1,0:T(8,128)S(1)} all-to-all(f32[16,96,128]{2,1,0:T(8,128)S(1)} %broadcast_in_dim.25), channel_id=1, replica_groups=mesh['gx'=16,'gy'=16] {'gy'}, dimensions={0} | all-to-all | bytes 1572864 | tf_op jit(solution)/shard_map/all_to_all | solution.py:499
  76.2 23.0 %up.1 = f32[2,16,16,128]{3,2,1,0:T(8,128)} custom-call(s32[2]{0:T(128)S(1)} %pad_add_fusion.idx, f32[3,22,24,128]{3,2,1,0:T(8,128)S(1)} %maximum_maximum_fusion.src.src0, f32[3,10,24,128]{3,2,1,0:T(8,128)S(1)} %pad_maximum_fusion.src.src1, f32[16,96,128]{2,1,0:T(8,128)S(1)} %all_to_all.10.got), custom_call_target="tpu_custom_call" | custom-call | tf_op jit(solution)/shard_map/up/pallas_call | solution.py:481
  (14 shorter events, 0.2 us)
Async XLA Ops:
  0.0 7.7 %copy-start = (f32[2,16,16,128]{3,2,1,0:T(8,128)S(1)}, f32[2,16,16,128]{3,2,1,0:T(8,128)}, u32[]{:S(2)}) copy-start(f32[2,16,16,128]{3,2,1,0:T(8,128)} %param.2) | copy-start | bytes 786436
  0.0 7.7 %copy-start.1 = (f32[16,16,128]{2,1,0:T(8,128)S(1)}, f32[16,16,128]{2,1,0:T(8,128)}, u32[]{:S(2)}) copy-start(f32[16,16,128]{2,1,0:T(8,128)} %param.3) | copy-start | bytes 393220
  0.9 4.4 %collective-permute-start = (f32[3,3,16,128]{3,2,1,0:T(8,128)S(1)}, f32[3,3,16,128]{3,2,1,0:T(8,128)S(1)}, u32[]{:S(2)}, u32[]{:S(2)}) collective-permute-start(f32[3,3,16,128]{3,2,1,0:T(8,128)S(1)} %get-tuple-element.7), channel_id=1, source_target_pairs={{0,16},{16,32},{32,48},{48,64},{64,80},{80,96},{96,112},{112,128},... | collective-permute-start | bytes 221192 | tf_op jit(solution)/shard_map/ppermute | solution.py:494
  4.0 3.8 %collective-permute-start.1 = (f32[3,3,16,128]{3,2,1,0:T(8,128)S(1)}, f32[3,3,16,128]{3,2,1,0:T(8,128)S(1)}, u32[]{:S(2)}, u32[]{:S(2)}) collective-permute-start(f32[3,3,16,128]{3,2,1,0:T(8,128)S(1)} %get-tuple-element.8), channel_id=1, source_target_pairs={{0,240},{16,0},{32,16},{48,32},{64,48},{80,64},{96,80},{112,96},{1... | collective-permute-start | bytes 221192 | tf_op jit(solution)/shard_map/ppermute | solution.py:494
  7.8 6.8 %collective-permute-start.3 = (f32[9,22,128]{2,1,0:T(8,128)S(1)}, f32[9,22,128]{2,1,0:T(8,128)S(1)}, u32[]{:S(2)}, u32[]{:S(2)}) collective-permute-start(f32[9,22,128]{2,1,0:T(8,128)S(1)} %bitcast.25), channel_id=1, source_target_pairs={{0,15},{1,0},{2,1},{3,2},{4,3},{5,4},{6,5},{7,6},{8,7},{9,8},{10,9... | collective-permute-start | bytes 304136 | tf_op jit(solution)/shard_map/ppermute | solution.py:494
  12.8 6.9 %collective-permute-start.2 = (f32[9,22,128]{2,1,0:T(8,128)S(1)}, f32[9,22,128]{2,1,0:T(8,128)S(1)}, u32[]{:S(2)}, u32[]{:S(2)}) collective-permute-start(f32[9,22,128]{2,1,0:T(8,128)S(1)} %bitcast.23), channel_id=1, source_target_pairs={{0,1},{1,2},{2,3},{3,4},{4,5},{5,6},{6,7},{7,8},{8,9},{9,10},{10,1... | collective-permute-start | bytes 304136 | tf_op jit(solution)/shard_map/ppermute | solution.py:494
  22.7 4.2 %collective-permute-start.4 = (f32[3,3,8,128]{3,2,1,0:T(8,128)S(1)}, f32[3,3,8,128]{3,2,1,0:T(8,128)S(1)}, u32[]{:S(2)}, u32[]{:S(2)}) collective-permute-start(f32[3,3,8,128]{3,2,1,0:T(8,128)S(1)} %get-tuple-element.11), channel_id=1, source_target_pairs={{0,16},{16,32},{32,48},{48,64},{64,80},{80,96},{96,112},{112,128},... | collective-permute-start | bytes 110600 | tf_op jit(solution)/shard_map/ppermute | solution.py:494
  24.6 3.4 %collective-permute-start.5 = (f32[3,3,8,128]{3,2,1,0:T(8,128)S(1)}, f32[3,3,8,128]{3,2,1,0:T(8,128)S(1)}, u32[]{:S(2)}, u32[]{:S(2)}) collective-permute-start(f32[3,3,8,128]{3,2,1,0:T(8,128)S(1)} %get-tuple-element.12), channel_id=1, source_target_pairs={{0,240},{16,0},{32,16},{48,32},{64,48},{80,64},{96,80},{112,96},{1... | collective-permute-start | bytes 110600 | tf_op jit(solution)/shard_map/ppermute | solution.py:494
  28.0 3.8 %collective-permute-start.7 = (f32[3,10,8,128]{3,2,1,0:T(8,128)S(1)}, f32[3,10,8,128]{3,2,1,0:T(8,128)S(1)}, u32[]{:S(2)}, u32[]{:S(2)}) collective-permute-start(f32[3,10,8,128]{3,2,1,0:T(8,128)S(1)} %pad_maximum_fusion.4), channel_id=1, source_target_pairs={{0,15},{1,0},{2,1},{3,2},{4,3},{5,4},{6,5},{7,6},{8,7},{9,8},{10,9... | collective-permute-start | bytes 368648 | tf_op jit(solution)/shard_map/ppermute | solution.py:494
  28.1 7.1 %collective-permute-start.6 = (f32[3,10,8,128]{3,2,1,0:T(8,128)S(1)}, f32[3,10,8,128]{3,2,1,0:T(8,128)S(1)}, u32[]{:S(2)}, u32[]{:S(2)}) collective-permute-start(f32[3,10,8,128]{3,2,1,0:T(8,128)S(1)} %pad_maximum_fusion.4), channel_id=1, source_target_pairs={{0,1},{1,2},{2,3},{3,4},{4,5},{5,6},{6,7},{7,8},{8,9},{9,10},{10,1... | collective-permute-start | bytes 368648 | tf_op jit(solution)/shard_map/ppermute | solution.py:494
  39.6 19.7 %all-to-all-start = ((f32[16,16,128]{2,1,0:T(8,128)}), f32[16,16,128]{2,1,0:T(8,128)S(1)}, u32[]{:S(2)}, u32[]{:S(2)}) async-start(f32[16,16,128]{2,1,0:T(8,128)} %broadcast_in_dim.23), calls=%async_computation | async-start | bytes 262144 | tf_op jit(solution)/shard_map/all_to_all | solution.py:499

commit v2 on v1

--- a/solution.py
+++ b/solution.py
@@ -144,10 +144,13 @@
     return win, inside
 
 
-def down0_kernel(idx, src, out, gain, ua, ub, tmp):
+def down0_kernel(idx, src, out, gain, ub, ua, tmp):
     ix, iy = idx[0], idx[1]
     win, _ = level0(src, gain, ua, ix, iy)
-    repeat(2, 20, lambda x: win.relax(x, ua, ub), 2)
+    repeat(1, 21, lambda x: win.relax(x, ua, ub), 4)
+    for c in range(2):
+        for x in (0, 21):
+            ub[c, x] = jnp.zeros((24, 128), F32)
     lane = lanes(8)
     even = lane % 2 == 0
 
@@ -170,14 +173,14 @@
     repeat(0, 4, halve)
 
 
-def down1_kernel(idx, src, out, gain, ua, ub, tmp, src2, gain2, va, vb):
+def down1_kernel(idx, src, out, gain, ub, ua, tmp, src2, gain2, va, vb):
     ix, iy = idx[0], idx[1]
     for buf in (ua, ub):
         for c in range(2):
             buf[c, 0] = jnp.zeros((24, 128), F32)
             buf[c, 11] = jnp.zeros((24, 128), F32)
     win, _ = level1(src, gain, ua, ix, iy)
-    repeat(0, 10, lambda q: win.relax(q, ua, ub), 2)
+    repeat(0, 10, lambda q: win.relax(q, ua, ub), 5)
     lane = lanes(8)
 
     def halve(q):
@@ -232,9 +235,8 @@
 
 
 def up_kernel(
-    idx, src0, src1, got, out,
-    f3, w3, ga3, gb3, ua3, ub3, f4, w4, ga4, gb4, ua4, ub4, e3,
-    src2, gain2, ua2, ub2, wide2, gain1, ua1, ub1, wide1, wide0, gain0, ua0, ub0,
+    idx, src0, gain0, ub0, src1, gain1, ub1, got, out,
+    f3, w3, ga3, gb3, u3, f4, w4, s4, e3, src2, gain2, u2, wide2, cell1, u1, wide1, wide0, ua0, ub0s,
 ):
     ix, iy = idx[0], idx[1]
     flat = got.reshape(16 * 96, 128)
@@ -243,6 +245,8 @@
     sign = jnp.where(real, F32(SHIFT), F32(-SHIFT))
     xlow = lane // 2 % 2 == 0
     ylow = lane % 2 == 0
+    zlow = lane // 8 % 2 == 0
+    slot = lane % 4
     row = sublanes(16)
     zero16 = jnp.zeros((16, 128), F32)
 
@@ -253,102 +257,122 @@
         gr, gi = inverse(w, scale, 1.0)
         return gr, jnp.where(real, -gi, gi)
 
-    def near3(ref, at, v):
+    def packed_misfit(f, w, v, nb, scale):
+        return f - scale * (6.0 * v - nb) + w * (v + sign * swap(v, real))
+
+    for at in (0, 1, 2, 19, 20, 21):
+        for ref in (f3, w3, ga3, gb3):
+            ref[at] = zero16
+        for p in range(2):
+            u3[p, at] = zero16
+        e3[at] = jnp.zeros((32, 128), F32)
+    for at in range(3, 19):
+        e3[at, pl.ds(0, 8), :] = jnp.zeros((8, 128), F32)
+        e3[at, pl.ds(24, 8), :] = jnp.zeros((8, 128), F32)
+
+    def start3(x):
+        at = x + 3
+        f3[at] = flat[pl.ds(2 * x, 16, 96), :]
+        w = flat[pl.ds(2 * x + 1, 16, 96), :]
+        w3[at] = w
+        ga, gb = packed_gain(w, 1.0 / 64)
+        ga3[at], gb3[at] = ga, gb
+        u3[0, at] = ga * f3[at] + gb * swap(f3[at], real)
+
+    def miss3(p, at):
+        v = u3[p, at]
         down, up = y_pair(v)
-        xs = jnp.where(xlow, lroll(ref[at - 1] + v, -2), lroll(v + ref[at + 1], 2))
+        xs = jnp.where(xlow, lroll(u3[p, at - 1] + v, -2), lroll(v + u3[p, at + 1], 2))
         ys = jnp.where(ylow, lroll(v + down, -1), lroll(v + up, 1))
-        return xs + ys + z_sum(v, lane, 8)
-
-    def near4(ref, at, v):
-        down, up = y_pair(v)
-        return ref[at - 1] + ref[at + 1] + down + up + z_sum(v, lane, 16)
-
-    def make(f, w, ga, gb, scale, near):
-        def start(x, out_ref):
-            ga[x], gb[x] = packed_gain(w[x], scale)
-            out_ref[x + 1] = ga[x] * f[x] + gb[x] * swap(f[x], real)
-
-        def miss(x, ref):
-            v = ref[x + 1]
-            m = f[x] - scale * (6.0 * v - near(ref, x + 1, v)) + w[x] * (v + sign * swap(v, real))
-            return v, m
-
-        def relax(x, ref, out_ref):
-            v, m = miss(x, ref)
-            out_ref[x + 1] = v + ga[x] * m + gb[x] * swap(m, real)
-
-        return start, miss, relax
-
-    for buf in (ua3, ub3, ua4, ub4):
-        buf[0] = zero16
-        buf[17] = zero16
-
-    for x in range(16):
-        f3[x] = flat[pl.ds(2 * x, 16, 96), :]
-        w3[x] = flat[pl.ds(2 * x + 1, 16, 96), :]
-    start3, miss3, relax3 = make(f3, w3, ga3, gb3, 1.0 / 64, near3)
-    start4, miss4, relax4 = make(f4, w4, ga4, gb4, 1.0 / 256, near4)
-    repeat(0, 16, lambda x: start3(x, ua3), 4)
-    repeat(0, 16, lambda x: relax3(x, ua3, ub3), 4)
+        return v, packed_misfit(f3[at], w3[at], v, xs + ys + z_sum(v, lane, 8), 1.0 / 64)
+
+    def relax3(p, at):
+        v, m = miss3(p, at)
+        u3[1 - p, at] = v + ga3[at] * m + gb3[at] * swap(m, real)
+
+    repeat(0, 16, start3, 8)
+    repeat(3, 19, lambda at: relax3(0, at), 8)
+
+    first = (slot == 0) & zlow
 
     def eighth(v):
         v = v + lroll(v, -1)
         v = v + lroll(v, -2)
-        return 0.125 * (v + lroll(v, -8))
-
-    def halve3(x):
-        f4[x] = eighth(miss3(x, ub3)[1])
-        w4[x] = eighth(w3[x])
-        start4(x, ua4)
-
-    repeat(0, 16, halve3, 4)
-    now, other = ua4, ub4
-    for _ in range(5):
-        repeat(0, 16, lambda x: relax4(x, now, other), 4)
-        now, other = other, now
-    total_m = zero16
-    total_w = zero16
-    for x in range(16):
-        total_m = total_m + miss4(x, now)[1]
-        total_w = total_w + w4[x]
-    sum_r = jnp.sum(jnp.where(lane % 16 == 0, total_m, 0.0))
-    sum_i = jnp.sum(jnp.where(lane % 16 == 4, total_m, 0.0))
-    sum_w = jnp.sum(jnp.where(lane % 16 == 0, total_w, 0.0))
+        return jnp.where(first, 0.125 * (v + lroll(v, -8)), 0.0)
+
+    def halve3(r):
+        f, w = zero16, zero16
+        for k in range(4):
+            at = 4 * k + r + 3
+            fk, wk = eighth(miss3(1, at)[1]), eighth(w3[at])
+            f = f + (lroll(fk, k) if k else fk)
+            w = w + (lroll(wk, k) if k else wk)
+        f4[r], w4[r] = f, w
+
+    repeat(0, 4, halve3, 2)
+    fs = [f4[r] for r in range(4)]
+    ws = [w4[r] for r in range(4)]
+    gs = [packed_gain(w, 1.0 / 256) for w in ws]
+
+    def miss4(us):
+        low = jnp.where(slot >= 1, lroll(us[3], 1), 0.0)
+        high = jnp.where(slot < 3, lroll(us[0], -1), 0.0)
+        wide = [low, *us, high]
+        ms = []
+        for r in range(4):
+            down, up = y_pair(us[r])
+            nb = wide[r] + wide[r + 2] + down + up + z_sum(us[r], lane, 16)
+            ms.append(packed_misfit(fs[r], ws[r], us[r], nb, 1.0 / 256))
+        return ms
+
+    def relax4(_, us):
+        ms = miss4(us)
+        return tuple(u + g[0] * m + g[1] * swap(m, real) for u, g, m in zip(us, gs, ms))
+
+    us = tuple(g[0] * f + g[1] * swap(f, real) for g, f in zip(gs, fs))
+    us = lax.fori_loop(0, 5, relax4, us)
+    ms = miss4(us)
+    total_m = ms[0] + ms[1] + ms[2] + ms[3]
+    total_w = ws[0] + ws[1] + ws[2] + ws[3]
+    sum_r = jnp.sum(jnp.where(zlow & real, total_m, 0.0))
+    sum_i = jnp.sum(jnp.where(zlow & ~real, total_m, 0.0))
+    sum_w = jnp.sum(jnp.where(zlow & real, total_w, 0.0))
     numer = jnp.where(real, sum_r - SHIFT * sum_i, sum_i + SHIFT * sum_r)
     const = -numer / (jnp.full((16, 128), (1.0 + SHIFT * SHIFT), F32) * sum_w)
-
-    keep4 = (lane % 16 == 0) | (lane % 16 == 4)
-    zlow = lane // 8 % 2 == 0
-
-    def spread4(x):
-        t = jnp.where(keep4, now[x + 1] + const, 0.0)
+    for r in range(4):
+        s4[r] = jnp.where(zlow, us[r] + const, 0.0)
+
+    def spread4(j):
+        x = ix - 4 + j
+        inside = (x >= 0) & (x < 16)
+        x = jnp.clip(x, 0, 15)
+        k = x // 4
+        t = jnp.where((slot == k) & inside, s4[x - 4 * k], 0.0)
+        t = pltpu.roll(t, lax.rem(128 - k, 128), 1)
         t = t + lroll(t, 1)
         t = t + lroll(t, 2)
         t = t + lroll(t, 8)
         low, high = z_pair(t, lane, 16)
         t = 0.75 * t + 0.25 * jnp.where(zlow, low, high)
         down, up = y_pair(t)
-        other[x + 1] = 0.75 * t + 0.25 * jnp.where(ylow, down, up)
-
-    repeat(0, 16, spread4, 4)
-
-    def correct3(x):
-        side = jnp.where(xlow, other[x], other[x + 2])
-        ub3[x + 1] = ub3[x + 1] + 0.75 * other[x + 1] + 0.25 * side
-
-    repeat(0, 16, correct3, 4)
-    repeat(0, 16, lambda x: relax3(x, ub3, ua3), 4)
-    for at in (0, 1, 2, 19, 20, 21):
-        e3[at] = jnp.zeros((32, 128), F32)
-    for at in range(3, 19):
-        e3[at, pl.ds(0, 8), :] = jnp.zeros((8, 128), F32)
-        e3[at, pl.ds(24, 8), :] = jnp.zeros((8, 128), F32)
-
-    def finish3(x):
-        relax3(x, ua3, ub3)
-        e3[x + 3, pl.ds(8, 16), :] = ub3[x + 1]
-
-    repeat(0, 16, finish3, 4)
+        return 0.75 * t + 0.25 * jnp.where(ylow, down, up)
+
+    wide = [spread4(j) for j in range(9)]
+    for j in range(7):
+        at = ix + j
+        fix = 0.75 * wide[j + 1] + 0.25 * jnp.where(xlow, wide[j], wide[j + 2])
+        fix = jnp.where((at >= 3) & (at < 19), fix, 0.0)
+        u3[1, at] = u3[1, at] + fix
+
+    def sweep3(i):
+        for j in range(1, 6):
+            relax3(1 - i, ix + j)
+
+    repeat(0, 2, sweep3)
+    for j in range(1, 6):
+        e3[ix + j, pl.ds(8, 16), :] = u3[1, ix + j]
+    for j in (0, 6):
+        e3[ix + j] = jnp.zeros((32, 128), F32)
 
     lane8 = lanes(8)
     lane24 = lanes(24)
@@ -356,42 +380,45 @@
     for b in range(5):
         for c in range(3):
             src2[c, b] = zero24
-    for g in range(5):
+
+    def fetch(g):
         other_y = lax.rem(iy + 14 + g, 16)
         for b in range(5):
             for c in range(3):
                 src2[c, b, pl.ds(4 * g, 4), :] = got[other_y, pl.ds(32 + 12 * b + 4 * c, 4), :]
-    for buf in (ua2, ub2):
-        for c in range(2):
-            buf[c, 0] = zero24
-            buf[c, 6] = zero24
+
+    for g in range(5):
+        fetch(g)
+    for p in range(2):
+        for c in range(2):
+            u2[p, c, 0] = zero24
+            u2[p, c, 6] = zero24
     win2 = Window(src2, gain2, 0.0625, 1, functools.partial(near2, lane24))
     inside2 = row_mask(24, iy * 4 - 8, 64)
     keep2 = [inside2 * scalar_mask(ix - 2 + b, 16) for b in range(5)]
     for b in range(5):
-        win2.start(b, keep2[b], ua2)
-    for b in range(5):
-        win2.relax(b, ua2, ub2)
-    near = [e3[ix + bb, pl.ds(iy + 5, 8), :] for bb in range(7)]
-    xl3 = lane8 // 2 % 2
+        win2.start(b, keep2[b], u2.at[0])
     a_low = lane8 % 2 == 0
     b_low = lane8 // 4 % 2 == 0
-    for c in range(2):
+    x_low = lane8 // 2 % 2 == 0
+
+    def widen3(c):
         sides = []
+        shift = jnp.where(c == 0, 4, 124)
         for yl in range(2):
             pick = (lane8 // 4 % 2 == c) & (lane8 % 2 == yl)
             cells = []
-            for v in near:
-                t = jnp.where(pick, v, 0.0)
+            for bb in range(7):
+                t = jnp.where(pick, e3[ix + bb, pl.ds(iy + 5, 8), :], 0.0)
                 t = t + lroll(t, 1 - 2 * yl)
-                t = t + lroll(t, 4 - 8 * c)
+                t = t + pltpu.roll(t, shift, 1)
                 low, high = z_pair(t, lane8, 8)
                 cells.append(0.75 * t + 0.25 * jnp.where(b_low, low, high))
             blocks = []
             for b in range(1, 6):
                 low = lroll(jnp.where(a_low, cells[b - 1], cells[b]), -2)
                 high = lroll(jnp.where(a_low, cells[b], cells[b + 1]), 2)
-                blocks.append(0.75 * cells[b] + 0.25 * jnp.where(xl3 == 0, low, high))
+                blocks.append(0.75 * cells[b] + 0.25 * jnp.where(x_low, low, high))
             sides.append(blocks)
         for b in range(5):
             t0, t1 = sides[0][b], sides[1][b]
@@ -399,81 +426,98 @@
             wide2[c, b, pl.ds(1, 8, 4), :] = 0.75 * t0 + 0.25 * t1
             wide2[c, b, pl.ds(2, 8, 4), :] = 0.75 * t1 + 0.25 * t0
             wide2[c, b, pl.ds(3, 8, 4), :] = 0.75 * t1 + 0.25 * sroll(t0, -1)
-            fix = wide2[c, b, pl.ds(4, 24), :]
-            ub2[c, b + 1] = ub2[c, b + 1] + jnp.where(keep2[b] > 0, fix, 0.0)
-    for b in range(5):
-        win2.relax(b, ub2, ua2)
-    for b in range(1, 4):
-        win2.relax(b, ua2, ub2)
-
-    for buf in (ua1, ub1):
-        for c in range(2):
-            buf[c, 0] = zero24
-            buf[c, 11] = zero24
-    win1, inside1 = level1(src1, gain1, ua1, ix, iy)
-    repeat(0, 10, lambda q: win1.relax(q, ua1, ub1), 2)
-    slot4 = lane24 % 4
-    for c in range(2):
-        cells = []
-        for at in range(12):
-            b, xl = 1 + at // 4, at % 4
-            t = jnp.where(slot4 == xl, ub2[c, b + 1], 0.0)
-            t = lroll(t, -xl) if xl else t
-            t = t + lroll(t, 1)
-            t = t + lroll(t, 2)
-            low, high = z_pair(t, lane24, 4)
-            cells.append(0.75 * t + 0.25 * jnp.where(slot4 < 2, low, high))
-        for q in range(10):
-            side = jnp.where(lane24 % 2 == 0, cells[q], cells[q + 2])
-            t = 0.75 * cells[q + 1] + 0.25 * side
-            wide1[c, q, pl.ds(0, 24, 2), :] = 0.75 * t + 0.25 * sroll(t, 1)
-            wide1[c, q, pl.ds(1, 24, 2), :] = 0.75 * t + 0.25 * sroll(t, -1)
-            keep = inside1 * scalar_mask(ix * 4 - 3 + q, 64)
-            fix = wide1[c, q, pl.ds(8, 24), :]
-            ub1[c, q + 1] = ub1[c, q + 1] + jnp.where(keep > 0, fix, 0.0)
-    repeat(0, 10, lambda q: win1.relax(q, ub1, ua1), 2)
-    repeat(1, 9, lambda q: win1.relax(q, ua1, ub1), 2)
-
-    win0, inside0 = level0(src0, gain0, ua0, ix, iy)
-    repeat(1, 21, lambda x: win0.relax(x, ua0, ub0), 2)
-    for c in range(2):
-        for x in (0, 21):
-            ub0[c, x] = zero24
-
-    def widen(q):
-        for c in range(2):
-            t = ub1[c, q + 1]
-            even = jnp.where(lane24 % 2 == 0, t, lroll(t, 1))
-            odd = jnp.where(lane24 % 2 == 0, lroll(t, -1), t)
-            for p, v in ((0, even), (1, odd)):
-                low, high = z_pair(v, lane24, 2)
-                v = 0.75 * v + 0.25 * jnp.where(lane24 % 2 == 0, low, high)
-                wide0[c, 2 * q + p, pl.ds(0, 24, 2), :] = 0.75 * v + 0.25 * sroll(v, 1)
-                wide0[c, 2 * q + p, pl.ds(1, 24, 2), :] = 0.75 * v + 0.25 * sroll(v, -1)
-
-    repeat(2, 8, widen)
+
+    repeat(0, 2, widen3)
+
+    def sweep2(i):
+        now, later = lax.rem(i, 2), 1 - lax.rem(i, 2)
+        add = jnp.where(i == 0, F32(1), F32(0))
+        for b in range(5):
+            new = win2.relaxed(b, u2.at[now])
+            for c in range(2):
+                fix = wide2[c, b, pl.ds(4, 24), :] * (keep2[b] * add)
+                u2[later, c, b + 1] = new[c] + fix
+
+    repeat(0, 3, sweep2)
+
+    lane16 = lanes(16)
+    slot4 = lane16 % 4
+
+    def widen2(b):
+        for xl in range(4):
+            for c in range(2):
+                t = jnp.where(slot4 == xl, u2[1, c, b + 1, pl.ds(4, 16), :], 0.0)
+                t = lroll(t, -xl) if xl else t
+                t = t + lroll(t, 1)
+                t = t + lroll(t, 2)
+                low, high = z_pair(t, lane16, 4)
+                cell1[c, 4 * b - 4 + xl] = 0.75 * t + 0.25 * jnp.where(slot4 < 2, low, high)
+
+    repeat(1, 4, widen2)
+    lane_even = lane16 % 2 == 0
+
+    def mix2(q):
+        for c in range(2):
+            side = jnp.where(lane_even, cell1[c, q], cell1[c, q + 2])
+            t = 0.75 * cell1[c, q + 1] + 0.25 * side
+            wide1[c, q, pl.ds(0, 16, 2), :] = 0.75 * t + 0.25 * sroll(t, 1)
+            wide1[c, q, pl.ds(1, 16, 2), :] = 0.75 * t + 0.25 * sroll(t, -1)
+
+    repeat(0, 10, mix2, 5)
+    for p in range(2):
+        for c in range(2):
+            u1[p, c, 0] = zero24
+            u1[p, c, 11] = zero24
+    inside1 = row_mask(24, iy * 8 - 8, 128)
+
+    def correct1(q):
+        keep = inside1 * scalar_mask(ix * 4 - 3 + q, 64)
+        for c in range(2):
+            u1[0, c, q + 1] = ub1[c, q + 1] + wide1[c, q, pl.ds(0, 24), :] * keep
+
+    repeat(0, 10, correct1, 5)
+    win1 = Window(src1, gain1, 0.25, 1, functools.partial(near1, lane24))
+
+    def sweep1(i):
+        repeat(0, 10, lambda q: win1.relax(q, u1.at[i], u1.at[1 - i]), 5)
+
+    repeat(0, 2, sweep1)
+
+    def widen1(q):
+        for c in range(2):
+            t = u1[0, c, q + 1, pl.ds(5, 16), :]
+            up, down = lroll(t, 1), lroll(t, -1)
+            for p in range(2):
+                v = jnp.where(lane_even, t, up) if p == 0 else jnp.where(lane_even, down, t)
+                low, high = z_pair(v, lane16, 2)
+                v = 0.75 * v + 0.25 * jnp.where(lane_even, low, high)
+                wide0[c, 2 * q + p, pl.ds(0, 16, 2), :] = 0.75 * v + 0.25 * sroll(v, 1)
+                wide0[c, 2 * q + p, pl.ds(1, 16, 2), :] = 0.75 * v + 0.25 * sroll(v, -1)
+
+    repeat(2, 8, widen1, 2)
+    inside0 = row_mask(24, iy * 16 - 3, 256)
 
     def correct0(at):
         for c in range(2):
-            low = wide0[c, at - 1, pl.ds(13, 24), :]
-            mid = wide0[c, at, pl.ds(13, 24), :]
-            high = wide0[c, at + 1, pl.ds(13, 24), :]
+            low = wide0[c, at - 1, pl.ds(3, 24), :]
+            mid = wide0[c, at, pl.ds(3, 24), :]
+            high = wide0[c, at + 1, pl.ds(3, 24), :]
             for child, side in ((0, low), (1, high)):
                 x = 2 * at - 9 + child
                 keep = inside0 * scalar_mask(ix * 16 - 3 + x, 256)
-                fix = 0.75 * mid + 0.25 * side
-                ub0[c, x] = ub0[c, x] + jnp.where(keep > 0, fix, 0.0)
-
-    repeat(5, 15, correct0)
-    repeat(2, 20, lambda x: win0.relax(x, ub0, ua0), 2)
+                ua0[c, x] = ub0[c, x] + (0.75 * mid + 0.25 * side) * keep
+
+    repeat(5, 15, correct0, 2)
+    win0 = Window(src0, gain0, 1.0, 0, functools.partial(near0, lane24))
+    repeat(2, 20, lambda x: win0.relax(x, ua0, ub0s), 3)
 
     def finish0(x):
-        ur, ui = win0.relaxed(x + 3, ua0)
-        ub0[0, x + 3], ub0[1, x + 3] = ur, ui
-        out[0, x] = ub0[0, x + 3, pl.ds(3, 16), :]
-        out[1, x] = ub0[1, x + 3, pl.ds(3, 16), :]
-
-    repeat(0, 16, finish0, 2)
+        new = win0.relaxed(x + 3, ub0s)
+        for c in range(2):
+            ua0[c, x + 3] = new[c]
+            out[c, x] = ua0[c, x + 3, pl.ds(3, 16), :]
+
+    repeat(0, 16, finish0, 4)
 
 
 def call(kernel, name, out_shape, scratch, *args):
@@ -481,9 +525,9 @@
     return pl.pallas_call(
         kernel,
         name=name,
-        out_shape=jax.ShapeDtypeStruct(out_shape, F32),
+        out_shape=[jax.ShapeDtypeStruct(shape, F32) for shape in out_shape],
         in_specs=[pl.BlockSpec(memory_space=pltpu.SMEM)] + [vmem] * (len(args) - 1),
-        out_specs=vmem,
+        out_specs=[vmem] * len(out_shape),
         scratch_shapes=[pltpu.VMEM(shape, F32) for shape in scratch],
         compiler_params=pltpu.CompilerParams(vmem_limit_bytes=40 * 1024 * 1024),
     )(*args)
@@ -516,8 +560,8 @@
 
     n0 = (2, 22, 24, 128)
     n1 = (2, 12, 24, 128)
-    own1 = call(
-        down0_kernel, "down0", (3, 4, 8, 128), [n0, n0, n0, (3, 8, 24, 128)], idx, src0
+    own1, gain0, first0 = call(
+        down0_kernel, "down0", [(3, 4, 8, 128), n0, n0], [n0, (3, 8, 24, 128)], idx, src0
     )
     low = send(own1[:, 1:], "gx", 1)
     high = send(own1[:, :3], "gx", -1)
@@ -526,12 +570,11 @@
     high = send(strip, "gy", -1)
     src1 = jnp.concatenate([low, strip, high], axis=2)
 
-    part = call(
+    part, gain1, first1 = call(
         down1_kernel,
         "down1",
-        (16, 128),
-        [(2, 10, 24, 128), n1, n1, (3, 10, 24, 128)]
-        + [(3, 8, 8, 128), (2, 8, 8, 128), (2, 10, 8, 128), (2, 10, 8, 128)],
+        [(16, 128), (2, 10, 24, 128), n1],
+        [n1, (3, 10, 24, 128), (3, 8, 8, 128), (2, 8, 8, 128), (2, 10, 8, 128), (2, 10, 8, 128)],
         idx,
         src1,
     )
@@ -543,20 +586,24 @@
     )
     got = share(mine, "gy")
 
-    one = (16, 16, 128)
-    two = (18, 16, 128)
+    wide = (22, 16, 128)
     return call(
         up_kernel,
         "up",
-        (2, 16, 16, 128),
-        [one, one, one, one, two, two, one, one, one, one, two, two, (22, 32, 128)]
-        + [(3, 5, 24, 128), (2, 5, 24, 128), (2, 7, 24, 128), (2, 7, 24, 128), (2, 5, 32, 128)]
-        + [(2, 10, 24, 128), n1, n1, (2, 10, 48, 128), (2, 16, 48, 128), n0, n0, n0],
+        [(2, 16, 16, 128)],
+        [wide, wide, wide, wide, (2, 22, 16, 128)]
+        + [(4, 16, 128), (4, 16, 128), (4, 16, 128), (22, 32, 128)]
+        + [(3, 5, 24, 128), (2, 5, 24, 128), (2, 2, 7, 24, 128), (2, 5, 32, 128)]
+        + [(2, 12, 16, 128), (2, 2, 12, 24, 128), (2, 10, 32, 128), (2, 16, 32, 128), n0, n0],
         idx,
         src0,
+        gain0,
+        first0,
         src1,
+        gain1,
+        first1,
         got,
-    )
+    )[0]
 
 
 def solution(mesh):

time: 99.4 us -> 91.3 us (0.919)
  Pallas kernels: 29.4 us -> 21.4 us
    pallas_call x3, Pallas kernels: 29.4 us -> 21.4 us  [call(): pl.pallas_call(kernel, name=name, out_shape=[jax.ShapeDtypeStruct(shape,...]
where the time goes in v2:
time: 91.3 us; the launch traced here: 91.1 us
  waiting for transfers between devices  26.8 us (29%)
  starting transfers between devices  23.8 us (26%)
  Pallas kernels  21.4 us (23%)
  blocking collectives  16.7 us (18%)
  other arithmetic  1.35 us (1%)
  local copies, waits for them, and re-layouts  1.04 us (1%)
    pallas_call x3, Pallas kernels, call(): pl.pallas_call(kernel, name=name, out_shape=[jax.ShapeDtypeStruct(shape,...  21.4 us
    ppermute x8, waiting for transfers between devices, send(): lax.ppermute(value, axis, [(i, (i + step) % count) for i in range(count)])  17.7 us
    all_to_all x1, blocking collectives, share(): lax.all_to_all(jnp.broadcast_to(value[None], (count,) + value.shape), axi...  16.7 us
    ppermute x8, starting transfers between devices, send(): lax.ppermute(value, axis, [(i, (i + step) % count) for i in range(count)])  13.3 us
    all_to_all x1, starting transfers between devices, share(): lax.all_to_all(jnp.broadcast_to(value[None], (count,) + value.shape), axi...  10.5 us
    all_to_all x1, waiting for transfers between devices, share(): lax.all_to_all(jnp.broadcast_to(value[None], (count,) + value.shape), axi...  9.09 us
  transfers between devices with their start and end apart: 9, of which 9 were waited for; matrix products, arithmetic and copies ran while one was open for 0% of the time, Pallas kernels for 0%

profile of v2, /device:TPU:1, one launch (start us, length us, event | category | flops | bytes accessed | tf_op | source)
XLA Modules:
  0.0 91.1 jit_solution(3765191254263065350)
XLA Ops:
  0.0 0.0 copy-start
  0.0 0.0 copy-start.1
  0.0 0.9 %pad_maximum_fusion.5 = (f32[3,3,16,128]{3,2,1,0:T(8,128)S(1)}, f32[3,3,16,128]{3,2,1,0:T(8,128)S(1)}) fusion(f32[1,16,16,128]{3,2,1,0:T(8,128)} %bitcast.18, f32[2,16,16,128]{3,2,1,0:T(8,128)} %param.2), kind=kLoop, calls=%fused_computation.13 | loop fusion | flops 36864 | bytes 540672 | tf_op jit(solution)/shard_map/slice | solution.py:552
  0.9 3.0 %collective-permute-start = (f32[3,3,16,128]{3,2,1,0:T(8,128)S(1)}, f32[3,3,16,128]{3,2,1,0:T(8,128)S(1)}, u32[]{:S(2)}, u32[]{:S(2)}) collective-permute-start(f32[3,3,16,128]{3,2,1,0:T(8,128)S(1)} %get-tuple-element.19), channel_id=1, source_target_pairs={{0,16},{16,32},{32,48},{48,64},{64,80},{80,96},{96,112},{112,128},... | collective-permute-start | bytes 221192 | tf_op jit(solution)/shard_map/ppermute | solution.py:538
  4.0 0.2 collective-permute-start.1
  4.2 0.1 pad.15.clone
  4.3 1.1 %collective-permute-done = f32[3,3,16,128]{3,2,1,0:T(8,128)S(1)} collective-permute-done((f32[3,3,16,128]{3,2,1,0:T(8,128)S(1)}, f32[3,3,16,128]{3,2,1,0:T(8,128)S(1)}, u32[]{:S(2)}, u32[]{:S(2)}) %collective-permute-start) | collective-permute-done | bytes 73760 | tf_op jit(solution)/shard_map/ppermute | solution.py:538
  5.4 2.4 %collective-permute-done.1 = f32[3,3,16,128]{3,2,1,0:T(8,128)S(1)} collective-permute-done((f32[3,3,16,128]{3,2,1,0:T(8,128)S(1)}, f32[3,3,16,128]{3,2,1,0:T(8,128)S(1)}, u32[]{:S(2)}, u32[]{:S(2)}) %collective-permute-start.1) | collective-permute-done | bytes 73760 | tf_op jit(solution)/shard_map/ppermute | solution.py:538
  7.7 0.0 copy-done
  7.7 0.0 copy-done.1
  7.8 5.0 %collective-permute-start.3 = (f32[9,22,128]{2,1,0:T(8,128)S(1)}, f32[9,22,128]{2,1,0:T(8,128)S(1)}, u32[]{:S(2)}, u32[]{:S(2)}) collective-permute-start(f32[9,22,128]{2,1,0:T(8,128)S(1)} %bitcast.25), channel_id=1, source_target_pairs={{0,15},{1,0},{2,1},{3,2},{4,3},{5,4},{6,5},{7,6},{8,7},{9,8},{10,9... | collective-permute-start | bytes 304136 | tf_op jit(solution)/shard_map/ppermute | solution.py:538
  12.8 0.0 collective-permute-start.2
  12.9 0.1 pad_add_fusion.idx
  12.9 1.7 %collective-permute-done.3 = f32[9,22,128]{2,1,0:T(8,128)S(1)} collective-permute-done((f32[9,22,128]{2,1,0:T(8,128)S(1)}, f32[9,22,128]{2,1,0:T(8,128)S(1)}, u32[]{:S(2)}, u32[]{:S(2)}) %collective-permute-start.3) | collective-permute-done | bytes 101408 | tf_op jit(solution)/shard_map/ppermute | solution.py:538
  14.6 5.1 %collective-permute-done.2 = f32[9,22,128]{2,1,0:T(8,128)S(1)} collective-permute-done((f32[9,22,128]{2,1,0:T(8,128)S(1)}, f32[9,22,128]{2,1,0:T(8,128)S(1)}, u32[]{:S(2)}, u32[]{:S(2)}) %collective-permute-start.2) | collective-permute-done | bytes 101408 | tf_op jit(solution)/shard_map/ppermute | solution.py:538
  19.8 0.2 maximum_maximum_fusion.src.src0
  20.0 2.4 %down0.1 = (f32[3,4,8,128]{3,2,1,0:T(8,128)S(1)}, f32[2,22,24,128]{3,2,1,0:T(8,128)S(1)}, f32[2,22,24,128]{3,2,1,0:T(8,128)S(1)}) custom-call(s32[2]{0:T(128)S(1)} %pad_add_fusion.idx, f32[3,22,24,128]{3,2,1,0:T(8,128)S(1)} %maximum_maximum_fusion.src.src0), custom_call_target="tpu_custom_call" | custom-call | tf_op jit(solution)/shard_map/down0/pallas_call | solution.py:525
  22.4 1.9 %collective-permute-start.4 = (f32[3,3,8,128]{3,2,1,0:T(8,128)S(1)}, f32[3,3,8,128]{3,2,1,0:T(8,128)S(1)}, u32[]{:S(2)}, u32[]{:S(2)}) collective-permute-start(f32[3,3,8,128]{3,2,1,0:T(8,128)S(1)} %get-tuple-element.24), channel_id=1, source_target_pairs={{0,16},{16,32},{32,48},{48,64},{64,80},{80,96},{96,112},{112,128},... | collective-permute-start | bytes 110600 | tf_op jit(solution)/shard_map/ppermute | solution.py:538
  24.3 1.6 %collective-permute-start.5 = (f32[3,3,8,128]{3,2,1,0:T(8,128)S(1)}, f32[3,3,8,128]{3,2,1,0:T(8,128)S(1)}, u32[]{:S(2)}, u32[]{:S(2)}) collective-permute-start(f32[3,3,8,128]{3,2,1,0:T(8,128)S(1)} %get-tuple-element.23), channel_id=1, source_target_pairs={{0,240},{16,0},{32,16},{48,32},{64,48},{80,64},{96,80},{112,96},{1... | collective-permute-start | bytes 110600 | tf_op jit(solution)/shard_map/ppermute | solution.py:538
  25.9 0.7 collective-permute-done.4
  26.6 1.1 %collective-permute-done.5 = f32[3,3,8,128]{3,2,1,0:T(8,128)S(1)} collective-permute-done((f32[3,3,8,128]{3,2,1,0:T(8,128)S(1)}, f32[3,3,8,128]{3,2,1,0:T(8,128)S(1)}, u32[]{:S(2)}, u32[]{:S(2)}) %collective-permute-start.5) | collective-permute-done | bytes 36896 | tf_op jit(solution)/shard_map/ppermute | solution.py:538
  27.7 0.0 collective-permute-start.7
  27.7 1.5 %collective-permute-start.6 = (f32[3,10,8,128]{3,2,1,0:T(8,128)S(1)}, f32[3,10,8,128]{3,2,1,0:T(8,128)S(1)}, u32[]{:S(2)}, u32[]{:S(2)}) collective-permute-start(f32[3,10,8,128]{3,2,1,0:T(8,128)S(1)} %constant_dynamic-update-slice_fusion), channel_id=1, source_target_pairs={{0,1},{1,2},{2,3},{3,4},{4,5},{5,6},{6,7},{7,8},{8,9},{9,10},{10,1... | collective-permute-start | bytes 368648 | tf_op jit(solution)/shard_map/ppermute | solution.py:538
  29.2 2.3 %collective-permute-done.7 = f32[3,10,8,128]{3,2,1,0:T(8,128)S(1)} collective-permute-done((f32[3,10,8,128]{3,2,1,0:T(8,128)S(1)}, f32[3,10,8,128]{3,2,1,0:T(8,128)S(1)}, u32[]{:S(2)}, u32[]{:S(2)}) %collective-permute-start.7) | collective-permute-done | bytes 122912 | tf_op jit(solution)/shard_map/ppermute | solution.py:538
  31.4 3.4 %collective-permute-done.6 = f32[3,10,8,128]{3,2,1,0:T(8,128)S(1)} collective-permute-done((f32[3,10,8,128]{3,2,1,0:T(8,128)S(1)}, f32[3,10,8,128]{3,2,1,0:T(8,128)S(1)}, u32[]{:S(2)}, u32[]{:S(2)}) %collective-permute-start.6) | collective-permute-done | bytes 122912 | tf_op jit(solution)/shard_map/ppermute | solution.py:538
  34.9 3.4 %down1.1 = (f32[16,128]{1,0:T(8,128)S(1)}, f32[2,10,24,128]{3,2,1,0:T(8,128)S(1)}, f32[2,12,24,128]{3,2,1,0:T(8,128)S(1)}) custom-call(s32[2]{0:T(128)S(1)} %pad_add_fusion.idx, f32[3,10,24,128]{3,2,1,0:T(8,128)S(1)} %pad_maximum_fusion.src.src1), custom_call_target="tpu_custom_call" | custom-call | tf_op jit(solution)/shard_map/down1/pallas_call | solution.py:525
  38.3 0.7 broadcast_in_dim.23
  39.0 10.5 %all-to-all-start = ((f32[16,16,128]{2,1,0:T(8,128)}), f32[16,16,128]{2,1,0:T(8,128)S(1)}, u32[]{:S(2)}, u32[]{:S(2)}) async-start(f32[16,16,128]{2,1,0:T(8,128)} %broadcast_in_dim.23), calls=%async_computation | async-start | bytes 262144 | tf_op jit(solution)/shard_map/all_to_all | solution.py:543
  49.5 0.1 pad.2.clone
  49.6 9.1 %all-to-all-done = f32[16,16,128]{2,1,0:T(8,128)S(1)} async-done(((f32[16,16,128]{2,1,0:T(8,128)}), f32[16,16,128]{2,1,0:T(8,128)S(1)}, u32[]{:S(2)}, u32[]{:S(2)}) %all-to-all-start) | async-done | bytes 131104 | tf_op jit(solution)/shard_map/all_to_all | solution.py:543
  58.7 0.1 maximum_maximum_fusion.1
  58.8 0.1 broadcast_in_dim.25
  58.9 16.7 %all_to_all.10.got = f32[16,96,128]{2,1,0:T(8,128)S(1)} all-to-all(f32[16,96,128]{2,1,0:T(8,128)S(1)} %broadcast_in_dim.25), channel_id=1, replica_groups=mesh['gx'=16,'gy'=16] {'gy'}, dimensions={0} | all-to-all | bytes 1572864 | tf_op jit(solution)/shard_map/all_to_all | solution.py:543
  75.6 15.6 %up.1 = f32[2,16,16,128]{3,2,1,0:T(8,128)} custom-call(s32[2]{0:T(128)S(1)} %pad_add_fusion.idx, f32[3,22,24,128]{3,2,1,0:T(8,128)S(1)} %maximum_maximum_fusion.src.src0, f32[2,22,24,128]{3,2,1,0:T(8,128)S(1)} %get-tuple-element.11.gain0, f32[2,22,24,128]{3,2,1,0:T(8,128)S(1)} %get-tuple-element.12.ub0, f32[3,10,24,128]{3,2,1,0:T(8,128)S(1)} %pad_maximum_fusion.src.src1, ...), custom_call_target="tpu_custom_call" | custom-call | tf_op jit(solution)/shard_map/up/pallas_call | solution.py:525
  (16 shorter events, 0.2 us)
Async XLA Ops:
  0.0 7.7 %copy-start = (f32[2,16,16,128]{3,2,1,0:T(8,128)S(1)}, f32[2,16,16,128]{3,2,1,0:T(8,128)}, u32[]{:S(2)}) copy-start(f32[2,16,16,128]{3,2,1,0:T(8,128)} %param.2) | copy-start | bytes 786436
  0.0 7.7 %copy-start.1 = (f32[16,16,128]{2,1,0:T(8,128)S(1)}, f32[16,16,128]{2,1,0:T(8,128)}, u32[]{:S(2)}) copy-start(f32[16,16,128]{2,1,0:T(8,128)} %param.3) | copy-start | bytes 393220
  0.9 4.4 %collective-permute-start = (f32[3,3,16,128]{3,2,1,0:T(8,128)S(1)}, f32[3,3,16,128]{3,2,1,0:T(8,128)S(1)}, u32[]{:S(2)}, u32[]{:S(2)}) collective-permute-start(f32[3,3,16,128]{3,2,1,0:T(8,128)S(1)} %get-tuple-element.19), channel_id=1, source_target_pairs={{0,16},{16,32},{32,48},{48,64},{64,80},{80,96},{96,112},{112,128},... | collective-permute-start | bytes 221192 | tf_op jit(solution)/shard_map/ppermute | solution.py:538
  4.0 3.8 %collective-permute-start.1 = (f32[3,3,16,128]{3,2,1,0:T(8,128)S(1)}, f32[3,3,16,128]{3,2,1,0:T(8,128)S(1)}, u32[]{:S(2)}, u32[]{:S(2)}) collective-permute-start(f32[3,3,16,128]{3,2,1,0:T(8,128)S(1)} %get-tuple-element.20), channel_id=1, source_target_pairs={{0,240},{16,0},{32,16},{48,32},{64,48},{80,64},{96,80},{112,96},{1... | collective-permute-start | bytes 221192 | tf_op jit(solution)/shard_map/ppermute | solution.py:538
  7.8 6.8 %collective-permute-start.3 = (f32[9,22,128]{2,1,0:T(8,128)S(1)}, f32[9,22,128]{2,1,0:T(8,128)S(1)}, u32[]{:S(2)}, u32[]{:S(2)}) collective-permute-start(f32[9,22,128]{2,1,0:T(8,128)S(1)} %bitcast.25), channel_id=1, source_target_pairs={{0,15},{1,0},{2,1},{3,2},{4,3},{5,4},{6,5},{7,6},{8,7},{9,8},{10,9... | collective-permute-start | bytes 304136 | tf_op jit(solution)/shard_map/ppermute | solution.py:538
  12.8 6.9 %collective-permute-start.2 = (f32[9,22,128]{2,1,0:T(8,128)S(1)}, f32[9,22,128]{2,1,0:T(8,128)S(1)}, u32[]{:S(2)}, u32[]{:S(2)}) collective-permute-start(f32[9,22,128]{2,1,0:T(8,128)S(1)} %bitcast.23), channel_id=1, source_target_pairs={{0,1},{1,2},{2,3},{3,4},{4,5},{5,6},{6,7},{7,8},{8,9},{9,10},{10,1... | collective-permute-start | bytes 304136 | tf_op jit(solution)/shard_map/ppermute | solution.py:538
  22.4 4.2 %collective-permute-start.4 = (f32[3,3,8,128]{3,2,1,0:T(8,128)S(1)}, f32[3,3,8,128]{3,2,1,0:T(8,128)S(1)}, u32[]{:S(2)}, u32[]{:S(2)}) collective-permute-start(f32[3,3,8,128]{3,2,1,0:T(8,128)S(1)} %get-tuple-element.24), channel_id=1, source_target_pairs={{0,16},{16,32},{32,48},{48,64},{64,80},{80,96},{96,112},{112,128},... | collective-permute-start | bytes 110600 | tf_op jit(solution)/shard_map/ppermute | solution.py:538
  24.3 3.4 %collective-permute-start.5 = (f32[3,3,8,128]{3,2,1,0:T(8,128)S(1)}, f32[3,3,8,128]{3,2,1,0:T(8,128)S(1)}, u32[]{:S(2)}, u32[]{:S(2)}) collective-permute-start(f32[3,3,8,128]{3,2,1,0:T(8,128)S(1)} %get-tuple-element.23), channel_id=1, source_target_pairs={{0,240},{16,0},{32,16},{48,32},{64,48},{80,64},{96,80},{112,96},{1... | collective-permute-start | bytes 110600 | tf_op jit(solution)/shard_map/ppermute | solution.py:538
  27.7 3.7 %collective-permute-start.7 = (f32[3,10,8,128]{3,2,1,0:T(8,128)S(1)}, f32[3,10,8,128]{3,2,1,0:T(8,128)S(1)}, u32[]{:S(2)}, u32[]{:S(2)}) collective-permute-start(f32[3,10,8,128]{3,2,1,0:T(8,128)S(1)} %constant_dynamic-update-slice_fusion), channel_id=1, source_target_pairs={{0,15},{1,0},{2,1},{3,2},{4,3},{5,4},{6,5},{7,6},{8,7},{9,8},{10,9... | collective-permute-start | bytes 368648 | tf_op jit(solution)/shard_map/ppermute | solution.py:538
  27.7 7.1 %collective-permute-start.6 = (f32[3,10,8,128]{3,2,1,0:T(8,128)S(1)}, f32[3,10,8,128]{3,2,1,0:T(8,128)S(1)}, u32[]{:S(2)}, u32[]{:S(2)}) collective-permute-start(f32[3,10,8,128]{3,2,1,0:T(8,128)S(1)} %constant_dynamic-update-slice_fusion), channel_id=1, source_target_pairs={{0,1},{1,2},{2,3},{3,4},{4,5},{5,6},{6,7},{7,8},{8,9},{9,10},{10,1... | collective-permute-start | bytes 368648 | tf_op jit(solution)/shard_map/ppermute | solution.py:538
  39.0 19.7 %all-to-all-start = ((f32[16,16,128]{2,1,0:T(8,128)}), f32[16,16,128]{2,1,0:T(8,128)S(1)}, u32[]{:S(2)}, u32[]{:S(2)}) async-start(f32[16,16,128]{2,1,0:T(8,128)} %broadcast_in_dim.23), calls=%async_computation | async-start | bytes 262144 | tf_op jit(solution)/shard_map/all_to_all | solution.py:543

commit v3 on v2

--- a/solution.py
+++ b/solution.py
@@ -117,10 +117,6 @@
     return jnp.where(lane % 2 == 0, low, high) + y_sum(v) + z_sum(v, lane, 2)
 
 
-def near2_sparse(lane, ref, c, at, v):
-    return ref[c, at - 1] + ref[c, at + 1] + y_sum(v) + z_sum(v, lane, 4)
-
-
 def near2(lane, ref, c, at, v):
     slot = lane % 4
     low = jnp.where(slot == 0, lroll(ref[c, at - 1], -3), lroll(v, 1))
@@ -133,14 +129,6 @@
     win = Window(src, gain, 1.0, 0, functools.partial(near0, lane))
     inside = row_mask(24, iy * 16 - 3, 256)
     repeat(0, 22, lambda x: win.start(x, inside * scalar_mask(ix * 16 - 3 + x, 256), first), 2)
-    return win, inside
-
-
-def level1(src, gain, first, ix, iy):
-    lane = lanes(24)
-    win = Window(src, gain, 0.25, 1, functools.partial(near1, lane))
-    inside = row_mask(24, iy * 8 - 8, 128)
-    repeat(0, 10, lambda q: win.start(q, inside * scalar_mask(ix * 4 - 3 + q, 64), first), 2)
     return win, inside
 
 
@@ -173,61 +161,67 @@
     repeat(0, 4, halve)
 
 
-def down1_kernel(idx, src, out, gain, ub, ua, tmp, src2, gain2, va, vb):
+def down1_kernel(idx, src, out, src2, gain, ub, ua, tmp, gain2, va, vb):
     ix, iy = idx[0], idx[1]
+    lane24 = lanes(24)
+    zero24 = jnp.zeros((24, 128), F32)
     for buf in (ua, ub):
         for c in range(2):
-            buf[c, 0] = jnp.zeros((24, 128), F32)
-            buf[c, 11] = jnp.zeros((24, 128), F32)
-    win, _ = level1(src, gain, ua, ix, iy)
-    repeat(0, 10, lambda q: win.relax(q, ua, ub), 5)
-    lane = lanes(8)
-
-    def halve(q):
-        _, m = win.misfit(q, ub)
-        parts = (m[0], m[1], src[2, q])
+            buf[c, 0] = zero24
+            buf[c, 13] = zero24
+    win = Window(src, gain, 0.25, 1, functools.partial(near1, lane24))
+    inside = row_mask(24, iy * 8 - 8, 128)
+    repeat(0, 12, lambda q: win.start(q, inside * scalar_mask(ix * 4 - 4 + q, 64), ua), 4)
+    repeat(0, 12, lambda q: win.relax(q, ua, ub), 4)
+    lane = lanes(16)
+    corner = lane % 4 == 0
+
+    def halve(b):
+        for j in range(4):
+            q = 4 * b + j
+            _, m = win.misfit(q, ub)
+            parts = (m[0], m[1], src[2, q])
+            for c in range(3):
+                t = parts[c] + lroll(parts[c], -1)
+                tmp[c, q, pl.ds(0, 24), :] = t + lroll(t, -2)
+                tmp[c, q, pl.ds(24, 8), :] = jnp.zeros((8, 128), F32)
         for c in range(3):
-            t = parts[c] + lroll(parts[c], -1)
-            tmp[c, q] = t + lroll(t, -2)
-            src2[c, q - 1] = 0.125 * (tmp[c, q, pl.ds(4, 8, 2)] + tmp[c, q, pl.ds(5, 8, 2)])
-
-    repeat(1, 9, halve)
+            packed = jnp.zeros((16, 128), F32)
+            for j in range(4):
+                q = 4 * b + j
+                t = tmp[c, q, pl.ds(0, 16, 2), :] + tmp[c, q, pl.ds(1, 16, 2), :]
+                t = jnp.where(corner, 0.125 * t, 0.0)
+                packed = packed + (lroll(t, j) if j else t)
+            src2[c, b] = packed
+
+    repeat(0, 3, halve)
     for buf in (va, vb):
         for c in range(2):
-            buf[c, 0] = jnp.zeros((8, 128), F32)
-            buf[c, 9] = jnp.zeros((8, 128), F32)
-    win2 = Window(src2, gain2, 0.0625, 1, functools.partial(near2_sparse, lane))
-    inside = row_mask(8, iy * 4 - 2, 64)
-    for q in range(8):
-        win2.start(q, inside * scalar_mask(ix * 4 - 2 + q, 64), va)
-    for q in range(1, 7):
-        win2.relax(q, va, vb)
-    res = [win2.misfit(q, vb)[1] for q in range(2, 6)]
-    for c in range(3):
-        packed = jnp.where(lane % 4 == 0, src2[c, 2], 0.0)
-        for j in range(1, 4):
-            packed = packed + lroll(jnp.where(lane % 4 == 0, src2[c, 2 + j], 0.0), j)
-        out[pl.ds(4 * c, 4), :] = packed[2:6]
-
-    def third(low, high):
-        t = low + high
-        t = t + sroll(t, -1)
-        t = 0.125 * (t + lroll(t, -4))
-        return jnp.where(lane % 8 == 0, t, 0.0)
-
-    def merged(values):
-        return values[2:3] + lroll(values[4:5], 1)
-
-    field = jnp.zeros((8, 128), F32)
-    wave = jnp.zeros((8, 128), F32)
-    for xl in range(2):
-        for part in range(2):
-            field = field + lroll(third(res[2 * xl][part], res[2 * xl + 1][part]), 4 * part + 2 * xl)
-        t = third(src2[2, 2 + 2 * xl], src2[2, 3 + 2 * xl])
-        wave = wave + lroll(t, 2 * xl) + lroll(t, 4 + 2 * xl)
-    out[pl.ds(12, 1), :] = merged(field)
-    out[pl.ds(13, 1), :] = merged(wave)
-    out[pl.ds(14, 2), :] = jnp.zeros((2, 128), F32)
+            buf[c, 0] = jnp.zeros((16, 128), F32)
+            buf[c, 4] = jnp.zeros((16, 128), F32)
+    win2 = Window(src2, gain2, 0.0625, 1, functools.partial(near2, lane))
+    inside2 = row_mask(16, iy * 4 - 4, 64)
+    for b in range(3):
+        win2.start(b, inside2 * scalar_mask(ix - 1 + b, 16), va)
+    for b in range(3):
+        win2.relax(b, va, vb)
+    _, m = win2.misfit(1, vb)
+
+    def third(v):
+        t = v + lroll(v, -1)
+        t = t + lroll(t, -4)
+        t = 0.125 * jnp.where((lane % 2 == 0) & (lane % 8 < 4), t + sroll(t, -1), 0.0)
+        return t[4:5] + lroll(t[6:7], 1)
+
+    field = third(m[0]) + lroll(third(m[1]), 4)
+    wave = third(src2[2, 1])
+    wave = wave + lroll(wave, 4)
+    pair = jnp.concatenate([field, wave] * 4, axis=0)
+
+    def spread(i):
+        out[i] = pair
+
+    repeat(0, 64, spread, 8)
 
 
 def swap(v, real):
@@ -235,11 +229,10 @@
 
 
 def up_kernel(
-    idx, src0, gain0, ub0, src1, gain1, ub1, got, out,
-    f3, w3, ga3, gb3, u3, f4, w4, s4, e3, src2, gain2, u2, wide2, cell1, u1, wide1, wide0, ua0, ub0s,
+    idx, src0, gain0, ub0, src1, gain1, ub1, src2, flat, out,
+    f3, w3, ga3, gb3, ua3, ub3, f4, w4, s4, e3, gain2, u2, wide2, cell1, ua1, ut1, wide1, wide0, ua0, ut0,
 ):
     ix, iy = idx[0], idx[1]
-    flat = got.reshape(16 * 96, 128)
     lane = lanes(16)
     real = lane // 4 % 2 == 0
     sign = jnp.where(real, F32(SHIFT), F32(-SHIFT))
@@ -263,35 +256,36 @@
     for at in (0, 1, 2, 19, 20, 21):
         for ref in (f3, w3, ga3, gb3):
             ref[at] = zero16
-        for p in range(2):
-            u3[p, at] = zero16
-        e3[at] = jnp.zeros((32, 128), F32)
-    for at in range(3, 19):
-        e3[at, pl.ds(0, 8), :] = jnp.zeros((8, 128), F32)
-        e3[at, pl.ds(24, 8), :] = jnp.zeros((8, 128), F32)
+        for ref in (ua3, ub3):
+            ref[at] = zero16
+    for j in range(7):
+        e3[j] = jnp.zeros((32, 128), F32)
 
     def start3(x):
         at = x + 3
-        f3[at] = flat[pl.ds(2 * x, 16, 96), :]
-        w = flat[pl.ds(2 * x + 1, 16, 96), :]
+        f3[at] = flat[pl.ds(32 * x, 16, 2), :]
+        w = flat[pl.ds(32 * x + 1, 16, 2), :]
         w3[at] = w
         ga, gb = packed_gain(w, 1.0 / 64)
         ga3[at], gb3[at] = ga, gb
-        u3[0, at] = ga * f3[at] + gb * swap(f3[at], real)
-
-    def miss3(p, at):
-        v = u3[p, at]
+        ua3[at] = ga * f3[at] + gb * swap(f3[at], real)
+
+    def miss3(ref, at):
+        v = ref[at]
         down, up = y_pair(v)
-        xs = jnp.where(xlow, lroll(u3[p, at - 1] + v, -2), lroll(v + u3[p, at + 1], 2))
+        xs = jnp.where(xlow, lroll(ref[at - 1] + v, -2), lroll(v + ref[at + 1], 2))
         ys = jnp.where(ylow, lroll(v + down, -1), lroll(v + up, 1))
         return v, packed_misfit(f3[at], w3[at], v, xs + ys + z_sum(v, lane, 8), 1.0 / 64)
 
-    def relax3(p, at):
-        v, m = miss3(p, at)
-        u3[1 - p, at] = v + ga3[at] * m + gb3[at] * swap(m, real)
+    def relaxed3(ref, at):
+        v, m = miss3(ref, at)
+        return v + ga3[at] * m + gb3[at] * swap(m, real)
+
+    def relax3(at):
+        ub3[at] = relaxed3(ua3, at)
 
     repeat(0, 16, start3, 8)
-    repeat(3, 19, lambda at: relax3(0, at), 8)
+    repeat(3, 19, relax3, 8)
 
     first = (slot == 0) & zlow
 
@@ -304,7 +298,7 @@
         f, w = zero16, zero16
         for k in range(4):
             at = 4 * k + r + 3
-            fk, wk = eighth(miss3(1, at)[1]), eighth(w3[at])
+            fk, wk = eighth(miss3(ub3, at)[1]), eighth(w3[at])
             f = f + (lroll(fk, k) if k else fk)
             w = w + (lroll(wk, k) if k else wk)
         f4[r], w4[r] = f, w
@@ -362,42 +356,28 @@
         at = ix + j
         fix = 0.75 * wide[j + 1] + 0.25 * jnp.where(xlow, wide[j], wide[j + 2])
         fix = jnp.where((at >= 3) & (at < 19), fix, 0.0)
-        u3[1, at] = u3[1, at] + fix
-
-    def sweep3(i):
+        ub3[at] = ub3[at] + fix
+
+    def sweep3(_):
+        new = [relaxed3(ub3, ix + j) for j in range(1, 6)]
         for j in range(1, 6):
-            relax3(1 - i, ix + j)
+            ub3[ix + j] = new[j - 1]
 
     repeat(0, 2, sweep3)
     for j in range(1, 6):
-        e3[ix + j, pl.ds(8, 16), :] = u3[1, ix + j]
-    for j in (0, 6):
-        e3[ix + j] = jnp.zeros((32, 128), F32)
+        e3[j, pl.ds(8, 16), :] = ub3[ix + j]
 
     lane8 = lanes(8)
     lane24 = lanes(24)
     zero24 = jnp.zeros((24, 128), F32)
-    for b in range(5):
-        for c in range(3):
-            src2[c, b] = zero24
-
-    def fetch(g):
-        other_y = lax.rem(iy + 14 + g, 16)
-        for b in range(5):
-            for c in range(3):
-                src2[c, b, pl.ds(4 * g, 4), :] = got[other_y, pl.ds(32 + 12 * b + 4 * c, 4), :]
-
-    for g in range(5):
-        fetch(g)
-    for p in range(2):
-        for c in range(2):
-            u2[p, c, 0] = zero24
-            u2[p, c, 6] = zero24
+    for c in range(2):
+        u2[c, 0] = zero24
+        u2[c, 6] = zero24
     win2 = Window(src2, gain2, 0.0625, 1, functools.partial(near2, lane24))
     inside2 = row_mask(24, iy * 4 - 8, 64)
     keep2 = [inside2 * scalar_mask(ix - 2 + b, 16) for b in range(5)]
     for b in range(5):
-        win2.start(b, keep2[b], u2.at[0])
+        win2.start(b, keep2[b], u2)
     a_low = lane8 % 2 == 0
     b_low = lane8 // 4 % 2 == 0
     x_low = lane8 // 2 % 2 == 0
@@ -409,7 +389,7 @@
             pick = (lane8 // 4 % 2 == c) & (lane8 % 2 == yl)
             cells = []
             for bb in range(7):
-                t = jnp.where(pick, e3[ix + bb, pl.ds(iy + 5, 8), :], 0.0)
+                t = jnp.where(pick, e3[bb, pl.ds(iy + 5, 8), :], 0.0)
                 t = t + lroll(t, 1 - 2 * yl)
                 t = t + pltpu.roll(t, shift, 1)
                 low, high = z_pair(t, lane8, 8)
@@ -430,13 +410,12 @@
     repeat(0, 2, widen3)
 
     def sweep2(i):
-        now, later = lax.rem(i, 2), 1 - lax.rem(i, 2)
         add = jnp.where(i == 0, F32(1), F32(0))
+        new = [win2.relaxed(b, u2) for b in range(5)]
         for b in range(5):
-            new = win2.relaxed(b, u2.at[now])
             for c in range(2):
                 fix = wide2[c, b, pl.ds(4, 24), :] * (keep2[b] * add)
-                u2[later, c, b + 1] = new[c] + fix
+                u2[c, b + 1] = new[b][c] + fix
 
     repeat(0, 3, sweep2)
 
@@ -446,7 +425,7 @@
     def widen2(b):
         for xl in range(4):
             for c in range(2):
-                t = jnp.where(slot4 == xl, u2[1, c, b + 1, pl.ds(4, 16), :], 0.0)
+                t = jnp.where(slot4 == xl, u2[c, b + 1, pl.ds(4, 16), :], 0.0)
                 t = lroll(t, -xl) if xl else t
                 t = t + lroll(t, 1)
                 t = t + lroll(t, 2)
@@ -458,43 +437,40 @@
 
     def mix2(q):
         for c in range(2):
-            side = jnp.where(lane_even, cell1[c, q], cell1[c, q + 2])
-            t = 0.75 * cell1[c, q + 1] + 0.25 * side
+            side = jnp.where(lane_even, cell1[c, q - 1], cell1[c, q + 1])
+            t = 0.75 * cell1[c, q] + 0.25 * side
             wide1[c, q, pl.ds(0, 16, 2), :] = 0.75 * t + 0.25 * sroll(t, 1)
             wide1[c, q, pl.ds(1, 16, 2), :] = 0.75 * t + 0.25 * sroll(t, -1)
 
-    repeat(0, 10, mix2, 5)
-    for p in range(2):
-        for c in range(2):
-            u1[p, c, 0] = zero24
-            u1[p, c, 11] = zero24
+    repeat(2, 10, mix2, 4)
+    for c in range(2):
+        ua1[c, 2] = zero24
+        ua1[c, 11] = zero24
     inside1 = row_mask(24, iy * 8 - 8, 128)
 
     def correct1(q):
-        keep = inside1 * scalar_mask(ix * 4 - 3 + q, 64)
-        for c in range(2):
-            u1[0, c, q + 1] = ub1[c, q + 1] + wide1[c, q, pl.ds(0, 24), :] * keep
-
-    repeat(0, 10, correct1, 5)
+        keep = inside1 * scalar_mask(ix * 4 - 4 + q, 64)
+        for c in range(2):
+            ua1[c, q + 1] = ub1[c, q + 1] + wide1[c, q, pl.ds(0, 24), :] * keep
+
+    repeat(2, 10, correct1, 4)
     win1 = Window(src1, gain1, 0.25, 1, functools.partial(near1, lane24))
 
-    def sweep1(i):
-        repeat(0, 10, lambda q: win1.relax(q, u1.at[i], u1.at[1 - i]), 5)
-
-    repeat(0, 2, sweep1)
+    repeat(2, 10, lambda q: win1.relax(q, ua1, ut1), 4)
+    repeat(3, 9, lambda q: win1.relax(q, ut1, ua1), 3)
 
     def widen1(q):
         for c in range(2):
-            t = u1[0, c, q + 1, pl.ds(5, 16), :]
+            t = ua1[c, q + 1, pl.ds(5, 16), :]
             up, down = lroll(t, 1), lroll(t, -1)
             for p in range(2):
                 v = jnp.where(lane_even, t, up) if p == 0 else jnp.where(lane_even, down, t)
                 low, high = z_pair(v, lane16, 2)
                 v = 0.75 * v + 0.25 * jnp.where(lane_even, low, high)
-                wide0[c, 2 * q + p, pl.ds(0, 16, 2), :] = 0.75 * v + 0.25 * sroll(v, 1)
-                wide0[c, 2 * q + p, pl.ds(1, 16, 2), :] = 0.75 * v + 0.25 * sroll(v, -1)
-
-    repeat(2, 8, widen1, 2)
+                wide0[c, 2 * q - 2 + p, pl.ds(0, 16, 2), :] = 0.75 * v + 0.25 * sroll(v, 1)
+                wide0[c, 2 * q - 2 + p, pl.ds(1, 16, 2), :] = 0.75 * v + 0.25 * sroll(v, -1)
+
+    repeat(3, 9, widen1, 2)
     inside0 = row_mask(24, iy * 16 - 3, 256)
 
     def correct0(at):
@@ -509,10 +485,10 @@
 
     repeat(5, 15, correct0, 2)
     win0 = Window(src0, gain0, 1.0, 0, functools.partial(near0, lane24))
-    repeat(2, 20, lambda x: win0.relax(x, ua0, ub0s), 3)
+    repeat(2, 20, lambda x: win0.relax(x, ua0, ut0), 3)
 
     def finish0(x):
-        new = win0.relaxed(x + 3, ub0s)
+        new = win0.relaxed(x + 3, ut0)
         for c in range(2):
             ua0[c, x + 3] = new[c]
             out[c, x] = ua0[c, x + 3, pl.ds(3, 16), :]
@@ -559,42 +535,45 @@
     src0 = jnp.concatenate([low, strip, high, jnp.zeros((3, 22, 2, 128), F32)], axis=2)
 
     n0 = (2, 22, 24, 128)
-    n1 = (2, 12, 24, 128)
+    n1 = (2, 14, 24, 128)
     own1, gain0, first0 = call(
         down0_kernel, "down0", [(3, 4, 8, 128), n0, n0], [n0, (3, 8, 24, 128)], idx, src0
     )
-    low = send(own1[:, 1:], "gx", 1)
-    high = send(own1[:, :3], "gx", -1)
+    low = send(own1, "gx", 1)
+    high = send(own1, "gx", -1)
     strip = jnp.concatenate([low, own1, high], axis=1)
     low = send(strip, "gy", 1)
     high = send(strip, "gy", -1)
     src1 = jnp.concatenate([low, strip, high], axis=2)
 
-    part, gain1, first1 = call(
+    part, own2, gain1, first1 = call(
         down1_kernel,
         "down1",
-        [(16, 128), (2, 10, 24, 128), n1],
-        [n1, (3, 10, 24, 128), (3, 8, 8, 128), (2, 8, 8, 128), (2, 10, 8, 128), (2, 10, 8, 128)],
+        [(64, 8, 128), (3, 3, 16, 128), (2, 12, 24, 128), n1],
+        [n1, (3, 12, 32, 128), (2, 3, 16, 128), (2, 5, 16, 128), (2, 5, 16, 128)],
         idx,
         src1,
     )
-    line = share(part, "gx")
-    ring = jnp.concatenate([line[14:], line, line[:2]], axis=0)
-    blocks = lax.dynamic_slice(ring, (ix, 0, 0), (5, 12, 128))
-    mine = jnp.concatenate(
-        [line[:, 12:14].reshape(32, 128), blocks.reshape(60, 128), jnp.zeros((4, 128), F32)], axis=0
+    part = part.reshape(256, 2, 128)
+    flat = lax.all_to_all(part, ("gx", "gy"), 0, 0).reshape(512, 128)
+    low = send(own2[:, :2], "gx", 1)
+    high = send(own2[:, 1:], "gx", -1)
+    strip = jnp.concatenate([low, own2[:, 1:2], high], axis=1)
+    low = send(strip[:, :, :8], "gy", 1)
+    high = send(strip[:, :, 4:12], "gy", -1)
+    src2 = jnp.concatenate(
+        [low, strip[:, :, 4:8], high, jnp.zeros((3, 5, 4, 128), F32)], axis=2
     )
-    got = share(mine, "gy")
 
     wide = (22, 16, 128)
     return call(
         up_kernel,
         "up",
         [(2, 16, 16, 128)],
-        [wide, wide, wide, wide, (2, 22, 16, 128)]
-        + [(4, 16, 128), (4, 16, 128), (4, 16, 128), (22, 32, 128)]
-        + [(3, 5, 24, 128), (2, 5, 24, 128), (2, 2, 7, 24, 128), (2, 5, 32, 128)]
-        + [(2, 12, 16, 128), (2, 2, 12, 24, 128), (2, 10, 32, 128), (2, 16, 32, 128), n0, n0],
+        [wide, wide, wide, wide, wide, wide]
+        + [(4, 16, 128), (4, 16, 128), (4, 16, 128), (7, 32, 128)]
+        + [(2, 5, 24, 128), (2, 7, 24, 128), (2, 5, 32, 128)]
+        + [(2, 12, 16, 128), n1, n1, (2, 12, 32, 128), (2, 16, 32, 128), n0, n0],
         idx,
         src0,
         gain0,
@@ -602,7 +581,8 @@
         src1,
         gain1,
         first1,
-        got,
+        src2,
+        flat,
     )[0]
 
 

time: 91.3 us -> 79.7 us (0.87)
  blocking collectives: 16.7 us -> 0 us
  starting transfers between devices: 23.8 us -> 32.5 us
  Pallas kernels: 21.4 us -> 16.7 us
  waiting for transfers between devices: 26.8 us -> 28.6 us
    all_to_all x1 -> x0, blocking collectives: 16.7 us -> none  [share(): lax.all_to_all(jnp.broadcast_to(value[None], (count,) + value.shape), axi...]
    ppermute x8 -> x12, starting transfers between devices: 13.3 us -> 22.4 us  [send(): lax.ppermute(value, axis, [(i, (i + step) % count) for i in range(count)])]
    pallas_call x3, Pallas kernels: 21.4 us -> 16.7 us  [call(): pl.pallas_call(kernel, name=name, out_shape=[jax.ShapeDtypeStruct(shape,...]
    ppermute x8 -> x12, waiting for transfers between devices: 17.7 us -> 20.1 us  [send(): lax.ppermute(value, axis, [(i, (i + step) % count) for i in range(count)])]
  transfers between devices with their start and end apart: 9 -> 13, of which waited for: 9 -> 10; matrix products, arithmetic and copies ran while one was open for 0% -> 0% of each run, Pallas kernels for 0% -> 0%
where the time goes in v3:
time: 79.7 us; the launch traced here: 79.6 us
  starting transfers between devices  32.5 us (41%)
  waiting for transfers between devices  28.6 us (36%)
  Pallas kernels  16.7 us (21%)
  other arithmetic  1.35 us (2%)
    ppermute x12, starting transfers between devices, send(): lax.ppermute(value, axis, [(i, (i + step) % count) for i in range(count)])  22.4 us
    ppermute x12, waiting for transfers between devices, send(): lax.ppermute(value, axis, [(i, (i + step) % count) for i in range(count)])  20.1 us
    pallas_call x3, Pallas kernels, call(): pl.pallas_call(kernel, name=name, out_shape=[jax.ShapeDtypeStruct(shape,...  16.7 us
    all_to_all x1, starting transfers between devices, body(): flat = lax.all_to_all(part, ('gx', 'gy'), 0, 0).reshape(512, 128)  10.1 us
    all_to_all x1, waiting for transfers between devices, body(): flat = lax.all_to_all(part, ('gx', 'gy'), 0, 0).reshape(512, 128)  8.48 us
  transfers between devices with their start and end apart: 13, of which 10 were waited for; matrix products, arithmetic and copies ran while one was open for 0% of the time, Pallas kernels for 0%

profile of v3, /device:TPU:1, one launch (start us, length us, event | category | flops | bytes accessed | tf_op | source)
XLA Modules:
  0.0 79.6 jit_solution(701981170178921711)
XLA Ops:
  0.0 0.0 copy-start
  0.0 0.0 copy-start.1
  0.0 0.9 %pad_maximum_fusion.6 = (f32[3,3,16,128]{3,2,1,0:T(8,128)S(1)}, f32[3,3,16,128]{3,2,1,0:T(8,128)S(1)}) fusion(f32[1,16,16,128]{3,2,1,0:T(8,128)} %bitcast.20, f32[2,16,16,128]{3,2,1,0:T(8,128)} %param.2), kind=kLoop, calls=%fused_computation.19 | loop fusion | flops 36864 | bytes 540672 | tf_op jit(solution)/shard_map/slice | solution.py:528
  0.9 3.0 %collective-permute-start = (f32[3,3,16,128]{3,2,1,0:T(8,128)S(1)}, f32[3,3,16,128]{3,2,1,0:T(8,128)S(1)}, u32[]{:S(2)}, u32[]{:S(2)}) collective-permute-start(f32[3,3,16,128]{3,2,1,0:T(8,128)S(1)} %get-tuple-element.21), channel_id=1, source_target_pairs={{0,16},{16,32},{32,48},{48,64},{64,80},{80,96},{96,112},{112,128},... | collective-permute-start | bytes 221192 | tf_op jit(solution)/shard_map/ppermute | solution.py:514
  4.0 0.2 collective-permute-start.1
  4.2 0.1 pad.16.clone
  4.3 1.1 %collective-permute-done = f32[3,3,16,128]{3,2,1,0:T(8,128)S(1)} collective-permute-done((f32[3,3,16,128]{3,2,1,0:T(8,128)S(1)}, f32[3,3,16,128]{3,2,1,0:T(8,128)S(1)}, u32[]{:S(2)}, u32[]{:S(2)}) %collective-permute-start) | collective-permute-done | bytes 73760 | tf_op jit(solution)/shard_map/ppermute | solution.py:514
  5.4 2.4 %collective-permute-done.1 = f32[3,3,16,128]{3,2,1,0:T(8,128)S(1)} collective-permute-done((f32[3,3,16,128]{3,2,1,0:T(8,128)S(1)}, f32[3,3,16,128]{3,2,1,0:T(8,128)S(1)}, u32[]{:S(2)}, u32[]{:S(2)}) %collective-permute-start.1) | collective-permute-done | bytes 73760 | tf_op jit(solution)/shard_map/ppermute | solution.py:514
  7.7 0.0 copy-done
  7.7 0.0 copy-done.1
  7.8 5.0 %collective-permute-start.3 = (f32[9,22,128]{2,1,0:T(8,128)S(1)}, f32[9,22,128]{2,1,0:T(8,128)S(1)}, u32[]{:S(2)}, u32[]{:S(2)}) collective-permute-start(f32[9,22,128]{2,1,0:T(8,128)S(1)} %bitcast.27), channel_id=1, source_target_pairs={{0,15},{1,0},{2,1},{3,2},{4,3},{5,4},{6,5},{7,6},{8,7},{9,8},{10,9... | collective-permute-start | bytes 304136 | tf_op jit(solution)/shard_map/ppermute | solution.py:514
  12.8 0.0 collective-permute-start.2
  12.9 0.1 pad_add_fusion.idx
  12.9 1.7 %collective-permute-done.3 = f32[9,22,128]{2,1,0:T(8,128)S(1)} collective-permute-done((f32[9,22,128]{2,1,0:T(8,128)S(1)}, f32[9,22,128]{2,1,0:T(8,128)S(1)}, u32[]{:S(2)}, u32[]{:S(2)}) %collective-permute-start.3) | collective-permute-done | bytes 101408 | tf_op jit(solution)/shard_map/ppermute | solution.py:514
  14.6 5.1 %collective-permute-done.2 = f32[9,22,128]{2,1,0:T(8,128)S(1)} collective-permute-done((f32[9,22,128]{2,1,0:T(8,128)S(1)}, f32[9,22,128]{2,1,0:T(8,128)S(1)}, u32[]{:S(2)}, u32[]{:S(2)}) %collective-permute-start.2) | collective-permute-done | bytes 101408 | tf_op jit(solution)/shard_map/ppermute | solution.py:514
  19.8 0.2 maximum_maximum_fusion.src.src0
  20.0 2.4 %down0.1 = (f32[3,4,8,128]{3,2,1,0:T(8,128)S(1)}, f32[2,22,24,128]{3,2,1,0:T(8,128)S(1)}, f32[2,22,24,128]{3,2,1,0:T(8,128)S(1)}) custom-call(s32[2]{0:T(128)S(1)} %pad_add_fusion.idx, f32[3,22,24,128]{3,2,1,0:T(8,128)S(1)} %maximum_maximum_fusion.src.src0), custom_call_target="tpu_custom_call" | custom-call | tf_op jit(solution)/shard_map/down0/pallas_call | solution.py:501
  22.4 1.9 %collective-permute-start.4 = (f32[3,4,8,128]{3,2,1,0:T(8,128)S(1)}, f32[3,4,8,128]{3,2,1,0:T(8,128)S(1)}, u32[]{:S(2)}, u32[]{:S(2)}) collective-permute-start(f32[3,4,8,128]{3,2,1,0:T(8,128)S(1)} %get-tuple-element.14), channel_id=1, source_target_pairs={{0,16},{16,32},{32,48},{48,64},{64,80},{80,96},{96,112},{112,128},... | collective-permute-start | bytes 147464 | tf_op jit(solution)/shard_map/ppermute | solution.py:514
  24.3 1.6 %collective-permute-start.5 = (f32[3,4,8,128]{3,2,1,0:T(8,128)S(1)}, f32[3,4,8,128]{3,2,1,0:T(8,128)S(1)}, u32[]{:S(2)}, u32[]{:S(2)}) collective-permute-start(f32[3,4,8,128]{3,2,1,0:T(8,128)S(1)} %get-tuple-element.14), channel_id=1, source_target_pairs={{0,240},{16,0},{32,16},{48,32},{64,48},{80,64},{96,80},{112,96},{1... | collective-permute-start | bytes 147464 | tf_op jit(solution)/shard_map/ppermute | solution.py:514
  25.9 0.7 collective-permute-done.4
  26.6 1.2 %collective-permute-done.5 = f32[3,4,8,128]{3,2,1,0:T(8,128)S(1)} collective-permute-done((f32[3,4,8,128]{3,2,1,0:T(8,128)S(1)}, f32[3,4,8,128]{3,2,1,0:T(8,128)S(1)}, u32[]{:S(2)}, u32[]{:S(2)}) %collective-permute-start.5) | collective-permute-done | bytes 49184 | tf_op jit(solution)/shard_map/ppermute | solution.py:514
  27.8 0.0 collective-permute-start.7
  27.8 1.5 %collective-permute-start.6 = (f32[3,12,8,128]{3,2,1,0:T(8,128)S(1)}, f32[3,12,8,128]{3,2,1,0:T(8,128)S(1)}, u32[]{:S(2)}, u32[]{:S(2)}) collective-permute-start(f32[3,12,8,128]{3,2,1,0:T(8,128)S(1)} %constant_dynamic-update-slice_fusion), channel_id=1, source_target_pairs={{0,1},{1,2},{2,3},{3,4},{4,5},{5,6},{6,7},{7,8},{8,9},{9,10},{10,1... | collective-permute-start | bytes 442376 | tf_op jit(solution)/shard_map/ppermute | solution.py:514
  29.3 2.5 %collective-permute-done.7 = f32[3,12,8,128]{3,2,1,0:T(8,128)S(1)} collective-permute-done((f32[3,12,8,128]{3,2,1,0:T(8,128)S(1)}, f32[3,12,8,128]{3,2,1,0:T(8,128)S(1)}, u32[]{:S(2)}, u32[]{:S(2)}) %collective-permute-start.7) | collective-permute-done | bytes 147488 | tf_op jit(solution)/shard_map/ppermute | solution.py:514
  31.8 3.4 %collective-permute-done.6 = f32[3,12,8,128]{3,2,1,0:T(8,128)S(1)} collective-permute-done((f32[3,12,8,128]{3,2,1,0:T(8,128)S(1)}, f32[3,12,8,128]{3,2,1,0:T(8,128)S(1)}, u32[]{:S(2)}, u32[]{:S(2)}) %collective-permute-start.6) | collective-permute-done | bytes 147488 | tf_op jit(solution)/shard_map/ppermute | solution.py:514
  35.3 3.8 %down1.1 = (f32[64,8,128]{2,1,0:T(8,128)}, f32[3,3,16,128]{3,2,1,0:T(8,128)S(1)}, f32[2,12,24,128]{3,2,1,0:T(8,128)S(1)}, f32[2,14,24,128]{3,2,1,0:T(8,128)S(1)}) custom-call(s32[2]{0:T(128)S(1)} %pad_add_fusion.idx, f32[3,12,24,128]{3,2,1,0:T(8,128)S(1)} %pad_maximum_fusion.src.src1), custom_call_target="tpu_custom_call" | custom-call | tf_op jit(solution)/shard_map/down1/pallas_call | solution.py:501
  39.0 1.9 %collective-permute-start.8 = (f32[3,2,16,128]{3,2,1,0:T(8,128)S(1)}, f32[3,2,16,128]{3,2,1,0:T(8,128)S(1)}, u32[]{:S(2)}, u32[]{:S(2)}) collective-permute-start(f32[3,2,16,128]{3,2,1,0:T(8,128)S(1)} %get-tuple-element.25), channel_id=1, source_target_pairs={{0,16},{16,32},{32,48},{48,64},{64,80},{80,96},{96,112},{112,128},... | collective-permute-start | bytes 147464 | tf_op jit(solution)/shard_map/ppermute | solution.py:514
  41.0 2.3 %collective-permute-start.9 = (f32[3,2,16,128]{3,2,1,0:T(8,128)S(1)}, f32[3,2,16,128]{3,2,1,0:T(8,128)S(1)}, u32[]{:S(2)}, u32[]{:S(2)}) collective-permute-start(f32[3,2,16,128]{3,2,1,0:T(8,128)S(1)} %get-tuple-element.26), channel_id=1, source_target_pairs={{0,240},{16,0},{32,16},{48,32},{64,48},{80,64},{96,80},{112,96},{1... | collective-permute-start | bytes 147464 | tf_op jit(solution)/shard_map/ppermute | solution.py:514
  43.3 10.1 %all-to-all-start = ((f32[256,2,128]{2,1,0:T(2,128)}), f32[256,2,128]{2,1,0:T(2,128)S(1)}, u32[]{:S(2)}, u32[]{:S(2)}) async-start(f32[256,2,128]{2,1,0:T(2,128)} %bitcast.11), calls=%async_computation | async-start | bytes 524288 | tf_op jit(solution)/shard_map/all_to_all | solution.py:558
  53.4 0.0 collective-permute-done.8
  53.4 0.0 collective-permute-done.9
  53.4 1.5 %collective-permute-start.10 = (f32[3,5,8,128]{3,2,1,0:T(8,128)S(1)}, f32[3,5,8,128]{3,2,1,0:T(8,128)S(1)}, u32[]{:S(2)}, u32[]{:S(2)}) collective-permute-start(f32[3,5,8,128]{3,2,1,0:T(8,128)S(1)} %get-tuple-element.23), channel_id=1, source_target_pairs={{0,1},{1,2},{2,3},{3,4},{4,5},{5,6},{6,7},{7,8},{8,9},{9,10},{10,1... | collective-permute-start | bytes 184328 | tf_op jit(solution)/shard_map/ppermute | solution.py:514
  54.9 3.5 %collective-permute-start.11 = (f32[3,5,8,128]{3,2,1,0:T(8,128)S(1)}, f32[3,5,8,128]{3,2,1,0:T(8,128)S(1)}, u32[]{:S(2)}, u32[]{:S(2)}) collective-permute-start(f32[3,5,8,128]{3,2,1,0:T(8,128)S(1)} %get-tuple-element.24), channel_id=1, source_target_pairs={{0,15},{1,0},{2,1},{3,2},{4,3},{5,4},{6,5},{7,6},{8,7},{9,8},{10,9... | collective-permute-start | bytes 184328 | tf_op jit(solution)/shard_map/ppermute | solution.py:514
  58.4 0.1 pad.3.clone
  58.5 2.0 %collective-permute-done.10 = f32[3,5,8,128]{3,2,1,0:T(8,128)S(1)} collective-permute-done((f32[3,5,8,128]{3,2,1,0:T(8,128)S(1)}, f32[3,5,8,128]{3,2,1,0:T(8,128)S(1)}, u32[]{:S(2)}, u32[]{:S(2)}) %collective-permute-start.10) | collective-permute-done | bytes 61472 | tf_op jit(solution)/shard_map/ppermute | solution.py:514
  60.5 0.0 collective-permute-done.11
  60.5 0.1 fusion.2.src2
  60.6 8.5 %all-to-all-done = f32[256,2,128]{2,1,0:T(2,128)S(1)} async-done(((f32[256,2,128]{2,1,0:T(2,128)}), f32[256,2,128]{2,1,0:T(2,128)S(1)}, u32[]{:S(2)}, u32[]{:S(2)}) %all-to-all-start) | async-done | bytes 262176 | tf_op jit(solution)/shard_map/all_to_all | solution.py:558
  69.1 10.5 %up.1 = f32[2,16,16,128]{3,2,1,0:T(8,128)} custom-call(s32[2]{0:T(128)S(1)} %pad_add_fusion.idx, f32[3,22,24,128]{3,2,1,0:T(8,128)S(1)} %maximum_maximum_fusion.src.src0, f32[2,22,24,128]{3,2,1,0:T(8,128)S(1)} %get-tuple-element.12.gain0, f32[2,22,24,128]{3,2,1,0:T(8,128)S(1)} %get-tuple-element.13.ub0, f32[3,12,24,128]{3,2,1,0:T(8,128)S(1)} %pad_maximum_fusion.src.src1, ...), custom_call_target="tpu_custom_call" | custom-call | tf_op jit(solution)/shard_map/up/pallas_call | solution.py:501
  (15 shorter events, 0.2 us)
Async XLA Ops:
  0.0 7.7 %copy-start = (f32[2,16,16,128]{3,2,1,0:T(8,128)S(1)}, f32[2,16,16,128]{3,2,1,0:T(8,128)}, u32[]{:S(2)}) copy-start(f32[2,16,16,128]{3,2,1,0:T(8,128)} %param.2) | copy-start | bytes 786436
  0.0 7.7 %copy-start.1 = (f32[16,16,128]{2,1,0:T(8,128)S(1)}, f32[16,16,128]{2,1,0:T(8,128)}, u32[]{:S(2)}) copy-start(f32[16,16,128]{2,1,0:T(8,128)} %param.3) | copy-start | bytes 393220
  0.9 4.4 %collective-permute-start = (f32[3,3,16,128]{3,2,1,0:T(8,128)S(1)}, f32[3,3,16,128]{3,2,1,0:T(8,128)S(1)}, u32[]{:S(2)}, u32[]{:S(2)}) collective-permute-start(f32[3,3,16,128]{3,2,1,0:T(8,128)S(1)} %get-tuple-element.21), channel_id=1, source_target_pairs={{0,16},{16,32},{32,48},{48,64},{64,80},{80,96},{96,112},{112,128},... | collective-permute-start | bytes 221192 | tf_op jit(solution)/shard_map/ppermute | solution.py:514
  4.0 3.8 %collective-permute-start.1 = (f32[3,3,16,128]{3,2,1,0:T(8,128)S(1)}, f32[3,3,16,128]{3,2,1,0:T(8,128)S(1)}, u32[]{:S(2)}, u32[]{:S(2)}) collective-permute-start(f32[3,3,16,128]{3,2,1,0:T(8,128)S(1)} %get-tuple-element.22), channel_id=1, source_target_pairs={{0,240},{16,0},{32,16},{48,32},{64,48},{80,64},{96,80},{112,96},{1... | collective-permute-start | bytes 221192 | tf_op jit(solution)/shard_map/ppermute | solution.py:514
  7.8 6.8 %collective-permute-start.3 = (f32[9,22,128]{2,1,0:T(8,128)S(1)}, f32[9,22,128]{2,1,0:T(8,128)S(1)}, u32[]{:S(2)}, u32[]{:S(2)}) collective-permute-start(f32[9,22,128]{2,1,0:T(8,128)S(1)} %bitcast.27), channel_id=1, source_target_pairs={{0,15},{1,0},{2,1},{3,2},{4,3},{5,4},{6,5},{7,6},{8,7},{9,8},{10,9... | collective-permute-start | bytes 304136 | tf_op jit(solution)/shard_map/ppermute | solution.py:514
  12.8 6.9 %collective-permute-start.2 = (f32[9,22,128]{2,1,0:T(8,128)S(1)}, f32[9,22,128]{2,1,0:T(8,128)S(1)}, u32[]{:S(2)}, u32[]{:S(2)}) collective-permute-start(f32[9,22,128]{2,1,0:T(8,128)S(1)} %bitcast.25), channel_id=1, source_target_pairs={{0,1},{1,2},{2,3},{3,4},{4,5},{5,6},{6,7},{7,8},{8,9},{9,10},{10,1... | collective-permute-start | bytes 304136 | tf_op jit(solution)/shard_map/ppermute | solution.py:514
  22.4 4.2 %collective-permute-start.4 = (f32[3,4,8,128]{3,2,1,0:T(8,128)S(1)}, f32[3,4,8,128]{3,2,1,0:T(8,128)S(1)}, u32[]{:S(2)}, u32[]{:S(2)}) collective-permute-start(f32[3,4,8,128]{3,2,1,0:T(8,128)S(1)} %get-tuple-element.14), channel_id=1, source_target_pairs={{0,16},{16,32},{32,48},{48,64},{64,80},{80,96},{96,112},{112,128},... | collective-permute-start | bytes 147464 | tf_op jit(solution)/shard_map/ppermute | solution.py:514
  24.3 3.5 %collective-permute-start.5 = (f32[3,4,8,128]{3,2,1,0:T(8,128)S(1)}, f32[3,4,8,128]{3,2,1,0:T(8,128)S(1)}, u32[]{:S(2)}, u32[]{:S(2)}) collective-permute-start(f32[3,4,8,128]{3,2,1,0:T(8,128)S(1)} %get-tuple-element.14), channel_id=1, source_target_pairs={{0,240},{16,0},{32,16},{48,32},{64,48},{80,64},{96,80},{112,96},{1... | collective-permute-start | bytes 147464 | tf_op jit(solution)/shard_map/ppermute | solution.py:514
  27.8 4.0 %collective-permute-start.7 = (f32[3,12,8,128]{3,2,1,0:T(8,128)S(1)}, f32[3,12,8,128]{3,2,1,0:T(8,128)S(1)}, u32[]{:S(2)}, u32[]{:S(2)}) collective-permute-start(f32[3,12,8,128]{3,2,1,0:T(8,128)S(1)} %constant_dynamic-update-slice_fusion), channel_id=1, source_target_pairs={{0,15},{1,0},{2,1},{3,2},{4,3},{5,4},{6,5},{7,6},{8,7},{9,8},{10,9... | collective-permute-start | bytes 442376 | tf_op jit(solution)/shard_map/ppermute | solution.py:514
  27.8 7.4 %collective-permute-start.6 = (f32[3,12,8,128]{3,2,1,0:T(8,128)S(1)}, f32[3,12,8,128]{3,2,1,0:T(8,128)S(1)}, u32[]{:S(2)}, u32[]{:S(2)}) collective-permute-start(f32[3,12,8,128]{3,2,1,0:T(8,128)S(1)} %constant_dynamic-update-slice_fusion), channel_id=1, source_target_pairs={{0,1},{1,2},{2,3},{3,4},{4,5},{5,6},{6,7},{7,8},{8,9},{9,10},{10,1... | collective-permute-start | bytes 442376 | tf_op jit(solution)/shard_map/ppermute | solution.py:514
  39.0 14.3 %collective-permute-start.8 = (f32[3,2,16,128]{3,2,1,0:T(8,128)S(1)}, f32[3,2,16,128]{3,2,1,0:T(8,128)S(1)}, u32[]{:S(2)}, u32[]{:S(2)}) collective-permute-start(f32[3,2,16,128]{3,2,1,0:T(8,128)S(1)} %get-tuple-element.25), channel_id=1, source_target_pairs={{0,16},{16,32},{32,48},{48,64},{64,80},{80,96},{96,112},{112,128},... | collective-permute-start | bytes 147464 | tf_op jit(solution)/shard_map/ppermute | solution.py:514
  41.0 12.4 %collective-permute-start.9 = (f32[3,2,16,128]{3,2,1,0:T(8,128)S(1)}, f32[3,2,16,128]{3,2,1,0:T(8,128)S(1)}, u32[]{:S(2)}, u32[]{:S(2)}) collective-permute-start(f32[3,2,16,128]{3,2,1,0:T(8,128)S(1)} %get-tuple-element.26), channel_id=1, source_target_pairs={{0,240},{16,0},{32,16},{48,32},{64,48},{80,64},{96,80},{112,96},{1... | collective-permute-start | bytes 147464 | tf_op jit(solution)/shard_map/ppermute | solution.py:514
  43.3 25.8 %all-to-all-start = ((f32[256,2,128]{2,1,0:T(2,128)}), f32[256,2,128]{2,1,0:T(2,128)S(1)}, u32[]{:S(2)}, u32[]{:S(2)}) async-start(f32[256,2,128]{2,1,0:T(2,128)} %bitcast.11), calls=%async_computation | async-start | bytes 524288 | tf_op jit(solution)/shard_map/all_to_all | solution.py:558
  53.4 7.1 %collective-permute-start.10 = (f32[3,5,8,128]{3,2,1,0:T(8,128)S(1)}, f32[3,5,8,128]{3,2,1,0:T(8,128)S(1)}, u32[]{:S(2)}, u32[]{:S(2)}) collective-permute-start(f32[3,5,8,128]{3,2,1,0:T(8,128)S(1)} %get-tuple-element.23), channel_id=1, source_target_pairs={{0,1},{1,2},{2,3},{3,4},{4,5},{5,6},{6,7},{7,8},{8,9},{9,10},{10,1... | collective-permute-start | bytes 184328 | tf_op jit(solution)/shard_map/ppermute | solution.py:514
  54.9 5.6 %collective-permute-start.11 = (f32[3,5,8,128]{3,2,1,0:T(8,128)S(1)}, f32[3,5,8,128]{3,2,1,0:T(8,128)S(1)}, u32[]{:S(2)}, u32[]{:S(2)}) collective-permute-start(f32[3,5,8,128]{3,2,1,0:T(8,128)S(1)} %get-tuple-element.24), channel_id=1, source_target_pairs={{0,15},{1,0},{2,1},{3,2},{4,3},{5,4},{6,5},{7,6},{8,7},{9,8},{10,9... | collective-permute-start | bytes 184328 | tf_op jit(solution)/shard_map/ppermute | solution.py:514

commit v4 on v3

--- a/solution.py
+++ b/solution.py
@@ -5,11 +5,12 @@
 from jax import lax
 from jax.experimental import pallas as pl
 from jax.experimental.pallas import tpu as pltpu
-from jax.sharding import PartitionSpec as P
+from jax.sharding import Mesh, PartitionSpec as P
 
 OMEGA = 0.6
 SHIFT = 0.5
 F32 = jnp.float32
+GX = ("z", "c")
 
 
 def lroll(v, shift):
@@ -221,17 +222,14 @@
     def spread(i):
         out[i] = pair
 
-    repeat(0, 64, spread, 8)
+    repeat(0, 32, spread, 8)
 
 
 def swap(v, real):
     return jnp.where(real, lroll(v, -4), lroll(v, 4))
 
 
-def up_kernel(
-    idx, src0, gain0, ub0, src1, gain1, ub1, src2, flat, out,
-    f3, w3, ga3, gb3, ua3, ub3, f4, w4, s4, e3, gain2, u2, wide2, cell1, ua1, ut1, wide1, wide0, ua0, ut0,
-):
+def coarse_kernel(idx, own, other, out, f3, w3, ga3, gb3, ua3, ub3, f4, w4, s4, e3):
     ix, iy = idx[0], idx[1]
     lane = lanes(16)
     real = lane // 4 % 2 == 0
@@ -261,14 +259,15 @@
     for j in range(7):
         e3[j] = jnp.zeros((32, 128), F32)
 
-    def start3(x):
-        at = x + 3
-        f3[at] = flat[pl.ds(32 * x, 16, 2), :]
-        w = flat[pl.ds(32 * x + 1, 16, 2), :]
-        w3[at] = w
-        ga, gb = packed_gain(w, 1.0 / 64)
-        ga3[at], gb3[at] = ga, gb
-        ua3[at] = ga * f3[at] + gb * swap(f3[at], real)
+    core = lax.rem(ix, 2)
+
+    def start3(z):
+        for part, at in ((own, 2 * z + core + 3), (other, 2 * z + 4 - core)):
+            f = part[pl.ds(32 * z, 16, 2), :]
+            w = part[pl.ds(32 * z + 1, 16, 2), :]
+            ga, gb = packed_gain(w, 1.0 / 64)
+            f3[at], w3[at], ga3[at], gb3[at] = f, w, ga, gb
+            ua3[at] = ga * f + gb * swap(f, real)
 
     def miss3(ref, at):
         v = ref[at]
@@ -284,7 +283,7 @@
     def relax3(at):
         ub3[at] = relaxed3(ua3, at)
 
-    repeat(0, 16, start3, 8)
+    repeat(0, 8, start3, 4)
     repeat(3, 19, relax3, 8)
 
     first = (slot == 0) & zlow
@@ -367,6 +366,15 @@
     for j in range(1, 6):
         e3[j, pl.ds(8, 16), :] = ub3[ix + j]
 
+    for j in range(7):
+        out[j] = e3[j, pl.ds(iy + 5, 8), :]
+
+
+def up_kernel(
+    idx, src0, gain0, ub0, src1, gain1, ub1, src2, near, out,
+    gain2, u2, wide2, cell1, ua1, ut1, wide1, wide0, ua0, ut0,
+):
+    ix, iy = idx[0], idx[1]
     lane8 = lanes(8)
     lane24 = lanes(24)
     zero24 = jnp.zeros((24, 128), F32)
@@ -389,7 +397,7 @@
             pick = (lane8 // 4 % 2 == c) & (lane8 % 2 == yl)
             cells = []
             for bb in range(7):
-                t = jnp.where(pick, e3[bb, pl.ds(iy + 5, 8), :], 0.0)
+                t = jnp.where(pick, near[bb], 0.0)
                 t = t + lroll(t, 1 - 2 * yl)
                 t = t + pltpu.roll(t, shift, 1)
                 low, high = z_pair(t, lane8, 8)
@@ -496,7 +504,7 @@
     repeat(0, 16, finish0, 4)
 
 
-def call(kernel, name, out_shape, scratch, *args):
+def call(kernel, name, out_shape, scratch, *args, micros=2):
     vmem = pl.BlockSpec(memory_space=pltpu.VMEM)
     return pl.pallas_call(
         kernel,
@@ -505,6 +513,9 @@
         in_specs=[pl.BlockSpec(memory_space=pltpu.SMEM)] + [vmem] * (len(args) - 1),
         out_specs=[vmem] * len(out_shape),
         scratch_shapes=[pltpu.VMEM(shape, F32) for shape in scratch],
+        cost_estimate=pl.CostEstimate(
+            flops=0, bytes_accessed=micros * 3_500_000, transcendentals=0
+        ),
         compiler_params=pltpu.CompilerParams(vmem_limit_bytes=40 * 1024 * 1024),
     )(*args)
 
@@ -514,19 +525,14 @@
     return lax.ppermute(value, axis, [(i, (i + step) % count) for i in range(count)])
 
 
-def share(value, axis):
-    count = lax.axis_size(axis)
-    return lax.all_to_all(jnp.broadcast_to(value[None], (count,) + value.shape), axis, 0, 0)
-
-
 def body(residual_in, wave_sq):
-    ix = lax.axis_index("gx")
+    ix = lax.axis_index(GX)
     iy = lax.axis_index("gy")
     idx = jnp.stack([ix, iy]).astype(jnp.int32)
 
     own = jnp.concatenate([residual_in, wave_sq[None]], axis=0)
-    low = send(own[:, 13:], "gx", 1)
-    high = send(own[:, :3], "gx", -1)
+    low = send(own[:, 13:], GX, 1)
+    high = send(own[:, :3], GX, -1)
     strip = jnp.concatenate([low, own, high], axis=1)
     low = send(strip[:, :, 13:].transpose(0, 2, 1, 3).reshape(9, 22, 128), "gy", 1)
     high = send(strip[:, :, :3].transpose(0, 2, 1, 3).reshape(9, 22, 128), "gy", -1)
@@ -539,8 +545,8 @@
     own1, gain0, first0 = call(
         down0_kernel, "down0", [(3, 4, 8, 128), n0, n0], [n0, (3, 8, 24, 128)], idx, src0
     )
-    low = send(own1, "gx", 1)
-    high = send(own1, "gx", -1)
+    low = send(own1, GX, 1)
+    high = send(own1, GX, -1)
     strip = jnp.concatenate([low, own1, high], axis=1)
     low = send(strip, "gy", 1)
     high = send(strip, "gy", -1)
@@ -549,15 +555,15 @@
     part, own2, gain1, first1 = call(
         down1_kernel,
         "down1",
-        [(64, 8, 128), (3, 3, 16, 128), (2, 12, 24, 128), n1],
+        [(32, 8, 128), (3, 3, 16, 128), (2, 12, 24, 128), n1],
         [n1, (3, 12, 32, 128), (2, 3, 16, 128), (2, 5, 16, 128), (2, 5, 16, 128)],
         idx,
         src1,
     )
-    part = part.reshape(256, 2, 128)
-    flat = lax.all_to_all(part, ("gx", "gy"), 0, 0).reshape(512, 128)
-    low = send(own2[:, :2], "gx", 1)
-    high = send(own2[:, 1:], "gx", -1)
+    part = part.reshape(128, 2, 128)
+    line = lax.all_to_all(part, ("z", "gy"), 0, 0).reshape(256, 128)
+    low = send(own2[:, :2], GX, 1)
+    high = send(own2[:, 1:], GX, -1)
     strip = jnp.concatenate([low, own2[:, 1:2], high], axis=1)
     low = send(strip[:, :, :8], "gy", 1)
     high = send(strip[:, :, 4:12], "gy", -1)
@@ -565,14 +571,25 @@
         [low, strip[:, :, 4:8], high, jnp.zeros((3, 5, 4, 128), F32)], axis=2
     )
 
+    cross = lax.ppermute(line, "c", [(0, 1), (1, 0)])
+
     wide = (22, 16, 128)
+    near = call(
+        coarse_kernel,
+        "coarse",
+        [(7, 8, 128)],
+        [wide, wide, wide, wide, wide, wide]
+        + [(4, 16, 128), (4, 16, 128), (4, 16, 128), (7, 32, 128)],
+        idx,
+        line,
+        cross,
+        micros=5,
+    )[0]
     return call(
         up_kernel,
         "up",
         [(2, 16, 16, 128)],
-        [wide, wide, wide, wide, wide, wide]
-        + [(4, 16, 128), (4, 16, 128), (4, 16, 128), (7, 32, 128)]
-        + [(2, 5, 24, 128), (2, 7, 24, 128), (2, 5, 32, 128)]
+        [(2, 5, 24, 128), (2, 7, 24, 128), (2, 5, 32, 128)]
         + [(2, 12, 16, 128), n1, n1, (2, 12, 32, 128), (2, 16, 32, 128), n0, n0],
         idx,
         src0,
@@ -582,12 +599,15 @@
         gain1,
         first1,
         src2,
-        flat,
+        near,
+        micros=6,
     )[0]
 
 
 def solution(mesh):
-    placed = (P(None, "gx", "gy", None), P("gx", "gy", None))
+    rows, columns = mesh.devices.shape
+    fine = Mesh(mesh.devices.reshape(rows // 2, 2, columns), ("z", "c", "gy"))
+    placed = (P(None, GX, "gy", None), P(GX, "gy", None))
     return jax.shard_map(
-        body, mesh=mesh, in_specs=placed, out_specs=P(None, "gx", "gy", None), check_vma=False
+        body, mesh=fine, in_specs=placed, out_specs=P(None, GX, "gy", None), check_vma=False
     )

time: 79.7 us -> 84 us (1.054)
  starting transfers between devices: 32.5 us -> 43.1 us
  waiting for transfers between devices: 28.6 us -> 21.8 us
    ppermute x12, waiting for transfers between devices: 20.1 us -> 14.7 us  [send(): lax.ppermute(value, axis, [(i, (i + step) % count) for i in range(count)])]
    ppermute x0 -> x1, starting transfers between devices: none -> 4.04 us  [body(): cross = lax.ppermute(line, 'c', [(0, 1), (1, 0)])]
    all_to_all x1, starting transfers between devices: 10.1 us -> 13.4 us  [body(): line = lax.all_to_all(part, ('z', 'gy'), 0, 0).reshape(256, 128)]
    ppermute x12, starting transfers between devices: 22.4 us -> 25.6 us  [send(): lax.ppermute(value, axis, [(i, (i + step) % count) for i in range(count)])]
    all_to_all x1, waiting for transfers between devices: 8.48 us -> 6.22 us  [body(): line = lax.all_to_all(part, ('z', 'gy'), 0, 0).reshape(256, 128)]
    ppermute x0 -> x1, waiting for transfers between devices: none -> 0.89 us  [body(): cross = lax.ppermute(line, 'c', [(0, 1), (1, 0)])]
    pallas_call x3 -> x4, Pallas kernels: 16.7 us -> 17.2 us  [call(): pl.pallas_call(kernel, name=name, out_shape=[jax.ShapeDtypeStruct(shape,...]
  transfers between devices with their start and end apart: 13 -> 14, of which waited for: 10 -> 9; matrix products, arithmetic and copies ran while one was open for 0% -> 0% of each run, Pallas kernels for 0% -> 0%
where the time goes in v4:
time: 84 us; the launch traced here: 83.8 us
  starting transfers between devices  43.1 us (51%)
  waiting for transfers between devices  21.8 us (26%)
  Pallas kernels  17.2 us (20%)
  other arithmetic  1.35 us (2%)
    ppermute x12, starting transfers between devices, send(): lax.ppermute(value, axis, [(i, (i + step) % count) for i in range(count)])  25.6 us
    pallas_call x4, Pallas kernels, call(): pl.pallas_call(kernel, name=name, out_shape=[jax.ShapeDtypeStruct(shape,...  17.2 us
    ppermute x12, waiting for transfers between devices, send(): lax.ppermute(value, axis, [(i, (i + step) % count) for i in range(count)])  14.7 us
    all_to_all x1, starting transfers between devices, body(): line = lax.all_to_all(part, ('z', 'gy'), 0, 0).reshape(256, 128)  13.4 us
    all_to_all x1, waiting for transfers between devices, body(): line = lax.all_to_all(part, ('z', 'gy'), 0, 0).reshape(256, 128)  6.22 us
    ppermute x1, starting transfers between devices, body(): cross = lax.ppermute(line, 'c', [(0, 1), (1, 0)])  4.04 us
  transfers between devices with their start and end apart: 14, of which 9 were waited for; matrix products, arithmetic and copies ran while one was open for 0% of the time, Pallas kernels for 0%

profile of v4, /device:TPU:1, one launch (start us, length us, event | category | flops | bytes accessed | tf_op | source)
XLA Modules:
  0.0 83.8 jit_solution(10915273365873979030)
XLA Ops:
  0.0 0.0 copy-start
  0.0 0.0 copy-start.1
  0.0 0.9 %pad_maximum_fusion.6 = (f32[3,3,16,128]{3,2,1,0:T(8,128)S(1)}, f32[3,3,16,128]{3,2,1,0:T(8,128)S(1)}) fusion(f32[1,16,16,128]{3,2,1,0:T(8,128)} %bitcast.21, f32[2,16,16,128]{3,2,1,0:T(8,128)} %param.2), kind=kLoop, calls=%fused_computation.19 | loop fusion | flops 36864 | bytes 540672 | tf_op jit(solution)/shard_map/slice | solution.py:534
  0.9 3.0 %collective-permute-start = (f32[3,3,16,128]{3,2,1,0:T(8,128)S(1)}, f32[3,3,16,128]{3,2,1,0:T(8,128)S(1)}, u32[]{:S(2)}, u32[]{:S(2)}) collective-permute-start(f32[3,3,16,128]{3,2,1,0:T(8,128)S(1)} %get-tuple-element.21), channel_id=1, source_target_pairs={{0,16},{16,32},{32,48},{48,64},{64,80},{80,96},{96,112},{112,128},... | collective-permute-start | bytes 221192 | tf_op jit(solution)/shard_map/ppermute | solution.py:525
  4.0 0.2 collective-permute-start.1
  4.2 0.1 pad.16.clone
  4.3 1.1 %collective-permute-done = f32[3,3,16,128]{3,2,1,0:T(8,128)S(1)} collective-permute-done((f32[3,3,16,128]{3,2,1,0:T(8,128)S(1)}, f32[3,3,16,128]{3,2,1,0:T(8,128)S(1)}, u32[]{:S(2)}, u32[]{:S(2)}) %collective-permute-start) | collective-permute-done | bytes 73760 | tf_op jit(solution)/shard_map/ppermute | solution.py:525
  5.4 2.4 %collective-permute-done.1 = f32[3,3,16,128]{3,2,1,0:T(8,128)S(1)} collective-permute-done((f32[3,3,16,128]{3,2,1,0:T(8,128)S(1)}, f32[3,3,16,128]{3,2,1,0:T(8,128)S(1)}, u32[]{:S(2)}, u32[]{:S(2)}) %collective-permute-start.1) | collective-permute-done | bytes 73760 | tf_op jit(solution)/shard_map/ppermute | solution.py:525
  7.7 0.0 copy-done
  7.7 0.0 copy-done.1
  7.8 5.0 %collective-permute-start.3 = (f32[9,22,128]{2,1,0:T(8,128)S(1)}, f32[9,22,128]{2,1,0:T(8,128)S(1)}, u32[]{:S(2)}, u32[]{:S(2)}) collective-permute-start(f32[9,22,128]{2,1,0:T(8,128)S(1)} %bitcast.26), channel_id=1, source_target_pairs={{0,15},{1,0},{2,1},{3,2},{4,3},{5,4},{6,5},{7,6},{8,7},{9,8},{10,9... | collective-permute-start | bytes 304136 | tf_op jit(solution)/shard_map/ppermute | solution.py:525
  12.8 0.1 collective-permute-start.2
  12.9 0.1 pad_add_fusion.idx
  13.0 1.6 %collective-permute-done.3 = f32[9,22,128]{2,1,0:T(8,128)S(1)} collective-permute-done((f32[9,22,128]{2,1,0:T(8,128)S(1)}, f32[9,22,128]{2,1,0:T(8,128)S(1)}, u32[]{:S(2)}, u32[]{:S(2)}) %collective-permute-start.3) | collective-permute-done | bytes 101408 | tf_op jit(solution)/shard_map/ppermute | solution.py:525
  14.6 5.2 %collective-permute-done.2 = f32[9,22,128]{2,1,0:T(8,128)S(1)} collective-permute-done((f32[9,22,128]{2,1,0:T(8,128)S(1)}, f32[9,22,128]{2,1,0:T(8,128)S(1)}, u32[]{:S(2)}, u32[]{:S(2)}) %collective-permute-start.2) | collective-permute-done | bytes 101408 | tf_op jit(solution)/shard_map/ppermute | solution.py:525
  19.9 0.2 maximum_maximum_fusion.src.src0
  20.1 2.4 %down0.1 = (f32[3,4,8,128]{3,2,1,0:T(8,128)S(1)}, f32[2,22,24,128]{3,2,1,0:T(8,128)S(1)}, f32[2,22,24,128]{3,2,1,0:T(8,128)S(1)}) custom-call(s32[2]{0:T(128)S(1)} %pad_add_fusion.idx, f32[3,22,24,128]{3,2,1,0:T(8,128)S(1)} %maximum_maximum_fusion.src.src0), custom_call_target="tpu_custom_call" | custom-call | bytes 7000000 | tf_op jit(solution)/shard_map/down0/pallas_call | solution.py:509
  22.5 1.9 %collective-permute-start.4 = (f32[3,4,8,128]{3,2,1,0:T(8,128)S(1)}, f32[3,4,8,128]{3,2,1,0:T(8,128)S(1)}, u32[]{:S(2)}, u32[]{:S(2)}) collective-permute-start(f32[3,4,8,128]{3,2,1,0:T(8,128)S(1)} %get-tuple-element.14), channel_id=1, source_target_pairs={{0,16},{16,32},{32,48},{48,64},{64,80},{80,96},{96,112},{112,128},... | collective-permute-start | bytes 147464 | tf_op jit(solution)/shard_map/ppermute | solution.py:525
  24.4 1.6 %collective-permute-start.5 = (f32[3,4,8,128]{3,2,1,0:T(8,128)S(1)}, f32[3,4,8,128]{3,2,1,0:T(8,128)S(1)}, u32[]{:S(2)}, u32[]{:S(2)}) collective-permute-start(f32[3,4,8,128]{3,2,1,0:T(8,128)S(1)} %get-tuple-element.14), channel_id=1, source_target_pairs={{0,240},{16,0},{32,16},{48,32},{64,48},{80,64},{96,80},{112,96},{1... | collective-permute-start | bytes 147464 | tf_op jit(solution)/shard_map/ppermute | solution.py:525
  26.0 0.7 collective-permute-done.4
  26.7 1.2 %collective-permute-done.5 = f32[3,4,8,128]{3,2,1,0:T(8,128)S(1)} collective-permute-done((f32[3,4,8,128]{3,2,1,0:T(8,128)S(1)}, f32[3,4,8,128]{3,2,1,0:T(8,128)S(1)}, u32[]{:S(2)}, u32[]{:S(2)}) %collective-permute-start.5) | collective-permute-done | bytes 49184 | tf_op jit(solution)/shard_map/ppermute | solution.py:525
  27.9 0.0 collective-permute-start.6
  27.9 4.8 %collective-permute-start.7 = (f32[3,12,8,128]{3,2,1,0:T(8,128)S(1)}, f32[3,12,8,128]{3,2,1,0:T(8,128)S(1)}, u32[]{:S(2)}, u32[]{:S(2)}) collective-permute-start(f32[3,12,8,128]{3,2,1,0:T(8,128)S(1)} %constant_dynamic-update-slice_fusion), channel_id=1, source_target_pairs={{0,15},{1,0},{2,1},{3,2},{4,3},{5,4},{6,5},{7,6},{8,7},{9,8},{10,9... | collective-permute-start | bytes 442376 | tf_op jit(solution)/shard_map/ppermute | solution.py:525
  32.7 2.5 %collective-permute-done.6 = f32[3,12,8,128]{3,2,1,0:T(8,128)S(1)} collective-permute-done((f32[3,12,8,128]{3,2,1,0:T(8,128)S(1)}, f32[3,12,8,128]{3,2,1,0:T(8,128)S(1)}, u32[]{:S(2)}, u32[]{:S(2)}) %collective-permute-start.6) | collective-permute-done | bytes 147488 | tf_op jit(solution)/shard_map/ppermute | solution.py:525
  35.2 0.0 collective-permute-done.7
  35.3 3.7 %down1.1 = (f32[32,8,128]{2,1,0:T(8,128)}, f32[3,3,16,128]{3,2,1,0:T(8,128)S(1)}, f32[2,12,24,128]{3,2,1,0:T(8,128)S(1)}, f32[2,14,24,128]{3,2,1,0:T(8,128)S(1)}) custom-call(s32[2]{0:T(128)S(1)} %pad_add_fusion.idx, f32[3,12,24,128]{3,2,1,0:T(8,128)S(1)} %pad_maximum_fusion.src.src1), custom_call_target="tpu_custom_call" | custom-call | bytes 7000000 | tf_op jit(solution)/shard_map/down1/pallas_call | solution.py:509
  39.0 1.9 %collective-permute-start.8 = (f32[3,2,16,128]{3,2,1,0:T(8,128)S(1)}, f32[3,2,16,128]{3,2,1,0:T(8,128)S(1)}, u32[]{:S(2)}, u32[]{:S(2)}) collective-permute-start(f32[3,2,16,128]{3,2,1,0:T(8,128)S(1)} %get-tuple-element.25), channel_id=1, source_target_pairs={{0,16},{16,32},{32,48},{48,64},{64,80},{80,96},{96,112},{112,128},... | collective-permute-start | bytes 147464 | tf_op jit(solution)/shard_map/ppermute | solution.py:525
  40.9 2.2 %collective-permute-start.9 = (f32[3,2,16,128]{3,2,1,0:T(8,128)S(1)}, f32[3,2,16,128]{3,2,1,0:T(8,128)S(1)}, u32[]{:S(2)}, u32[]{:S(2)}) collective-permute-start(f32[3,2,16,128]{3,2,1,0:T(8,128)S(1)} %get-tuple-element.26), channel_id=1, source_target_pairs={{0,240},{16,0},{32,16},{48,32},{64,48},{80,64},{96,80},{112,96},{1... | collective-permute-start | bytes 147464 | tf_op jit(solution)/shard_map/ppermute | solution.py:525
  43.1 13.4 %all-to-all-start = ((f32[128,2,128]{2,1,0:T(2,128)}), f32[128,2,128]{2,1,0:T(2,128)S(1)}, u32[]{:S(2)}, u32[]{:S(2)}) async-start(f32[128,2,128]{2,1,0:T(2,128)} %bitcast.11), calls=%async_computation | async-start | bytes 262144 | tf_op jit(solution)/shard_map/all_to_all | solution.py:564
  56.5 0.0 collective-permute-done.8
  56.5 0.0 collective-permute-done.9
  56.6 0.7 collective-permute-start.10
  57.2 4.2 %collective-permute-start.11 = (f32[3,5,8,128]{3,2,1,0:T(8,128)S(1)}, f32[3,5,8,128]{3,2,1,0:T(8,128)S(1)}, u32[]{:S(2)}, u32[]{:S(2)}) collective-permute-start(f32[3,5,8,128]{3,2,1,0:T(8,128)S(1)} %get-tuple-element.24), channel_id=1, source_target_pairs={{0,15},{1,0},{2,1},{3,2},{4,3},{5,4},{6,5},{7,6},{8,7},{9,8},{10,9... | collective-permute-start | bytes 184328 | tf_op jit(solution)/shard_map/ppermute | solution.py:525
  61.4 0.1 pad.3.clone
  61.5 6.2 %all-to-all-done = f32[128,2,128]{2,1,0:T(2,128)S(1)} async-done(((f32[128,2,128]{2,1,0:T(2,128)}), f32[128,2,128]{2,1,0:T(2,128)S(1)}, u32[]{:S(2)}, u32[]{:S(2)}) %all-to-all-start) | async-done | bytes 131104 | tf_op jit(solution)/shard_map/all_to_all | solution.py:564
  67.7 4.0 %collective-permute-start.12 = (f32[256,128]{1,0:T(8,128)S(1)}, f32[256,128]{1,0:T(8,128)S(1)}, u32[]{:S(2)}, u32[]{:S(2)}) collective-permute-start(f32[256,128]{1,0:T(8,128)S(1)} %bitcast.19), channel_id=1, source_target_pairs={{0,16},{16,0},{1,17},{17,1},{2,18},{18,2},{3,19},{19,3},{4,20},{20... | collective-permute-start | bytes 393224 | tf_op jit(solution)/shard_map/ppermute | solution.py:574
  71.8 0.0 collective-permute-done.10
  71.8 0.0 collective-permute-done.11
  71.8 0.1 fusion.2.src2
  71.9 0.9 %collective-permute-done.12.other = f32[256,128]{1,0:T(8,128)S(1)} collective-permute-done((f32[256,128]{1,0:T(8,128)S(1)}, f32[256,128]{1,0:T(8,128)S(1)}, u32[]{:S(2)}, u32[]{:S(2)}) %collective-permute-start.12) | collective-permute-done | bytes 131104 | tf_op jit(solution)/shard_map/ppermute | solution.py:574
  72.8 4.7 %coarse.1.near = f32[7,8,128]{2,1,0:T(8,128)S(1)} custom-call(s32[2]{0:T(128)S(1)} %pad_add_fusion.idx, f32[256,128]{1,0:T(8,128)S(1)} %bitcast.20, f32[256,128]{1,0:T(8,128)S(1)} %collective-permute-done.12.other), custom_call_target="tpu_custom_call" | custom-call | bytes 17500000 | tf_op jit(solution)/shard_map/coarse/pallas_call | solution.py:509
  77.5 6.4 %up.1 = f32[2,16,16,128]{3,2,1,0:T(8,128)} custom-call(s32[2]{0:T(128)S(1)} %pad_add_fusion.idx, f32[3,22,24,128]{3,2,1,0:T(8,128)S(1)} %maximum_maximum_fusion.src.src0, f32[2,22,24,128]{3,2,1,0:T(8,128)S(1)} %get-tuple-element.12.gain0, f32[2,22,24,128]{3,2,1,0:T(8,128)S(1)} %get-tuple-element.13.ub0, f32[3,12,24,128]{3,2,1,0:T(8,128)S(1)} %pad_maximum_fusion.src.src1, ...), custom_call_target="tpu_custom_call" | custom-call | bytes 21000000 | tf_op jit(solution)/shard_map/up/pallas_call | solution.py:509
  (15 shorter events, 0.2 us)
Async XLA Ops:
  0.0 7.7 %copy-start = (f32[2,16,16,128]{3,2,1,0:T(8,128)S(1)}, f32[2,16,16,128]{3,2,1,0:T(8,128)}, u32[]{:S(2)}) copy-start(f32[2,16,16,128]{3,2,1,0:T(8,128)} %param.2) | copy-start | bytes 786436
  0.0 7.7 %copy-start.1 = (f32[16,16,128]{2,1,0:T(8,128)S(1)}, f32[16,16,128]{2,1,0:T(8,128)}, u32[]{:S(2)}) copy-start(f32[16,16,128]{2,1,0:T(8,128)} %param.3) | copy-start | bytes 393220
  0.9 4.4 %collective-permute-start = (f32[3,3,16,128]{3,2,1,0:T(8,128)S(1)}, f32[3,3,16,128]{3,2,1,0:T(8,128)S(1)}, u32[]{:S(2)}, u32[]{:S(2)}) collective-permute-start(f32[3,3,16,128]{3,2,1,0:T(8,128)S(1)} %get-tuple-element.21), channel_id=1, source_target_pairs={{0,16},{16,32},{32,48},{48,64},{64,80},{80,96},{96,112},{112,128},... | collective-permute-start | bytes 221192 | tf_op jit(solution)/shard_map/ppermute | solution.py:525
  4.0 3.8 %collective-permute-start.1 = (f32[3,3,16,128]{3,2,1,0:T(8,128)S(1)}, f32[3,3,16,128]{3,2,1,0:T(8,128)S(1)}, u32[]{:S(2)}, u32[]{:S(2)}) collective-permute-start(f32[3,3,16,128]{3,2,1,0:T(8,128)S(1)} %get-tuple-element.22), channel_id=1, source_target_pairs={{0,240},{16,0},{32,16},{48,32},{64,48},{80,64},{96,80},{112,96},{1... | collective-permute-start | bytes 221192 | tf_op jit(solution)/shard_map/ppermute | solution.py:525
  7.8 6.8 %collective-permute-start.3 = (f32[9,22,128]{2,1,0:T(8,128)S(1)}, f32[9,22,128]{2,1,0:T(8,128)S(1)}, u32[]{:S(2)}, u32[]{:S(2)}) collective-permute-start(f32[9,22,128]{2,1,0:T(8,128)S(1)} %bitcast.26), channel_id=1, source_target_pairs={{0,15},{1,0},{2,1},{3,2},{4,3},{5,4},{6,5},{7,6},{8,7},{9,8},{10,9... | collective-permute-start | bytes 304136 | tf_op jit(solution)/shard_map/ppermute | solution.py:525
  12.8 7.0 %collective-permute-start.2 = (f32[9,22,128]{2,1,0:T(8,128)S(1)}, f32[9,22,128]{2,1,0:T(8,128)S(1)}, u32[]{:S(2)}, u32[]{:S(2)}) collective-permute-start(f32[9,22,128]{2,1,0:T(8,128)S(1)} %bitcast.28), channel_id=1, source_target_pairs={{0,1},{1,2},{2,3},{3,4},{4,5},{5,6},{6,7},{7,8},{8,9},{9,10},{10,1... | collective-permute-start | bytes 304136 | tf_op jit(solution)/shard_map/ppermute | solution.py:525
  22.5 4.2 %collective-permute-start.4 = (f32[3,4,8,128]{3,2,1,0:T(8,128)S(1)}, f32[3,4,8,128]{3,2,1,0:T(8,128)S(1)}, u32[]{:S(2)}, u32[]{:S(2)}) collective-permute-start(f32[3,4,8,128]{3,2,1,0:T(8,128)S(1)} %get-tuple-element.14), channel_id=1, source_target_pairs={{0,16},{16,32},{32,48},{48,64},{64,80},{80,96},{96,112},{112,128},... | collective-permute-start | bytes 147464 | tf_op jit(solution)/shard_map/ppermute | solution.py:525
  24.4 3.5 %collective-permute-start.5 = (f32[3,4,8,128]{3,2,1,0:T(8,128)S(1)}, f32[3,4,8,128]{3,2,1,0:T(8,128)S(1)}, u32[]{:S(2)}, u32[]{:S(2)}) collective-permute-start(f32[3,4,8,128]{3,2,1,0:T(8,128)S(1)} %get-tuple-element.14), channel_id=1, source_target_pairs={{0,240},{16,0},{32,16},{48,32},{64,48},{80,64},{96,80},{112,96},{1... | collective-permute-start | bytes 147464 | tf_op jit(solution)/shard_map/ppermute | solution.py:525
  27.9 7.3 %collective-permute-start.6 = (f32[3,12,8,128]{3,2,1,0:T(8,128)S(1)}, f32[3,12,8,128]{3,2,1,0:T(8,128)S(1)}, u32[]{:S(2)}, u32[]{:S(2)}) collective-permute-start(f32[3,12,8,128]{3,2,1,0:T(8,128)S(1)} %constant_dynamic-update-slice_fusion), channel_id=1, source_target_pairs={{0,1},{1,2},{2,3},{3,4},{4,5},{5,6},{6,7},{7,8},{8,9},{9,10},{10,1... | collective-permute-start | bytes 442376 | tf_op jit(solution)/shard_map/ppermute | solution.py:525
  27.9 7.3 %collective-permute-start.7 = (f32[3,12,8,128]{3,2,1,0:T(8,128)S(1)}, f32[3,12,8,128]{3,2,1,0:T(8,128)S(1)}, u32[]{:S(2)}, u32[]{:S(2)}) collective-permute-start(f32[3,12,8,128]{3,2,1,0:T(8,128)S(1)} %constant_dynamic-update-slice_fusion), channel_id=1, source_target_pairs={{0,15},{1,0},{2,1},{3,2},{4,3},{5,4},{6,5},{7,6},{8,7},{9,8},{10,9... | collective-permute-start | bytes 442376 | tf_op jit(solution)/shard_map/ppermute | solution.py:525
  39.0 17.6 %collective-permute-start.8 = (f32[3,2,16,128]{3,2,1,0:T(8,128)S(1)}, f32[3,2,16,128]{3,2,1,0:T(8,128)S(1)}, u32[]{:S(2)}, u32[]{:S(2)}) collective-permute-start(f32[3,2,16,128]{3,2,1,0:T(8,128)S(1)} %get-tuple-element.25), channel_id=1, source_target_pairs={{0,16},{16,32},{32,48},{48,64},{64,80},{80,96},{96,112},{112,128},... | collective-permute-start | bytes 147464 | tf_op jit(solution)/shard_map/ppermute | solution.py:525
  40.9 15.7 %collective-permute-start.9 = (f32[3,2,16,128]{3,2,1,0:T(8,128)S(1)}, f32[3,2,16,128]{3,2,1,0:T(8,128)S(1)}, u32[]{:S(2)}, u32[]{:S(2)}) collective-permute-start(f32[3,2,16,128]{3,2,1,0:T(8,128)S(1)} %get-tuple-element.26), channel_id=1, source_target_pairs={{0,240},{16,0},{32,16},{48,32},{64,48},{80,64},{96,80},{112,96},{1... | collective-permute-start | bytes 147464 | tf_op jit(solution)/shard_map/ppermute | solution.py:525
  43.1 24.7 %all-to-all-start = ((f32[128,2,128]{2,1,0:T(2,128)}), f32[128,2,128]{2,1,0:T(2,128)S(1)}, u32[]{:S(2)}, u32[]{:S(2)}) async-start(f32[128,2,128]{2,1,0:T(2,128)} %bitcast.11), calls=%async_computation | async-start | bytes 262144 | tf_op jit(solution)/shard_map/all_to_all | solution.py:564
  56.6 15.2 %collective-permute-start.10 = (f32[3,5,8,128]{3,2,1,0:T(8,128)S(1)}, f32[3,5,8,128]{3,2,1,0:T(8,128)S(1)}, u32[]{:S(2)}, u32[]{:S(2)}) collective-permute-start(f32[3,5,8,128]{3,2,1,0:T(8,128)S(1)} %get-tuple-element.23), channel_id=1, source_target_pairs={{0,1},{1,2},{2,3},{3,4},{4,5},{5,6},{6,7},{7,8},{8,9},{9,10},{10,1... | collective-permute-start | bytes 184328 | tf_op jit(solution)/shard_map/ppermute | solution.py:525
  57.2 14.6 %collective-permute-start.11 = (f32[3,5,8,128]{3,2,1,0:T(8,128)S(1)}, f32[3,5,8,128]{3,2,1,0:T(8,128)S(1)}, u32[]{:S(2)}, u32[]{:S(2)}) collective-permute-start(f32[3,5,8,128]{3,2,1,0:T(8,128)S(1)} %get-tuple-element.24), channel_id=1, source_target_pairs={{0,15},{1,0},{2,1},{3,2},{4,3},{5,4},{6,5},{7,6},{8,7},{9,8},{10,9... | collective-permute-start | bytes 184328 | tf_op jit(solution)/shard_map/ppermute | solution.py:525
  67.7 5.0 %collective-permute-start.12 = (f32[256,128]{1,0:T(8,128)S(1)}, f32[256,128]{1,0:T(8,128)S(1)}, u32[]{:S(2)}, u32[]{:S(2)}) collective-permute-start(f32[256,128]{1,0:T(8,128)S(1)} %bitcast.19), channel_id=1, source_target_pairs={{0,16},{16,0},{1,17},{17,1},{2,18},{18,2},{3,19},{19,3},{4,20},{20... | collective-permute-start | bytes 393224 | tf_op jit(solution)/shard_map/ppermute | solution.py:574

commit v5 on v3

--- a/solution.py
+++ b/solution.py
@@ -509,14 +509,35 @@
     )(*args)
 
 
-def send(value, axis, step):
-    count = lax.axis_size(axis)
-    return lax.ppermute(value, axis, [(i, (i + step) % count) for i in range(count)])
-
-
-def share(value, axis):
-    count = lax.axis_size(axis)
-    return lax.all_to_all(jnp.broadcast_to(value[None], (count,) + value.shape), axis, 0, 0)
+BOTH = ("gx", "gy")
+
+
+def partners(axis, first):
+    counts = [lax.axis_size(name) for name in BOTH]
+    along = BOTH.index(axis)
+    pairs = []
+    for i in range(counts[0]):
+        for j in range(counts[1]):
+            place = [i, j]
+            other = ((place[along] + first) ^ 1) - first
+            if 0 <= other < counts[along]:
+                place[along] = other
+            else:
+                place[1 - along] ^= 1
+            pairs.append((i * counts[1] + j, place[0] * counts[1] + place[1]))
+    return pairs
+
+
+def trade(to_low, to_high, axis):
+    even = lax.axis_index(axis) % 2 == 0
+    if to_low is to_high:
+        one = two = to_low
+    else:
+        one = jnp.where(even, to_high, to_low)
+        two = jnp.where(even, to_low, to_high)
+    one = lax.ppermute(one, BOTH, partners(axis, 0))
+    two = lax.ppermute(two, BOTH, partners(axis, 1))
+    return jnp.where(even, two, one), jnp.where(even, one, two)
 
 
 def body(residual_in, wave_sq):
@@ -525,11 +546,13 @@
     idx = jnp.stack([ix, iy]).astype(jnp.int32)
 
     own = jnp.concatenate([residual_in, wave_sq[None]], axis=0)
-    low = send(own[:, 13:], "gx", 1)
-    high = send(own[:, :3], "gx", -1)
+    low, high = trade(own[:, :3], own[:, 13:], "gx")
     strip = jnp.concatenate([low, own, high], axis=1)
-    low = send(strip[:, :, 13:].transpose(0, 2, 1, 3).reshape(9, 22, 128), "gy", 1)
-    high = send(strip[:, :, :3].transpose(0, 2, 1, 3).reshape(9, 22, 128), "gy", -1)
+    low, high = trade(
+        strip[:, :, :3].transpose(0, 2, 1, 3).reshape(9, 22, 128),
+        strip[:, :, 13:].transpose(0, 2, 1, 3).reshape(9, 22, 128),
+        "gy",
+    )
     low = low.reshape(3, 3, 22, 128).transpose(0, 2, 1, 3)
     high = high.reshape(3, 3, 22, 128).transpose(0, 2, 1, 3)
     src0 = jnp.concatenate([low, strip, high, jnp.zeros((3, 22, 2, 128), F32)], axis=2)
@@ -539,11 +562,9 @@
     own1, gain0, first0 = call(
         down0_kernel, "down0", [(3, 4, 8, 128), n0, n0], [n0, (3, 8, 24, 128)], idx, src0
     )
-    low = send(own1, "gx", 1)
-    high = send(own1, "gx", -1)
+    low, high = trade(own1, own1, "gx")
     strip = jnp.concatenate([low, own1, high], axis=1)
-    low = send(strip, "gy", 1)
-    high = send(strip, "gy", -1)
+    low, high = trade(strip, strip, "gy")
     src1 = jnp.concatenate([low, strip, high], axis=2)
 
     part, own2, gain1, first1 = call(
@@ -556,11 +577,9 @@
     )
     part = part.reshape(256, 2, 128)
     flat = lax.all_to_all(part, ("gx", "gy"), 0, 0).reshape(512, 128)
-    low = send(own2[:, :2], "gx", 1)
-    high = send(own2[:, 1:], "gx", -1)
+    low, high = trade(own2[:, 1:], own2[:, :2], "gx")
     strip = jnp.concatenate([low, own2[:, 1:2], high], axis=1)
-    low = send(strip[:, :, :8], "gy", 1)
-    high = send(strip[:, :, 4:12], "gy", -1)
+    low, high = trade(strip[:, :, 4:12], strip[:, :, :8], "gy")
     src2 = jnp.concatenate(
         [low, strip[:, :, 4:8], high, jnp.zeros((3, 5, 4, 128), F32)], axis=2
     )

time: 79.7 us -> 74.7 us (0.937)
  starting transfers between devices: 32.5 us -> 27.8 us
    ppermute x12, starting transfers between devices: 22.4 us -> 13.2 us  [the longest x6 8.08 us: trade(): one = lax.ppermute(one, BOTH, partners(axis, 0))]
    all_to_all x1, starting transfers between devices: 10.1 us -> 14.7 us  [body(): flat = lax.all_to_all(part, ('gx', 'gy'), 0, 0).reshape(512, 128)]
    ppermute x12, waiting for transfers between devices: 20.1 us -> 18.6 us  [the longest x6 11.9 us: trade(): one = lax.ppermute(one, BOTH, partners(axis, 0))]
    select_n x0 -> x12, other arithmetic: none -> 1.11 us  [the longest x4 0.96 us: trade(): two = jnp.where(even, to_low, to_high)]
    all_to_all x1, waiting for transfers between devices: 8.48 us -> 9.46 us  [body(): flat = lax.all_to_all(part, ('gx', 'gy'), 0, 0).reshape(512, 128)]
    slice x1 -> x0, other arithmetic: 0.92 us -> none  [body(): low = send(own[:, 13:], 'gx', 1)]
  transfers between devices with their start and end apart: 13 -> 13, of which waited for: 10 -> 10; matrix products, arithmetic and copies ran while one was open for 0% -> 1% of each run, Pallas kernels for 0% -> 0%
where the time goes in v5:
time: 74.7 us; the launch traced here: 74.6 us
  waiting for transfers between devices  28.1 us (38%)
  starting transfers between devices  27.8 us (37%)
  Pallas kernels  16.7 us (22%)
  other arithmetic  1.5 us (2%)
    pallas_call x3, Pallas kernels, call(): pl.pallas_call(kernel, name=name, out_shape=[jax.ShapeDtypeStruct(shape,...  16.7 us
    all_to_all x1, starting transfers between devices, body(): flat = lax.all_to_all(part, ('gx', 'gy'), 0, 0).reshape(512, 128)  14.7 us
    ppermute x6, waiting for transfers between devices, trade(): one = lax.ppermute(one, BOTH, partners(axis, 0))  11.9 us
    all_to_all x1, waiting for transfers between devices, body(): flat = lax.all_to_all(part, ('gx', 'gy'), 0, 0).reshape(512, 128)  9.46 us
    ppermute x6, starting transfers between devices, trade(): one = lax.ppermute(one, BOTH, partners(axis, 0))  8.08 us
    ppermute x6, waiting for transfers between devices, trade(): two = lax.ppermute(two, BOTH, partners(axis, 1))  6.72 us
    ppermute x6, starting transfers between devices, trade(): two = lax.ppermute(two, BOTH, partners(axis, 1))  5.07 us
  transfers between devices with their start and end apart: 13, of which 10 were waited for; matrix products, arithmetic and copies ran while one was open for 1% of the time, Pallas kernels for 0%

profile of v5, /device:TPU:1, one launch (start us, length us, event | category | flops | bytes accessed | tf_op | source)
XLA Modules:
  0.0 74.6 jit_solution(14534797585817594188)
XLA Ops:
  0.0 0.9 %broadcast_select_fusion.7 = (f32[3,3,16,128]{3,2,1,0:T(8,128)S(1)}, f32[3,3,16,128]{3,2,1,0:T(8,128)S(1)}, f32[3,3,16,128]{3,2,1,0:T(8,128)S(1)}) fusion(pred[]{:T(512)S(6)} %eq.18, f32[1,16,16,128]{3,2,1,0:T(8,128)} %bitcast.18, f32[2,16,16,128]{3,2,1,0:T(8,128)} %param.2), kind=kLoop, calls=%fused_computation.33 | loop fusion | flops 55296 | bytes 614401 | tf_op jit(solution)/shard_map/jit(_where)/select_n | solution.py:537
  0.9 0.0 copy-start
  0.9 3.3 %collective-permute-start.1 = (f32[3,3,16,128]{3,2,1,0:T(8,128)S(1)}, f32[3,3,16,128]{3,2,1,0:T(8,128)S(1)}, u32[]{:S(2)}, u32[]{:S(2)}) collective-permute-start(f32[3,3,16,128]{3,2,1,0:T(8,128)S(1)} %broadcast_select_fusion.6), channel_id=1, source_target_pairs={{0,16},{1,17},{2,18},{3,19},{4,20},{5,21},{6,22},{7,23},{8,24},{9,... | collective-permute-start | bytes 221192 | tf_op jit(solution)/shard_map/ppermute | solution.py:538
  4.2 0.0 collective-permute-start
  4.2 0.1 pad.21.clone
  4.3 0.0 copy-start.1
  4.3 0.8 %collective-permute-done.1 = f32[3,3,16,128]{3,2,1,0:T(8,128)S(1)} collective-permute-done((f32[3,3,16,128]{3,2,1,0:T(8,128)S(1)}, f32[3,3,16,128]{3,2,1,0:T(8,128)S(1)}, u32[]{:S(2)}, u32[]{:S(2)}) %collective-permute-start.1) | collective-permute-done | bytes 73760 | tf_op jit(solution)/shard_map/ppermute | solution.py:538
  5.2 3.1 %collective-permute-done = f32[3,3,16,128]{3,2,1,0:T(8,128)S(1)} collective-permute-done((f32[3,3,16,128]{3,2,1,0:T(8,128)S(1)}, f32[3,3,16,128]{3,2,1,0:T(8,128)S(1)}, u32[]{:S(2)}, u32[]{:S(2)}) %collective-permute-start) | collective-permute-done | bytes 73760 | tf_op jit(solution)/shard_map/ppermute | solution.py:539
  8.3 0.0 copy-done
  8.3 0.0 copy-done.1
  8.3 0.1 select_bitcast_fusion.1
  8.4 0.5 collective-permute-start.2
  9.0 0.5 collective-permute-start.3
  9.5 0.1 pad_add_fusion.idx
  9.6 0.3 collective-permute-done.2
  9.9 3.7 %collective-permute-done.3 = f32[9,22,128]{2,1,0:T(8,128)S(1)} collective-permute-done((f32[9,22,128]{2,1,0:T(8,128)S(1)}, f32[9,22,128]{2,1,0:T(8,128)S(1)}, u32[]{:S(2)}, u32[]{:S(2)}) %collective-permute-start.3) | collective-permute-done | bytes 101408 | tf_op jit(solution)/shard_map/ppermute | solution.py:538
  13.6 0.1 copy_bitcast_fusion
  13.7 0.2 maximum_maximum_fusion.src.src0
  13.9 2.4 %down0.1 = (f32[3,4,8,128]{3,2,1,0:T(8,128)S(1)}, f32[2,22,24,128]{3,2,1,0:T(8,128)S(1)}, f32[2,22,24,128]{3,2,1,0:T(8,128)S(1)}) custom-call(s32[2]{0:T(128)S(1)} %pad_add_fusion.idx, f32[3,22,24,128]{3,2,1,0:T(8,128)S(1)} %maximum_maximum_fusion.src.src0), custom_call_target="tpu_custom_call" | custom-call | tf_op jit(solution)/shard_map/down0/pallas_call | solution.py:501
  16.3 1.0 %collective-permute-start.5 = (f32[3,4,8,128]{3,2,1,0:T(8,128)S(1)}, f32[3,4,8,128]{3,2,1,0:T(8,128)S(1)}, u32[]{:S(2)}, u32[]{:S(2)}) collective-permute-start(f32[3,4,8,128]{3,2,1,0:T(8,128)S(1)} %get-tuple-element.14), channel_id=1, source_target_pairs={{0,16},{1,17},{2,18},{3,19},{4,20},{5,21},{6,22},{7,23},{8,24},{9,... | collective-permute-start | bytes 147464 | tf_op jit(solution)/shard_map/ppermute | solution.py:538
  17.3 0.4 collective-permute-start.4
  17.7 0.5 collective-permute-done.5
  18.2 2.9 %collective-permute-done.4 = f32[3,4,8,128]{3,2,1,0:T(8,128)S(1)} collective-permute-done((f32[3,4,8,128]{3,2,1,0:T(8,128)S(1)}, f32[3,4,8,128]{3,2,1,0:T(8,128)S(1)}, u32[]{:S(2)}, u32[]{:S(2)}) %collective-permute-start.4) | collective-permute-done | bytes 49184 | tf_op jit(solution)/shard_map/ppermute | solution.py:539
  21.1 0.5 collective-permute-start.7
  21.7 0.7 collective-permute-start.6
  22.3 3.9 %collective-permute-done.7 = f32[3,12,8,128]{3,2,1,0:T(8,128)S(1)} collective-permute-done((f32[3,12,8,128]{3,2,1,0:T(8,128)S(1)}, f32[3,12,8,128]{3,2,1,0:T(8,128)S(1)}, u32[]{:S(2)}, u32[]{:S(2)}) %collective-permute-start.7) | collective-permute-done | bytes 147488 | tf_op jit(solution)/shard_map/ppermute | solution.py:538
  26.2 0.0 collective-permute-done.6
  26.3 3.8 %down1.1 = (f32[64,8,128]{2,1,0:T(8,128)}, f32[3,3,16,128]{3,2,1,0:T(8,128)S(1)}, f32[2,12,24,128]{3,2,1,0:T(8,128)S(1)}, f32[2,14,24,128]{3,2,1,0:T(8,128)S(1)}) custom-call(s32[2]{0:T(128)S(1)} %pad_add_fusion.idx, f32[3,12,24,128]{3,2,1,0:T(8,128)S(1)} %pad_maximum_fusion.src.src1), custom_call_target="tpu_custom_call" | custom-call | tf_op jit(solution)/shard_map/down1/pallas_call | solution.py:501
  30.1 1.3 %collective-permute-start.8 = (f32[3,2,16,128]{3,2,1,0:T(8,128)S(1)}, f32[3,2,16,128]{3,2,1,0:T(8,128)S(1)}, u32[]{:S(2)}, u32[]{:S(2)}) collective-permute-start(f32[3,2,16,128]{3,2,1,0:T(8,128)S(1)} %get-tuple-element.39), channel_id=1, source_target_pairs={{0,1},{1,0},{2,3},{3,2},{4,5},{5,4},{6,7},{7,6},{8,9},{9,8},{10,11... | collective-permute-start | bytes 147464 | tf_op jit(solution)/shard_map/ppermute | solution.py:539
  31.4 2.2 %collective-permute-start.9 = (f32[3,2,16,128]{3,2,1,0:T(8,128)S(1)}, f32[3,2,16,128]{3,2,1,0:T(8,128)S(1)}, u32[]{:S(2)}, u32[]{:S(2)}) collective-permute-start(f32[3,2,16,128]{3,2,1,0:T(8,128)S(1)} %get-tuple-element.40), channel_id=1, source_target_pairs={{0,16},{1,17},{2,18},{3,19},{4,20},{5,21},{6,22},{7,23},{8,24},{9,... | collective-permute-start | bytes 147464 | tf_op jit(solution)/shard_map/ppermute | solution.py:538
  33.7 14.7 %all-to-all-start = ((f32[256,2,128]{2,1,0:T(2,128)}), f32[256,2,128]{2,1,0:T(2,128)S(1)}, u32[]{:S(2)}, u32[]{:S(2)}) async-start(f32[256,2,128]{2,1,0:T(2,128)} %bitcast.11), calls=%async_computation | async-start | bytes 524288 | tf_op jit(solution)/shard_map/all_to_all | solution.py:579
  48.3 0.0 collective-permute-done.8
  48.3 0.0 collective-permute-done.9
  48.4 2.2 %collective-permute-start.10 = (f32[3,5,8,128]{3,2,1,0:T(8,128)S(1)}, f32[3,5,8,128]{3,2,1,0:T(8,128)S(1)}, u32[]{:S(2)}, u32[]{:S(2)}) collective-permute-start(f32[3,5,8,128]{3,2,1,0:T(8,128)S(1)} %get-tuple-element.33), channel_id=1, source_target_pairs={{0,16},{1,2},{2,1},{3,4},{4,3},{5,6},{6,5},{7,8},{8,7},{9,10},{10,... | collective-permute-start | bytes 184328 | tf_op jit(solution)/shard_map/ppermute | solution.py:539
  50.6 0.4 collective-permute-start.11
  51.1 0.1 pad.3.clone
  51.2 0.4 collective-permute-done.10
  51.5 2.9 %collective-permute-done.11 = f32[3,5,8,128]{3,2,1,0:T(8,128)S(1)} collective-permute-done((f32[3,5,8,128]{3,2,1,0:T(8,128)S(1)}, f32[3,5,8,128]{3,2,1,0:T(8,128)S(1)}, u32[]{:S(2)}, u32[]{:S(2)}) %collective-permute-start.11) | collective-permute-done | bytes 61472 | tf_op jit(solution)/shard_map/ppermute | solution.py:538
  54.5 0.1 fusion.2.src2
  54.6 9.5 %all-to-all-done = f32[256,2,128]{2,1,0:T(2,128)S(1)} async-done(((f32[256,2,128]{2,1,0:T(2,128)}), f32[256,2,128]{2,1,0:T(2,128)S(1)}, u32[]{:S(2)}, u32[]{:S(2)}) %all-to-all-start) | async-done | bytes 262176 | tf_op jit(solution)/shard_map/all_to_all | solution.py:579
  64.1 10.5 %up.1 = f32[2,16,16,128]{3,2,1,0:T(8,128)} custom-call(s32[2]{0:T(128)S(1)} %pad_add_fusion.idx, f32[3,22,24,128]{3,2,1,0:T(8,128)S(1)} %maximum_maximum_fusion.src.src0, f32[2,22,24,128]{3,2,1,0:T(8,128)S(1)} %get-tuple-element.12.gain0, f32[2,22,24,128]{3,2,1,0:T(8,128)S(1)} %get-tuple-element.13.ub0, f32[3,12,24,128]{3,2,1,0:T(8,128)S(1)} %pad_maximum_fusion.src.src1, ...), custom_call_target="tpu_custom_call" | custom-call | tf_op jit(solution)/shard_map/up/pallas_call | solution.py:501
  (18 shorter events, 0.3 us)
Async XLA Ops:
  0.9 7.4 %copy-start = (f32[2,16,16,128]{3,2,1,0:T(8,128)S(1)}, f32[2,16,16,128]{3,2,1,0:T(8,128)}, u32[]{:S(2)}) copy-start(f32[2,16,16,128]{3,2,1,0:T(8,128)} %param.2) | copy-start | bytes 786436
  0.9 4.2 %collective-permute-start.1 = (f32[3,3,16,128]{3,2,1,0:T(8,128)S(1)}, f32[3,3,16,128]{3,2,1,0:T(8,128)S(1)}, u32[]{:S(2)}, u32[]{:S(2)}) collective-permute-start(f32[3,3,16,128]{3,2,1,0:T(8,128)S(1)} %broadcast_select_fusion.6), channel_id=1, source_target_pairs={{0,16},{1,17},{2,18},{3,19},{4,20},{5,21},{6,22},{7,23},{8,24},{9,... | collective-permute-start | bytes 221192 | tf_op jit(solution)/shard_map/ppermute | solution.py:538
  4.2 4.1 %collective-permute-start = (f32[3,3,16,128]{3,2,1,0:T(8,128)S(1)}, f32[3,3,16,128]{3,2,1,0:T(8,128)S(1)}, u32[]{:S(2)}, u32[]{:S(2)}) collective-permute-start(f32[3,3,16,128]{3,2,1,0:T(8,128)S(1)} %get-tuple-element.22), channel_id=1, source_target_pairs={{0,1},{1,0},{2,3},{3,2},{4,5},{5,4},{6,7},{7,6},{8,9},{9,8},{10,11... | collective-permute-start | bytes 221192 | tf_op jit(solution)/shard_map/ppermute | solution.py:539
  4.3 4.0 %copy-start.1 = (f32[16,16,128]{2,1,0:T(8,128)S(1)}, f32[16,16,128]{2,1,0:T(8,128)}, u32[]{:S(2)}) copy-start(f32[16,16,128]{2,1,0:T(8,128)} %param.3) | copy-start | bytes 393220
  8.4 1.4 %collective-permute-start.2 = (f32[9,22,128]{2,1,0:T(8,128)S(1)}, f32[9,22,128]{2,1,0:T(8,128)S(1)}, u32[]{:S(2)}, u32[]{:S(2)}) collective-permute-start(f32[9,22,128]{2,1,0:T(8,128)S(1)} %bitcast.23), channel_id=1, source_target_pairs={{0,16},{1,2},{2,1},{3,4},{4,3},{5,6},{6,5},{7,8},{8,7},{9,10},{10,... | collective-permute-start | bytes 304136 | tf_op jit(solution)/shard_map/ppermute | solution.py:539
  9.0 4.6 %collective-permute-start.3 = (f32[9,22,128]{2,1,0:T(8,128)S(1)}, f32[9,22,128]{2,1,0:T(8,128)S(1)}, u32[]{:S(2)}, u32[]{:S(2)}) collective-permute-start(f32[9,22,128]{2,1,0:T(8,128)S(1)} %bitcast.24), channel_id=1, source_target_pairs={{0,1},{1,0},{2,3},{3,2},{4,5},{5,4},{6,7},{7,6},{8,9},{9,8},{10,11... | collective-permute-start | bytes 304136 | tf_op jit(solution)/shard_map/ppermute | solution.py:538
  16.3 1.9 %collective-permute-start.5 = (f32[3,4,8,128]{3,2,1,0:T(8,128)S(1)}, f32[3,4,8,128]{3,2,1,0:T(8,128)S(1)}, u32[]{:S(2)}, u32[]{:S(2)}) collective-permute-start(f32[3,4,8,128]{3,2,1,0:T(8,128)S(1)} %get-tuple-element.14), channel_id=1, source_target_pairs={{0,16},{1,17},{2,18},{3,19},{4,20},{5,21},{6,22},{7,23},{8,24},{9,... | collective-permute-start | bytes 147464 | tf_op jit(solution)/shard_map/ppermute | solution.py:538
  17.3 3.8 %collective-permute-start.4 = (f32[3,4,8,128]{3,2,1,0:T(8,128)S(1)}, f32[3,4,8,128]{3,2,1,0:T(8,128)S(1)}, u32[]{:S(2)}, u32[]{:S(2)}) collective-permute-start(f32[3,4,8,128]{3,2,1,0:T(8,128)S(1)} %get-tuple-element.14), channel_id=1, source_target_pairs={{0,1},{1,0},{2,3},{3,2},{4,5},{5,4},{6,7},{7,6},{8,9},{9,8},{10,11... | collective-permute-start | bytes 147464 | tf_op jit(solution)/shard_map/ppermute | solution.py:539
  21.1 5.1 %collective-permute-start.7 = (f32[3,12,8,128]{3,2,1,0:T(8,128)S(1)}, f32[3,12,8,128]{3,2,1,0:T(8,128)S(1)}, u32[]{:S(2)}, u32[]{:S(2)}) collective-permute-start(f32[3,12,8,128]{3,2,1,0:T(8,128)S(1)} %pad_maximum_fusion.1), channel_id=1, source_target_pairs={{0,1},{1,0},{2,3},{3,2},{4,5},{5,4},{6,7},{7,6},{8,9},{9,8},{10,11... | collective-permute-start | bytes 442376 | tf_op jit(solution)/shard_map/ppermute | solution.py:538
  21.7 4.6 %collective-permute-start.6 = (f32[3,12,8,128]{3,2,1,0:T(8,128)S(1)}, f32[3,12,8,128]{3,2,1,0:T(8,128)S(1)}, u32[]{:S(2)}, u32[]{:S(2)}) collective-permute-start(f32[3,12,8,128]{3,2,1,0:T(8,128)S(1)} %pad_maximum_fusion.1), channel_id=1, source_target_pairs={{0,16},{1,2},{2,1},{3,4},{4,3},{5,6},{6,5},{7,8},{8,7},{9,10},{10,... | collective-permute-start | bytes 442376 | tf_op jit(solution)/shard_map/ppermute | solution.py:539
  30.1 18.2 %collective-permute-start.8 = (f32[3,2,16,128]{3,2,1,0:T(8,128)S(1)}, f32[3,2,16,128]{3,2,1,0:T(8,128)S(1)}, u32[]{:S(2)}, u32[]{:S(2)}) collective-permute-start(f32[3,2,16,128]{3,2,1,0:T(8,128)S(1)} %get-tuple-element.39), channel_id=1, source_target_pairs={{0,1},{1,0},{2,3},{3,2},{4,5},{5,4},{6,7},{7,6},{8,9},{9,8},{10,11... | collective-permute-start | bytes 147464 | tf_op jit(solution)/shard_map/ppermute | solution.py:539
  31.4 16.9 %collective-permute-start.9 = (f32[3,2,16,128]{3,2,1,0:T(8,128)S(1)}, f32[3,2,16,128]{3,2,1,0:T(8,128)S(1)}, u32[]{:S(2)}, u32[]{:S(2)}) collective-permute-start(f32[3,2,16,128]{3,2,1,0:T(8,128)S(1)} %get-tuple-element.40), channel_id=1, source_target_pairs={{0,16},{1,17},{2,18},{3,19},{4,20},{5,21},{6,22},{7,23},{8,24},{9,... | collective-permute-start | bytes 147464 | tf_op jit(solution)/shard_map/ppermute | solution.py:538
  33.7 30.4 %all-to-all-start = ((f32[256,2,128]{2,1,0:T(2,128)}), f32[256,2,128]{2,1,0:T(2,128)S(1)}, u32[]{:S(2)}, u32[]{:S(2)}) async-start(f32[256,2,128]{2,1,0:T(2,128)} %bitcast.11), calls=%async_computation | async-start | bytes 524288 | tf_op jit(solution)/shard_map/all_to_all | solution.py:579
  48.4 3.1 %collective-permute-start.10 = (f32[3,5,8,128]{3,2,1,0:T(8,128)S(1)}, f32[3,5,8,128]{3,2,1,0:T(8,128)S(1)}, u32[]{:S(2)}, u32[]{:S(2)}) collective-permute-start(f32[3,5,8,128]{3,2,1,0:T(8,128)S(1)} %get-tuple-element.33), channel_id=1, source_target_pairs={{0,16},{1,2},{2,1},{3,4},{4,3},{5,6},{6,5},{7,8},{8,7},{9,10},{10,... | collective-permute-start | bytes 184328 | tf_op jit(solution)/shard_map/ppermute | solution.py:539
  50.6 3.8 %collective-permute-start.11 = (f32[3,5,8,128]{3,2,1,0:T(8,128)S(1)}, f32[3,5,8,128]{3,2,1,0:T(8,128)S(1)}, u32[]{:S(2)}, u32[]{:S(2)}) collective-permute-start(f32[3,5,8,128]{3,2,1,0:T(8,128)S(1)} %get-tuple-element.34), channel_id=1, source_target_pairs={{0,1},{1,0},{2,3},{3,2},{4,5},{5,4},{6,7},{7,6},{8,9},{9,8},{10,11... | collective-permute-start | bytes 184328 | tf_op jit(solution)/shard_map/ppermute | solution.py:538

commit v6 on v5

--- a/solution.py
+++ b/solution.py
@@ -168,33 +168,32 @@
     for buf in (ua, ub):
         for c in range(2):
             buf[c, 0] = zero24
-            buf[c, 13] = zero24
+            buf[c, 11] = zero24
     win = Window(src, gain, 0.25, 1, functools.partial(near1, lane24))
     inside = row_mask(24, iy * 8 - 8, 128)
-    repeat(0, 12, lambda q: win.start(q, inside * scalar_mask(ix * 4 - 4 + q, 64), ua), 4)
-    repeat(0, 12, lambda q: win.relax(q, ua, ub), 4)
+    repeat(0, 10, lambda q: win.start(q, inside * scalar_mask(ix * 4 - 3 + q, 64), ua), 5)
+    repeat(0, 10, lambda q: win.relax(q, ua, ub), 5)
     lane = lanes(16)
     corner = lane % 4 == 0
 
-    def halve(b):
-        for j in range(4):
-            q = 4 * b + j
-            _, m = win.misfit(q, ub)
-            parts = (m[0], m[1], src[2, q])
-            for c in range(3):
-                t = parts[c] + lroll(parts[c], -1)
-                tmp[c, q, pl.ds(0, 24), :] = t + lroll(t, -2)
-                tmp[c, q, pl.ds(24, 8), :] = jnp.zeros((8, 128), F32)
+    def halve(q):
+        _, m = win.misfit(q, ub)
+        parts = (m[0], m[1], src[2, q])
         for c in range(3):
-            packed = jnp.zeros((16, 128), F32)
-            for j in range(4):
-                q = 4 * b + j
-                t = tmp[c, q, pl.ds(0, 16, 2), :] + tmp[c, q, pl.ds(1, 16, 2), :]
-                t = jnp.where(corner, 0.125 * t, 0.0)
-                packed = packed + (lroll(t, j) if j else t)
-            src2[c, b] = packed
-
-    repeat(0, 3, halve)
+            t = parts[c] + lroll(parts[c], -1)
+            tmp[c, q, pl.ds(0, 24), :] = t + lroll(t, -2)
+            tmp[c, q, pl.ds(24, 8), :] = jnp.zeros((8, 128), F32)
+
+    repeat(1, 9, halve, 4)
+
+    def cell(c, q):
+        t = tmp[c, q, pl.ds(0, 16, 2), :] + tmp[c, q, pl.ds(1, 16, 2), :]
+        return jnp.where(corner, 0.125 * t, 0.0)
+
+    for c in range(3):
+        src2[c, 0] = lroll(cell(c, 1), 2) + lroll(cell(c, 2), 3)
+        src2[c, 1] = sum((lroll(cell(c, 3 + j), j) for j in range(1, 4)), cell(c, 3))
+        src2[c, 2] = cell(c, 7) + lroll(cell(c, 8), 1)
     for buf in (va, vb):
         for c in range(2):
             buf[c, 0] = jnp.zeros((16, 128), F32)
@@ -228,10 +227,7 @@
     return jnp.where(real, lroll(v, -4), lroll(v, 4))
 
 
-def up_kernel(
-    idx, src0, gain0, ub0, src1, gain1, ub1, src2, flat, out,
-    f3, w3, ga3, gb3, ua3, ub3, f4, w4, s4, e3, gain2, u2, wide2, cell1, ua1, ut1, wide1, wide0, ua0, ut0,
-):
+def coarse_kernel(idx, flat, out, f3, w3, ga3, gb3, ua3, ub3, f4, w4, s4, e3):
     ix, iy = idx[0], idx[1]
     lane = lanes(16)
     real = lane // 4 % 2 == 0
@@ -367,6 +363,15 @@
     for j in range(1, 6):
         e3[j, pl.ds(8, 16), :] = ub3[ix + j]
 
+    for j in range(7):
+        out[j] = e3[j, pl.ds(iy + 5, 8), :]
+
+
+def up_kernel(
+    idx, src0, gain0, ub0, src1, gain1, ub1, src2, near, out,
+    gain2, u2, wide2, cell1, ua1, ut1, wide1, wide0, ua0, ut0,
+):
+    ix, iy = idx[0], idx[1]
     lane8 = lanes(8)
     lane24 = lanes(24)
     zero24 = jnp.zeros((24, 128), F32)
@@ -389,7 +394,7 @@
             pick = (lane8 // 4 % 2 == c) & (lane8 % 2 == yl)
             cells = []
             for bb in range(7):
-                t = jnp.where(pick, e3[bb, pl.ds(iy + 5, 8), :], 0.0)
+                t = jnp.where(pick, near[bb], 0.0)
                 t = t + lroll(t, 1 - 2 * yl)
                 t = t + pltpu.roll(t, shift, 1)
                 low, high = z_pair(t, lane8, 8)
@@ -437,27 +442,27 @@
 
     def mix2(q):
         for c in range(2):
-            side = jnp.where(lane_even, cell1[c, q - 1], cell1[c, q + 1])
-            t = 0.75 * cell1[c, q] + 0.25 * side
+            side = jnp.where(lane_even, cell1[c, q], cell1[c, q + 2])
+            t = 0.75 * cell1[c, q + 1] + 0.25 * side
             wide1[c, q, pl.ds(0, 16, 2), :] = 0.75 * t + 0.25 * sroll(t, 1)
             wide1[c, q, pl.ds(1, 16, 2), :] = 0.75 * t + 0.25 * sroll(t, -1)
 
-    repeat(2, 10, mix2, 4)
+    repeat(1, 9, mix2, 4)
     for c in range(2):
-        ua1[c, 2] = zero24
-        ua1[c, 11] = zero24
+        ua1[c, 1] = zero24
+        ua1[c, 10] = zero24
     inside1 = row_mask(24, iy * 8 - 8, 128)
 
     def correct1(q):
-        keep = inside1 * scalar_mask(ix * 4 - 4 + q, 64)
+        keep = inside1 * scalar_mask(ix * 4 - 3 + q, 64)
         for c in range(2):
             ua1[c, q + 1] = ub1[c, q + 1] + wide1[c, q, pl.ds(0, 24), :] * keep
 
-    repeat(2, 10, correct1, 4)
+    repeat(1, 9, correct1, 4)
     win1 = Window(src1, gain1, 0.25, 1, functools.partial(near1, lane24))
 
-    repeat(2, 10, lambda q: win1.relax(q, ua1, ut1), 4)
-    repeat(3, 9, lambda q: win1.relax(q, ut1, ua1), 3)
+    repeat(1, 9, lambda q: win1.relax(q, ua1, ut1), 4)
+    repeat(2, 8, lambda q: win1.relax(q, ut1, ua1), 3)
 
     def widen1(q):
         for c in range(2):
@@ -467,10 +472,10 @@
                 v = jnp.where(lane_even, t, up) if p == 0 else jnp.where(lane_even, down, t)
                 low, high = z_pair(v, lane16, 2)
                 v = 0.75 * v + 0.25 * jnp.where(lane_even, low, high)
-                wide0[c, 2 * q - 2 + p, pl.ds(0, 16, 2), :] = 0.75 * v + 0.25 * sroll(v, 1)
-                wide0[c, 2 * q - 2 + p, pl.ds(1, 16, 2), :] = 0.75 * v + 0.25 * sroll(v, -1)
-
-    repeat(3, 9, widen1, 2)
+                wide0[c, 2 * q + p, pl.ds(0, 16, 2), :] = 0.75 * v + 0.25 * sroll(v, 1)
+                wide0[c, 2 * q + p, pl.ds(1, 16, 2), :] = 0.75 * v + 0.25 * sroll(v, -1)
+
+    repeat(2, 8, widen1, 2)
     inside0 = row_mask(24, iy * 16 - 3, 256)
 
     def correct0(at):
@@ -496,7 +501,7 @@
     repeat(0, 16, finish0, 4)
 
 
-def call(kernel, name, out_shape, scratch, *args):
+def call(kernel, name, out_shape, scratch, *args, micros=2):
     vmem = pl.BlockSpec(memory_space=pltpu.VMEM)
     return pl.pallas_call(
         kernel,
@@ -505,6 +510,9 @@
         in_specs=[pl.BlockSpec(memory_space=pltpu.SMEM)] + [vmem] * (len(args) - 1),
         out_specs=[vmem] * len(out_shape),
         scratch_shapes=[pltpu.VMEM(shape, F32) for shape in scratch],
+        cost_estimate=pl.CostEstimate(
+            flops=0, bytes_accessed=micros * 3_500_000, transcendentals=0
+        ),
         compiler_params=pltpu.CompilerParams(vmem_limit_bytes=40 * 1024 * 1024),
     )(*args)
 
@@ -558,11 +566,11 @@
     src0 = jnp.concatenate([low, strip, high, jnp.zeros((3, 22, 2, 128), F32)], axis=2)
 
     n0 = (2, 22, 24, 128)
-    n1 = (2, 14, 24, 128)
+    n1 = (2, 12, 24, 128)
     own1, gain0, first0 = call(
         down0_kernel, "down0", [(3, 4, 8, 128), n0, n0], [n0, (3, 8, 24, 128)], idx, src0
     )
-    low, high = trade(own1, own1, "gx")
+    low, high = trade(own1[:, :3], own1[:, 1:], "gx")
     strip = jnp.concatenate([low, own1, high], axis=1)
     low, high = trade(strip, strip, "gy")
     src1 = jnp.concatenate([low, strip, high], axis=2)
@@ -570,8 +578,8 @@
     part, own2, gain1, first1 = call(
         down1_kernel,
         "down1",
-        [(64, 8, 128), (3, 3, 16, 128), (2, 12, 24, 128), n1],
-        [n1, (3, 12, 32, 128), (2, 3, 16, 128), (2, 5, 16, 128), (2, 5, 16, 128)],
+        [(64, 8, 128), (3, 3, 16, 128), (2, 10, 24, 128), n1],
+        [n1, (3, 10, 32, 128), (2, 3, 16, 128), (2, 5, 16, 128), (2, 5, 16, 128)],
         idx,
         src1,
     )
@@ -579,20 +587,29 @@
     flat = lax.all_to_all(part, ("gx", "gy"), 0, 0).reshape(512, 128)
     low, high = trade(own2[:, 1:], own2[:, :2], "gx")
     strip = jnp.concatenate([low, own2[:, 1:2], high], axis=1)
+    strip, flat = lax.optimization_barrier((strip, flat))
     low, high = trade(strip[:, :, 4:12], strip[:, :, :8], "gy")
     src2 = jnp.concatenate(
         [low, strip[:, :, 4:8], high, jnp.zeros((3, 5, 4, 128), F32)], axis=2
     )
 
     wide = (22, 16, 128)
+    near = call(
+        coarse_kernel,
+        "coarse",
+        [(7, 8, 128)],
+        [wide, wide, wide, wide, wide, wide]
+        + [(4, 16, 128), (4, 16, 128), (4, 16, 128), (7, 32, 128)],
+        idx,
+        flat,
+        micros=5,
+    )[0]
     return call(
         up_kernel,
         "up",
         [(2, 16, 16, 128)],
-        [wide, wide, wide, wide, wide, wide]
-        + [(4, 16, 128), (4, 16, 128), (4, 16, 128), (7, 32, 128)]
-        + [(2, 5, 24, 128), (2, 7, 24, 128), (2, 5, 32, 128)]
-        + [(2, 12, 16, 128), n1, n1, (2, 12, 32, 128), (2, 16, 32, 128), n0, n0],
+        [(2, 5, 24, 128), (2, 7, 24, 128), (2, 5, 32, 128)]
+        + [(2, 12, 16, 128), n1, n1, (2, 10, 32, 128), (2, 16, 32, 128), n0, n0],
         idx,
         src0,
         gain0,
@@ -601,7 +618,8 @@
         gain1,
         first1,
         src2,
-        flat,
+        near,
+        micros=6,
     )[0]
 
 

time: 74.7 us -> 74.8 us (level)
  waiting for transfers between devices: 28.1 us -> 24.5 us
  starting transfers between devices: 27.8 us -> 31 us
    ppermute x6, waiting for transfers between devices: 11.9 us -> 6.01 us  [trade(): one = lax.ppermute(one, BOTH, partners(axis, 0))]
    all_to_all x1, starting transfers between devices: 14.7 us -> 19.6 us  [body(): flat = lax.all_to_all(part, ('gx', 'gy'), 0, 0).reshape(512, 128)]
    ppermute x6, waiting for transfers between devices: 6.72 us -> 10 us  [trade(): two = lax.ppermute(two, BOTH, partners(axis, 1))]
    ppermute x6, starting transfers between devices: 8.08 us -> 6.59 us  [trade(): one = lax.ppermute(one, BOTH, partners(axis, 0))]
    all_to_all x1, waiting for transfers between devices: 9.46 us -> 8.48 us  [body(): flat = lax.all_to_all(part, ('gx', 'gy'), 0, 0).reshape(512, 128)]
    pallas_call x3 -> x4, Pallas kernels: 16.7 us -> 16.6 us  [call(): pl.pallas_call(kernel, name=name, out_shape=[jax.ShapeDtypeStruct(shape,...]
  transfers between devices with their start and end apart: 13 -> 13, of which waited for: 10 -> 8; matrix products, arithmetic and copies ran while one was open for 1% -> 0% of each run, Pallas kernels for 0% -> 6%
where the time goes in v6:
time: 74.8 us; the launch traced here: 74.1 us
  starting transfers between devices  31 us (41%)
  waiting for transfers between devices  24.5 us (33%)
  Pallas kernels  16.6 us (22%)
  other arithmetic  1.51 us (2%)
    all_to_all x1, starting transfers between devices, body(): flat = lax.all_to_all(part, ('gx', 'gy'), 0, 0).reshape(512, 128)  19.6 us
    pallas_call x4, Pallas kernels, call(): pl.pallas_call(kernel, name=name, out_shape=[jax.ShapeDtypeStruct(shape,...  16.6 us
    ppermute x6, waiting for transfers between devices, trade(): two = lax.ppermute(two, BOTH, partners(axis, 1))  10 us
    all_to_all x1, waiting for transfers between devices, body(): flat = lax.all_to_all(part, ('gx', 'gy'), 0, 0).reshape(512, 128)  8.48 us
    ppermute x6, starting transfers between devices, trade(): one = lax.ppermute(one, BOTH, partners(axis, 0))  6.59 us
    ppermute x6, waiting for transfers between devices, trade(): one = lax.ppermute(one, BOTH, partners(axis, 0))  6.01 us
    ppermute x6, starting transfers between devices, trade(): two = lax.ppermute(two, BOTH, partners(axis, 1))  4.76 us
  transfers between devices with their start and end apart: 13, of which 8 were waited for; matrix products, arithmetic and copies ran while one was open for 0% of the time, Pallas kernels for 6%

profile of v6, /device:TPU:1, one launch (start us, length us, event | category | flops | bytes accessed | tf_op | source)
XLA Modules:
  0.0 74.1 jit_solution(10232592020410055800)
XLA Ops:
  0.0 0.9 %broadcast_select_fusion.7 = (f32[3,3,16,128]{3,2,1,0:T(8,128)S(1)}, f32[3,3,16,128]{3,2,1,0:T(8,128)S(1)}, f32[3,3,16,128]{3,2,1,0:T(8,128)S(1)}) fusion(pred[]{:T(512)S(6)} %eq.18, f32[1,16,16,128]{3,2,1,0:T(8,128)} %bitcast.18, f32[2,16,16,128]{3,2,1,0:T(8,128)} %param.2), kind=kLoop, calls=%fused_computation.26 | loop fusion | flops 55296 | bytes 614401 | tf_op jit(solution)/shard_map/jit(_where)/select_n | solution.py:545
  0.9 0.0 copy-start
  0.9 3.3 %collective-permute-start.1 = (f32[3,3,16,128]{3,2,1,0:T(8,128)S(1)}, f32[3,3,16,128]{3,2,1,0:T(8,128)S(1)}, u32[]{:S(2)}, u32[]{:S(2)}) collective-permute-start(f32[3,3,16,128]{3,2,1,0:T(8,128)S(1)} %broadcast_select_fusion.6), channel_id=1, source_target_pairs={{0,16},{1,17},{2,18},{3,19},{4,20},{5,21},{6,22},{7,23},{8,24},{9,... | collective-permute-start | bytes 221192 | tf_op jit(solution)/shard_map/ppermute | solution.py:546
  4.2 0.0 collective-permute-start
  4.2 0.1 pad.21.clone
  4.3 0.0 copy-start.1
  4.3 0.8 %collective-permute-done.1 = f32[3,3,16,128]{3,2,1,0:T(8,128)S(1)} collective-permute-done((f32[3,3,16,128]{3,2,1,0:T(8,128)S(1)}, f32[3,3,16,128]{3,2,1,0:T(8,128)S(1)}, u32[]{:S(2)}, u32[]{:S(2)}) %collective-permute-start.1) | collective-permute-done | bytes 73760 | tf_op jit(solution)/shard_map/ppermute | solution.py:546
  5.2 3.1 %collective-permute-done = f32[3,3,16,128]{3,2,1,0:T(8,128)S(1)} collective-permute-done((f32[3,3,16,128]{3,2,1,0:T(8,128)S(1)}, f32[3,3,16,128]{3,2,1,0:T(8,128)S(1)}, u32[]{:S(2)}, u32[]{:S(2)}) %collective-permute-start) | collective-permute-done | bytes 73760 | tf_op jit(solution)/shard_map/ppermute | solution.py:547
  8.3 0.0 copy-done
  8.3 0.0 copy-done.1
  8.3 0.1 select_bitcast_fusion.1
  8.4 0.5 collective-permute-start.2
  9.0 0.5 collective-permute-start.3
  9.5 0.1 pad_add_fusion.idx
  9.6 0.3 collective-permute-done.2
  9.9 3.7 %collective-permute-done.3 = f32[9,22,128]{2,1,0:T(8,128)S(1)} collective-permute-done((f32[9,22,128]{2,1,0:T(8,128)S(1)}, f32[9,22,128]{2,1,0:T(8,128)S(1)}, u32[]{:S(2)}, u32[]{:S(2)}) %collective-permute-start.3) | collective-permute-done | bytes 101408 | tf_op jit(solution)/shard_map/ppermute | solution.py:546
  13.6 0.1 copy_bitcast_fusion
  13.7 0.2 maximum_maximum_fusion.src.src0
  13.9 2.4 %down0.1 = (f32[3,4,8,128]{3,2,1,0:T(8,128)S(1)}, f32[2,22,24,128]{3,2,1,0:T(8,128)S(1)}, f32[2,22,24,128]{3,2,1,0:T(8,128)S(1)}) custom-call(s32[2]{0:T(128)S(1)} %pad_add_fusion.idx, f32[3,22,24,128]{3,2,1,0:T(8,128)S(1)} %maximum_maximum_fusion.src.src0), custom_call_target="tpu_custom_call" | custom-call | bytes 7000000 | tf_op jit(solution)/shard_map/down0/pallas_call | solution.py:506
  16.3 1.3 %collective-permute-start.4 = (f32[3,3,8,128]{3,2,1,0:T(8,128)S(1)}, f32[3,3,8,128]{3,2,1,0:T(8,128)S(1)}, u32[]{:S(2)}, u32[]{:S(2)}) collective-permute-start(f32[3,3,8,128]{3,2,1,0:T(8,128)S(1)} %get-tuple-element.45), channel_id=1, source_target_pairs={{0,1},{1,0},{2,3},{3,2},{4,5},{5,4},{6,7},{7,6},{8,9},{9,8},{10,11... | collective-permute-start | bytes 110600 | tf_op jit(solution)/shard_map/ppermute | solution.py:547
  17.6 0.5 collective-permute-start.5
  18.1 1.7 %collective-permute-done.4 = f32[3,3,8,128]{3,2,1,0:T(8,128)S(1)} collective-permute-done((f32[3,3,8,128]{3,2,1,0:T(8,128)S(1)}, f32[3,3,8,128]{3,2,1,0:T(8,128)S(1)}, u32[]{:S(2)}, u32[]{:S(2)}) %collective-permute-start.4) | collective-permute-done | bytes 36896 | tf_op jit(solution)/shard_map/ppermute | solution.py:547
  19.8 0.0 collective-permute-done.5
  19.8 1.3 %collective-permute-start.7 = (f32[3,10,8,128]{3,2,1,0:T(8,128)S(1)}, f32[3,10,8,128]{3,2,1,0:T(8,128)S(1)}, u32[]{:S(2)}, u32[]{:S(2)}) collective-permute-start(f32[3,10,8,128]{3,2,1,0:T(8,128)S(1)} %pad_maximum_fusion.5), channel_id=1, source_target_pairs={{0,1},{1,0},{2,3},{3,2},{4,5},{5,4},{6,7},{7,6},{8,9},{9,8},{10,11... | collective-permute-start | bytes 368648 | tf_op jit(solution)/shard_map/ppermute | solution.py:546
  21.1 1.0 %collective-permute-start.6 = (f32[3,10,8,128]{3,2,1,0:T(8,128)S(1)}, f32[3,10,8,128]{3,2,1,0:T(8,128)S(1)}, u32[]{:S(2)}, u32[]{:S(2)}) collective-permute-start(f32[3,10,8,128]{3,2,1,0:T(8,128)S(1)} %pad_maximum_fusion.5), channel_id=1, source_target_pairs={{0,16},{1,2},{2,1},{3,4},{4,3},{5,6},{6,5},{7,8},{8,7},{9,10},{10,... | collective-permute-start | bytes 368648 | tf_op jit(solution)/shard_map/ppermute | solution.py:547
  22.2 1.5 %collective-permute-done.7 = f32[3,10,8,128]{3,2,1,0:T(8,128)S(1)} collective-permute-done((f32[3,10,8,128]{3,2,1,0:T(8,128)S(1)}, f32[3,10,8,128]{3,2,1,0:T(8,128)S(1)}, u32[]{:S(2)}, u32[]{:S(2)}) %collective-permute-start.7) | collective-permute-done | bytes 122912 | tf_op jit(solution)/shard_map/ppermute | solution.py:546
  23.6 0.0 collective-permute-done.6
  23.7 3.1 %down1.1 = (f32[64,8,128]{2,1,0:T(8,128)}, f32[3,3,16,128]{3,2,1,0:T(8,128)S(1)}, f32[2,10,24,128]{3,2,1,0:T(8,128)S(1)}, f32[2,12,24,128]{3,2,1,0:T(8,128)S(1)}) custom-call(s32[2]{0:T(128)S(1)} %pad_add_fusion.idx, f32[3,10,24,128]{3,2,1,0:T(8,128)S(1)} %pad_maximum_fusion.src.src1), custom_call_target="tpu_custom_call" | custom-call | bytes 7000000 | tf_op jit(solution)/shard_map/down1/pallas_call | solution.py:506
  26.8 19.6 %all-to-all-start = ((f32[256,2,128]{2,1,0:T(2,128)}), f32[256,2,128]{2,1,0:T(2,128)S(1)}, u32[]{:S(2)}, u32[]{:S(2)}) async-start(f32[256,2,128]{2,1,0:T(2,128)} %bitcast.11), calls=%async_computation | async-start | bytes 524288 | tf_op jit(solution)/shard_map/all_to_all | solution.py:587
  46.5 1.8 %collective-permute-start.8 = (f32[3,2,16,128]{3,2,1,0:T(8,128)S(1)}, f32[3,2,16,128]{3,2,1,0:T(8,128)S(1)}, u32[]{:S(2)}, u32[]{:S(2)}) collective-permute-start(f32[3,2,16,128]{3,2,1,0:T(8,128)S(1)} %get-tuple-element.41), channel_id=1, source_target_pairs={{0,1},{1,0},{2,3},{3,2},{4,5},{5,4},{6,7},{7,6},{8,9},{9,8},{10,11... | collective-permute-start | bytes 147464 | tf_op jit(solution)/shard_map/ppermute | solution.py:547
  48.3 0.5 collective-permute-start.9
  48.8 4.9 %collective-permute-done.8 = f32[3,2,16,128]{3,2,1,0:T(8,128)S(1)} collective-permute-done((f32[3,2,16,128]{3,2,1,0:T(8,128)S(1)}, f32[3,2,16,128]{3,2,1,0:T(8,128)S(1)}, u32[]{:S(2)}, u32[]{:S(2)}) %collective-permute-start.8) | collective-permute-done | bytes 49184 | tf_op jit(solution)/shard_map/ppermute | solution.py:547
  53.8 0.0 collective-permute-done.9
  53.8 8.5 %all-to-all-done = f32[256,2,128]{2,1,0:T(2,128)S(1)} async-done(((f32[256,2,128]{2,1,0:T(2,128)}), f32[256,2,128]{2,1,0:T(2,128)S(1)}, u32[]{:S(2)}, u32[]{:S(2)}) %all-to-all-start) | async-done | bytes 262176 | tf_op jit(solution)/shard_map/all_to_all | solution.py:587
  62.3 0.1 collective-permute-start.10
  62.4 0.4 collective-permute-start.11
  62.8 0.1 pad.3.clone
  62.9 4.7 %coarse.1.near = f32[7,8,128]{2,1,0:T(8,128)S(1)} custom-call(s32[2]{0:T(128)S(1)} %pad_add_fusion.idx, f32[512,128]{1,0:T(8,128)S(1)} %bitcast.17), custom_call_target="tpu_custom_call" | custom-call | bytes 17500000 | tf_op jit(solution)/shard_map/coarse/pallas_call | solution.py:506
  67.6 0.0 collective-permute-done.10
  67.6 0.0 collective-permute-done.11
  67.7 0.1 maximum_maximum_fusion.1.src2
  67.7 6.4 %up.1 = f32[2,16,16,128]{3,2,1,0:T(8,128)} custom-call(s32[2]{0:T(128)S(1)} %pad_add_fusion.idx, f32[3,22,24,128]{3,2,1,0:T(8,128)S(1)} %maximum_maximum_fusion.src.src0, f32[2,22,24,128]{3,2,1,0:T(8,128)S(1)} %get-tuple-element.14.gain0, f32[2,22,24,128]{3,2,1,0:T(8,128)S(1)} %get-tuple-element.15.ub0, f32[3,10,24,128]{3,2,1,0:T(8,128)S(1)} %pad_maximum_fusion.src.src1, ...), custom_call_target="tpu_custom_call" | custom-call | bytes 21000000 | tf_op jit(solution)/shard_map/up/pallas_call | solution.py:506
  (20 shorter events, 0.3 us)
Async XLA Ops:
  0.9 7.4 %copy-start = (f32[2,16,16,128]{3,2,1,0:T(8,128)S(1)}, f32[2,16,16,128]{3,2,1,0:T(8,128)}, u32[]{:S(2)}) copy-start(f32[2,16,16,128]{3,2,1,0:T(8,128)} %param.2) | copy-start | bytes 786436
  0.9 4.2 %collective-permute-start.1 = (f32[3,3,16,128]{3,2,1,0:T(8,128)S(1)}, f32[3,3,16,128]{3,2,1,0:T(8,128)S(1)}, u32[]{:S(2)}, u32[]{:S(2)}) collective-permute-start(f32[3,3,16,128]{3,2,1,0:T(8,128)S(1)} %broadcast_select_fusion.6), channel_id=1, source_target_pairs={{0,16},{1,17},{2,18},{3,19},{4,20},{5,21},{6,22},{7,23},{8,24},{9,... | collective-permute-start | bytes 221192 | tf_op jit(solution)/shard_map/ppermute | solution.py:546
  4.2 4.1 %collective-permute-start = (f32[3,3,16,128]{3,2,1,0:T(8,128)S(1)}, f32[3,3,16,128]{3,2,1,0:T(8,128)S(1)}, u32[]{:S(2)}, u32[]{:S(2)}) collective-permute-start(f32[3,3,16,128]{3,2,1,0:T(8,128)S(1)} %get-tuple-element.26), channel_id=1, source_target_pairs={{0,1},{1,0},{2,3},{3,2},{4,5},{5,4},{6,7},{7,6},{8,9},{9,8},{10,11... | collective-permute-start | bytes 221192 | tf_op jit(solution)/shard_map/ppermute | solution.py:547
  4.3 4.0 %copy-start.1 = (f32[16,16,128]{2,1,0:T(8,128)S(1)}, f32[16,16,128]{2,1,0:T(8,128)}, u32[]{:S(2)}) copy-start(f32[16,16,128]{2,1,0:T(8,128)} %param.3) | copy-start | bytes 393220
  8.4 1.4 %collective-permute-start.2 = (f32[9,22,128]{2,1,0:T(8,128)S(1)}, f32[9,22,128]{2,1,0:T(8,128)S(1)}, u32[]{:S(2)}, u32[]{:S(2)}) collective-permute-start(f32[9,22,128]{2,1,0:T(8,128)S(1)} %bitcast.23), channel_id=1, source_target_pairs={{0,16},{1,2},{2,1},{3,4},{4,3},{5,6},{6,5},{7,8},{8,7},{9,10},{10,... | collective-permute-start | bytes 304136 | tf_op jit(solution)/shard_map/ppermute | solution.py:547
  9.0 4.6 %collective-permute-start.3 = (f32[9,22,128]{2,1,0:T(8,128)S(1)}, f32[9,22,128]{2,1,0:T(8,128)S(1)}, u32[]{:S(2)}, u32[]{:S(2)}) collective-permute-start(f32[9,22,128]{2,1,0:T(8,128)S(1)} %bitcast.24), channel_id=1, source_target_pairs={{0,1},{1,0},{2,3},{3,2},{4,5},{5,4},{6,7},{7,6},{8,9},{9,8},{10,11... | collective-permute-start | bytes 304136 | tf_op jit(solution)/shard_map/ppermute | solution.py:546
  16.3 3.5 %collective-permute-start.4 = (f32[3,3,8,128]{3,2,1,0:T(8,128)S(1)}, f32[3,3,8,128]{3,2,1,0:T(8,128)S(1)}, u32[]{:S(2)}, u32[]{:S(2)}) collective-permute-start(f32[3,3,8,128]{3,2,1,0:T(8,128)S(1)} %get-tuple-element.45), channel_id=1, source_target_pairs={{0,1},{1,0},{2,3},{3,2},{4,5},{5,4},{6,7},{7,6},{8,9},{9,8},{10,11... | collective-permute-start | bytes 110600 | tf_op jit(solution)/shard_map/ppermute | solution.py:547
  17.6 2.2 %collective-permute-start.5 = (f32[3,3,8,128]{3,2,1,0:T(8,128)S(1)}, f32[3,3,8,128]{3,2,1,0:T(8,128)S(1)}, u32[]{:S(2)}, u32[]{:S(2)}) collective-permute-start(f32[3,3,8,128]{3,2,1,0:T(8,128)S(1)} %get-tuple-element.46), channel_id=1, source_target_pairs={{0,16},{1,17},{2,18},{3,19},{4,20},{5,21},{6,22},{7,23},{8,24},{9,... | collective-permute-start | bytes 110600 | tf_op jit(solution)/shard_map/ppermute | solution.py:546
  19.8 3.8 %collective-permute-start.7 = (f32[3,10,8,128]{3,2,1,0:T(8,128)S(1)}, f32[3,10,8,128]{3,2,1,0:T(8,128)S(1)}, u32[]{:S(2)}, u32[]{:S(2)}) collective-permute-start(f32[3,10,8,128]{3,2,1,0:T(8,128)S(1)} %pad_maximum_fusion.5), channel_id=1, source_target_pairs={{0,1},{1,0},{2,3},{3,2},{4,5},{5,4},{6,7},{7,6},{8,9},{9,8},{10,11... | collective-permute-start | bytes 368648 | tf_op jit(solution)/shard_map/ppermute | solution.py:546
  21.1 2.5 %collective-permute-start.6 = (f32[3,10,8,128]{3,2,1,0:T(8,128)S(1)}, f32[3,10,8,128]{3,2,1,0:T(8,128)S(1)}, u32[]{:S(2)}, u32[]{:S(2)}) collective-permute-start(f32[3,10,8,128]{3,2,1,0:T(8,128)S(1)} %pad_maximum_fusion.5), channel_id=1, source_target_pairs={{0,16},{1,2},{2,1},{3,4},{4,3},{5,6},{6,5},{7,8},{8,7},{9,10},{10,... | collective-permute-start | bytes 368648 | tf_op jit(solution)/shard_map/ppermute | solution.py:547
  26.8 35.4 %all-to-all-start = ((f32[256,2,128]{2,1,0:T(2,128)}), f32[256,2,128]{2,1,0:T(2,128)S(1)}, u32[]{:S(2)}, u32[]{:S(2)}) async-start(f32[256,2,128]{2,1,0:T(2,128)} %bitcast.11), calls=%async_computation | async-start | bytes 524288 | tf_op jit(solution)/shard_map/all_to_all | solution.py:587
  46.5 7.3 %collective-permute-start.8 = (f32[3,2,16,128]{3,2,1,0:T(8,128)S(1)}, f32[3,2,16,128]{3,2,1,0:T(8,128)S(1)}, u32[]{:S(2)}, u32[]{:S(2)}) collective-permute-start(f32[3,2,16,128]{3,2,1,0:T(8,128)S(1)} %get-tuple-element.41), channel_id=1, source_target_pairs={{0,1},{1,0},{2,3},{3,2},{4,5},{5,4},{6,7},{7,6},{8,9},{9,8},{10,11... | collective-permute-start | bytes 147464 | tf_op jit(solution)/shard_map/ppermute | solution.py:547
  48.3 5.4 %collective-permute-start.9 = (f32[3,2,16,128]{3,2,1,0:T(8,128)S(1)}, f32[3,2,16,128]{3,2,1,0:T(8,128)S(1)}, u32[]{:S(2)}, u32[]{:S(2)}) collective-permute-start(f32[3,2,16,128]{3,2,1,0:T(8,128)S(1)} %get-tuple-element.42), channel_id=1, source_target_pairs={{0,16},{1,17},{2,18},{3,19},{4,20},{5,21},{6,22},{7,23},{8,24},{9,... | collective-permute-start | bytes 147464 | tf_op jit(solution)/shard_map/ppermute | solution.py:546
  62.3 5.3 %collective-permute-start.10 = (f32[3,5,8,128]{3,2,1,0:T(8,128)S(1)}, f32[3,5,8,128]{3,2,1,0:T(8,128)S(1)}, u32[]{:S(2)}, u32[]{:S(2)}) collective-permute-start(f32[3,5,8,128]{3,2,1,0:T(8,128)S(1)} %get-tuple-element.37), channel_id=1, source_target_pairs={{0,16},{1,2},{2,1},{3,4},{4,3},{5,6},{6,5},{7,8},{8,7},{9,10},{10,... | collective-permute-start | bytes 184328 | tf_op jit(solution)/shard_map/ppermute | solution.py:547
  62.4 5.2 %collective-permute-start.11 = (f32[3,5,8,128]{3,2,1,0:T(8,128)S(1)}, f32[3,5,8,128]{3,2,1,0:T(8,128)S(1)}, u32[]{:S(2)}, u32[]{:S(2)}) collective-permute-start(f32[3,5,8,128]{3,2,1,0:T(8,128)S(1)} %get-tuple-element.38), channel_id=1, source_target_pairs={{0,1},{1,0},{2,3},{3,2},{4,5},{5,4},{6,7},{7,6},{8,9},{9,8},{10,11... | collective-permute-start | bytes 184328 | tf_op jit(solution)/shard_map/ppermute | solution.py:546

commit v7 on v6

--- a/solution.py
+++ b/solution.py
@@ -31,6 +31,12 @@
 def row_mask(rows, first, count):
     place = sublanes(rows) + first
     return jnp.where((place >= 0) & (place < count), F32(1), F32(0))
+
+
+def block_mask(rows, lane, x_first, y_first):
+    x = lane % 4 + x_first
+    y = sublanes(rows) + y_first
+    return jnp.where((x >= 0) & (x < 64) & (y >= 0) & (y < 64), F32(1), F32(0))
 
 
 def scalar_mask(place, count):
@@ -173,7 +179,7 @@
     inside = row_mask(24, iy * 8 - 8, 128)
     repeat(0, 10, lambda q: win.start(q, inside * scalar_mask(ix * 4 - 3 + q, 64), ua), 5)
     repeat(0, 10, lambda q: win.relax(q, ua, ub), 5)
-    lane = lanes(16)
+    lane = lanes(8)
     corner = lane % 4 == 0
 
     def halve(q):
@@ -181,39 +187,44 @@
         parts = (m[0], m[1], src[2, q])
         for c in range(3):
             t = parts[c] + lroll(parts[c], -1)
-            tmp[c, q, pl.ds(0, 24), :] = t + lroll(t, -2)
-            tmp[c, q, pl.ds(24, 8), :] = jnp.zeros((8, 128), F32)
+            tmp[c, q] = t + lroll(t, -2)
 
     repeat(1, 9, halve, 4)
 
-    def cell(c, q):
-        t = tmp[c, q, pl.ds(0, 16, 2), :] + tmp[c, q, pl.ds(1, 16, 2), :]
-        return jnp.where(corner, 0.125 * t, 0.0)
-
-    for c in range(3):
-        src2[c, 0] = lroll(cell(c, 1), 2) + lroll(cell(c, 2), 3)
-        src2[c, 1] = sum((lroll(cell(c, 3 + j), j) for j in range(1, 4)), cell(c, 3))
-        src2[c, 2] = cell(c, 7) + lroll(cell(c, 8), 1)
+    def gather(b):
+        for c in range(3):
+            packed = jnp.zeros((8, 128), F32)
+            for j in range(4):
+                q = 4 * b + 1 + j
+                t = tmp[c, q, pl.ds(4, 8, 2), :] + tmp[c, q, pl.ds(5, 8, 2), :]
+                t = jnp.where(corner, 0.125 * t, 0.0)
+                packed = packed + (lroll(t, j) if j else t)
+            src2[c, b] = packed
+
+    for b in range(2):
+        gather(b)
     for buf in (va, vb):
         for c in range(2):
-            buf[c, 0] = jnp.zeros((16, 128), F32)
-            buf[c, 4] = jnp.zeros((16, 128), F32)
+            buf[c, 0] = jnp.zeros((8, 128), F32)
+            buf[c, 3] = jnp.zeros((8, 128), F32)
     win2 = Window(src2, gain2, 0.0625, 1, functools.partial(near2, lane))
-    inside2 = row_mask(16, iy * 4 - 4, 64)
-    for b in range(3):
-        win2.start(b, inside2 * scalar_mask(ix - 1 + b, 16), va)
-    for b in range(3):
+    for b in range(2):
+        win2.start(b, block_mask(8, lane, ix * 4 - 2 + 4 * b, iy * 4 - 2), va)
+    for b in range(2):
         win2.relax(b, va, vb)
-    _, m = win2.misfit(1, vb)
-
-    def third(v):
-        t = v + lroll(v, -1)
-        t = t + lroll(t, -4)
-        t = 0.125 * jnp.where((lane % 2 == 0) & (lane % 8 < 4), t + sroll(t, -1), 0.0)
-        return t[4:5] + lroll(t[6:7], 1)
-
-    field = third(m[0]) + lroll(third(m[1]), 4)
-    wave = third(src2[2, 1])
+    m = [win2.misfit(b, vb)[1] for b in range(2)]
+
+    def third(v0, v1):
+        total = jnp.zeros((1, 128), F32)
+        for v, slot, move in ((v0, 2, -2), (v1, 0, 2)):
+            t = v + lroll(v, -1)
+            t = t + lroll(t, -4)
+            t = 0.125 * jnp.where(lane % 8 == slot, t + sroll(t, -1), 0.0)
+            total = total + lroll(t[2:3], move) + lroll(t[4:5], move + 1)
+        return total
+
+    field = third(m[0][0], m[1][0]) + lroll(third(m[0][1], m[1][1]), 4)
+    wave = third(src2[2, 0], src2[2, 1])
     wave = wave + lroll(wave, 4)
     pair = jnp.concatenate([field, wave] * 4, axis=0)
 
@@ -227,7 +238,10 @@
     return jnp.where(real, lroll(v, -4), lroll(v, 4))
 
 
-def coarse_kernel(idx, flat, out, f3, w3, ga3, gb3, ua3, ub3, f4, w4, s4, e3):
+def up_kernel(
+    idx, src0, gain0, ub0, src1, gain1, ub1, src2, flat, out,
+    f3, w3, ga3, gb3, ua3, ub3, f4, w4, s4, e3, gain2, u2, wide2, cell1, ua1, ut1, wide1, wide0, ua0, ut0,
+):
     ix, iy = idx[0], idx[1]
     lane = lanes(16)
     real = lane // 4 % 2 == 0
@@ -254,7 +268,7 @@
             ref[at] = zero16
         for ref in (ua3, ub3):
             ref[at] = zero16
-    for j in range(7):
+    for j in range(5):
         e3[j] = jnp.zeros((32, 128), F32)
 
     def start3(x):
@@ -361,51 +375,46 @@
 
     repeat(0, 2, sweep3)
     for j in range(1, 6):
-        e3[j, pl.ds(8, 16), :] = ub3[ix + j]
-
-    for j in range(7):
-        out[j] = e3[j, pl.ds(iy + 5, 8), :]
-
-
-def up_kernel(
-    idx, src0, gain0, ub0, src1, gain1, ub1, src2, near, out,
-    gain2, u2, wide2, cell1, ua1, ut1, wide1, wide0, ua0, ut0,
-):
-    ix, iy = idx[0], idx[1]
+        e3[j - 1, pl.ds(8, 16), :] = ub3[ix + j]
+
     lane8 = lanes(8)
     lane24 = lanes(24)
     zero24 = jnp.zeros((24, 128), F32)
     for c in range(2):
-        u2[c, 0] = zero24
-        u2[c, 6] = zero24
-    win2 = Window(src2, gain2, 0.0625, 1, functools.partial(near2, lane24))
-    inside2 = row_mask(24, iy * 4 - 8, 64)
-    keep2 = [inside2 * scalar_mask(ix - 2 + b, 16) for b in range(5)]
-    for b in range(5):
+        u2[c, 0] = zero16
+        u2[c, 5] = zero16
+    win2 = Window(src2, gain2, 0.0625, 1, functools.partial(near2, lane))
+    keep2 = [block_mask(16, lane, ix * 4 - 6 + 4 * b, iy * 4 - 6) for b in range(4)]
+    for b in range(4):
         win2.start(b, keep2[b], u2)
     a_low = lane8 % 2 == 0
     b_low = lane8 // 4 % 2 == 0
-    x_low = lane8 // 2 % 2 == 0
+    h_low = lane8 // 2 % 2 == 0
 
     def widen3(c):
         sides = []
         shift = jnp.where(c == 0, 4, 124)
         for yl in range(2):
             pick = (lane8 // 4 % 2 == c) & (lane8 % 2 == yl)
-            cells = []
-            for bb in range(7):
-                t = jnp.where(pick, near[bb], 0.0)
+            ups, downs = [], []
+            for bb in range(5):
+                t = jnp.where(pick, e3[bb, pl.ds(iy + 5, 8), :], 0.0)
                 t = t + lroll(t, 1 - 2 * yl)
                 t = t + pltpu.roll(t, shift, 1)
                 low, high = z_pair(t, lane8, 8)
-                cells.append(0.75 * t + 0.25 * jnp.where(b_low, low, high))
+                t = 0.75 * t + 0.25 * jnp.where(b_low, low, high)
+                ups.append(lroll(t, 2))
+                downs.append(lroll(t, -2))
+            cells = [ups[0]]
+            cells += [jnp.where(h_low, downs[b], ups[b + 1]) for b in range(4)]
+            cells += [downs[4]]
             blocks = []
-            for b in range(1, 6):
+            for b in range(1, 5):
                 low = lroll(jnp.where(a_low, cells[b - 1], cells[b]), -2)
                 high = lroll(jnp.where(a_low, cells[b], cells[b + 1]), 2)
-                blocks.append(0.75 * cells[b] + 0.25 * jnp.where(x_low, low, high))
+                blocks.append(0.75 * cells[b] + 0.25 * jnp.where(h_low, low, high))
             sides.append(blocks)
-        for b in range(5):
+        for b in range(4):
             t0, t1 = sides[0][b], sides[1][b]
             wide2[c, b, pl.ds(0, 8, 4), :] = 0.75 * t0 + 0.25 * sroll(t1, 1)
             wide2[c, b, pl.ds(1, 8, 4), :] = 0.75 * t0 + 0.25 * t1
@@ -416,34 +425,38 @@
 
     def sweep2(i):
         add = jnp.where(i == 0, F32(1), F32(0))
-        new = [win2.relaxed(b, u2) for b in range(5)]
-        for b in range(5):
+        new = [win2.relaxed(b, u2) for b in range(4)]
+        for b in range(4):
             for c in range(2):
-                fix = wide2[c, b, pl.ds(4, 24), :] * (keep2[b] * add)
+                fix = wide2[c, b, pl.ds(6, 16), :] * (keep2[b] * add)
                 u2[c, b + 1] = new[b][c] + fix
 
     repeat(0, 3, sweep2)
 
-    lane16 = lanes(16)
-    slot4 = lane16 % 4
-
-    def widen2(b):
+    slot4 = lane % 4
+
+    def widen2(at, b, xl):
+        for c in range(2):
+            t = jnp.where(slot4 == xl, u2[c, b + 1], 0.0)
+            t = lroll(t, -xl) if xl else t
+            t = t + lroll(t, 1)
+            t = t + lroll(t, 2)
+            low, high = z_pair(t, lane, 4)
+            cell1[c, at] = 0.75 * t + 0.25 * jnp.where(slot4 < 2, low, high)
+
+    def widen_block(b):
         for xl in range(4):
-            for c in range(2):
-                t = jnp.where(slot4 == xl, u2[c, b + 1, pl.ds(4, 16), :], 0.0)
-                t = lroll(t, -xl) if xl else t
-                t = t + lroll(t, 1)
-                t = t + lroll(t, 2)
-                low, high = z_pair(t, lane16, 4)
-                cell1[c, 4 * b - 4 + xl] = 0.75 * t + 0.25 * jnp.where(slot4 < 2, low, high)
-
-    repeat(1, 4, widen2)
-    lane_even = lane16 % 2 == 0
+            widen2(4 * b - 3 + xl, b, xl)
+
+    widen2(0, 0, 3)
+    repeat(1, 3, widen_block)
+    widen2(9, 3, 0)
+    lane_even = lane % 2 == 0
 
     def mix2(q):
         for c in range(2):
-            side = jnp.where(lane_even, cell1[c, q], cell1[c, q + 2])
-            t = 0.75 * cell1[c, q + 1] + 0.25 * side
+            side = jnp.where(lane_even, cell1[c, q - 1], cell1[c, q + 1])
+            t = 0.75 * cell1[c, q] + 0.25 * side
             wide1[c, q, pl.ds(0, 16, 2), :] = 0.75 * t + 0.25 * sroll(t, 1)
             wide1[c, q, pl.ds(1, 16, 2), :] = 0.75 * t + 0.25 * sroll(t, -1)
 
@@ -456,7 +469,7 @@
     def correct1(q):
         keep = inside1 * scalar_mask(ix * 4 - 3 + q, 64)
         for c in range(2):
-            ua1[c, q + 1] = ub1[c, q + 1] + wide1[c, q, pl.ds(0, 24), :] * keep
+            ua1[c, q + 1] = ub1[c, q + 1] + wide1[c, q, pl.ds(4, 24), :] * keep
 
     repeat(1, 9, correct1, 4)
     win1 = Window(src1, gain1, 0.25, 1, functools.partial(near1, lane24))
@@ -470,7 +483,7 @@
             up, down = lroll(t, 1), lroll(t, -1)
             for p in range(2):
                 v = jnp.where(lane_even, t, up) if p == 0 else jnp.where(lane_even, down, t)
-                low, high = z_pair(v, lane16, 2)
+                low, high = z_pair(v, lane, 2)
                 v = 0.75 * v + 0.25 * jnp.where(lane_even, low, high)
                 wide0[c, 2 * q + p, pl.ds(0, 16, 2), :] = 0.75 * v + 0.25 * sroll(v, 1)
                 wide0[c, 2 * q + p, pl.ds(1, 16, 2), :] = 0.75 * v + 0.25 * sroll(v, -1)
@@ -578,38 +591,27 @@
     part, own2, gain1, first1 = call(
         down1_kernel,
         "down1",
-        [(64, 8, 128), (3, 3, 16, 128), (2, 10, 24, 128), n1],
-        [n1, (3, 10, 32, 128), (2, 3, 16, 128), (2, 5, 16, 128), (2, 5, 16, 128)],
+        [(64, 8, 128), (3, 2, 8, 128), (2, 10, 24, 128), n1],
+        [n1, (3, 10, 24, 128), (2, 2, 8, 128), (2, 4, 8, 128), (2, 4, 8, 128)],
         idx,
         src1,
     )
     part = part.reshape(256, 2, 128)
     flat = lax.all_to_all(part, ("gx", "gy"), 0, 0).reshape(512, 128)
-    low, high = trade(own2[:, 1:], own2[:, :2], "gx")
-    strip = jnp.concatenate([low, own2[:, 1:2], high], axis=1)
-    strip, flat = lax.optimization_barrier((strip, flat))
-    low, high = trade(strip[:, :, 4:12], strip[:, :, :8], "gy")
-    src2 = jnp.concatenate(
-        [low, strip[:, :, 4:8], high, jnp.zeros((3, 5, 4, 128), F32)], axis=2
-    )
+    low, high = trade(own2[:, 1:], own2[:, :1], "gx")
+    strip = jnp.concatenate([low, own2, high], axis=1)
+    low, high = trade(strip[:, :, 4:], strip[:, :, :4], "gy")
+    src2 = jnp.concatenate([low, strip, high], axis=2)
 
     wide = (22, 16, 128)
-    near = call(
-        coarse_kernel,
-        "coarse",
-        [(7, 8, 128)],
-        [wide, wide, wide, wide, wide, wide]
-        + [(4, 16, 128), (4, 16, 128), (4, 16, 128), (7, 32, 128)],
-        idx,
-        flat,
-        micros=5,
-    )[0]
     return call(
         up_kernel,
         "up",
         [(2, 16, 16, 128)],
-        [(2, 5, 24, 128), (2, 7, 24, 128), (2, 5, 32, 128)]
-        + [(2, 12, 16, 128), n1, n1, (2, 10, 32, 128), (2, 16, 32, 128), n0, n0],
+        [wide, wide, wide, wide, wide, wide]
+        + [(4, 16, 128), (4, 16, 128), (4, 16, 128), (5, 32, 128)]
+        + [(2, 4, 16, 128), (2, 6, 16, 128), (2, 4, 32, 128)]
+        + [(2, 10, 16, 128), n1, n1, (2, 10, 32, 128), (2, 16, 32, 128), n0, n0],
         idx,
         src0,
         gain0,
@@ -618,8 +620,8 @@
         gain1,
         first1,
         src2,
-        near,
-        micros=6,
+        flat,
+        micros=10,
     )[0]
 
 

time: 74.8 us -> 73.5 us (0.983)
    ppermute x6, waiting for transfers between devices: 10 us -> 5.53 us  [trade(): two = lax.ppermute(two, BOTH, partners(axis, 1))]
    all_to_all x1, starting transfers between devices: 19.6 us -> 15.3 us  [body(): flat = lax.all_to_all(part, ('gx', 'gy'), 0, 0).reshape(512, 128)]
    ppermute x6, starting transfers between devices: 4.76 us -> 8.06 us  [trade(): two = lax.ppermute(two, BOTH, partners(axis, 1))]
    ppermute x6, waiting for transfers between devices: 6.01 us -> 8.22 us  [trade(): one = lax.ppermute(one, BOTH, partners(axis, 0))]
    all_to_all x1, waiting for transfers between devices: 8.48 us -> 10.3 us  [body(): flat = lax.all_to_all(part, ('gx', 'gy'), 0, 0).reshape(512, 128)]
    ppermute x6, starting transfers between devices: 6.59 us -> 8.11 us  [trade(): one = lax.ppermute(one, BOTH, partners(axis, 0))]
    pallas_call x4 -> x3, Pallas kernels: 16.6 us -> 16 us  [call(): pl.pallas_call(kernel, name=name, out_shape=[jax.ShapeDtypeStruct(shape,...]
  transfers between devices with their start and end apart: 13 -> 13, of which waited for: 8 -> 9; matrix products, arithmetic and copies ran while one was open for 0% -> 0% of each run, Pallas kernels for 6% -> 0%
where the time goes in v7:
time: 73.5 us; the launch traced here: 73.3 us
  starting transfers between devices  31.5 us (43%)
  waiting for transfers between devices  24.1 us (33%)
  Pallas kernels  16 us (22%)
  other arithmetic  1.43 us (2%)
    pallas_call x3, Pallas kernels, call(): pl.pallas_call(kernel, name=name, out_shape=[jax.ShapeDtypeStruct(shape,...  16 us
    all_to_all x1, starting transfers between devices, body(): flat = lax.all_to_all(part, ('gx', 'gy'), 0, 0).reshape(512, 128)  15.3 us
    all_to_all x1, waiting for transfers between devices, body(): flat = lax.all_to_all(part, ('gx', 'gy'), 0, 0).reshape(512, 128)  10.3 us
    ppermute x6, waiting for transfers between devices, trade(): one = lax.ppermute(one, BOTH, partners(axis, 0))  8.22 us
    ppermute x6, starting transfers between devices, trade(): one = lax.ppermute(one, BOTH, partners(axis, 0))  8.11 us
    ppermute x6, starting transfers between devices, trade(): two = lax.ppermute(two, BOTH, partners(axis, 1))  8.06 us
    ppermute x6, waiting for transfers between devices, trade(): two = lax.ppermute(two, BOTH, partners(axis, 1))  5.53 us
  transfers between devices with their start and end apart: 13, of which 9 were waited for; matrix products, arithmetic and copies ran while one was open for 0% of the time, Pallas kernels for 0%

profile of v7, /device:TPU:1, one launch (start us, length us, event | category | flops | bytes accessed | tf_op | source)
XLA Modules:
  0.0 73.3 jit_solution(13011500289836526169)
XLA Ops:
  0.0 0.9 %broadcast_select_fusion.7 = (f32[3,3,16,128]{3,2,1,0:T(8,128)S(1)}, f32[3,3,16,128]{3,2,1,0:T(8,128)S(1)}, f32[3,3,16,128]{3,2,1,0:T(8,128)S(1)}) fusion(pred[]{:T(512)S(6)} %eq.18, f32[1,16,16,128]{3,2,1,0:T(8,128)} %bitcast.22, f32[2,16,16,128]{3,2,1,0:T(8,128)} %param.2), kind=kLoop, calls=%fused_computation.22 | loop fusion | flops 55296 | bytes 614401 | tf_op jit(solution)/shard_map/jit(_where)/select_n | solution.py:558
  0.9 0.0 copy-start
  0.9 3.3 %collective-permute-start.1 = (f32[3,3,16,128]{3,2,1,0:T(8,128)S(1)}, f32[3,3,16,128]{3,2,1,0:T(8,128)S(1)}, u32[]{:S(2)}, u32[]{:S(2)}) collective-permute-start(f32[3,3,16,128]{3,2,1,0:T(8,128)S(1)} %broadcast_select_fusion.6), channel_id=1, source_target_pairs={{0,16},{1,17},{2,18},{3,19},{4,20},{5,21},{6,22},{7,23},{8,24},{9,... | collective-permute-start | bytes 221192 | tf_op jit(solution)/shard_map/ppermute | solution.py:559
  4.2 0.0 collective-permute-start
  4.2 0.1 pad.22.clone
  4.3 0.0 copy-start.1
  4.3 0.8 %collective-permute-done.1 = f32[3,3,16,128]{3,2,1,0:T(8,128)S(1)} collective-permute-done((f32[3,3,16,128]{3,2,1,0:T(8,128)S(1)}, f32[3,3,16,128]{3,2,1,0:T(8,128)S(1)}, u32[]{:S(2)}, u32[]{:S(2)}) %collective-permute-start.1) | collective-permute-done | bytes 73760 | tf_op jit(solution)/shard_map/ppermute | solution.py:559
  5.2 3.1 %collective-permute-done = f32[3,3,16,128]{3,2,1,0:T(8,128)S(1)} collective-permute-done((f32[3,3,16,128]{3,2,1,0:T(8,128)S(1)}, f32[3,3,16,128]{3,2,1,0:T(8,128)S(1)}, u32[]{:S(2)}, u32[]{:S(2)}) %collective-permute-start) | collective-permute-done | bytes 73760 | tf_op jit(solution)/shard_map/ppermute | solution.py:560
  8.3 0.0 copy-done
  8.3 0.0 copy-done.1
  8.3 0.1 select_bitcast_fusion.1
  8.4 0.5 collective-permute-start.2
  9.0 0.5 collective-permute-start.3
  9.5 0.1 pad_add_fusion.idx
  9.6 0.3 collective-permute-done.2
  9.9 3.7 %collective-permute-done.3 = f32[9,22,128]{2,1,0:T(8,128)S(1)} collective-permute-done((f32[9,22,128]{2,1,0:T(8,128)S(1)}, f32[9,22,128]{2,1,0:T(8,128)S(1)}, u32[]{:S(2)}, u32[]{:S(2)}) %collective-permute-start.3) | collective-permute-done | bytes 101408 | tf_op jit(solution)/shard_map/ppermute | solution.py:559
  13.6 0.1 copy_bitcast_fusion
  13.7 0.2 maximum_maximum_fusion.src.src0
  13.9 2.4 %down0.1 = (f32[3,4,8,128]{3,2,1,0:T(8,128)S(1)}, f32[2,22,24,128]{3,2,1,0:T(8,128)S(1)}, f32[2,22,24,128]{3,2,1,0:T(8,128)S(1)}) custom-call(s32[2]{0:T(128)S(1)} %pad_add_fusion.idx, f32[3,22,24,128]{3,2,1,0:T(8,128)S(1)} %maximum_maximum_fusion.src.src0), custom_call_target="tpu_custom_call" | custom-call | bytes 7000000 | tf_op jit(solution)/shard_map/down0/pallas_call | solution.py:519
  16.3 1.3 %collective-permute-start.4 = (f32[3,3,8,128]{3,2,1,0:T(8,128)S(1)}, f32[3,3,8,128]{3,2,1,0:T(8,128)S(1)}, u32[]{:S(2)}, u32[]{:S(2)}) collective-permute-start(f32[3,3,8,128]{3,2,1,0:T(8,128)S(1)} %get-tuple-element.37), channel_id=1, source_target_pairs={{0,1},{1,0},{2,3},{3,2},{4,5},{5,4},{6,7},{7,6},{8,9},{9,8},{10,11... | collective-permute-start | bytes 110600 | tf_op jit(solution)/shard_map/ppermute | solution.py:560
  17.6 0.5 collective-permute-start.5
  18.1 1.7 %collective-permute-done.4 = f32[3,3,8,128]{3,2,1,0:T(8,128)S(1)} collective-permute-done((f32[3,3,8,128]{3,2,1,0:T(8,128)S(1)}, f32[3,3,8,128]{3,2,1,0:T(8,128)S(1)}, u32[]{:S(2)}, u32[]{:S(2)}) %collective-permute-start.4) | collective-permute-done | bytes 36896 | tf_op jit(solution)/shard_map/ppermute | solution.py:560
  19.8 0.0 collective-permute-done.5
  19.8 1.3 %collective-permute-start.7 = (f32[3,10,8,128]{3,2,1,0:T(8,128)S(1)}, f32[3,10,8,128]{3,2,1,0:T(8,128)S(1)}, u32[]{:S(2)}, u32[]{:S(2)}) collective-permute-start(f32[3,10,8,128]{3,2,1,0:T(8,128)S(1)} %pad_maximum_fusion.5), channel_id=1, source_target_pairs={{0,1},{1,0},{2,3},{3,2},{4,5},{5,4},{6,7},{7,6},{8,9},{9,8},{10,11... | collective-permute-start | bytes 368648 | tf_op jit(solution)/shard_map/ppermute | solution.py:559
  21.1 1.0 %collective-permute-start.6 = (f32[3,10,8,128]{3,2,1,0:T(8,128)S(1)}, f32[3,10,8,128]{3,2,1,0:T(8,128)S(1)}, u32[]{:S(2)}, u32[]{:S(2)}) collective-permute-start(f32[3,10,8,128]{3,2,1,0:T(8,128)S(1)} %pad_maximum_fusion.5), channel_id=1, source_target_pairs={{0,16},{1,2},{2,1},{3,4},{4,3},{5,6},{6,5},{7,8},{8,7},{9,10},{10,... | collective-permute-start | bytes 368648 | tf_op jit(solution)/shard_map/ppermute | solution.py:560
  22.2 1.5 %collective-permute-done.7 = f32[3,10,8,128]{3,2,1,0:T(8,128)S(1)} collective-permute-done((f32[3,10,8,128]{3,2,1,0:T(8,128)S(1)}, f32[3,10,8,128]{3,2,1,0:T(8,128)S(1)}, u32[]{:S(2)}, u32[]{:S(2)}) %collective-permute-start.7) | collective-permute-done | bytes 122912 | tf_op jit(solution)/shard_map/ppermute | solution.py:559
  23.6 0.0 collective-permute-done.6
  23.7 3.1 %down1.1 = (f32[64,8,128]{2,1,0:T(8,128)}, f32[3,2,8,128]{3,2,1,0:T(8,128)S(1)}, f32[2,10,24,128]{3,2,1,0:T(8,128)S(1)}, f32[2,12,24,128]{3,2,1,0:T(8,128)S(1)}) custom-call(s32[2]{0:T(128)S(1)} %pad_add_fusion.idx, f32[3,10,24,128]{3,2,1,0:T(8,128)S(1)} %pad_maximum_fusion.src.src1), custom_call_target="tpu_custom_call" | custom-call | bytes 7000000 | tf_op jit(solution)/shard_map/down1/pallas_call | solution.py:519
  26.8 3.0 %collective-permute-start.8 = (f32[3,1,8,128]{3,2,1,0:T(8,128)S(1)}, f32[3,1,8,128]{3,2,1,0:T(8,128)S(1)}, u32[]{:S(2)}, u32[]{:S(2)}) collective-permute-start(f32[3,1,8,128]{3,2,1,0:T(8,128)S(1)} %get-tuple-element.41), channel_id=1, source_target_pairs={{0,1},{1,0},{2,3},{3,2},{4,5},{5,4},{6,7},{7,6},{8,9},{9,8},{10,11... | collective-permute-start | bytes 36872 | tf_op jit(solution)/shard_map/ppermute | solution.py:560
  29.8 2.0 %collective-permute-start.9 = (f32[3,1,8,128]{3,2,1,0:T(8,128)S(1)}, f32[3,1,8,128]{3,2,1,0:T(8,128)S(1)}, u32[]{:S(2)}, u32[]{:S(2)}) collective-permute-start(f32[3,1,8,128]{3,2,1,0:T(8,128)S(1)} %get-tuple-element.42), channel_id=1, source_target_pairs={{0,16},{1,17},{2,18},{3,19},{4,20},{5,21},{6,22},{7,23},{8,24},{9,... | collective-permute-start | bytes 36872 | tf_op jit(solution)/shard_map/ppermute | solution.py:559
  31.8 15.3 %all-to-all-start = ((f32[256,2,128]{2,1,0:T(2,128)}), f32[256,2,128]{2,1,0:T(2,128)S(1)}, u32[]{:S(2)}, u32[]{:S(2)}) async-start(f32[256,2,128]{2,1,0:T(2,128)} %bitcast.11), calls=%async_computation | async-start | bytes 524288 | tf_op jit(solution)/shard_map/all_to_all | solution.py:600
  47.1 0.0 collective-permute-done.8
  47.1 0.0 collective-permute-done.9
  47.2 2.2 %collective-permute-start.10 = (f32[3,4,4,128]{3,2,1,0:T(4,128)S(1)}, f32[3,4,4,128]{3,2,1,0:T(4,128)S(1)}, u32[]{:S(2)}, u32[]{:S(2)}) collective-permute-start(f32[3,4,4,128]{3,2,1,0:T(4,128)S(1)} %get-tuple-element.35), channel_id=1, source_target_pairs={{0,16},{1,2},{2,1},{3,4},{4,3},{5,6},{6,5},{7,8},{8,7},{9,10},{10,... | collective-permute-start | bytes 73736 | tf_op jit(solution)/shard_map/ppermute | solution.py:560
  49.4 0.4 collective-permute-start.11
  49.8 0.4 collective-permute-done.10
  50.2 2.2 %collective-permute-done.11 = f32[3,4,4,128]{3,2,1,0:T(4,128)S(1)} collective-permute-done((f32[3,4,4,128]{3,2,1,0:T(4,128)S(1)}, f32[3,4,4,128]{3,2,1,0:T(4,128)S(1)}, u32[]{:S(2)}, u32[]{:S(2)}) %collective-permute-start.11) | collective-permute-done | bytes 24608 | tf_op jit(solution)/shard_map/ppermute | solution.py:559
  52.5 10.3 %all-to-all-done = f32[256,2,128]{2,1,0:T(2,128)S(1)} async-done(((f32[256,2,128]{2,1,0:T(2,128)}), f32[256,2,128]{2,1,0:T(2,128)S(1)}, u32[]{:S(2)}, u32[]{:S(2)}) %all-to-all-start) | async-done | bytes 262176 | tf_op jit(solution)/shard_map/all_to_all | solution.py:600
  62.8 10.5 %up.1 = f32[2,16,16,128]{3,2,1,0:T(8,128)} custom-call(s32[2]{0:T(128)S(1)} %pad_add_fusion.idx, f32[3,22,24,128]{3,2,1,0:T(8,128)S(1)} %maximum_maximum_fusion.src.src0, f32[2,22,24,128]{3,2,1,0:T(8,128)S(1)} %get-tuple-element.12.gain0, f32[2,22,24,128]{3,2,1,0:T(8,128)S(1)} %get-tuple-element.13.ub0, f32[3,10,24,128]{3,2,1,0:T(8,128)S(1)} %pad_maximum_fusion.src.src1, ...), custom_call_target="tpu_custom_call" | custom-call | bytes 35000000 | tf_op jit(solution)/shard_map/up/pallas_call | solution.py:519
  (18 shorter events, 0.3 us)
Async XLA Ops:
  0.9 7.4 %copy-start = (f32[2,16,16,128]{3,2,1,0:T(8,128)S(1)}, f32[2,16,16,128]{3,2,1,0:T(8,128)}, u32[]{:S(2)}) copy-start(f32[2,16,16,128]{3,2,1,0:T(8,128)} %param.2) | copy-start | bytes 786436
  0.9 4.2 %collective-permute-start.1 = (f32[3,3,16,128]{3,2,1,0:T(8,128)S(1)}, f32[3,3,16,128]{3,2,1,0:T(8,128)S(1)}, u32[]{:S(2)}, u32[]{:S(2)}) collective-permute-start(f32[3,3,16,128]{3,2,1,0:T(8,128)S(1)} %broadcast_select_fusion.6), channel_id=1, source_target_pairs={{0,16},{1,17},{2,18},{3,19},{4,20},{5,21},{6,22},{7,23},{8,24},{9,... | collective-permute-start | bytes 221192 | tf_op jit(solution)/shard_map/ppermute | solution.py:559
  4.2 4.1 %collective-permute-start = (f32[3,3,16,128]{3,2,1,0:T(8,128)S(1)}, f32[3,3,16,128]{3,2,1,0:T(8,128)S(1)}, u32[]{:S(2)}, u32[]{:S(2)}) collective-permute-start(f32[3,3,16,128]{3,2,1,0:T(8,128)S(1)} %get-tuple-element.22), channel_id=1, source_target_pairs={{0,1},{1,0},{2,3},{3,2},{4,5},{5,4},{6,7},{7,6},{8,9},{9,8},{10,11... | collective-permute-start | bytes 221192 | tf_op jit(solution)/shard_map/ppermute | solution.py:560
  4.3 4.0 %copy-start.1 = (f32[16,16,128]{2,1,0:T(8,128)S(1)}, f32[16,16,128]{2,1,0:T(8,128)}, u32[]{:S(2)}) copy-start(f32[16,16,128]{2,1,0:T(8,128)} %param.3) | copy-start | bytes 393220
  8.4 1.4 %collective-permute-start.2 = (f32[9,22,128]{2,1,0:T(8,128)S(1)}, f32[9,22,128]{2,1,0:T(8,128)S(1)}, u32[]{:S(2)}, u32[]{:S(2)}) collective-permute-start(f32[9,22,128]{2,1,0:T(8,128)S(1)} %bitcast.27), channel_id=1, source_target_pairs={{0,16},{1,2},{2,1},{3,4},{4,3},{5,6},{6,5},{7,8},{8,7},{9,10},{10,... | collective-permute-start | bytes 304136 | tf_op jit(solution)/shard_map/ppermute | solution.py:560
  9.0 4.6 %collective-permute-start.3 = (f32[9,22,128]{2,1,0:T(8,128)S(1)}, f32[9,22,128]{2,1,0:T(8,128)S(1)}, u32[]{:S(2)}, u32[]{:S(2)}) collective-permute-start(f32[9,22,128]{2,1,0:T(8,128)S(1)} %bitcast.28), channel_id=1, source_target_pairs={{0,1},{1,0},{2,3},{3,2},{4,5},{5,4},{6,7},{7,6},{8,9},{9,8},{10,11... | collective-permute-start | bytes 304136 | tf_op jit(solution)/shard_map/ppermute | solution.py:559
  16.3 3.5 %collective-permute-start.4 = (f32[3,3,8,128]{3,2,1,0:T(8,128)S(1)}, f32[3,3,8,128]{3,2,1,0:T(8,128)S(1)}, u32[]{:S(2)}, u32[]{:S(2)}) collective-permute-start(f32[3,3,8,128]{3,2,1,0:T(8,128)S(1)} %get-tuple-element.37), channel_id=1, source_target_pairs={{0,1},{1,0},{2,3},{3,2},{4,5},{5,4},{6,7},{7,6},{8,9},{9,8},{10,11... | collective-permute-start | bytes 110600 | tf_op jit(solution)/shard_map/ppermute | solution.py:560
  17.6 2.2 %collective-permute-start.5 = (f32[3,3,8,128]{3,2,1,0:T(8,128)S(1)}, f32[3,3,8,128]{3,2,1,0:T(8,128)S(1)}, u32[]{:S(2)}, u32[]{:S(2)}) collective-permute-start(f32[3,3,8,128]{3,2,1,0:T(8,128)S(1)} %get-tuple-element.38), channel_id=1, source_target_pairs={{0,16},{1,17},{2,18},{3,19},{4,20},{5,21},{6,22},{7,23},{8,24},{9,... | collective-permute-start | bytes 110600 | tf_op jit(solution)/shard_map/ppermute | solution.py:559
  19.8 3.8 %collective-permute-start.7 = (f32[3,10,8,128]{3,2,1,0:T(8,128)S(1)}, f32[3,10,8,128]{3,2,1,0:T(8,128)S(1)}, u32[]{:S(2)}, u32[]{:S(2)}) collective-permute-start(f32[3,10,8,128]{3,2,1,0:T(8,128)S(1)} %pad_maximum_fusion.5), channel_id=1, source_target_pairs={{0,1},{1,0},{2,3},{3,2},{4,5},{5,4},{6,7},{7,6},{8,9},{9,8},{10,11... | collective-permute-start | bytes 368648 | tf_op jit(solution)/shard_map/ppermute | solution.py:559
  21.1 2.5 %collective-permute-start.6 = (f32[3,10,8,128]{3,2,1,0:T(8,128)S(1)}, f32[3,10,8,128]{3,2,1,0:T(8,128)S(1)}, u32[]{:S(2)}, u32[]{:S(2)}) collective-permute-start(f32[3,10,8,128]{3,2,1,0:T(8,128)S(1)} %pad_maximum_fusion.5), channel_id=1, source_target_pairs={{0,16},{1,2},{2,1},{3,4},{4,3},{5,6},{6,5},{7,8},{8,7},{9,10},{10,... | collective-permute-start | bytes 368648 | tf_op jit(solution)/shard_map/ppermute | solution.py:560
  26.8 20.3 %collective-permute-start.8 = (f32[3,1,8,128]{3,2,1,0:T(8,128)S(1)}, f32[3,1,8,128]{3,2,1,0:T(8,128)S(1)}, u32[]{:S(2)}, u32[]{:S(2)}) collective-permute-start(f32[3,1,8,128]{3,2,1,0:T(8,128)S(1)} %get-tuple-element.41), channel_id=1, source_target_pairs={{0,1},{1,0},{2,3},{3,2},{4,5},{5,4},{6,7},{7,6},{8,9},{9,8},{10,11... | collective-permute-start | bytes 36872 | tf_op jit(solution)/shard_map/ppermute | solution.py:560
  29.8 17.3 %collective-permute-start.9 = (f32[3,1,8,128]{3,2,1,0:T(8,128)S(1)}, f32[3,1,8,128]{3,2,1,0:T(8,128)S(1)}, u32[]{:S(2)}, u32[]{:S(2)}) collective-permute-start(f32[3,1,8,128]{3,2,1,0:T(8,128)S(1)} %get-tuple-element.42), channel_id=1, source_target_pairs={{0,16},{1,17},{2,18},{3,19},{4,20},{5,21},{6,22},{7,23},{8,24},{9,... | collective-permute-start | bytes 36872 | tf_op jit(solution)/shard_map/ppermute | solution.py:559
  31.8 31.0 %all-to-all-start = ((f32[256,2,128]{2,1,0:T(2,128)}), f32[256,2,128]{2,1,0:T(2,128)S(1)}, u32[]{:S(2)}, u32[]{:S(2)}) async-start(f32[256,2,128]{2,1,0:T(2,128)} %bitcast.11), calls=%async_computation | async-start | bytes 524288 | tf_op jit(solution)/shard_map/all_to_all | solution.py:600
  47.2 3.1 %collective-permute-start.10 = (f32[3,4,4,128]{3,2,1,0:T(4,128)S(1)}, f32[3,4,4,128]{3,2,1,0:T(4,128)S(1)}, u32[]{:S(2)}, u32[]{:S(2)}) collective-permute-start(f32[3,4,4,128]{3,2,1,0:T(4,128)S(1)} %get-tuple-element.35), channel_id=1, source_target_pairs={{0,16},{1,2},{2,1},{3,4},{4,3},{5,6},{6,5},{7,8},{8,7},{9,10},{10,... | collective-permute-start | bytes 73736 | tf_op jit(solution)/shard_map/ppermute | solution.py:560
  49.4 3.1 %collective-permute-start.11 = (f32[3,4,4,128]{3,2,1,0:T(4,128)S(1)}, f32[3,4,4,128]{3,2,1,0:T(4,128)S(1)}, u32[]{:S(2)}, u32[]{:S(2)}) collective-permute-start(f32[3,4,4,128]{3,2,1,0:T(4,128)S(1)} %get-tuple-element.36), channel_id=1, source_target_pairs={{0,1},{1,0},{2,3},{3,2},{4,5},{5,4},{6,7},{7,6},{8,9},{9,8},{10,11... | collective-permute-start | bytes 73736 | tf_op jit(solution)/shard_map/ppermute | solution.py:559

commit v8 on v7

--- a/solution.py
+++ b/solution.py
@@ -228,10 +228,8 @@
     wave = wave + lroll(wave, 4)
     pair = jnp.concatenate([field, wave] * 4, axis=0)
 
-    def spread(i):
+    for i in range(4):
         out[i] = pair
-
-    repeat(0, 64, spread, 8)
 
 
 def swap(v, real):
@@ -273,8 +271,8 @@
 
     def start3(x):
         at = x + 3
-        f3[at] = flat[pl.ds(32 * x, 16, 2), :]
-        w = flat[pl.ds(32 * x + 1, 16, 2), :]
+        f3[at] = flat[pl.ds(2 * x, 16, 32), :]
+        w = flat[pl.ds(2 * x + 1, 16, 32), :]
         w3[at] = w
         ga, gb = packed_gain(w, 1.0 / 64)
         ga3[at], gb3[at] = ga, gb
@@ -591,13 +589,14 @@
     part, own2, gain1, first1 = call(
         down1_kernel,
         "down1",
-        [(64, 8, 128), (3, 2, 8, 128), (2, 10, 24, 128), n1],
+        [(4, 8, 128), (3, 2, 8, 128), (2, 10, 24, 128), n1],
         [n1, (3, 10, 24, 128), (2, 2, 8, 128), (2, 4, 8, 128), (2, 4, 8, 128)],
         idx,
         src1,
     )
-    part = part.reshape(256, 2, 128)
-    flat = lax.all_to_all(part, ("gx", "gy"), 0, 0).reshape(512, 128)
+    line = lax.all_to_all(part.reshape(16, 2, 128), "gx", 0, 0).reshape(1, 32, 128)
+    line = jnp.broadcast_to(line, (16, 32, 128))
+    flat = lax.all_to_all(line, "gy", 0, 0).reshape(512, 128)
     low, high = trade(own2[:, 1:], own2[:, :1], "gx")
     strip = jnp.concatenate([low, own2, high], axis=1)
     low, high = trade(strip[:, :, 4:], strip[:, :, :4], "gy")

time: 73.5 us -> 74.6 us (1.015)
  starting transfers between devices: 31.5 us -> 34.7 us
  waiting for transfers between devices: 24.1 us -> 21.1 us
    ppermute x6, starting transfers between devices: 8.11 us -> 12.3 us  [trade(): one = lax.ppermute(one, BOTH, partners(axis, 0))]
    ppermute x6, waiting for transfers between devices: 8.22 us -> 6.01 us  [trade(): one = lax.ppermute(one, BOTH, partners(axis, 0))]
    ppermute x6, starting transfers between devices: 8.06 us -> 6.01 us  [trade(): two = lax.ppermute(two, BOTH, partners(axis, 1))]
    all_to_all x1 -> x2, starting transfers between devices: 15.3 us -> 16.4 us  [the longest x1 9.61 us: body(): flat = lax.all_to_all(line, 'gy', 0, 0).reshape(512, 128)]
    all_to_all x1 -> x2, waiting for transfers between devices: 10.3 us -> 9.93 us  [the longest x1 7.47 us: body(): flat = lax.all_to_all(line, 'gy', 0, 0).reshape(512, 128)]
  transfers between devices with their start and end apart: 13 -> 14, of which waited for: 9 -> 8; matrix products, arithmetic and copies ran while one was open for 0% -> 1% of each run, Pallas kernels for 0% -> 0%
where the time goes in v8:
time: 74.6 us; the launch traced here: 74.3 us
  starting transfers between devices  34.7 us (47%)
  waiting for transfers between devices  21.1 us (28%)
  Pallas kernels  16 us (21%)
  other arithmetic  1.43 us (2%)
  local copies, waits for them, and re-layouts  0.91 us (1%)
    pallas_call x3, Pallas kernels, call(): pl.pallas_call(kernel, name=name, out_shape=[jax.ShapeDtypeStruct(shape,...  16 us
    ppermute x6, starting transfers between devices, trade(): one = lax.ppermute(one, BOTH, partners(axis, 0))  12.3 us
    all_to_all x1, starting transfers between devices, body(): flat = lax.all_to_all(line, 'gy', 0, 0).reshape(512, 128)  9.61 us
    all_to_all x1, waiting for transfers between devices, body(): flat = lax.all_to_all(line, 'gy', 0, 0).reshape(512, 128)  7.47 us
    all_to_all x1, starting transfers between devices, body(): lax.all_to_all(part.reshape(16, 2, 128), 'gx', 0, 0).reshape(1, 32, 128)  6.76 us
    ppermute x6, starting transfers between devices, trade(): two = lax.ppermute(two, BOTH, partners(axis, 1))  6.01 us
    ppermute x6, waiting for transfers between devices, trade(): one = lax.ppermute(one, BOTH, partners(axis, 0))  6.01 us
    ppermute x6, waiting for transfers between devices, trade(): two = lax.ppermute(two, BOTH, partners(axis, 1))  5.12 us
  transfers between devices with their start and end apart: 14, of which 8 were waited for; matrix products, arithmetic and copies ran while one was open for 1% of the time, Pallas kernels for 0%

profile of v8, /device:TPU:1, one launch (start us, length us, event | category | flops | bytes accessed | tf_op | source)
XLA Modules:
  0.0 74.3 jit_solution(7498717278422760049)
XLA Ops:
  0.0 0.9 %broadcast_select_fusion.7 = (f32[3,3,16,128]{3,2,1,0:T(8,128)S(1)}, f32[3,3,16,128]{3,2,1,0:T(8,128)S(1)}, f32[3,3,16,128]{3,2,1,0:T(8,128)S(1)}) fusion(pred[]{:T(512)S(6)} %eq.18, f32[1,16,16,128]{3,2,1,0:T(8,128)} %bitcast.23, f32[2,16,16,128]{3,2,1,0:T(8,128)} %param.2), kind=kLoop, calls=%fused_computation.22 | loop fusion | flops 55296 | bytes 614401 | tf_op jit(solution)/shard_map/jit(_where)/select_n | solution.py:556
  0.9 0.0 copy-start
  0.9 3.3 %collective-permute-start.1 = (f32[3,3,16,128]{3,2,1,0:T(8,128)S(1)}, f32[3,3,16,128]{3,2,1,0:T(8,128)S(1)}, u32[]{:S(2)}, u32[]{:S(2)}) collective-permute-start(f32[3,3,16,128]{3,2,1,0:T(8,128)S(1)} %broadcast_select_fusion.6), channel_id=1, source_target_pairs={{0,16},{1,17},{2,18},{3,19},{4,20},{5,21},{6,22},{7,23},{8,24},{9,... | collective-permute-start | bytes 221192 | tf_op jit(solution)/shard_map/ppermute | solution.py:557
  4.2 0.0 collective-permute-start
  4.2 0.1 pad.22.clone
  4.3 0.0 copy-start.1
  4.3 0.8 %collective-permute-done.1 = f32[3,3,16,128]{3,2,1,0:T(8,128)S(1)} collective-permute-done((f32[3,3,16,128]{3,2,1,0:T(8,128)S(1)}, f32[3,3,16,128]{3,2,1,0:T(8,128)S(1)}, u32[]{:S(2)}, u32[]{:S(2)}) %collective-permute-start.1) | collective-permute-done | bytes 73760 | tf_op jit(solution)/shard_map/ppermute | solution.py:557
  5.2 3.1 %collective-permute-done = f32[3,3,16,128]{3,2,1,0:T(8,128)S(1)} collective-permute-done((f32[3,3,16,128]{3,2,1,0:T(8,128)S(1)}, f32[3,3,16,128]{3,2,1,0:T(8,128)S(1)}, u32[]{:S(2)}, u32[]{:S(2)}) %collective-permute-start) | collective-permute-done | bytes 73760 | tf_op jit(solution)/shard_map/ppermute | solution.py:558
  8.3 0.0 copy-done
  8.3 0.0 copy-done.1
  8.3 0.1 select_bitcast_fusion.1
  8.4 0.5 collective-permute-start.2
  9.0 0.5 collective-permute-start.3
  9.5 0.1 pad_add_fusion.idx
  9.6 0.3 collective-permute-done.2
  9.9 3.7 %collective-permute-done.3 = f32[9,22,128]{2,1,0:T(8,128)S(1)} collective-permute-done((f32[9,22,128]{2,1,0:T(8,128)S(1)}, f32[9,22,128]{2,1,0:T(8,128)S(1)}, u32[]{:S(2)}, u32[]{:S(2)}) %collective-permute-start.3) | collective-permute-done | bytes 101408 | tf_op jit(solution)/shard_map/ppermute | solution.py:557
  13.6 0.1 copy_bitcast_fusion
  13.7 0.2 maximum_maximum_fusion.src.src0
  13.9 2.4 %down0.1 = (f32[3,4,8,128]{3,2,1,0:T(8,128)S(1)}, f32[2,22,24,128]{3,2,1,0:T(8,128)S(1)}, f32[2,22,24,128]{3,2,1,0:T(8,128)S(1)}) custom-call(s32[2]{0:T(128)S(1)} %pad_add_fusion.idx, f32[3,22,24,128]{3,2,1,0:T(8,128)S(1)} %maximum_maximum_fusion.src.src0), custom_call_target="tpu_custom_call" | custom-call | bytes 7000000 | tf_op jit(solution)/shard_map/down0/pallas_call | solution.py:517
  16.3 1.3 %collective-permute-start.4 = (f32[3,3,8,128]{3,2,1,0:T(8,128)S(1)}, f32[3,3,8,128]{3,2,1,0:T(8,128)S(1)}, u32[]{:S(2)}, u32[]{:S(2)}) collective-permute-start(f32[3,3,8,128]{3,2,1,0:T(8,128)S(1)} %get-tuple-element.37), channel_id=1, source_target_pairs={{0,1},{1,0},{2,3},{3,2},{4,5},{5,4},{6,7},{7,6},{8,9},{9,8},{10,11... | collective-permute-start | bytes 110600 | tf_op jit(solution)/shard_map/ppermute | solution.py:558
  17.6 0.5 collective-permute-start.5
  18.1 1.7 %collective-permute-done.4 = f32[3,3,8,128]{3,2,1,0:T(8,128)S(1)} collective-permute-done((f32[3,3,8,128]{3,2,1,0:T(8,128)S(1)}, f32[3,3,8,128]{3,2,1,0:T(8,128)S(1)}, u32[]{:S(2)}, u32[]{:S(2)}) %collective-permute-start.4) | collective-permute-done | bytes 36896 | tf_op jit(solution)/shard_map/ppermute | solution.py:558
  19.8 0.0 collective-permute-done.5
  19.8 1.3 %collective-permute-start.7 = (f32[3,10,8,128]{3,2,1,0:T(8,128)S(1)}, f32[3,10,8,128]{3,2,1,0:T(8,128)S(1)}, u32[]{:S(2)}, u32[]{:S(2)}) collective-permute-start(f32[3,10,8,128]{3,2,1,0:T(8,128)S(1)} %pad_maximum_fusion.5), channel_id=1, source_target_pairs={{0,1},{1,0},{2,3},{3,2},{4,5},{5,4},{6,7},{7,6},{8,9},{9,8},{10,11... | collective-permute-start | bytes 368648 | tf_op jit(solution)/shard_map/ppermute | solution.py:557
  21.1 1.0 %collective-permute-start.6 = (f32[3,10,8,128]{3,2,1,0:T(8,128)S(1)}, f32[3,10,8,128]{3,2,1,0:T(8,128)S(1)}, u32[]{:S(2)}, u32[]{:S(2)}) collective-permute-start(f32[3,10,8,128]{3,2,1,0:T(8,128)S(1)} %pad_maximum_fusion.5), channel_id=1, source_target_pairs={{0,16},{1,2},{2,1},{3,4},{4,3},{5,6},{6,5},{7,8},{8,7},{9,10},{10,... | collective-permute-start | bytes 368648 | tf_op jit(solution)/shard_map/ppermute | solution.py:558
  22.2 1.5 %collective-permute-done.7 = f32[3,10,8,128]{3,2,1,0:T(8,128)S(1)} collective-permute-done((f32[3,10,8,128]{3,2,1,0:T(8,128)S(1)}, f32[3,10,8,128]{3,2,1,0:T(8,128)S(1)}, u32[]{:S(2)}, u32[]{:S(2)}) %collective-permute-start.7) | collective-permute-done | bytes 122912 | tf_op jit(solution)/shard_map/ppermute | solution.py:557
  23.6 0.0 collective-permute-done.6
  23.7 2.9 %down1.1 = (f32[4,8,128]{2,1,0:T(8,128)}, f32[3,2,8,128]{3,2,1,0:T(8,128)S(1)}, f32[2,10,24,128]{3,2,1,0:T(8,128)S(1)}, f32[2,12,24,128]{3,2,1,0:T(8,128)S(1)}) custom-call(s32[2]{0:T(128)S(1)} %pad_add_fusion.idx, f32[3,10,24,128]{3,2,1,0:T(8,128)S(1)} %pad_maximum_fusion.src.src1), custom_call_target="tpu_custom_call" | custom-call | bytes 7000000 | tf_op jit(solution)/shard_map/down1/pallas_call | solution.py:517
  26.6 3.0 %collective-permute-start.8 = (f32[3,1,8,128]{3,2,1,0:T(8,128)S(1)}, f32[3,1,8,128]{3,2,1,0:T(8,128)S(1)}, u32[]{:S(2)}, u32[]{:S(2)}) collective-permute-start(f32[3,1,8,128]{3,2,1,0:T(8,128)S(1)} %get-tuple-element.41), channel_id=1, source_target_pairs={{0,1},{1,0},{2,3},{3,2},{4,5},{5,4},{6,7},{7,6},{8,9},{9,8},{10,11... | collective-permute-start | bytes 36872 | tf_op jit(solution)/shard_map/ppermute | solution.py:558
  29.6 2.0 %collective-permute-start.9 = (f32[3,1,8,128]{3,2,1,0:T(8,128)S(1)}, f32[3,1,8,128]{3,2,1,0:T(8,128)S(1)}, u32[]{:S(2)}, u32[]{:S(2)}) collective-permute-start(f32[3,1,8,128]{3,2,1,0:T(8,128)S(1)} %get-tuple-element.42), channel_id=1, source_target_pairs={{0,16},{1,17},{2,18},{3,19},{4,20},{5,21},{6,22},{7,23},{8,24},{9,... | collective-permute-start | bytes 36872 | tf_op jit(solution)/shard_map/ppermute | solution.py:557
  31.7 6.8 %all-to-all-start = ((f32[16,2,128]{2,1,0:T(2,128)}), f32[16,2,128]{2,1,0:T(2,128)S(1)}, u32[]{:S(2)}, u32[]{:S(2)}) async-start(f32[16,2,128]{2,1,0:T(2,128)} %bitcast.11), calls=%async_computation | async-start | bytes 32768 | tf_op jit(solution)/shard_map/all_to_all | solution.py:597
  38.4 0.0 collective-permute-done.8
  38.4 0.0 collective-permute-done.9
  38.5 0.2 collective-permute-start.10
  38.7 4.6 %collective-permute-start.11 = (f32[3,4,4,128]{3,2,1,0:T(4,128)S(1)}, f32[3,4,4,128]{3,2,1,0:T(4,128)S(1)}, u32[]{:S(2)}, u32[]{:S(2)}) collective-permute-start(f32[3,4,4,128]{3,2,1,0:T(4,128)S(1)} %get-tuple-element.36), channel_id=1, source_target_pairs={{0,1},{1,0},{2,3},{3,2},{4,5},{5,4},{6,7},{7,6},{8,9},{9,8},{10,11... | collective-permute-start | bytes 73736 | tf_op jit(solution)/shard_map/ppermute | solution.py:557
  43.3 2.5 %all-to-all-done = f32[16,2,128]{2,1,0:T(2,128)S(1)} async-done(((f32[16,2,128]{2,1,0:T(2,128)}), f32[16,2,128]{2,1,0:T(2,128)S(1)}, u32[]{:S(2)}, u32[]{:S(2)}) %all-to-all-start) | async-done | bytes 16416 | tf_op jit(solution)/shard_map/all_to_all | solution.py:597
  45.7 0.7 broadcast_in_dim.16
  46.5 9.6 %all-to-all-start.1 = ((f32[16,32,128]{2,1,0:T(8,128)}), f32[16,32,128]{2,1,0:T(8,128)S(1)}, u32[]{:S(2)}, u32[]{:S(2)}) async-start(f32[16,32,128]{2,1,0:T(8,128)} %broadcast_in_dim.16), calls=%async_computation.1 | async-start | bytes 524288 | tf_op jit(solution)/shard_map/all_to_all | solution.py:599
  56.1 0.0 collective-permute-done.10
  56.1 0.0 collective-permute-done.11
  56.2 7.5 %all-to-all-done.1 = f32[16,32,128]{2,1,0:T(8,128)S(1)} async-done(((f32[16,32,128]{2,1,0:T(8,128)}), f32[16,32,128]{2,1,0:T(8,128)S(1)}, u32[]{:S(2)}, u32[]{:S(2)}) %all-to-all-start.1) | async-done | bytes 262176 | tf_op jit(solution)/shard_map/all_to_all | solution.py:599
  63.6 10.6 %up.1 = f32[2,16,16,128]{3,2,1,0:T(8,128)} custom-call(s32[2]{0:T(128)S(1)} %pad_add_fusion.idx, f32[3,22,24,128]{3,2,1,0:T(8,128)S(1)} %maximum_maximum_fusion.src.src0, f32[2,22,24,128]{3,2,1,0:T(8,128)S(1)} %get-tuple-element.12.gain0, f32[2,22,24,128]{3,2,1,0:T(8,128)S(1)} %get-tuple-element.13.ub0, f32[3,10,24,128]{3,2,1,0:T(8,128)S(1)} %pad_maximum_fusion.src.src1, ...), custom_call_target="tpu_custom_call" | custom-call | bytes 35000000 | tf_op jit(solution)/shard_map/up/pallas_call | solution.py:517
  (18 shorter events, 0.3 us)
Async XLA Ops:
  0.9 7.4 %copy-start = (f32[2,16,16,128]{3,2,1,0:T(8,128)S(1)}, f32[2,16,16,128]{3,2,1,0:T(8,128)}, u32[]{:S(2)}) copy-start(f32[2,16,16,128]{3,2,1,0:T(8,128)} %param.2) | copy-start | bytes 786436
  0.9 4.2 %collective-permute-start.1 = (f32[3,3,16,128]{3,2,1,0:T(8,128)S(1)}, f32[3,3,16,128]{3,2,1,0:T(8,128)S(1)}, u32[]{:S(2)}, u32[]{:S(2)}) collective-permute-start(f32[3,3,16,128]{3,2,1,0:T(8,128)S(1)} %broadcast_select_fusion.6), channel_id=1, source_target_pairs={{0,16},{1,17},{2,18},{3,19},{4,20},{5,21},{6,22},{7,23},{8,24},{9,... | collective-permute-start | bytes 221192 | tf_op jit(solution)/shard_map/ppermute | solution.py:557
  4.2 4.1 %collective-permute-start = (f32[3,3,16,128]{3,2,1,0:T(8,128)S(1)}, f32[3,3,16,128]{3,2,1,0:T(8,128)S(1)}, u32[]{:S(2)}, u32[]{:S(2)}) collective-permute-start(f32[3,3,16,128]{3,2,1,0:T(8,128)S(1)} %get-tuple-element.22), channel_id=1, source_target_pairs={{0,1},{1,0},{2,3},{3,2},{4,5},{5,4},{6,7},{7,6},{8,9},{9,8},{10,11... | collective-permute-start | bytes 221192 | tf_op jit(solution)/shard_map/ppermute | solution.py:558
  4.3 4.0 %copy-start.1 = (f32[16,16,128]{2,1,0:T(8,128)S(1)}, f32[16,16,128]{2,1,0:T(8,128)}, u32[]{:S(2)}) copy-start(f32[16,16,128]{2,1,0:T(8,128)} %param.3) | copy-start | bytes 393220
  8.4 1.4 %collective-permute-start.2 = (f32[9,22,128]{2,1,0:T(8,128)S(1)}, f32[9,22,128]{2,1,0:T(8,128)S(1)}, u32[]{:S(2)}, u32[]{:S(2)}) collective-permute-start(f32[9,22,128]{2,1,0:T(8,128)S(1)} %bitcast.28), channel_id=1, source_target_pairs={{0,16},{1,2},{2,1},{3,4},{4,3},{5,6},{6,5},{7,8},{8,7},{9,10},{10,... | collective-permute-start | bytes 304136 | tf_op jit(solution)/shard_map/ppermute | solution.py:558
  9.0 4.6 %collective-permute-start.3 = (f32[9,22,128]{2,1,0:T(8,128)S(1)}, f32[9,22,128]{2,1,0:T(8,128)S(1)}, u32[]{:S(2)}, u32[]{:S(2)}) collective-permute-start(f32[9,22,128]{2,1,0:T(8,128)S(1)} %bitcast.29), channel_id=1, source_target_pairs={{0,1},{1,0},{2,3},{3,2},{4,5},{5,4},{6,7},{7,6},{8,9},{9,8},{10,11... | collective-permute-start | bytes 304136 | tf_op jit(solution)/shard_map/ppermute | solution.py:557
  16.3 3.5 %collective-permute-start.4 = (f32[3,3,8,128]{3,2,1,0:T(8,128)S(1)}, f32[3,3,8,128]{3,2,1,0:T(8,128)S(1)}, u32[]{:S(2)}, u32[]{:S(2)}) collective-permute-start(f32[3,3,8,128]{3,2,1,0:T(8,128)S(1)} %get-tuple-element.37), channel_id=1, source_target_pairs={{0,1},{1,0},{2,3},{3,2},{4,5},{5,4},{6,7},{7,6},{8,9},{9,8},{10,11... | collective-permute-start | bytes 110600 | tf_op jit(solution)/shard_map/ppermute | solution.py:558
  17.6 2.2 %collective-permute-start.5 = (f32[3,3,8,128]{3,2,1,0:T(8,128)S(1)}, f32[3,3,8,128]{3,2,1,0:T(8,128)S(1)}, u32[]{:S(2)}, u32[]{:S(2)}) collective-permute-start(f32[3,3,8,128]{3,2,1,0:T(8,128)S(1)} %get-tuple-element.38), channel_id=1, source_target_pairs={{0,16},{1,17},{2,18},{3,19},{4,20},{5,21},{6,22},{7,23},{8,24},{9,... | collective-permute-start | bytes 110600 | tf_op jit(solution)/shard_map/ppermute | solution.py:557
  19.8 3.8 %collective-permute-start.7 = (f32[3,10,8,128]{3,2,1,0:T(8,128)S(1)}, f32[3,10,8,128]{3,2,1,0:T(8,128)S(1)}, u32[]{:S(2)}, u32[]{:S(2)}) collective-permute-start(f32[3,10,8,128]{3,2,1,0:T(8,128)S(1)} %pad_maximum_fusion.5), channel_id=1, source_target_pairs={{0,1},{1,0},{2,3},{3,2},{4,5},{5,4},{6,7},{7,6},{8,9},{9,8},{10,11... | collective-permute-start | bytes 368648 | tf_op jit(solution)/shard_map/ppermute | solution.py:557
  21.1 2.5 %collective-permute-start.6 = (f32[3,10,8,128]{3,2,1,0:T(8,128)S(1)}, f32[3,10,8,128]{3,2,1,0:T(8,128)S(1)}, u32[]{:S(2)}, u32[]{:S(2)}) collective-permute-start(f32[3,10,8,128]{3,2,1,0:T(8,128)S(1)} %pad_maximum_fusion.5), channel_id=1, source_target_pairs={{0,16},{1,2},{2,1},{3,4},{4,3},{5,6},{6,5},{7,8},{8,7},{9,10},{10,... | collective-permute-start | bytes 368648 | tf_op jit(solution)/shard_map/ppermute | solution.py:558
  26.6 11.8 %collective-permute-start.8 = (f32[3,1,8,128]{3,2,1,0:T(8,128)S(1)}, f32[3,1,8,128]{3,2,1,0:T(8,128)S(1)}, u32[]{:S(2)}, u32[]{:S(2)}) collective-permute-start(f32[3,1,8,128]{3,2,1,0:T(8,128)S(1)} %get-tuple-element.41), channel_id=1, source_target_pairs={{0,1},{1,0},{2,3},{3,2},{4,5},{5,4},{6,7},{7,6},{8,9},{9,8},{10,11... | collective-permute-start | bytes 36872 | tf_op jit(solution)/shard_map/ppermute | solution.py:558
  29.6 8.8 %collective-permute-start.9 = (f32[3,1,8,128]{3,2,1,0:T(8,128)S(1)}, f32[3,1,8,128]{3,2,1,0:T(8,128)S(1)}, u32[]{:S(2)}, u32[]{:S(2)}) collective-permute-start(f32[3,1,8,128]{3,2,1,0:T(8,128)S(1)} %get-tuple-element.42), channel_id=1, source_target_pairs={{0,16},{1,17},{2,18},{3,19},{4,20},{5,21},{6,22},{7,23},{8,24},{9,... | collective-permute-start | bytes 36872 | tf_op jit(solution)/shard_map/ppermute | solution.py:557
  31.7 14.1 %all-to-all-start = ((f32[16,2,128]{2,1,0:T(2,128)}), f32[16,2,128]{2,1,0:T(2,128)S(1)}, u32[]{:S(2)}, u32[]{:S(2)}) async-start(f32[16,2,128]{2,1,0:T(2,128)} %bitcast.11), calls=%async_computation | async-start | bytes 32768 | tf_op jit(solution)/shard_map/all_to_all | solution.py:597
  38.5 17.6 %collective-permute-start.10 = (f32[3,4,4,128]{3,2,1,0:T(4,128)S(1)}, f32[3,4,4,128]{3,2,1,0:T(4,128)S(1)}, u32[]{:S(2)}, u32[]{:S(2)}) collective-permute-start(f32[3,4,4,128]{3,2,1,0:T(4,128)S(1)} %get-tuple-element.35), channel_id=1, source_target_pairs={{0,16},{1,2},{2,1},{3,4},{4,3},{5,6},{6,5},{7,8},{8,7},{9,10},{10,... | collective-permute-start | bytes 73736 | tf_op jit(solution)/shard_map/ppermute | solution.py:558
  38.7 17.4 %collective-permute-start.11 = (f32[3,4,4,128]{3,2,1,0:T(4,128)S(1)}, f32[3,4,4,128]{3,2,1,0:T(4,128)S(1)}, u32[]{:S(2)}, u32[]{:S(2)}) collective-permute-start(f32[3,4,4,128]{3,2,1,0:T(4,128)S(1)} %get-tuple-element.36), channel_id=1, source_target_pairs={{0,1},{1,0},{2,3},{3,2},{4,5},{5,4},{6,7},{7,6},{8,9},{9,8},{10,11... | collective-permute-start | bytes 73736 | tf_op jit(solution)/shard_map/ppermute | solution.py:557
  46.5 17.2 %all-to-all-start.1 = ((f32[16,32,128]{2,1,0:T(8,128)}), f32[16,32,128]{2,1,0:T(8,128)S(1)}, u32[]{:S(2)}, u32[]{:S(2)}) async-start(f32[16,32,128]{2,1,0:T(8,128)} %broadcast_in_dim.16), calls=%async_computation.1 | async-start | bytes 524288 | tf_op jit(solution)/shard_map/all_to_all | solution.py:599

commit v9 on v7

--- a/solution.py
+++ b/solution.py
@@ -141,7 +141,7 @@
 def down0_kernel(idx, src, out, gain, ub, ua, tmp):
     ix, iy = idx[0], idx[1]
     win, _ = level0(src, gain, ua, ix, iy)
-    repeat(1, 21, lambda x: win.relax(x, ua, ub), 4)
+    repeat(1, 21, lambda x: win.relax(x, ua, ub), 10)
     for c in range(2):
         for x in (0, 21):
             ub[c, x] = jnp.zeros((24, 128), F32)
@@ -164,7 +164,7 @@
         for c in range(3):
             out[c, q] = jnp.where(even, rows[0][c], lroll(rows[1][c], 1))
 
-    repeat(0, 4, halve)
+    repeat(0, 4, halve, 2)
 
 
 def down1_kernel(idx, src, out, src2, gain, ub, ua, tmp, gain2, va, vb):
@@ -178,7 +178,7 @@
     win = Window(src, gain, 0.25, 1, functools.partial(near1, lane24))
     inside = row_mask(24, iy * 8 - 8, 128)
     repeat(0, 10, lambda q: win.start(q, inside * scalar_mask(ix * 4 - 3 + q, 64), ua), 5)
-    repeat(0, 10, lambda q: win.relax(q, ua, ub), 5)
+    repeat(0, 10, lambda q: win.relax(q, ua, ub), 10)
     lane = lanes(8)
     corner = lane % 4 == 0
 
@@ -189,7 +189,7 @@
             t = parts[c] + lroll(parts[c], -1)
             tmp[c, q] = t + lroll(t, -2)
 
-    repeat(1, 9, halve, 4)
+    repeat(1, 9, halve, 8)
 
     def gather(b):
         for c in range(3):
@@ -460,7 +460,7 @@
             wide1[c, q, pl.ds(0, 16, 2), :] = 0.75 * t + 0.25 * sroll(t, 1)
             wide1[c, q, pl.ds(1, 16, 2), :] = 0.75 * t + 0.25 * sroll(t, -1)
 
-    repeat(1, 9, mix2, 4)
+    repeat(1, 9, mix2, 8)
     for c in range(2):
         ua1[c, 1] = zero24
         ua1[c, 10] = zero24
@@ -474,8 +474,8 @@
     repeat(1, 9, correct1, 4)
     win1 = Window(src1, gain1, 0.25, 1, functools.partial(near1, lane24))
 
-    repeat(1, 9, lambda q: win1.relax(q, ua1, ut1), 4)
-    repeat(2, 8, lambda q: win1.relax(q, ut1, ua1), 3)
+    repeat(1, 9, lambda q: win1.relax(q, ua1, ut1), 8)
+    repeat(2, 8, lambda q: win1.relax(q, ut1, ua1), 6)
 
     def widen1(q):
         for c in range(2):
@@ -488,7 +488,7 @@
                 wide0[c, 2 * q + p, pl.ds(0, 16, 2), :] = 0.75 * v + 0.25 * sroll(v, 1)
                 wide0[c, 2 * q + p, pl.ds(1, 16, 2), :] = 0.75 * v + 0.25 * sroll(v, -1)
 
-    repeat(2, 8, widen1, 2)
+    repeat(2, 8, widen1, 3)
     inside0 = row_mask(24, iy * 16 - 3, 256)
 
     def correct0(at):
@@ -503,7 +503,7 @@
 
     repeat(5, 15, correct0, 2)
     win0 = Window(src0, gain0, 1.0, 0, functools.partial(near0, lane24))
-    repeat(2, 20, lambda x: win0.relax(x, ua0, ut0), 3)
+    repeat(2, 20, lambda x: win0.relax(x, ua0, ut0), 6)
 
     def finish0(x):
         new = win0.relaxed(x + 3, ut0)

time: 73.5 us -> 72.1 us (0.981)
  Pallas kernels: 16 us -> 14.6 us
    pallas_call x3, Pallas kernels: 16 us -> 14.6 us  [call(): pl.pallas_call(kernel, name=name, out_shape=[jax.ShapeDtypeStruct(shape,...]
where the time goes in v9:
time: 72.1 us; the launch traced here: 71.9 us
  starting transfers between devices  31.5 us (44%)
  waiting for transfers between devices  24.1 us (33%)
  Pallas kernels  14.6 us (20%)
  other arithmetic  1.43 us (2%)
    all_to_all x1, starting transfers between devices, body(): flat = lax.all_to_all(part, ('gx', 'gy'), 0, 0).reshape(512, 128)  15.3 us
    pallas_call x3, Pallas kernels, call(): pl.pallas_call(kernel, name=name, out_shape=[jax.ShapeDtypeStruct(shape,...  14.6 us
    all_to_all x1, waiting for transfers between devices, body(): flat = lax.all_to_all(part, ('gx', 'gy'), 0, 0).reshape(512, 128)  10.3 us
    ppermute x6, waiting for transfers between devices, trade(): one = lax.ppermute(one, BOTH, partners(axis, 0))  8.22 us
    ppermute x6, starting transfers between devices, trade(): one = lax.ppermute(one, BOTH, partners(axis, 0))  8.11 us
    ppermute x6, starting transfers between devices, trade(): two = lax.ppermute(two, BOTH, partners(axis, 1))  8.06 us
    ppermute x6, waiting for transfers between devices, trade(): two = lax.ppermute(two, BOTH, partners(axis, 1))  5.53 us
  transfers between devices with their start and end apart: 13, of which 9 were waited for; matrix products, arithmetic and copies ran while one was open for 0% of the time, Pallas kernels for 0%

profile of v9, /device:TPU:1, one launch (start us, length us, event | category | flops | bytes accessed | tf_op | source)
XLA Modules:
  0.0 71.9 jit_solution(13599235829363645652)
XLA Ops:
  0.0 0.9 %broadcast_select_fusion.7 = (f32[3,3,16,128]{3,2,1,0:T(8,128)S(1)}, f32[3,3,16,128]{3,2,1,0:T(8,128)S(1)}, f32[3,3,16,128]{3,2,1,0:T(8,128)S(1)}) fusion(pred[]{:T(512)S(6)} %eq.18, f32[1,16,16,128]{3,2,1,0:T(8,128)} %bitcast.22, f32[2,16,16,128]{3,2,1,0:T(8,128)} %param.2), kind=kLoop, calls=%fused_computation.22 | loop fusion | flops 55296 | bytes 614401 | tf_op jit(solution)/shard_map/jit(_where)/select_n | solution.py:558
  0.9 0.0 copy-start
  0.9 3.3 %collective-permute-start.1 = (f32[3,3,16,128]{3,2,1,0:T(8,128)S(1)}, f32[3,3,16,128]{3,2,1,0:T(8,128)S(1)}, u32[]{:S(2)}, u32[]{:S(2)}) collective-permute-start(f32[3,3,16,128]{3,2,1,0:T(8,128)S(1)} %broadcast_select_fusion.6), channel_id=1, source_target_pairs={{0,16},{1,17},{2,18},{3,19},{4,20},{5,21},{6,22},{7,23},{8,24},{9,... | collective-permute-start | bytes 221192 | tf_op jit(solution)/shard_map/ppermute | solution.py:559
  4.2 0.0 collective-permute-start
  4.2 0.1 pad.22.clone
  4.3 0.0 copy-start.1
  4.3 0.8 %collective-permute-done.1 = f32[3,3,16,128]{3,2,1,0:T(8,128)S(1)} collective-permute-done((f32[3,3,16,128]{3,2,1,0:T(8,128)S(1)}, f32[3,3,16,128]{3,2,1,0:T(8,128)S(1)}, u32[]{:S(2)}, u32[]{:S(2)}) %collective-permute-start.1) | collective-permute-done | bytes 73760 | tf_op jit(solution)/shard_map/ppermute | solution.py:559
  5.2 3.1 %collective-permute-done = f32[3,3,16,128]{3,2,1,0:T(8,128)S(1)} collective-permute-done((f32[3,3,16,128]{3,2,1,0:T(8,128)S(1)}, f32[3,3,16,128]{3,2,1,0:T(8,128)S(1)}, u32[]{:S(2)}, u32[]{:S(2)}) %collective-permute-start) | collective-permute-done | bytes 73760 | tf_op jit(solution)/shard_map/ppermute | solution.py:560
  8.3 0.0 copy-done
  8.3 0.0 copy-done.1
  8.3 0.1 select_bitcast_fusion.1
  8.4 0.5 collective-permute-start.2
  9.0 0.5 collective-permute-start.3
  9.5 0.1 pad_add_fusion.idx
  9.6 0.3 collective-permute-done.2
  9.9 3.7 %collective-permute-done.3 = f32[9,22,128]{2,1,0:T(8,128)S(1)} collective-permute-done((f32[9,22,128]{2,1,0:T(8,128)S(1)}, f32[9,22,128]{2,1,0:T(8,128)S(1)}, u32[]{:S(2)}, u32[]{:S(2)}) %collective-permute-start.3) | collective-permute-done | bytes 101408 | tf_op jit(solution)/shard_map/ppermute | solution.py:559
  13.6 0.1 copy_bitcast_fusion
  13.7 0.2 maximum_maximum_fusion.src.src0
  13.9 1.8 %down0.1 = (f32[3,4,8,128]{3,2,1,0:T(8,128)S(1)}, f32[2,22,24,128]{3,2,1,0:T(8,128)S(1)}, f32[2,22,24,128]{3,2,1,0:T(8,128)S(1)}) custom-call(s32[2]{0:T(128)S(1)} %pad_add_fusion.idx, f32[3,22,24,128]{3,2,1,0:T(8,128)S(1)} %maximum_maximum_fusion.src.src0), custom_call_target="tpu_custom_call" | custom-call | bytes 7000000 | tf_op jit(solution)/shard_map/down0/pallas_call | solution.py:519
  15.7 1.3 %collective-permute-start.4 = (f32[3,3,8,128]{3,2,1,0:T(8,128)S(1)}, f32[3,3,8,128]{3,2,1,0:T(8,128)S(1)}, u32[]{:S(2)}, u32[]{:S(2)}) collective-permute-start(f32[3,3,8,128]{3,2,1,0:T(8,128)S(1)} %get-tuple-element.37), channel_id=1, source_target_pairs={{0,1},{1,0},{2,3},{3,2},{4,5},{5,4},{6,7},{7,6},{8,9},{9,8},{10,11... | collective-permute-start | bytes 110600 | tf_op jit(solution)/shard_map/ppermute | solution.py:560
  17.0 0.5 collective-permute-start.5
  17.5 1.7 %collective-permute-done.4 = f32[3,3,8,128]{3,2,1,0:T(8,128)S(1)} collective-permute-done((f32[3,3,8,128]{3,2,1,0:T(8,128)S(1)}, f32[3,3,8,128]{3,2,1,0:T(8,128)S(1)}, u32[]{:S(2)}, u32[]{:S(2)}) %collective-permute-start.4) | collective-permute-done | bytes 36896 | tf_op jit(solution)/shard_map/ppermute | solution.py:560
  19.2 0.0 collective-permute-done.5
  19.2 1.3 %collective-permute-start.7 = (f32[3,10,8,128]{3,2,1,0:T(8,128)S(1)}, f32[3,10,8,128]{3,2,1,0:T(8,128)S(1)}, u32[]{:S(2)}, u32[]{:S(2)}) collective-permute-start(f32[3,10,8,128]{3,2,1,0:T(8,128)S(1)} %pad_maximum_fusion.5), channel_id=1, source_target_pairs={{0,1},{1,0},{2,3},{3,2},{4,5},{5,4},{6,7},{7,6},{8,9},{9,8},{10,11... | collective-permute-start | bytes 368648 | tf_op jit(solution)/shard_map/ppermute | solution.py:559
  20.5 1.0 %collective-permute-start.6 = (f32[3,10,8,128]{3,2,1,0:T(8,128)S(1)}, f32[3,10,8,128]{3,2,1,0:T(8,128)S(1)}, u32[]{:S(2)}, u32[]{:S(2)}) collective-permute-start(f32[3,10,8,128]{3,2,1,0:T(8,128)S(1)} %pad_maximum_fusion.5), channel_id=1, source_target_pairs={{0,16},{1,2},{2,1},{3,4},{4,3},{5,6},{6,5},{7,8},{8,7},{9,10},{10,... | collective-permute-start | bytes 368648 | tf_op jit(solution)/shard_map/ppermute | solution.py:560
  21.5 1.5 %collective-permute-done.7 = f32[3,10,8,128]{3,2,1,0:T(8,128)S(1)} collective-permute-done((f32[3,10,8,128]{3,2,1,0:T(8,128)S(1)}, f32[3,10,8,128]{3,2,1,0:T(8,128)S(1)}, u32[]{:S(2)}, u32[]{:S(2)}) %collective-permute-start.7) | collective-permute-done | bytes 122912 | tf_op jit(solution)/shard_map/ppermute | solution.py:559
  23.0 0.0 collective-permute-done.6
  23.1 2.9 %down1.1 = (f32[64,8,128]{2,1,0:T(8,128)}, f32[3,2,8,128]{3,2,1,0:T(8,128)S(1)}, f32[2,10,24,128]{3,2,1,0:T(8,128)S(1)}, f32[2,12,24,128]{3,2,1,0:T(8,128)S(1)}) custom-call(s32[2]{0:T(128)S(1)} %pad_add_fusion.idx, f32[3,10,24,128]{3,2,1,0:T(8,128)S(1)} %pad_maximum_fusion.src.src1), custom_call_target="tpu_custom_call" | custom-call | bytes 7000000 | tf_op jit(solution)/shard_map/down1/pallas_call | solution.py:519
  26.0 3.0 %collective-permute-start.8 = (f32[3,1,8,128]{3,2,1,0:T(8,128)S(1)}, f32[3,1,8,128]{3,2,1,0:T(8,128)S(1)}, u32[]{:S(2)}, u32[]{:S(2)}) collective-permute-start(f32[3,1,8,128]{3,2,1,0:T(8,128)S(1)} %get-tuple-element.41), channel_id=1, source_target_pairs={{0,1},{1,0},{2,3},{3,2},{4,5},{5,4},{6,7},{7,6},{8,9},{9,8},{10,11... | collective-permute-start | bytes 36872 | tf_op jit(solution)/shard_map/ppermute | solution.py:560
  29.0 2.0 %collective-permute-start.9 = (f32[3,1,8,128]{3,2,1,0:T(8,128)S(1)}, f32[3,1,8,128]{3,2,1,0:T(8,128)S(1)}, u32[]{:S(2)}, u32[]{:S(2)}) collective-permute-start(f32[3,1,8,128]{3,2,1,0:T(8,128)S(1)} %get-tuple-element.42), channel_id=1, source_target_pairs={{0,16},{1,17},{2,18},{3,19},{4,20},{5,21},{6,22},{7,23},{8,24},{9,... | collective-permute-start | bytes 36872 | tf_op jit(solution)/shard_map/ppermute | solution.py:559
  31.0 15.3 %all-to-all-start = ((f32[256,2,128]{2,1,0:T(2,128)}), f32[256,2,128]{2,1,0:T(2,128)S(1)}, u32[]{:S(2)}, u32[]{:S(2)}) async-start(f32[256,2,128]{2,1,0:T(2,128)} %bitcast.11), calls=%async_computation | async-start | bytes 524288 | tf_op jit(solution)/shard_map/all_to_all | solution.py:600
  46.3 0.0 collective-permute-done.8
  46.3 0.0 collective-permute-done.9
  46.3 2.2 %collective-permute-start.10 = (f32[3,4,4,128]{3,2,1,0:T(4,128)S(1)}, f32[3,4,4,128]{3,2,1,0:T(4,128)S(1)}, u32[]{:S(2)}, u32[]{:S(2)}) collective-permute-start(f32[3,4,4,128]{3,2,1,0:T(4,128)S(1)} %get-tuple-element.35), channel_id=1, source_target_pairs={{0,16},{1,2},{2,1},{3,4},{4,3},{5,6},{6,5},{7,8},{8,7},{9,10},{10,... | collective-permute-start | bytes 73736 | tf_op jit(solution)/shard_map/ppermute | solution.py:560
  48.6 0.4 collective-permute-start.11
  49.0 0.4 collective-permute-done.10
  49.4 2.2 %collective-permute-done.11 = f32[3,4,4,128]{3,2,1,0:T(4,128)S(1)} collective-permute-done((f32[3,4,4,128]{3,2,1,0:T(4,128)S(1)}, f32[3,4,4,128]{3,2,1,0:T(4,128)S(1)}, u32[]{:S(2)}, u32[]{:S(2)}) %collective-permute-start.11) | collective-permute-done | bytes 24608 | tf_op jit(solution)/shard_map/ppermute | solution.py:559
  51.7 10.3 %all-to-all-done = f32[256,2,128]{2,1,0:T(2,128)S(1)} async-done(((f32[256,2,128]{2,1,0:T(2,128)}), f32[256,2,128]{2,1,0:T(2,128)S(1)}, u32[]{:S(2)}, u32[]{:S(2)}) %all-to-all-start) | async-done | bytes 262176 | tf_op jit(solution)/shard_map/all_to_all | solution.py:600
  62.0 9.9 %up.1 = f32[2,16,16,128]{3,2,1,0:T(8,128)} custom-call(s32[2]{0:T(128)S(1)} %pad_add_fusion.idx, f32[3,22,24,128]{3,2,1,0:T(8,128)S(1)} %maximum_maximum_fusion.src.src0, f32[2,22,24,128]{3,2,1,0:T(8,128)S(1)} %get-tuple-element.12.gain0, f32[2,22,24,128]{3,2,1,0:T(8,128)S(1)} %get-tuple-element.13.ub0, f32[3,10,24,128]{3,2,1,0:T(8,128)S(1)} %pad_maximum_fusion.src.src1, ...), custom_call_target="tpu_custom_call" | custom-call | bytes 35000000 | tf_op jit(solution)/shard_map/up/pallas_call | solution.py:519
  (18 shorter events, 0.3 us)
Async XLA Ops:
  0.9 7.4 %copy-start = (f32[2,16,16,128]{3,2,1,0:T(8,128)S(1)}, f32[2,16,16,128]{3,2,1,0:T(8,128)}, u32[]{:S(2)}) copy-start(f32[2,16,16,128]{3,2,1,0:T(8,128)} %param.2) | copy-start | bytes 786436
  0.9 4.2 %collective-permute-start.1 = (f32[3,3,16,128]{3,2,1,0:T(8,128)S(1)}, f32[3,3,16,128]{3,2,1,0:T(8,128)S(1)}, u32[]{:S(2)}, u32[]{:S(2)}) collective-permute-start(f32[3,3,16,128]{3,2,1,0:T(8,128)S(1)} %broadcast_select_fusion.6), channel_id=1, source_target_pairs={{0,16},{1,17},{2,18},{3,19},{4,20},{5,21},{6,22},{7,23},{8,24},{9,... | collective-permute-start | bytes 221192 | tf_op jit(solution)/shard_map/ppermute | solution.py:559
  4.2 4.1 %collective-permute-start = (f32[3,3,16,128]{3,2,1,0:T(8,128)S(1)}, f32[3,3,16,128]{3,2,1,0:T(8,128)S(1)}, u32[]{:S(2)}, u32[]{:S(2)}) collective-permute-start(f32[3,3,16,128]{3,2,1,0:T(8,128)S(1)} %get-tuple-element.22), channel_id=1, source_target_pairs={{0,1},{1,0},{2,3},{3,2},{4,5},{5,4},{6,7},{7,6},{8,9},{9,8},{10,11... | collective-permute-start | bytes 221192 | tf_op jit(solution)/shard_map/ppermute | solution.py:560
  4.3 4.0 %copy-start.1 = (f32[16,16,128]{2,1,0:T(8,128)S(1)}, f32[16,16,128]{2,1,0:T(8,128)}, u32[]{:S(2)}) copy-start(f32[16,16,128]{2,1,0:T(8,128)} %param.3) | copy-start | bytes 393220
  8.4 1.4 %collective-permute-start.2 = (f32[9,22,128]{2,1,0:T(8,128)S(1)}, f32[9,22,128]{2,1,0:T(8,128)S(1)}, u32[]{:S(2)}, u32[]{:S(2)}) collective-permute-start(f32[9,22,128]{2,1,0:T(8,128)S(1)} %bitcast.27), channel_id=1, source_target_pairs={{0,16},{1,2},{2,1},{3,4},{4,3},{5,6},{6,5},{7,8},{8,7},{9,10},{10,... | collective-permute-start | bytes 304136 | tf_op jit(solution)/shard_map/ppermute | solution.py:560
  9.0 4.6 %collective-permute-start.3 = (f32[9,22,128]{2,1,0:T(8,128)S(1)}, f32[9,22,128]{2,1,0:T(8,128)S(1)}, u32[]{:S(2)}, u32[]{:S(2)}) collective-permute-start(f32[9,22,128]{2,1,0:T(8,128)S(1)} %bitcast.28), channel_id=1, source_target_pairs={{0,1},{1,0},{2,3},{3,2},{4,5},{5,4},{6,7},{7,6},{8,9},{9,8},{10,11... | collective-permute-start | bytes 304136 | tf_op jit(solution)/shard_map/ppermute | solution.py:559
  15.7 3.5 %collective-permute-start.4 = (f32[3,3,8,128]{3,2,1,0:T(8,128)S(1)}, f32[3,3,8,128]{3,2,1,0:T(8,128)S(1)}, u32[]{:S(2)}, u32[]{:S(2)}) collective-permute-start(f32[3,3,8,128]{3,2,1,0:T(8,128)S(1)} %get-tuple-element.37), channel_id=1, source_target_pairs={{0,1},{1,0},{2,3},{3,2},{4,5},{5,4},{6,7},{7,6},{8,9},{9,8},{10,11... | collective-permute-start | bytes 110600 | tf_op jit(solution)/shard_map/ppermute | solution.py:560
  17.0 2.2 %collective-permute-start.5 = (f32[3,3,8,128]{3,2,1,0:T(8,128)S(1)}, f32[3,3,8,128]{3,2,1,0:T(8,128)S(1)}, u32[]{:S(2)}, u32[]{:S(2)}) collective-permute-start(f32[3,3,8,128]{3,2,1,0:T(8,128)S(1)} %get-tuple-element.38), channel_id=1, source_target_pairs={{0,16},{1,17},{2,18},{3,19},{4,20},{5,21},{6,22},{7,23},{8,24},{9,... | collective-permute-start | bytes 110600 | tf_op jit(solution)/shard_map/ppermute | solution.py:559
  19.2 3.8 %collective-permute-start.7 = (f32[3,10,8,128]{3,2,1,0:T(8,128)S(1)}, f32[3,10,8,128]{3,2,1,0:T(8,128)S(1)}, u32[]{:S(2)}, u32[]{:S(2)}) collective-permute-start(f32[3,10,8,128]{3,2,1,0:T(8,128)S(1)} %pad_maximum_fusion.5), channel_id=1, source_target_pairs={{0,1},{1,0},{2,3},{3,2},{4,5},{5,4},{6,7},{7,6},{8,9},{9,8},{10,11... | collective-permute-start | bytes 368648 | tf_op jit(solution)/shard_map/ppermute | solution.py:559
  20.5 2.5 %collective-permute-start.6 = (f32[3,10,8,128]{3,2,1,0:T(8,128)S(1)}, f32[3,10,8,128]{3,2,1,0:T(8,128)S(1)}, u32[]{:S(2)}, u32[]{:S(2)}) collective-permute-start(f32[3,10,8,128]{3,2,1,0:T(8,128)S(1)} %pad_maximum_fusion.5), channel_id=1, source_target_pairs={{0,16},{1,2},{2,1},{3,4},{4,3},{5,6},{6,5},{7,8},{8,7},{9,10},{10,... | collective-permute-start | bytes 368648 | tf_op jit(solution)/shard_map/ppermute | solution.py:560
  26.0 20.3 %collective-permute-start.8 = (f32[3,1,8,128]{3,2,1,0:T(8,128)S(1)}, f32[3,1,8,128]{3,2,1,0:T(8,128)S(1)}, u32[]{:S(2)}, u32[]{:S(2)}) collective-permute-start(f32[3,1,8,128]{3,2,1,0:T(8,128)S(1)} %get-tuple-element.41), channel_id=1, source_target_pairs={{0,1},{1,0},{2,3},{3,2},{4,5},{5,4},{6,7},{7,6},{8,9},{9,8},{10,11... | collective-permute-start | bytes 36872 | tf_op jit(solution)/shard_map/ppermute | solution.py:560
  29.0 17.3 %collective-permute-start.9 = (f32[3,1,8,128]{3,2,1,0:T(8,128)S(1)}, f32[3,1,8,128]{3,2,1,0:T(8,128)S(1)}, u32[]{:S(2)}, u32[]{:S(2)}) collective-permute-start(f32[3,1,8,128]{3,2,1,0:T(8,128)S(1)} %get-tuple-element.42), channel_id=1, source_target_pairs={{0,16},{1,17},{2,18},{3,19},{4,20},{5,21},{6,22},{7,23},{8,24},{9,... | collective-permute-start | bytes 36872 | tf_op jit(solution)/shard_map/ppermute | solution.py:559
  31.0 31.0 %all-to-all-start = ((f32[256,2,128]{2,1,0:T(2,128)}), f32[256,2,128]{2,1,0:T(2,128)S(1)}, u32[]{:S(2)}, u32[]{:S(2)}) async-start(f32[256,2,128]{2,1,0:T(2,128)} %bitcast.11), calls=%async_computation | async-start | bytes 524288 | tf_op jit(solution)/shard_map/all_to_all | solution.py:600
  46.3 3.1 %collective-permute-start.10 = (f32[3,4,4,128]{3,2,1,0:T(4,128)S(1)}, f32[3,4,4,128]{3,2,1,0:T(4,128)S(1)}, u32[]{:S(2)}, u32[]{:S(2)}) collective-permute-start(f32[3,4,4,128]{3,2,1,0:T(4,128)S(1)} %get-tuple-element.35), channel_id=1, source_target_pairs={{0,16},{1,2},{2,1},{3,4},{4,3},{5,6},{6,5},{7,8},{8,7},{9,10},{10,... | collective-permute-start | bytes 73736 | tf_op jit(solution)/shard_map/ppermute | solution.py:560
  48.6 3.1 %collective-permute-start.11 = (f32[3,4,4,128]{3,2,1,0:T(4,128)S(1)}, f32[3,4,4,128]{3,2,1,0:T(4,128)S(1)}, u32[]{:S(2)}, u32[]{:S(2)}) collective-permute-start(f32[3,4,4,128]{3,2,1,0:T(4,128)S(1)} %get-tuple-element.36), channel_id=1, source_target_pairs={{0,1},{1,0},{2,3},{3,2},{4,5},{5,4},{6,7},{7,6},{8,9},{9,8},{10,11... | collective-permute-start | bytes 73736 | tf_op jit(solution)/shard_map/ppermute | solution.py:559

commit v10 on v9

--- a/solution.py
+++ b/solution.py
@@ -177,7 +177,7 @@
             buf[c, 11] = zero24
     win = Window(src, gain, 0.25, 1, functools.partial(near1, lane24))
     inside = row_mask(24, iy * 8 - 8, 128)
-    repeat(0, 10, lambda q: win.start(q, inside * scalar_mask(ix * 4 - 3 + q, 64), ua), 5)
+    repeat(0, 10, lambda q: win.start(q, inside * scalar_mask(ix * 4 - 3 + q, 64), ua), 10)
     repeat(0, 10, lambda q: win.relax(q, ua, ub), 10)
     lane = lanes(8)
     corner = lane % 4 == 0
@@ -186,8 +186,8 @@
         _, m = win.misfit(q, ub)
         parts = (m[0], m[1], src[2, q])
         for c in range(3):
-            t = parts[c] + lroll(parts[c], -1)
-            tmp[c, q] = t + lroll(t, -2)
+            t = parts[c]
+            tmp[c, q] = (t + lroll(t, -1)) + (lroll(t, -2) + lroll(t, -3))
 
     repeat(1, 9, halve, 8)
 
@@ -214,18 +214,17 @@
         win2.relax(b, va, vb)
     m = [win2.misfit(b, vb)[1] for b in range(2)]
 
-    def third(v0, v1):
+    def third(v0, v1, moves):
         total = jnp.zeros((1, 128), F32)
         for v, slot, move in ((v0, 2, -2), (v1, 0, 2)):
-            t = v + lroll(v, -1)
-            t = t + lroll(t, -4)
+            t = (v + lroll(v, -1)) + (lroll(v, -4) + lroll(v, -5))
             t = 0.125 * jnp.where(lane % 8 == slot, t + sroll(t, -1), 0.0)
-            total = total + lroll(t[2:3], move) + lroll(t[4:5], move + 1)
+            for extra in moves:
+                total = total + lroll(t[2:3], move + extra) + lroll(t[4:5], move + extra + 1)
         return total
 
-    field = third(m[0][0], m[1][0]) + lroll(third(m[0][1], m[1][1]), 4)
-    wave = third(src2[2, 0], src2[2, 1])
-    wave = wave + lroll(wave, 4)
+    field = third(m[0][0], m[1][0], (0,)) + third(m[0][1], m[1][1], (4,))
+    wave = third(src2[2, 0], src2[2, 1], (0, 4))
     pair = jnp.concatenate([field, wave] * 4, axis=0)
 
     def spread(i):
@@ -297,45 +296,57 @@
     repeat(0, 16, start3, 8)
     repeat(3, 19, relax3, 8)
 
-    first = (slot == 0) & zlow
-
-    def eighth(v):
-        v = v + lroll(v, -1)
-        v = v + lroll(v, -2)
-        return jnp.where(first, 0.125 * (v + lroll(v, -8)), 0.0)
+    first, second = (slot == 0) & zlow, (slot == 0) & ~zlow
+
+    def eighth(v, k):
+        v = 0.125 * ((v + lroll(v, -1)) + (lroll(v, -2) + lroll(v, -3)))
+        low = jnp.where(first, v, 0.0)
+        return (lroll(low, k) if k else low) + lroll(jnp.where(second, v, 0.0), k - 8)
 
     def halve3(r):
         f, w = zero16, zero16
         for k in range(4):
             at = 4 * k + r + 3
-            fk, wk = eighth(miss3(ub3, at)[1]), eighth(w3[at])
-            f = f + (lroll(fk, k) if k else fk)
-            w = w + (lroll(wk, k) if k else wk)
+            f = f + eighth(miss3(ub3, at)[1], k)
+            w = w + eighth(w3[at], k)
         f4[r], w4[r] = f, w
 
-    repeat(0, 4, halve3, 2)
+    repeat(0, 4, halve3, 1)
     fs = [f4[r] for r in range(4)]
     ws = [w4[r] for r in range(4)]
     gs = [packed_gain(w, 1.0 / 256) for w in ws]
 
-    def miss4(us):
+    swapped = [swap(f, real) for f in fs]
+
+    def near4(us):
         low = jnp.where(slot >= 1, lroll(us[3], 1), 0.0)
         high = jnp.where(slot < 3, lroll(us[0], -1), 0.0)
         wide = [low, *us, high]
-        ms = []
+        nbs = []
         for r in range(4):
             down, up = y_pair(us[r])
-            nb = wide[r] + wide[r + 2] + down + up + z_sum(us[r], lane, 16)
-            ms.append(packed_misfit(fs[r], ws[r], us[r], nb, 1.0 / 256))
-        return ms
-
-    def relax4(_, us):
-        ms = miss4(us)
-        return tuple(u + g[0] * m + g[1] * swap(m, real) for u, g, m in zip(us, gs, ms))
-
-    us = tuple(g[0] * f + g[1] * swap(f, real) for g, f in zip(gs, fs))
-    us = lax.fori_loop(0, 5, relax4, us)
-    ms = miss4(us)
+            nbs.append(wide[r] + wide[r + 2] + down + up + z_sum(us[r], lane, 16))
+        return nbs
+
+    def miss4(f, w, v, other, nb, turn):
+        return f - (6.0 * v - nb) * (1.0 / 256) + w * (v + turn * other)
+
+    def relax4(_, both):
+        us, vs = both
+        nus, nvs = near4(us), near4(vs)
+        new = []
+        for r in range(4):
+            m = miss4(fs[r], ws[r], us[r], vs[r], nus[r], sign)
+            n = miss4(swapped[r], ws[r], vs[r], us[r], nvs[r], -sign)
+            ga, gb = gs[r]
+            new.append((us[r] + ga * m + gb * n, vs[r] + ga * n - gb * m))
+        return tuple(x for x, _ in new), tuple(x for _, x in new)
+
+    us = tuple(g[0] * f + g[1] * h for g, f, h in zip(gs, fs, swapped))
+    vs = tuple(g[0] * h - g[1] * f for g, f, h in zip(gs, fs, swapped))
+    us, vs = lax.fori_loop(0, 5, relax4, (us, vs))
+    nus = near4(us)
+    ms = [miss4(fs[r], ws[r], us[r], vs[r], nus[r], sign) for r in range(4)]
     total_m = ms[0] + ms[1] + ms[2] + ms[3]
     total_w = ws[0] + ws[1] + ws[2] + ws[3]
     sum_r = jnp.sum(jnp.where(zlow & real, total_m, 0.0))
@@ -352,12 +363,11 @@
         x = jnp.clip(x, 0, 15)
         k = x // 4
         t = jnp.where((slot == k) & inside, s4[x - 4 * k], 0.0)
-        t = pltpu.roll(t, lax.rem(128 - k, 128), 1)
-        t = t + lroll(t, 1)
-        t = t + lroll(t, 2)
-        t = t + lroll(t, 8)
-        low, high = z_pair(t, lane, 16)
-        t = 0.75 * t + 0.25 * jnp.where(zlow, low, high)
+        t = [pltpu.roll(t, lax.rem(128 - k + d, 128), 1) for d in range(4)]
+        t = (t[0] + t[1]) + (t[2] + t[3])
+        above = lroll(jnp.where(lane < 112, t, 0.0), 16)
+        below = lroll(jnp.where(lane >= 16, t, 0.0), -8)
+        t = 0.75 * (t + lroll(t, 8)) + 0.25 * (above + below)
         down, up = y_pair(t)
         return 0.75 * t + 0.25 * jnp.where(ylow, down, up)
 
@@ -373,7 +383,7 @@
         for j in range(1, 6):
             ub3[ix + j] = new[j - 1]
 
-    repeat(0, 2, sweep3)
+    repeat(0, 2, sweep3, 2)
     for j in range(1, 6):
         e3[j - 1, pl.ds(8, 16), :] = ub3[ix + j]
 
@@ -388,21 +398,19 @@
     for b in range(4):
         win2.start(b, keep2[b], u2)
     a_low = lane8 % 2 == 0
-    b_low = lane8 // 4 % 2 == 0
     h_low = lane8 // 2 % 2 == 0
 
     def widen3(c):
         sides = []
-        shift = jnp.where(c == 0, 4, 124)
         for yl in range(2):
             pick = (lane8 // 4 % 2 == c) & (lane8 % 2 == yl)
             ups, downs = [], []
             for bb in range(5):
                 t = jnp.where(pick, e3[bb, pl.ds(iy + 5, 8), :], 0.0)
                 t = t + lroll(t, 1 - 2 * yl)
-                t = t + pltpu.roll(t, shift, 1)
-                low, high = z_pair(t, lane8, 8)
-                t = 0.75 * t + 0.25 * jnp.where(b_low, low, high)
+                above = lroll(jnp.where(lane8 < 120, t, 0.0), 8 - 4 * c)
+                below = lroll(jnp.where(lane8 >= 8, t, 0.0), -4 - 4 * c)
+                t = 0.75 * (t + lroll(t, 4 - 8 * c)) + 0.25 * (above + below)
                 ups.append(lroll(t, 2))
                 downs.append(lroll(t, -2))
             cells = [ups[0]]
@@ -421,7 +429,8 @@
             wide2[c, b, pl.ds(2, 8, 4), :] = 0.75 * t1 + 0.25 * t0
             wide2[c, b, pl.ds(3, 8, 4), :] = 0.75 * t1 + 0.25 * sroll(t0, -1)
 
-    repeat(0, 2, widen3)
+    for c in range(2):
+        widen3(c)
 
     def sweep2(i):
         add = jnp.where(i == 0, F32(1), F32(0))
@@ -431,26 +440,20 @@
                 fix = wide2[c, b, pl.ds(6, 16), :] * (keep2[b] * add)
                 u2[c, b + 1] = new[b][c] + fix
 
-    repeat(0, 3, sweep2)
-
-    slot4 = lane % 4
+    repeat(0, 3, sweep2, 3)
+
 
     def widen2(at, b, xl):
         for c in range(2):
-            t = jnp.where(slot4 == xl, u2[c, b + 1], 0.0)
+            t = jnp.where(slot == xl, u2[c, b + 1], 0.0)
             t = lroll(t, -xl) if xl else t
             t = t + lroll(t, 1)
-            t = t + lroll(t, 2)
-            low, high = z_pair(t, lane, 4)
-            cell1[c, at] = 0.75 * t + 0.25 * jnp.where(slot4 < 2, low, high)
-
-    def widen_block(b):
-        for xl in range(4):
-            widen2(4 * b - 3 + xl, b, xl)
-
-    widen2(0, 0, 3)
-    repeat(1, 3, widen_block)
-    widen2(9, 3, 0)
+            above = lroll(jnp.where(lane < 124, t, 0.0), 4)
+            below = lroll(jnp.where(lane >= 4, t, 0.0), -2)
+            cell1[c, at] = 0.75 * (t + lroll(t, 2)) + 0.25 * (above + below)
+
+    for at in range(10):
+        widen2(at, (at + 3) // 4, (at + 3) % 4)
     lane_even = lane % 2 == 0
 
     def mix2(q):
@@ -480,15 +483,15 @@
     def widen1(q):
         for c in range(2):
             t = ua1[c, q + 1, pl.ds(5, 16), :]
-            up, down = lroll(t, 1), lroll(t, -1)
             for p in range(2):
-                v = jnp.where(lane_even, t, up) if p == 0 else jnp.where(lane_even, down, t)
-                low, high = z_pair(v, lane, 2)
-                v = 0.75 * v + 0.25 * jnp.where(lane_even, low, high)
+                v = jnp.where(lane_even, t, 0.0) if p == 0 else jnp.where(lane_even, 0.0, t)
+                above = lroll(jnp.where(lane < 126, v, 0.0), 2 - p)
+                below = lroll(jnp.where(lane >= 2, v, 0.0), -1 - p)
+                v = 0.75 * (v + lroll(v, 1 - 2 * p)) + 0.25 * (above + below)
                 wide0[c, 2 * q + p, pl.ds(0, 16, 2), :] = 0.75 * v + 0.25 * sroll(v, 1)
                 wide0[c, 2 * q + p, pl.ds(1, 16, 2), :] = 0.75 * v + 0.25 * sroll(v, -1)
 
-    repeat(2, 8, widen1, 3)
+    repeat(2, 8, widen1, 6)
     inside0 = row_mask(24, iy * 16 - 3, 256)
 
     def correct0(at):
@@ -501,9 +504,9 @@
                 keep = inside0 * scalar_mask(ix * 16 - 3 + x, 256)
                 ua0[c, x] = ub0[c, x] + (0.75 * mid + 0.25 * side) * keep
 
-    repeat(5, 15, correct0, 2)
+    repeat(5, 15, correct0, 5)
     win0 = Window(src0, gain0, 1.0, 0, functools.partial(near0, lane24))
-    repeat(2, 20, lambda x: win0.relax(x, ua0, ut0), 6)
+    repeat(2, 20, lambda x: win0.relax(x, ua0, ut0), 9)
 
     def finish0(x):
         new = win0.relaxed(x + 3, ut0)
@@ -511,7 +514,7 @@
             ua0[c, x + 3] = new[c]
             out[c, x] = ua0[c, x + 3, pl.ds(3, 16), :]
 
-    repeat(0, 16, finish0, 4)
+    repeat(0, 16, finish0, 8)
 
 
 def call(kernel, name, out_shape, scratch, *args, micros=2):

time: 72.1 us -> 69.7 us (0.967)
  Pallas kernels: 14.6 us -> 12.2 us
    pallas_call x3, Pallas kernels: 14.6 us -> 12.2 us  [call(): pl.pallas_call(kernel, name=name, out_shape=[jax.ShapeDtypeStruct(shape,...]
where the time goes in v10:
time: 69.7 us; the launch traced here: 69.5 us
  starting transfers between devices  31.5 us (45%)
  waiting for transfers between devices  24.1 us (35%)
  Pallas kernels  12.2 us (18%)
  other arithmetic  1.43 us (2%)
    all_to_all x1, starting transfers between devices, body(): flat = lax.all_to_all(part, ('gx', 'gy'), 0, 0).reshape(512, 128)  15.3 us
    pallas_call x3, Pallas kernels, call(): pl.pallas_call(kernel, name=name, out_shape=[jax.ShapeDtypeStruct(shape,...  12.2 us
    all_to_all x1, waiting for transfers between devices, body(): flat = lax.all_to_all(part, ('gx', 'gy'), 0, 0).reshape(512, 128)  10.3 us
    ppermute x6, waiting for transfers between devices, trade(): one = lax.ppermute(one, BOTH, partners(axis, 0))  8.22 us
    ppermute x6, starting transfers between devices, trade(): one = lax.ppermute(one, BOTH, partners(axis, 0))  8.11 us
    ppermute x6, starting transfers between devices, trade(): two = lax.ppermute(two, BOTH, partners(axis, 1))  8.06 us
    ppermute x6, waiting for transfers between devices, trade(): two = lax.ppermute(two, BOTH, partners(axis, 1))  5.53 us
  transfers between devices with their start and end apart: 13, of which 9 were waited for; matrix products, arithmetic and copies ran while one was open for 0% of the time, Pallas kernels for 0%

profile of v10, /device:TPU:1, one launch (start us, length us, event | category | flops | bytes accessed | tf_op | source)
XLA Modules:
  0.0 69.5 jit_solution(4478149418949480171)
XLA Ops:
  0.0 0.9 %broadcast_select_fusion.7 = (f32[3,3,16,128]{3,2,1,0:T(8,128)S(1)}, f32[3,3,16,128]{3,2,1,0:T(8,128)S(1)}, f32[3,3,16,128]{3,2,1,0:T(8,128)S(1)}) fusion(pred[]{:T(512)S(6)} %eq.18, f32[1,16,16,128]{3,2,1,0:T(8,128)} %bitcast.22, f32[2,16,16,128]{3,2,1,0:T(8,128)} %param.2), kind=kLoop, calls=%fused_computation.22 | loop fusion | flops 55296 | bytes 614401 | tf_op jit(solution)/shard_map/jit(_where)/select_n | solution.py:561
  0.9 0.0 copy-start
  0.9 3.3 %collective-permute-start.1 = (f32[3,3,16,128]{3,2,1,0:T(8,128)S(1)}, f32[3,3,16,128]{3,2,1,0:T(8,128)S(1)}, u32[]{:S(2)}, u32[]{:S(2)}) collective-permute-start(f32[3,3,16,128]{3,2,1,0:T(8,128)S(1)} %broadcast_select_fusion.6), channel_id=1, source_target_pairs={{0,16},{1,17},{2,18},{3,19},{4,20},{5,21},{6,22},{7,23},{8,24},{9,... | collective-permute-start | bytes 221192 | tf_op jit(solution)/shard_map/ppermute | solution.py:562
  4.2 0.0 collective-permute-start
  4.2 0.1 pad.22.clone
  4.3 0.0 copy-start.1
  4.3 0.8 %collective-permute-done.1 = f32[3,3,16,128]{3,2,1,0:T(8,128)S(1)} collective-permute-done((f32[3,3,16,128]{3,2,1,0:T(8,128)S(1)}, f32[3,3,16,128]{3,2,1,0:T(8,128)S(1)}, u32[]{:S(2)}, u32[]{:S(2)}) %collective-permute-start.1) | collective-permute-done | bytes 73760 | tf_op jit(solution)/shard_map/ppermute | solution.py:562
  5.2 3.1 %collective-permute-done = f32[3,3,16,128]{3,2,1,0:T(8,128)S(1)} collective-permute-done((f32[3,3,16,128]{3,2,1,0:T(8,128)S(1)}, f32[3,3,16,128]{3,2,1,0:T(8,128)S(1)}, u32[]{:S(2)}, u32[]{:S(2)}) %collective-permute-start) | collective-permute-done | bytes 73760 | tf_op jit(solution)/shard_map/ppermute | solution.py:563
  8.3 0.0 copy-done
  8.3 0.0 copy-done.1
  8.3 0.1 select_bitcast_fusion.1
  8.4 0.5 collective-permute-start.2
  9.0 0.5 collective-permute-start.3
  9.5 0.1 pad_add_fusion.idx
  9.6 0.3 collective-permute-done.2
  9.9 3.7 %collective-permute-done.3 = f32[9,22,128]{2,1,0:T(8,128)S(1)} collective-permute-done((f32[9,22,128]{2,1,0:T(8,128)S(1)}, f32[9,22,128]{2,1,0:T(8,128)S(1)}, u32[]{:S(2)}, u32[]{:S(2)}) %collective-permute-start.3) | collective-permute-done | bytes 101408 | tf_op jit(solution)/shard_map/ppermute | solution.py:562
  13.6 0.1 copy_bitcast_fusion
  13.7 0.2 maximum_maximum_fusion.src.src0
  13.9 1.8 %down0.1 = (f32[3,4,8,128]{3,2,1,0:T(8,128)S(1)}, f32[2,22,24,128]{3,2,1,0:T(8,128)S(1)}, f32[2,22,24,128]{3,2,1,0:T(8,128)S(1)}) custom-call(s32[2]{0:T(128)S(1)} %pad_add_fusion.idx, f32[3,22,24,128]{3,2,1,0:T(8,128)S(1)} %maximum_maximum_fusion.src.src0), custom_call_target="tpu_custom_call" | custom-call | bytes 7000000 | tf_op jit(solution)/shard_map/down0/pallas_call | solution.py:522
  15.7 1.3 %collective-permute-start.4 = (f32[3,3,8,128]{3,2,1,0:T(8,128)S(1)}, f32[3,3,8,128]{3,2,1,0:T(8,128)S(1)}, u32[]{:S(2)}, u32[]{:S(2)}) collective-permute-start(f32[3,3,8,128]{3,2,1,0:T(8,128)S(1)} %get-tuple-element.37), channel_id=1, source_target_pairs={{0,1},{1,0},{2,3},{3,2},{4,5},{5,4},{6,7},{7,6},{8,9},{9,8},{10,11... | collective-permute-start | bytes 110600 | tf_op jit(solution)/shard_map/ppermute | solution.py:563
  17.0 0.5 collective-permute-start.5
  17.5 1.7 %collective-permute-done.4 = f32[3,3,8,128]{3,2,1,0:T(8,128)S(1)} collective-permute-done((f32[3,3,8,128]{3,2,1,0:T(8,128)S(1)}, f32[3,3,8,128]{3,2,1,0:T(8,128)S(1)}, u32[]{:S(2)}, u32[]{:S(2)}) %collective-permute-start.4) | collective-permute-done | bytes 36896 | tf_op jit(solution)/shard_map/ppermute | solution.py:563
  19.2 0.0 collective-permute-done.5
  19.2 1.3 %collective-permute-start.7 = (f32[3,10,8,128]{3,2,1,0:T(8,128)S(1)}, f32[3,10,8,128]{3,2,1,0:T(8,128)S(1)}, u32[]{:S(2)}, u32[]{:S(2)}) collective-permute-start(f32[3,10,8,128]{3,2,1,0:T(8,128)S(1)} %pad_maximum_fusion.5), channel_id=1, source_target_pairs={{0,1},{1,0},{2,3},{3,2},{4,5},{5,4},{6,7},{7,6},{8,9},{9,8},{10,11... | collective-permute-start | bytes 368648 | tf_op jit(solution)/shard_map/ppermute | solution.py:562
  20.5 1.0 %collective-permute-start.6 = (f32[3,10,8,128]{3,2,1,0:T(8,128)S(1)}, f32[3,10,8,128]{3,2,1,0:T(8,128)S(1)}, u32[]{:S(2)}, u32[]{:S(2)}) collective-permute-start(f32[3,10,8,128]{3,2,1,0:T(8,128)S(1)} %pad_maximum_fusion.5), channel_id=1, source_target_pairs={{0,16},{1,2},{2,1},{3,4},{4,3},{5,6},{6,5},{7,8},{8,7},{9,10},{10,... | collective-permute-start | bytes 368648 | tf_op jit(solution)/shard_map/ppermute | solution.py:563
  21.5 1.5 %collective-permute-done.7 = f32[3,10,8,128]{3,2,1,0:T(8,128)S(1)} collective-permute-done((f32[3,10,8,128]{3,2,1,0:T(8,128)S(1)}, f32[3,10,8,128]{3,2,1,0:T(8,128)S(1)}, u32[]{:S(2)}, u32[]{:S(2)}) %collective-permute-start.7) | collective-permute-done | bytes 122912 | tf_op jit(solution)/shard_map/ppermute | solution.py:562
  23.0 0.0 collective-permute-done.6
  23.1 2.7 %down1.1 = (f32[64,8,128]{2,1,0:T(8,128)}, f32[3,2,8,128]{3,2,1,0:T(8,128)S(1)}, f32[2,10,24,128]{3,2,1,0:T(8,128)S(1)}, f32[2,12,24,128]{3,2,1,0:T(8,128)S(1)}) custom-call(s32[2]{0:T(128)S(1)} %pad_add_fusion.idx, f32[3,10,24,128]{3,2,1,0:T(8,128)S(1)} %pad_maximum_fusion.src.src1), custom_call_target="tpu_custom_call" | custom-call | bytes 7000000 | tf_op jit(solution)/shard_map/down1/pallas_call | solution.py:522
  25.8 3.0 %collective-permute-start.8 = (f32[3,1,8,128]{3,2,1,0:T(8,128)S(1)}, f32[3,1,8,128]{3,2,1,0:T(8,128)S(1)}, u32[]{:S(2)}, u32[]{:S(2)}) collective-permute-start(f32[3,1,8,128]{3,2,1,0:T(8,128)S(1)} %get-tuple-element.41), channel_id=1, source_target_pairs={{0,1},{1,0},{2,3},{3,2},{4,5},{5,4},{6,7},{7,6},{8,9},{9,8},{10,11... | collective-permute-start | bytes 36872 | tf_op jit(solution)/shard_map/ppermute | solution.py:563
  28.8 2.0 %collective-permute-start.9 = (f32[3,1,8,128]{3,2,1,0:T(8,128)S(1)}, f32[3,1,8,128]{3,2,1,0:T(8,128)S(1)}, u32[]{:S(2)}, u32[]{:S(2)}) collective-permute-start(f32[3,1,8,128]{3,2,1,0:T(8,128)S(1)} %get-tuple-element.42), channel_id=1, source_target_pairs={{0,16},{1,17},{2,18},{3,19},{4,20},{5,21},{6,22},{7,23},{8,24},{9,... | collective-permute-start | bytes 36872 | tf_op jit(solution)/shard_map/ppermute | solution.py:562
  30.8 15.3 %all-to-all-start = ((f32[256,2,128]{2,1,0:T(2,128)}), f32[256,2,128]{2,1,0:T(2,128)S(1)}, u32[]{:S(2)}, u32[]{:S(2)}) async-start(f32[256,2,128]{2,1,0:T(2,128)} %bitcast.11), calls=%async_computation | async-start | bytes 524288 | tf_op jit(solution)/shard_map/all_to_all | solution.py:603
  46.1 0.0 collective-permute-done.8
  46.1 0.0 collective-permute-done.9
  46.2 2.2 %collective-permute-start.10 = (f32[3,4,4,128]{3,2,1,0:T(4,128)S(1)}, f32[3,4,4,128]{3,2,1,0:T(4,128)S(1)}, u32[]{:S(2)}, u32[]{:S(2)}) collective-permute-start(f32[3,4,4,128]{3,2,1,0:T(4,128)S(1)} %get-tuple-element.35), channel_id=1, source_target_pairs={{0,16},{1,2},{2,1},{3,4},{4,3},{5,6},{6,5},{7,8},{8,7},{9,10},{10,... | collective-permute-start | bytes 73736 | tf_op jit(solution)/shard_map/ppermute | solution.py:563
  48.4 0.4 collective-permute-start.11
  48.8 0.4 collective-permute-done.10
  49.3 2.2 %collective-permute-done.11 = f32[3,4,4,128]{3,2,1,0:T(4,128)S(1)} collective-permute-done((f32[3,4,4,128]{3,2,1,0:T(4,128)S(1)}, f32[3,4,4,128]{3,2,1,0:T(4,128)S(1)}, u32[]{:S(2)}, u32[]{:S(2)}) %collective-permute-start.11) | collective-permute-done | bytes 24608 | tf_op jit(solution)/shard_map/ppermute | solution.py:562
  51.5 10.3 %all-to-all-done = f32[256,2,128]{2,1,0:T(2,128)S(1)} async-done(((f32[256,2,128]{2,1,0:T(2,128)}), f32[256,2,128]{2,1,0:T(2,128)S(1)}, u32[]{:S(2)}, u32[]{:S(2)}) %all-to-all-start) | async-done | bytes 262176 | tf_op jit(solution)/shard_map/all_to_all | solution.py:603
  61.8 7.7 %up.1 = f32[2,16,16,128]{3,2,1,0:T(8,128)} custom-call(s32[2]{0:T(128)S(1)} %pad_add_fusion.idx, f32[3,22,24,128]{3,2,1,0:T(8,128)S(1)} %maximum_maximum_fusion.src.src0, f32[2,22,24,128]{3,2,1,0:T(8,128)S(1)} %get-tuple-element.12.gain0, f32[2,22,24,128]{3,2,1,0:T(8,128)S(1)} %get-tuple-element.13.ub0, f32[3,10,24,128]{3,2,1,0:T(8,128)S(1)} %pad_maximum_fusion.src.src1, ...), custom_call_target="tpu_custom_call" | custom-call | bytes 35000000 | tf_op jit(solution)/shard_map/up/pallas_call | solution.py:522
  (18 shorter events, 0.3 us)
Async XLA Ops:
  0.9 7.4 %copy-start = (f32[2,16,16,128]{3,2,1,0:T(8,128)S(1)}, f32[2,16,16,128]{3,2,1,0:T(8,128)}, u32[]{:S(2)}) copy-start(f32[2,16,16,128]{3,2,1,0:T(8,128)} %param.2) | copy-start | bytes 786436
  0.9 4.2 %collective-permute-start.1 = (f32[3,3,16,128]{3,2,1,0:T(8,128)S(1)}, f32[3,3,16,128]{3,2,1,0:T(8,128)S(1)}, u32[]{:S(2)}, u32[]{:S(2)}) collective-permute-start(f32[3,3,16,128]{3,2,1,0:T(8,128)S(1)} %broadcast_select_fusion.6), channel_id=1, source_target_pairs={{0,16},{1,17},{2,18},{3,19},{4,20},{5,21},{6,22},{7,23},{8,24},{9,... | collective-permute-start | bytes 221192 | tf_op jit(solution)/shard_map/ppermute | solution.py:562
  4.2 4.1 %collective-permute-start = (f32[3,3,16,128]{3,2,1,0:T(8,128)S(1)}, f32[3,3,16,128]{3,2,1,0:T(8,128)S(1)}, u32[]{:S(2)}, u32[]{:S(2)}) collective-permute-start(f32[3,3,16,128]{3,2,1,0:T(8,128)S(1)} %get-tuple-element.22), channel_id=1, source_target_pairs={{0,1},{1,0},{2,3},{3,2},{4,5},{5,4},{6,7},{7,6},{8,9},{9,8},{10,11... | collective-permute-start | bytes 221192 | tf_op jit(solution)/shard_map/ppermute | solution.py:563
  4.3 4.0 %copy-start.1 = (f32[16,16,128]{2,1,0:T(8,128)S(1)}, f32[16,16,128]{2,1,0:T(8,128)}, u32[]{:S(2)}) copy-start(f32[16,16,128]{2,1,0:T(8,128)} %param.3) | copy-start | bytes 393220
  8.4 1.4 %collective-permute-start.2 = (f32[9,22,128]{2,1,0:T(8,128)S(1)}, f32[9,22,128]{2,1,0:T(8,128)S(1)}, u32[]{:S(2)}, u32[]{:S(2)}) collective-permute-start(f32[9,22,128]{2,1,0:T(8,128)S(1)} %bitcast.27), channel_id=1, source_target_pairs={{0,16},{1,2},{2,1},{3,4},{4,3},{5,6},{6,5},{7,8},{8,7},{9,10},{10,... | collective-permute-start | bytes 304136 | tf_op jit(solution)/shard_map/ppermute | solution.py:563
  9.0 4.6 %collective-permute-start.3 = (f32[9,22,128]{2,1,0:T(8,128)S(1)}, f32[9,22,128]{2,1,0:T(8,128)S(1)}, u32[]{:S(2)}, u32[]{:S(2)}) collective-permute-start(f32[9,22,128]{2,1,0:T(8,128)S(1)} %bitcast.28), channel_id=1, source_target_pairs={{0,1},{1,0},{2,3},{3,2},{4,5},{5,4},{6,7},{7,6},{8,9},{9,8},{10,11... | collective-permute-start | bytes 304136 | tf_op jit(solution)/shard_map/ppermute | solution.py:562
  15.7 3.5 %collective-permute-start.4 = (f32[3,3,8,128]{3,2,1,0:T(8,128)S(1)}, f32[3,3,8,128]{3,2,1,0:T(8,128)S(1)}, u32[]{:S(2)}, u32[]{:S(2)}) collective-permute-start(f32[3,3,8,128]{3,2,1,0:T(8,128)S(1)} %get-tuple-element.37), channel_id=1, source_target_pairs={{0,1},{1,0},{2,3},{3,2},{4,5},{5,4},{6,7},{7,6},{8,9},{9,8},{10,11... | collective-permute-start | bytes 110600 | tf_op jit(solution)/shard_map/ppermute | solution.py:563
  17.0 2.2 %collective-permute-start.5 = (f32[3,3,8,128]{3,2,1,0:T(8,128)S(1)}, f32[3,3,8,128]{3,2,1,0:T(8,128)S(1)}, u32[]{:S(2)}, u32[]{:S(2)}) collective-permute-start(f32[3,3,8,128]{3,2,1,0:T(8,128)S(1)} %get-tuple-element.38), channel_id=1, source_target_pairs={{0,16},{1,17},{2,18},{3,19},{4,20},{5,21},{6,22},{7,23},{8,24},{9,... | collective-permute-start | bytes 110600 | tf_op jit(solution)/shard_map/ppermute | solution.py:562
  19.2 3.8 %collective-permute-start.7 = (f32[3,10,8,128]{3,2,1,0:T(8,128)S(1)}, f32[3,10,8,128]{3,2,1,0:T(8,128)S(1)}, u32[]{:S(2)}, u32[]{:S(2)}) collective-permute-start(f32[3,10,8,128]{3,2,1,0:T(8,128)S(1)} %pad_maximum_fusion.5), channel_id=1, source_target_pairs={{0,1},{1,0},{2,3},{3,2},{4,5},{5,4},{6,7},{7,6},{8,9},{9,8},{10,11... | collective-permute-start | bytes 368648 | tf_op jit(solution)/shard_map/ppermute | solution.py:562
  20.5 2.5 %collective-permute-start.6 = (f32[3,10,8,128]{3,2,1,0:T(8,128)S(1)}, f32[3,10,8,128]{3,2,1,0:T(8,128)S(1)}, u32[]{:S(2)}, u32[]{:S(2)}) collective-permute-start(f32[3,10,8,128]{3,2,1,0:T(8,128)S(1)} %pad_maximum_fusion.5), channel_id=1, source_target_pairs={{0,16},{1,2},{2,1},{3,4},{4,3},{5,6},{6,5},{7,8},{8,7},{9,10},{10,... | collective-permute-start | bytes 368648 | tf_op jit(solution)/shard_map/ppermute | solution.py:563
  25.8 20.3 %collective-permute-start.8 = (f32[3,1,8,128]{3,2,1,0:T(8,128)S(1)}, f32[3,1,8,128]{3,2,1,0:T(8,128)S(1)}, u32[]{:S(2)}, u32[]{:S(2)}) collective-permute-start(f32[3,1,8,128]{3,2,1,0:T(8,128)S(1)} %get-tuple-element.41), channel_id=1, source_target_pairs={{0,1},{1,0},{2,3},{3,2},{4,5},{5,4},{6,7},{7,6},{8,9},{9,8},{10,11... | collective-permute-start | bytes 36872 | tf_op jit(solution)/shard_map/ppermute | solution.py:563
  28.8 17.3 %collective-permute-start.9 = (f32[3,1,8,128]{3,2,1,0:T(8,128)S(1)}, f32[3,1,8,128]{3,2,1,0:T(8,128)S(1)}, u32[]{:S(2)}, u32[]{:S(2)}) collective-permute-start(f32[3,1,8,128]{3,2,1,0:T(8,128)S(1)} %get-tuple-element.42), channel_id=1, source_target_pairs={{0,16},{1,17},{2,18},{3,19},{4,20},{5,21},{6,22},{7,23},{8,24},{9,... | collective-permute-start | bytes 36872 | tf_op jit(solution)/shard_map/ppermute | solution.py:562
  30.8 31.0 %all-to-all-start = ((f32[256,2,128]{2,1,0:T(2,128)}), f32[256,2,128]{2,1,0:T(2,128)S(1)}, u32[]{:S(2)}, u32[]{:S(2)}) async-start(f32[256,2,128]{2,1,0:T(2,128)} %bitcast.11), calls=%async_computation | async-start | bytes 524288 | tf_op jit(solution)/shard_map/all_to_all | solution.py:603
  46.2 3.1 %collective-permute-start.10 = (f32[3,4,4,128]{3,2,1,0:T(4,128)S(1)}, f32[3,4,4,128]{3,2,1,0:T(4,128)S(1)}, u32[]{:S(2)}, u32[]{:S(2)}) collective-permute-start(f32[3,4,4,128]{3,2,1,0:T(4,128)S(1)} %get-tuple-element.35), channel_id=1, source_target_pairs={{0,16},{1,2},{2,1},{3,4},{4,3},{5,6},{6,5},{7,8},{8,7},{9,10},{10,... | collective-permute-start | bytes 73736 | tf_op jit(solution)/shard_map/ppermute | solution.py:563
  48.4 3.1 %collective-permute-start.11 = (f32[3,4,4,128]{3,2,1,0:T(4,128)S(1)}, f32[3,4,4,128]{3,2,1,0:T(4,128)S(1)}, u32[]{:S(2)}, u32[]{:S(2)}) collective-permute-start(f32[3,4,4,128]{3,2,1,0:T(4,128)S(1)} %get-tuple-element.36), channel_id=1, source_target_pairs={{0,1},{1,0},{2,3},{3,2},{4,5},{5,4},{6,7},{7,6},{8,9},{9,8},{10,11... | collective-permute-start | bytes 73736 | tf_op jit(solution)/shard_map/ppermute | solution.py:562

commit v11 on v10

--- a/solution.py
+++ b/solution.py
@@ -552,15 +552,17 @@
     return pairs
 
 
-def trade(to_low, to_high, axis):
+def trade(to_low, to_high, axis, near=None):
     even = lax.axis_index(axis) % 2 == 0
     if to_low is to_high:
         one = two = to_low
     else:
-        one = jnp.where(even, to_high, to_low)
+        low, high = near or (to_low, to_high)
+        one = jnp.where(even, high, low)
         two = jnp.where(even, to_low, to_high)
+    two = lax.ppermute(two, BOTH, partners(axis, 1))
     one = lax.ppermute(one, BOTH, partners(axis, 0))
-    two = lax.ppermute(two, BOTH, partners(axis, 1))
+    one, two = lax.optimization_barrier((one, two))
     return jnp.where(even, two, one), jnp.where(even, one, two)
 
 
@@ -570,7 +572,9 @@
     idx = jnp.stack([ix, iy]).astype(jnp.int32)
 
     own = jnp.concatenate([residual_in, wave_sq[None]], axis=0)
-    low, high = trade(own[:, :3], own[:, 13:], "gx")
+    near_f, near_w = lax.optimization_barrier((residual_in, wave_sq))
+    near = jnp.concatenate([near_f, near_w[None]], axis=0)
+    low, high = trade(own[:, :3], own[:, 13:], "gx", (near[:, :3], near[:, 13:]))
     strip = jnp.concatenate([low, own, high], axis=1)
     low, high = trade(
         strip[:, :, :3].transpose(0, 2, 1, 3).reshape(9, 22, 128),

time: 69.7 us -> 69.5 us (level)
  starting transfers between devices: 31.5 us -> 30.3 us
  waiting for transfers between devices: 24.1 us -> 25.1 us
    ppermute x6, starting transfers between devices: 8.11 us -> 3.84 us  [trade(): one = lax.ppermute(one, BOTH, partners(axis, 0))]
    ppermute x6, starting transfers between devices: 8.06 us -> 11 us  [trade(): two = lax.ppermute(two, BOTH, partners(axis, 1))]
    ppermute x6, waiting for transfers between devices: 8.22 us -> 9.96 us  [trade(): one = lax.ppermute(one, BOTH, partners(axis, 0))]
    ppermute x6, waiting for transfers between devices: 5.53 us -> 4.76 us  [trade(): two = lax.ppermute(two, BOTH, partners(axis, 1))]
where the time goes in v11:
time: 69.5 us; the launch traced here: 69.3 us
  starting transfers between devices  30.3 us (44%)
  waiting for transfers between devices  25.1 us (36%)
  Pallas kernels  12.2 us (18%)
  other arithmetic  1.47 us (2%)
    all_to_all x1, starting transfers between devices, body(): flat = lax.all_to_all(part, ('gx', 'gy'), 0, 0).reshape(512, 128)  15.5 us
    pallas_call x3, Pallas kernels, call(): pl.pallas_call(kernel, name=name, out_shape=[jax.ShapeDtypeStruct(shape,...  12.2 us
    ppermute x6, starting transfers between devices, trade(): two = lax.ppermute(two, BOTH, partners(axis, 1))  11 us
    all_to_all x1, waiting for transfers between devices, body(): flat = lax.all_to_all(part, ('gx', 'gy'), 0, 0).reshape(512, 128)  10.3 us
    ppermute x6, waiting for transfers between devices, trade(): one = lax.ppermute(one, BOTH, partners(axis, 0))  9.96 us
    ppermute x6, waiting for transfers between devices, trade(): two = lax.ppermute(two, BOTH, partners(axis, 1))  4.76 us
    ppermute x6, starting transfers between devices, trade(): one = lax.ppermute(one, BOTH, partners(axis, 0))  3.84 us
  transfers between devices with their start and end apart: 13, of which 9 were waited for; matrix products, arithmetic and copies ran while one was open for 0% of the time, Pallas kernels for 0%

profile of v11, /device:TPU:1, one launch (start us, length us, event | category | flops | bytes accessed | tf_op | source)
XLA Modules:
  0.0 69.3 jit_solution(15737039679537078476)
XLA Ops:
  0.0 0.0 copy-start
  0.0 0.0 copy-start.1
  0.0 0.9 %fusion = f32[3,3,16,128]{3,2,1,0:T(8,128)S(1)} fusion(f32[1,16,16,128]{3,2,1,0:T(8,128)} %bitcast.23, f32[2,16,16,128]{3,2,1,0:T(8,128)} %param.2, pred[]{:T(512)S(6)} %eq.18), kind=kLoop, calls=%fused_computation.13 | loop fusion | flops 55296 | bytes 466945 | tf_op jit(solution)/shard_map/jit(_where)/select_n | solution.py:562
  0.9 3.1 %collective-permute-start.1 = (f32[3,3,16,128]{3,2,1,0:T(8,128)S(1)}, f32[3,3,16,128]{3,2,1,0:T(8,128)S(1)}, u32[]{:S(2)}, u32[]{:S(2)}) collective-permute-start(f32[3,3,16,128]{3,2,1,0:T(8,128)S(1)} %fusion), channel_id=1, source_target_pairs={{0,1},{1,0},{2,3},{3,2},{4,5},{5,4},{6,7},{7,6},{8,9},{9,8},{10,11... | collective-permute-start | bytes 221192 | tf_op jit(solution)/shard_map/ppermute | solution.py:563
  4.0 0.0 copy-done
  4.0 0.0 copy-done.1
  4.1 0.3 collective-permute-start
  4.4 0.1 pad.22.clone
  4.5 1.6 %collective-permute-done.1 = f32[3,3,16,128]{3,2,1,0:T(8,128)S(1)} collective-permute-done((f32[3,3,16,128]{3,2,1,0:T(8,128)S(1)}, f32[3,3,16,128]{3,2,1,0:T(8,128)S(1)}, u32[]{:S(2)}, u32[]{:S(2)}) %collective-permute-start.1) | collective-permute-done | bytes 73760 | tf_op jit(solution)/shard_map/ppermute | solution.py:563
  6.1 0.0 collective-permute-done
  6.1 0.1 select_bitcast_fusion
  6.2 2.6 %collective-permute-start.3 = (f32[9,22,128]{2,1,0:T(8,128)S(1)}, f32[9,22,128]{2,1,0:T(8,128)S(1)}, u32[]{:S(2)}, u32[]{:S(2)}) collective-permute-start(f32[9,22,128]{2,1,0:T(8,128)S(1)} %bitcast.29), channel_id=1, source_target_pairs={{0,16},{1,2},{2,1},{3,4},{4,3},{5,6},{6,5},{7,8},{8,7},{9,10},{10,... | collective-permute-start | bytes 304136 | tf_op jit(solution)/shard_map/ppermute | solution.py:563
  8.9 0.4 collective-permute-start.2
  9.3 0.1 pad_add_fusion.idx
  9.4 0.4 collective-permute-done.3
  9.8 3.9 %collective-permute-done.2 = f32[9,22,128]{2,1,0:T(8,128)S(1)} collective-permute-done((f32[9,22,128]{2,1,0:T(8,128)S(1)}, f32[9,22,128]{2,1,0:T(8,128)S(1)}, u32[]{:S(2)}, u32[]{:S(2)}) %collective-permute-start.2) | collective-permute-done | bytes 101408 | tf_op jit(solution)/shard_map/ppermute | solution.py:564
  13.7 0.1 copy_bitcast_fusion
  13.7 0.2 maximum_maximum_fusion.src.src0
  13.9 1.8 %down0.1 = (f32[3,4,8,128]{3,2,1,0:T(8,128)S(1)}, f32[2,22,24,128]{3,2,1,0:T(8,128)S(1)}, f32[2,22,24,128]{3,2,1,0:T(8,128)S(1)}) custom-call(s32[2]{0:T(128)S(1)} %pad_add_fusion.idx, f32[3,22,24,128]{3,2,1,0:T(8,128)S(1)} %maximum_maximum_fusion.src.src0), custom_call_target="tpu_custom_call" | custom-call | bytes 7000000 | tf_op jit(solution)/shard_map/down0/pallas_call | solution.py:522
  15.7 1.0 %collective-permute-start.5 = (f32[3,3,8,128]{3,2,1,0:T(8,128)S(1)}, f32[3,3,8,128]{3,2,1,0:T(8,128)S(1)}, u32[]{:S(2)}, u32[]{:S(2)}) collective-permute-start(f32[3,3,8,128]{3,2,1,0:T(8,128)S(1)} %get-tuple-element.62), channel_id=1, source_target_pairs={{0,1},{1,0},{2,3},{3,2},{4,5},{5,4},{6,7},{7,6},{8,9},{9,8},{10,11... | collective-permute-start | bytes 110600 | tf_op jit(solution)/shard_map/ppermute | solution.py:563
  16.7 0.6 collective-permute-start.4
  17.3 1.9 %collective-permute-done.5 = f32[3,3,8,128]{3,2,1,0:T(8,128)S(1)} collective-permute-done((f32[3,3,8,128]{3,2,1,0:T(8,128)S(1)}, f32[3,3,8,128]{3,2,1,0:T(8,128)S(1)}, u32[]{:S(2)}, u32[]{:S(2)}) %collective-permute-start.5) | collective-permute-done | bytes 36896 | tf_op jit(solution)/shard_map/ppermute | solution.py:563
  19.2 0.0 collective-permute-done.4
  19.2 1.5 %collective-permute-start.7 = (f32[3,10,8,128]{3,2,1,0:T(8,128)S(1)}, f32[3,10,8,128]{3,2,1,0:T(8,128)S(1)}, u32[]{:S(2)}, u32[]{:S(2)}) collective-permute-start(f32[3,10,8,128]{3,2,1,0:T(8,128)S(1)} %pad_maximum_fusion.5), channel_id=1, source_target_pairs={{0,16},{1,2},{2,1},{3,4},{4,3},{5,6},{6,5},{7,8},{8,7},{9,10},{10,... | collective-permute-start | bytes 368648 | tf_op jit(solution)/shard_map/ppermute | solution.py:563
  20.7 0.5 collective-permute-start.6
  21.2 0.5 collective-permute-done.7
  21.7 3.9 %collective-permute-done.6 = f32[3,10,8,128]{3,2,1,0:T(8,128)S(1)} collective-permute-done((f32[3,10,8,128]{3,2,1,0:T(8,128)S(1)}, f32[3,10,8,128]{3,2,1,0:T(8,128)S(1)}, u32[]{:S(2)}, u32[]{:S(2)}) %collective-permute-start.6) | collective-permute-done | bytes 122912 | tf_op jit(solution)/shard_map/ppermute | solution.py:564
  25.6 2.7 %down1.1 = (f32[64,8,128]{2,1,0:T(8,128)}, f32[3,2,8,128]{3,2,1,0:T(8,128)S(1)}, f32[2,10,24,128]{3,2,1,0:T(8,128)S(1)}, f32[2,12,24,128]{3,2,1,0:T(8,128)S(1)}) custom-call(s32[2]{0:T(128)S(1)} %pad_add_fusion.idx, f32[3,10,24,128]{3,2,1,0:T(8,128)S(1)} %pad_maximum_fusion.src.src1), custom_call_target="tpu_custom_call" | custom-call | bytes 7000000 | tf_op jit(solution)/shard_map/down1/pallas_call | solution.py:522
  28.3 0.6 collective-permute-start.9
  29.0 1.5 %collective-permute-start.8 = (f32[3,1,8,128]{3,2,1,0:T(8,128)S(1)}, f32[3,1,8,128]{3,2,1,0:T(8,128)S(1)}, u32[]{:S(2)}, u32[]{:S(2)}) collective-permute-start(f32[3,1,8,128]{3,2,1,0:T(8,128)S(1)} %get-tuple-element.67), channel_id=1, source_target_pairs={{0,16},{1,17},{2,18},{3,19},{4,20},{5,21},{6,22},{7,23},{8,24},{9,... | collective-permute-start | bytes 36872 | tf_op jit(solution)/shard_map/ppermute | solution.py:564
  30.5 15.5 %all-to-all-start = ((f32[256,2,128]{2,1,0:T(2,128)}), f32[256,2,128]{2,1,0:T(2,128)S(1)}, u32[]{:S(2)}, u32[]{:S(2)}) async-start(f32[256,2,128]{2,1,0:T(2,128)} %bitcast.12), calls=%async_computation | async-start | bytes 524288 | tf_op jit(solution)/shard_map/all_to_all | solution.py:607
  46.0 0.0 collective-permute-done.9
  46.0 0.0 collective-permute-done.8
  46.0 2.2 %collective-permute-start.11 = (f32[3,4,4,128]{3,2,1,0:T(4,128)S(1)}, f32[3,4,4,128]{3,2,1,0:T(4,128)S(1)}, u32[]{:S(2)}, u32[]{:S(2)}) collective-permute-start(f32[3,4,4,128]{3,2,1,0:T(4,128)S(1)} %get-tuple-element.60), channel_id=1, source_target_pairs={{0,16},{1,2},{2,1},{3,4},{4,3},{5,6},{6,5},{7,8},{8,7},{9,10},{10,... | collective-permute-start | bytes 73736 | tf_op jit(solution)/shard_map/ppermute | solution.py:563
  48.3 0.4 collective-permute-start.10
  48.7 0.4 collective-permute-done.11
  49.1 2.2 %collective-permute-done.10 = f32[3,4,4,128]{3,2,1,0:T(4,128)S(1)} collective-permute-done((f32[3,4,4,128]{3,2,1,0:T(4,128)S(1)}, f32[3,4,4,128]{3,2,1,0:T(4,128)S(1)}, u32[]{:S(2)}, u32[]{:S(2)}) %collective-permute-start.10) | collective-permute-done | bytes 24608 | tf_op jit(solution)/shard_map/ppermute | solution.py:564
  51.4 10.3 %all-to-all-done = f32[256,2,128]{2,1,0:T(2,128)S(1)} async-done(((f32[256,2,128]{2,1,0:T(2,128)}), f32[256,2,128]{2,1,0:T(2,128)S(1)}, u32[]{:S(2)}, u32[]{:S(2)}) %all-to-all-start) | async-done | bytes 262176 | tf_op jit(solution)/shard_map/all_to_all | solution.py:607
  61.7 7.7 %up.1 = f32[2,16,16,128]{3,2,1,0:T(8,128)} custom-call(s32[2]{0:T(128)S(1)} %pad_add_fusion.idx, f32[3,22,24,128]{3,2,1,0:T(8,128)S(1)} %maximum_maximum_fusion.src.src0, f32[2,22,24,128]{3,2,1,0:T(8,128)S(1)} %get-tuple-element.32.gain0, f32[2,22,24,128]{3,2,1,0:T(8,128)S(1)} %get-tuple-element.33.ub0, f32[3,10,24,128]{3,2,1,0:T(8,128)S(1)} %pad_maximum_fusion.src.src1, ...), custom_call_target="tpu_custom_call" | custom-call | bytes 35000000 | tf_op jit(solution)/shard_map/up/pallas_call | solution.py:522
  (18 shorter events, 0.3 us)
Async XLA Ops:
  0.0 4.0 %copy-start = (f32[2,16,16,128]{3,2,1,0:T(8,128)S(1)}, f32[2,16,16,128]{3,2,1,0:T(8,128)}, u32[]{:S(2)}) copy-start(f32[2,16,16,128]{3,2,1,0:T(8,128)} %param.2) | copy-start | bytes 786436
  0.0 4.0 %copy-start.1 = (f32[16,16,128]{2,1,0:T(8,128)S(1)}, f32[16,16,128]{2,1,0:T(8,128)}, u32[]{:S(2)}) copy-start(f32[16,16,128]{2,1,0:T(8,128)} %param.3) | copy-start | bytes 393220
  0.9 5.2 %collective-permute-start.1 = (f32[3,3,16,128]{3,2,1,0:T(8,128)S(1)}, f32[3,3,16,128]{3,2,1,0:T(8,128)S(1)}, u32[]{:S(2)}, u32[]{:S(2)}) collective-permute-start(f32[3,3,16,128]{3,2,1,0:T(8,128)S(1)} %fusion), channel_id=1, source_target_pairs={{0,1},{1,0},{2,3},{3,2},{4,5},{5,4},{6,7},{7,6},{8,9},{9,8},{10,11... | collective-permute-start | bytes 221192 | tf_op jit(solution)/shard_map/ppermute | solution.py:563
  4.1 2.0 %collective-permute-start = (f32[3,3,16,128]{3,2,1,0:T(8,128)S(1)}, f32[3,3,16,128]{3,2,1,0:T(8,128)S(1)}, u32[]{:S(2)}, u32[]{:S(2)}) collective-permute-start(f32[3,3,16,128]{3,2,1,0:T(8,128)S(1)} %fusion.1), channel_id=1, source_target_pairs={{0,16},{1,17},{2,18},{3,19},{4,20},{5,21},{6,22},{7,23},{8,24},{9,... | collective-permute-start | bytes 221192 | tf_op jit(solution)/shard_map/ppermute | solution.py:564
  6.2 3.6 %collective-permute-start.3 = (f32[9,22,128]{2,1,0:T(8,128)S(1)}, f32[9,22,128]{2,1,0:T(8,128)S(1)}, u32[]{:S(2)}, u32[]{:S(2)}) collective-permute-start(f32[9,22,128]{2,1,0:T(8,128)S(1)} %bitcast.29), channel_id=1, source_target_pairs={{0,16},{1,2},{2,1},{3,4},{4,3},{5,6},{6,5},{7,8},{8,7},{9,10},{10,... | collective-permute-start | bytes 304136 | tf_op jit(solution)/shard_map/ppermute | solution.py:563
  8.9 4.8 %collective-permute-start.2 = (f32[9,22,128]{2,1,0:T(8,128)S(1)}, f32[9,22,128]{2,1,0:T(8,128)S(1)}, u32[]{:S(2)}, u32[]{:S(2)}) collective-permute-start(f32[9,22,128]{2,1,0:T(8,128)S(1)} %bitcast.30), channel_id=1, source_target_pairs={{0,1},{1,0},{2,3},{3,2},{4,5},{5,4},{6,7},{7,6},{8,9},{9,8},{10,11... | collective-permute-start | bytes 304136 | tf_op jit(solution)/shard_map/ppermute | solution.py:564
  15.7 3.5 %collective-permute-start.5 = (f32[3,3,8,128]{3,2,1,0:T(8,128)S(1)}, f32[3,3,8,128]{3,2,1,0:T(8,128)S(1)}, u32[]{:S(2)}, u32[]{:S(2)}) collective-permute-start(f32[3,3,8,128]{3,2,1,0:T(8,128)S(1)} %get-tuple-element.62), channel_id=1, source_target_pairs={{0,1},{1,0},{2,3},{3,2},{4,5},{5,4},{6,7},{7,6},{8,9},{9,8},{10,11... | collective-permute-start | bytes 110600 | tf_op jit(solution)/shard_map/ppermute | solution.py:563
  16.7 2.5 %collective-permute-start.4 = (f32[3,3,8,128]{3,2,1,0:T(8,128)S(1)}, f32[3,3,8,128]{3,2,1,0:T(8,128)S(1)}, u32[]{:S(2)}, u32[]{:S(2)}) collective-permute-start(f32[3,3,8,128]{3,2,1,0:T(8,128)S(1)} %get-tuple-element.63), channel_id=1, source_target_pairs={{0,16},{1,17},{2,18},{3,19},{4,20},{5,21},{6,22},{7,23},{8,24},{9,... | collective-permute-start | bytes 110600 | tf_op jit(solution)/shard_map/ppermute | solution.py:564
  19.2 2.4 %collective-permute-start.7 = (f32[3,10,8,128]{3,2,1,0:T(8,128)S(1)}, f32[3,10,8,128]{3,2,1,0:T(8,128)S(1)}, u32[]{:S(2)}, u32[]{:S(2)}) collective-permute-start(f32[3,10,8,128]{3,2,1,0:T(8,128)S(1)} %pad_maximum_fusion.5), channel_id=1, source_target_pairs={{0,16},{1,2},{2,1},{3,4},{4,3},{5,6},{6,5},{7,8},{8,7},{9,10},{10,... | collective-permute-start | bytes 368648 | tf_op jit(solution)/shard_map/ppermute | solution.py:563
  20.7 4.9 %collective-permute-start.6 = (f32[3,10,8,128]{3,2,1,0:T(8,128)S(1)}, f32[3,10,8,128]{3,2,1,0:T(8,128)S(1)}, u32[]{:S(2)}, u32[]{:S(2)}) collective-permute-start(f32[3,10,8,128]{3,2,1,0:T(8,128)S(1)} %pad_maximum_fusion.5), channel_id=1, source_target_pairs={{0,1},{1,0},{2,3},{3,2},{4,5},{5,4},{6,7},{7,6},{8,9},{9,8},{10,11... | collective-permute-start | bytes 368648 | tf_op jit(solution)/shard_map/ppermute | solution.py:564
  28.3 17.6 %collective-permute-start.9 = (f32[3,1,8,128]{3,2,1,0:T(8,128)S(1)}, f32[3,1,8,128]{3,2,1,0:T(8,128)S(1)}, u32[]{:S(2)}, u32[]{:S(2)}) collective-permute-start(f32[3,1,8,128]{3,2,1,0:T(8,128)S(1)} %get-tuple-element.66), channel_id=1, source_target_pairs={{0,1},{1,0},{2,3},{3,2},{4,5},{5,4},{6,7},{7,6},{8,9},{9,8},{10,11... | collective-permute-start | bytes 36872 | tf_op jit(solution)/shard_map/ppermute | solution.py:563
  29.0 17.0 %collective-permute-start.8 = (f32[3,1,8,128]{3,2,1,0:T(8,128)S(1)}, f32[3,1,8,128]{3,2,1,0:T(8,128)S(1)}, u32[]{:S(2)}, u32[]{:S(2)}) collective-permute-start(f32[3,1,8,128]{3,2,1,0:T(8,128)S(1)} %get-tuple-element.67), channel_id=1, source_target_pairs={{0,16},{1,17},{2,18},{3,19},{4,20},{5,21},{6,22},{7,23},{8,24},{9,... | collective-permute-start | bytes 36872 | tf_op jit(solution)/shard_map/ppermute | solution.py:564
  30.5 31.2 %all-to-all-start = ((f32[256,2,128]{2,1,0:T(2,128)}), f32[256,2,128]{2,1,0:T(2,128)S(1)}, u32[]{:S(2)}, u32[]{:S(2)}) async-start(f32[256,2,128]{2,1,0:T(2,128)} %bitcast.12), calls=%async_computation | async-start | bytes 524288 | tf_op jit(solution)/shard_map/all_to_all | solution.py:607
  46.0 3.1 %collective-permute-start.11 = (f32[3,4,4,128]{3,2,1,0:T(4,128)S(1)}, f32[3,4,4,128]{3,2,1,0:T(4,128)S(1)}, u32[]{:S(2)}, u32[]{:S(2)}) collective-permute-start(f32[3,4,4,128]{3,2,1,0:T(4,128)S(1)} %get-tuple-element.60), channel_id=1, source_target_pairs={{0,16},{1,2},{2,1},{3,4},{4,3},{5,6},{6,5},{7,8},{8,7},{9,10},{10,... | collective-permute-start | bytes 73736 | tf_op jit(solution)/shard_map/ppermute | solution.py:563
  48.3 3.1 %collective-permute-start.10 = (f32[3,4,4,128]{3,2,1,0:T(4,128)S(1)}, f32[3,4,4,128]{3,2,1,0:T(4,128)S(1)}, u32[]{:S(2)}, u32[]{:S(2)}) collective-permute-start(f32[3,4,4,128]{3,2,1,0:T(4,128)S(1)} %get-tuple-element.61), channel_id=1, source_target_pairs={{0,1},{1,0},{2,3},{3,2},{4,5},{5,4},{6,7},{7,6},{8,9},{9,8},{10,11... | collective-permute-start | bytes 73736 | tf_op jit(solution)/shard_map/ppermute | solution.py:564

commit v12 on v11

--- a/solution.py
+++ b/solution.py
@@ -141,7 +141,7 @@
 def down0_kernel(idx, src, out, gain, ub, ua, tmp):
     ix, iy = idx[0], idx[1]
     win, _ = level0(src, gain, ua, ix, iy)
-    repeat(1, 21, lambda x: win.relax(x, ua, ub), 10)
+    repeat(1, 21, lambda x: win.relax(x, ua, ub), 20)
     for c in range(2):
         for x in (0, 21):
             ub[c, x] = jnp.zeros((24, 128), F32)
@@ -238,8 +238,8 @@
 
 
 def up_kernel(
-    idx, src0, gain0, ub0, src1, gain1, ub1, src2, flat, out,
-    f3, w3, ga3, gb3, ua3, ub3, f4, w4, s4, e3, gain2, u2, wide2, cell1, ua1, ut1, wide1, wide0, ua0, ut0,
+    idx, src0, gain0, ub0, src1, gain1, ub1, src2, shared, out,
+    flat, f3, w3, ga3, gb3, ua3, ub3, f4, w4, s4, e3, gain2, u2, wide2, cell1, ua1, ut1, wide1, wide0, ua0, ut0,
 ):
     ix, iy = idx[0], idx[1]
     lane = lanes(16)
@@ -261,6 +261,8 @@
 
     def packed_misfit(f, w, v, nb, scale):
         return f - scale * (6.0 * v - nb) + w * (v + sign * swap(v, real))
+
+    flat[pl.ds(0, 512), :] = shared[...]
 
     for at in (0, 1, 2, 19, 20, 21):
         for ref in (f3, w3, ga3, gb3):
@@ -504,9 +506,9 @@
                 keep = inside0 * scalar_mask(ix * 16 - 3 + x, 256)
                 ua0[c, x] = ub0[c, x] + (0.75 * mid + 0.25 * side) * keep
 
-    repeat(5, 15, correct0, 5)
+    repeat(5, 15, correct0, 10)
     win0 = Window(src0, gain0, 1.0, 0, functools.partial(near0, lane24))
-    repeat(2, 20, lambda x: win0.relax(x, ua0, ut0), 9)
+    repeat(2, 20, lambda x: win0.relax(x, ua0, ut0), 18)
 
     def finish0(x):
         new = win0.relaxed(x + 3, ut0)
@@ -514,7 +516,7 @@
             ua0[c, x + 3] = new[c]
             out[c, x] = ua0[c, x + 3, pl.ds(3, 16), :]
 
-    repeat(0, 16, finish0, 8)
+    repeat(0, 16, finish0, 16)
 
 
 def call(kernel, name, out_shape, scratch, *args, micros=2):
@@ -615,10 +617,10 @@
         up_kernel,
         "up",
         [(2, 16, 16, 128)],
-        [wide, wide, wide, wide, wide, wide]
+        [(520, 128), wide, wide, wide, wide, wide, wide]
         + [(4, 16, 128), (4, 16, 128), (4, 16, 128), (5, 32, 128)]
-        + [(2, 4, 16, 128), (2, 6, 16, 128), (2, 4, 32, 128)]
-        + [(2, 10, 16, 128), n1, n1, (2, 10, 32, 128), (2, 16, 32, 128), n0, n0],
+        + [(2, 4, 16, 128), (2, 6, 16, 128), (2, 4, 40, 128)]
+        + [(2, 10, 16, 128), n1, n1, (2, 10, 40, 128), (2, 16, 40, 128), n0, n0],
         idx,
         src0,
         gain0,

time: 69.5 us -> 69.2 us (level)
  no operation moved by 1% of the time
where the time goes in v12:
time: 69.2 us; the launch traced here: 69.1 us
  starting transfers between devices  30.3 us (44%)
  waiting for transfers between devices  25.1 us (36%)
  Pallas kernels  11.9 us (17%)
  other arithmetic  1.47 us (2%)
    all_to_all x1, starting transfers between devices, body(): flat = lax.all_to_all(part, ('gx', 'gy'), 0, 0).reshape(512, 128)  15.5 us
    pallas_call x3, Pallas kernels, call(): pl.pallas_call(kernel, name=name, out_shape=[jax.ShapeDtypeStruct(shape,...  11.9 us
    ppermute x6, starting transfers between devices, trade(): two = lax.ppermute(two, BOTH, partners(axis, 1))  11 us
    all_to_all x1, waiting for transfers between devices, body(): flat = lax.all_to_all(part, ('gx', 'gy'), 0, 0).reshape(512, 128)  10.3 us
    ppermute x6, waiting for transfers between devices, trade(): one = lax.ppermute(one, BOTH, partners(axis, 0))  9.96 us
    ppermute x6, waiting for transfers between devices, trade(): two = lax.ppermute(two, BOTH, partners(axis, 1))  4.76 us
    ppermute x6, starting transfers between devices, trade(): one = lax.ppermute(one, BOTH, partners(axis, 0))  3.84 us
  transfers between devices with their start and end apart: 13, of which 9 were waited for; matrix products, arithmetic and copies ran while one was open for 0% of the time, Pallas kernels for 0%

profile of v12, /device:TPU:1, one launch (start us, length us, event | category | flops | bytes accessed | tf_op | source)
XLA Modules:
  0.0 69.1 jit_solution(13537321408601628540)
XLA Ops:
  0.0 0.0 copy-start
  0.0 0.0 copy-start.1
  0.0 0.9 %fusion = f32[3,3,16,128]{3,2,1,0:T(8,128)S(1)} fusion(f32[1,16,16,128]{3,2,1,0:T(8,128)} %bitcast.23, f32[2,16,16,128]{3,2,1,0:T(8,128)} %param.2, pred[]{:T(512)S(6)} %eq.18), kind=kLoop, calls=%fused_computation.13 | loop fusion | flops 55296 | bytes 466945 | tf_op jit(solution)/shard_map/jit(_where)/select_n | solution.py:564
  0.9 3.1 %collective-permute-start.1 = (f32[3,3,16,128]{3,2,1,0:T(8,128)S(1)}, f32[3,3,16,128]{3,2,1,0:T(8,128)S(1)}, u32[]{:S(2)}, u32[]{:S(2)}) collective-permute-start(f32[3,3,16,128]{3,2,1,0:T(8,128)S(1)} %fusion), channel_id=1, source_target_pairs={{0,1},{1,0},{2,3},{3,2},{4,5},{5,4},{6,7},{7,6},{8,9},{9,8},{10,11... | collective-permute-start | bytes 221192 | tf_op jit(solution)/shard_map/ppermute | solution.py:565
  4.0 0.0 copy-done
  4.0 0.0 copy-done.1
  4.1 0.3 collective-permute-start
  4.4 0.1 pad.22.clone
  4.5 1.6 %collective-permute-done.1 = f32[3,3,16,128]{3,2,1,0:T(8,128)S(1)} collective-permute-done((f32[3,3,16,128]{3,2,1,0:T(8,128)S(1)}, f32[3,3,16,128]{3,2,1,0:T(8,128)S(1)}, u32[]{:S(2)}, u32[]{:S(2)}) %collective-permute-start.1) | collective-permute-done | bytes 73760 | tf_op jit(solution)/shard_map/ppermute | solution.py:565
  6.1 0.0 collective-permute-done
  6.1 0.1 select_bitcast_fusion
  6.2 2.6 %collective-permute-start.3 = (f32[9,22,128]{2,1,0:T(8,128)S(1)}, f32[9,22,128]{2,1,0:T(8,128)S(1)}, u32[]{:S(2)}, u32[]{:S(2)}) collective-permute-start(f32[9,22,128]{2,1,0:T(8,128)S(1)} %bitcast.29), channel_id=1, source_target_pairs={{0,16},{1,2},{2,1},{3,4},{4,3},{5,6},{6,5},{7,8},{8,7},{9,10},{10,... | collective-permute-start | bytes 304136 | tf_op jit(solution)/shard_map/ppermute | solution.py:565
  8.9 0.4 collective-permute-start.2
  9.3 0.1 pad_add_fusion.idx
  9.4 0.4 collective-permute-done.3
  9.8 3.9 %collective-permute-done.2 = f32[9,22,128]{2,1,0:T(8,128)S(1)} collective-permute-done((f32[9,22,128]{2,1,0:T(8,128)S(1)}, f32[9,22,128]{2,1,0:T(8,128)S(1)}, u32[]{:S(2)}, u32[]{:S(2)}) %collective-permute-start.2) | collective-permute-done | bytes 101408 | tf_op jit(solution)/shard_map/ppermute | solution.py:566
  13.7 0.1 copy_bitcast_fusion
  13.7 0.2 maximum_maximum_fusion.src.src0
  13.9 1.7 %down0.1 = (f32[3,4,8,128]{3,2,1,0:T(8,128)S(1)}, f32[2,22,24,128]{3,2,1,0:T(8,128)S(1)}, f32[2,22,24,128]{3,2,1,0:T(8,128)S(1)}) custom-call(s32[2]{0:T(128)S(1)} %pad_add_fusion.idx, f32[3,22,24,128]{3,2,1,0:T(8,128)S(1)} %maximum_maximum_fusion.src.src0), custom_call_target="tpu_custom_call" | custom-call | bytes 7000000 | tf_op jit(solution)/shard_map/down0/pallas_call | solution.py:524
  15.7 1.0 %collective-permute-start.5 = (f32[3,3,8,128]{3,2,1,0:T(8,128)S(1)}, f32[3,3,8,128]{3,2,1,0:T(8,128)S(1)}, u32[]{:S(2)}, u32[]{:S(2)}) collective-permute-start(f32[3,3,8,128]{3,2,1,0:T(8,128)S(1)} %get-tuple-element.62), channel_id=1, source_target_pairs={{0,1},{1,0},{2,3},{3,2},{4,5},{5,4},{6,7},{7,6},{8,9},{9,8},{10,11... | collective-permute-start | bytes 110600 | tf_op jit(solution)/shard_map/ppermute | solution.py:565
  16.7 0.6 collective-permute-start.4
  17.2 1.9 %collective-permute-done.5 = f32[3,3,8,128]{3,2,1,0:T(8,128)S(1)} collective-permute-done((f32[3,3,8,128]{3,2,1,0:T(8,128)S(1)}, f32[3,3,8,128]{3,2,1,0:T(8,128)S(1)}, u32[]{:S(2)}, u32[]{:S(2)}) %collective-permute-start.5) | collective-permute-done | bytes 36896 | tf_op jit(solution)/shard_map/ppermute | solution.py:565
  19.1 0.0 collective-permute-done.4
  19.2 1.5 %collective-permute-start.7 = (f32[3,10,8,128]{3,2,1,0:T(8,128)S(1)}, f32[3,10,8,128]{3,2,1,0:T(8,128)S(1)}, u32[]{:S(2)}, u32[]{:S(2)}) collective-permute-start(f32[3,10,8,128]{3,2,1,0:T(8,128)S(1)} %pad_maximum_fusion.5), channel_id=1, source_target_pairs={{0,16},{1,2},{2,1},{3,4},{4,3},{5,6},{6,5},{7,8},{8,7},{9,10},{10,... | collective-permute-start | bytes 368648 | tf_op jit(solution)/shard_map/ppermute | solution.py:565
  20.6 0.5 collective-permute-start.6
  21.1 0.5 collective-permute-done.7
  21.6 3.9 %collective-permute-done.6 = f32[3,10,8,128]{3,2,1,0:T(8,128)S(1)} collective-permute-done((f32[3,10,8,128]{3,2,1,0:T(8,128)S(1)}, f32[3,10,8,128]{3,2,1,0:T(8,128)S(1)}, u32[]{:S(2)}, u32[]{:S(2)}) %collective-permute-start.6) | collective-permute-done | bytes 122912 | tf_op jit(solution)/shard_map/ppermute | solution.py:566
  25.6 2.7 %down1.1 = (f32[64,8,128]{2,1,0:T(8,128)}, f32[3,2,8,128]{3,2,1,0:T(8,128)S(1)}, f32[2,10,24,128]{3,2,1,0:T(8,128)S(1)}, f32[2,12,24,128]{3,2,1,0:T(8,128)S(1)}) custom-call(s32[2]{0:T(128)S(1)} %pad_add_fusion.idx, f32[3,10,24,128]{3,2,1,0:T(8,128)S(1)} %pad_maximum_fusion.src.src1), custom_call_target="tpu_custom_call" | custom-call | bytes 7000000 | tf_op jit(solution)/shard_map/down1/pallas_call | solution.py:524
  28.3 0.6 collective-permute-start.9
  28.9 1.5 %collective-permute-start.8 = (f32[3,1,8,128]{3,2,1,0:T(8,128)S(1)}, f32[3,1,8,128]{3,2,1,0:T(8,128)S(1)}, u32[]{:S(2)}, u32[]{:S(2)}) collective-permute-start(f32[3,1,8,128]{3,2,1,0:T(8,128)S(1)} %get-tuple-element.67), channel_id=1, source_target_pairs={{0,16},{1,17},{2,18},{3,19},{4,20},{5,21},{6,22},{7,23},{8,24},{9,... | collective-permute-start | bytes 36872 | tf_op jit(solution)/shard_map/ppermute | solution.py:566
  30.4 15.5 %all-to-all-start = ((f32[256,2,128]{2,1,0:T(2,128)}), f32[256,2,128]{2,1,0:T(2,128)S(1)}, u32[]{:S(2)}, u32[]{:S(2)}) async-start(f32[256,2,128]{2,1,0:T(2,128)} %bitcast.12), calls=%async_computation | async-start | bytes 524288 | tf_op jit(solution)/shard_map/all_to_all | solution.py:609
  45.9 0.0 collective-permute-done.9
  45.9 0.0 collective-permute-done.8
  46.0 2.2 %collective-permute-start.11 = (f32[3,4,4,128]{3,2,1,0:T(4,128)S(1)}, f32[3,4,4,128]{3,2,1,0:T(4,128)S(1)}, u32[]{:S(2)}, u32[]{:S(2)}) collective-permute-start(f32[3,4,4,128]{3,2,1,0:T(4,128)S(1)} %get-tuple-element.60), channel_id=1, source_target_pairs={{0,16},{1,2},{2,1},{3,4},{4,3},{5,6},{6,5},{7,8},{8,7},{9,10},{10,... | collective-permute-start | bytes 73736 | tf_op jit(solution)/shard_map/ppermute | solution.py:565
  48.2 0.4 collective-permute-start.10
  48.6 0.4 collective-permute-done.11
  49.0 2.2 %collective-permute-done.10 = f32[3,4,4,128]{3,2,1,0:T(4,128)S(1)} collective-permute-done((f32[3,4,4,128]{3,2,1,0:T(4,128)S(1)}, f32[3,4,4,128]{3,2,1,0:T(4,128)S(1)}, u32[]{:S(2)}, u32[]{:S(2)}) %collective-permute-start.10) | collective-permute-done | bytes 24608 | tf_op jit(solution)/shard_map/ppermute | solution.py:566
  51.3 10.3 %all-to-all-done = f32[256,2,128]{2,1,0:T(2,128)S(1)} async-done(((f32[256,2,128]{2,1,0:T(2,128)}), f32[256,2,128]{2,1,0:T(2,128)S(1)}, u32[]{:S(2)}, u32[]{:S(2)}) %all-to-all-start) | async-done | bytes 262176 | tf_op jit(solution)/shard_map/all_to_all | solution.py:609
  61.6 7.4 %up.1 = f32[2,16,16,128]{3,2,1,0:T(8,128)} custom-call(s32[2]{0:T(128)S(1)} %pad_add_fusion.idx, f32[3,22,24,128]{3,2,1,0:T(8,128)S(1)} %maximum_maximum_fusion.src.src0, f32[2,22,24,128]{3,2,1,0:T(8,128)S(1)} %get-tuple-element.32.gain0, f32[2,22,24,128]{3,2,1,0:T(8,128)S(1)} %get-tuple-element.33.ub0, f32[3,10,24,128]{3,2,1,0:T(8,128)S(1)} %pad_maximum_fusion.src.src1, ...), custom_call_target="tpu_custom_call" | custom-call | bytes 35000000 | tf_op jit(solution)/shard_map/up/pallas_call | solution.py:524
  (18 shorter events, 0.3 us)
Async XLA Ops:
  0.0 4.0 %copy-start = (f32[2,16,16,128]{3,2,1,0:T(8,128)S(1)}, f32[2,16,16,128]{3,2,1,0:T(8,128)}, u32[]{:S(2)}) copy-start(f32[2,16,16,128]{3,2,1,0:T(8,128)} %param.2) | copy-start | bytes 786436
  0.0 4.0 %copy-start.1 = (f32[16,16,128]{2,1,0:T(8,128)S(1)}, f32[16,16,128]{2,1,0:T(8,128)}, u32[]{:S(2)}) copy-start(f32[16,16,128]{2,1,0:T(8,128)} %param.3) | copy-start | bytes 393220
  0.9 5.2 %collective-permute-start.1 = (f32[3,3,16,128]{3,2,1,0:T(8,128)S(1)}, f32[3,3,16,128]{3,2,1,0:T(8,128)S(1)}, u32[]{:S(2)}, u32[]{:S(2)}) collective-permute-start(f32[3,3,16,128]{3,2,1,0:T(8,128)S(1)} %fusion), channel_id=1, source_target_pairs={{0,1},{1,0},{2,3},{3,2},{4,5},{5,4},{6,7},{7,6},{8,9},{9,8},{10,11... | collective-permute-start | bytes 221192 | tf_op jit(solution)/shard_map/ppermute | solution.py:565
  4.1 2.0 %collective-permute-start = (f32[3,3,16,128]{3,2,1,0:T(8,128)S(1)}, f32[3,3,16,128]{3,2,1,0:T(8,128)S(1)}, u32[]{:S(2)}, u32[]{:S(2)}) collective-permute-start(f32[3,3,16,128]{3,2,1,0:T(8,128)S(1)} %fusion.1), channel_id=1, source_target_pairs={{0,16},{1,17},{2,18},{3,19},{4,20},{5,21},{6,22},{7,23},{8,24},{9,... | collective-permute-start | bytes 221192 | tf_op jit(solution)/shard_map/ppermute | solution.py:566
  6.2 3.6 %collective-permute-start.3 = (f32[9,22,128]{2,1,0:T(8,128)S(1)}, f32[9,22,128]{2,1,0:T(8,128)S(1)}, u32[]{:S(2)}, u32[]{:S(2)}) collective-permute-start(f32[9,22,128]{2,1,0:T(8,128)S(1)} %bitcast.29), channel_id=1, source_target_pairs={{0,16},{1,2},{2,1},{3,4},{4,3},{5,6},{6,5},{7,8},{8,7},{9,10},{10,... | collective-permute-start | bytes 304136 | tf_op jit(solution)/shard_map/ppermute | solution.py:565
  8.9 4.8 %collective-permute-start.2 = (f32[9,22,128]{2,1,0:T(8,128)S(1)}, f32[9,22,128]{2,1,0:T(8,128)S(1)}, u32[]{:S(2)}, u32[]{:S(2)}) collective-permute-start(f32[9,22,128]{2,1,0:T(8,128)S(1)} %bitcast.30), channel_id=1, source_target_pairs={{0,1},{1,0},{2,3},{3,2},{4,5},{5,4},{6,7},{7,6},{8,9},{9,8},{10,11... | collective-permute-start | bytes 304136 | tf_op jit(solution)/shard_map/ppermute | solution.py:566
  15.7 3.5 %collective-permute-start.5 = (f32[3,3,8,128]{3,2,1,0:T(8,128)S(1)}, f32[3,3,8,128]{3,2,1,0:T(8,128)S(1)}, u32[]{:S(2)}, u32[]{:S(2)}) collective-permute-start(f32[3,3,8,128]{3,2,1,0:T(8,128)S(1)} %get-tuple-element.62), channel_id=1, source_target_pairs={{0,1},{1,0},{2,3},{3,2},{4,5},{5,4},{6,7},{7,6},{8,9},{9,8},{10,11... | collective-permute-start | bytes 110600 | tf_op jit(solution)/shard_map/ppermute | solution.py:565
  16.7 2.5 %collective-permute-start.4 = (f32[3,3,8,128]{3,2,1,0:T(8,128)S(1)}, f32[3,3,8,128]{3,2,1,0:T(8,128)S(1)}, u32[]{:S(2)}, u32[]{:S(2)}) collective-permute-start(f32[3,3,8,128]{3,2,1,0:T(8,128)S(1)} %get-tuple-element.63), channel_id=1, source_target_pairs={{0,16},{1,17},{2,18},{3,19},{4,20},{5,21},{6,22},{7,23},{8,24},{9,... | collective-permute-start | bytes 110600 | tf_op jit(solution)/shard_map/ppermute | solution.py:566
  19.2 2.4 %collective-permute-start.7 = (f32[3,10,8,128]{3,2,1,0:T(8,128)S(1)}, f32[3,10,8,128]{3,2,1,0:T(8,128)S(1)}, u32[]{:S(2)}, u32[]{:S(2)}) collective-permute-start(f32[3,10,8,128]{3,2,1,0:T(8,128)S(1)} %pad_maximum_fusion.5), channel_id=1, source_target_pairs={{0,16},{1,2},{2,1},{3,4},{4,3},{5,6},{6,5},{7,8},{8,7},{9,10},{10,... | collective-permute-start | bytes 368648 | tf_op jit(solution)/shard_map/ppermute | solution.py:565
  20.6 4.9 %collective-permute-start.6 = (f32[3,10,8,128]{3,2,1,0:T(8,128)S(1)}, f32[3,10,8,128]{3,2,1,0:T(8,128)S(1)}, u32[]{:S(2)}, u32[]{:S(2)}) collective-permute-start(f32[3,10,8,128]{3,2,1,0:T(8,128)S(1)} %pad_maximum_fusion.5), channel_id=1, source_target_pairs={{0,1},{1,0},{2,3},{3,2},{4,5},{5,4},{6,7},{7,6},{8,9},{9,8},{10,11... | collective-permute-start | bytes 368648 | tf_op jit(solution)/shard_map/ppermute | solution.py:566
  28.3 17.6 %collective-permute-start.9 = (f32[3,1,8,128]{3,2,1,0:T(8,128)S(1)}, f32[3,1,8,128]{3,2,1,0:T(8,128)S(1)}, u32[]{:S(2)}, u32[]{:S(2)}) collective-permute-start(f32[3,1,8,128]{3,2,1,0:T(8,128)S(1)} %get-tuple-element.66), channel_id=1, source_target_pairs={{0,1},{1,0},{2,3},{3,2},{4,5},{5,4},{6,7},{7,6},{8,9},{9,8},{10,11... | collective-permute-start | bytes 36872 | tf_op jit(solution)/shard_map/ppermute | solution.py:565
  28.9 17.0 %collective-permute-start.8 = (f32[3,1,8,128]{3,2,1,0:T(8,128)S(1)}, f32[3,1,8,128]{3,2,1,0:T(8,128)S(1)}, u32[]{:S(2)}, u32[]{:S(2)}) collective-permute-start(f32[3,1,8,128]{3,2,1,0:T(8,128)S(1)} %get-tuple-element.67), channel_id=1, source_target_pairs={{0,16},{1,17},{2,18},{3,19},{4,20},{5,21},{6,22},{7,23},{8,24},{9,... | collective-permute-start | bytes 36872 | tf_op jit(solution)/shard_map/ppermute | solution.py:566
  30.4 31.2 %all-to-all-start = ((f32[256,2,128]{2,1,0:T(2,128)}), f32[256,2,128]{2,1,0:T(2,128)S(1)}, u32[]{:S(2)}, u32[]{:S(2)}) async-start(f32[256,2,128]{2,1,0:T(2,128)} %bitcast.12), calls=%async_computation | async-start | bytes 524288 | tf_op jit(solution)/shard_map/all_to_all | solution.py:609
  46.0 3.1 %collective-permute-start.11 = (f32[3,4,4,128]{3,2,1,0:T(4,128)S(1)}, f32[3,4,4,128]{3,2,1,0:T(4,128)S(1)}, u32[]{:S(2)}, u32[]{:S(2)}) collective-permute-start(f32[3,4,4,128]{3,2,1,0:T(4,128)S(1)} %get-tuple-element.60), channel_id=1, source_target_pairs={{0,16},{1,2},{2,1},{3,4},{4,3},{5,6},{6,5},{7,8},{8,7},{9,10},{10,... | collective-permute-start | bytes 73736 | tf_op jit(solution)/shard_map/ppermute | solution.py:565
  48.2 3.1 %collective-permute-start.10 = (f32[3,4,4,128]{3,2,1,0:T(4,128)S(1)}, f32[3,4,4,128]{3,2,1,0:T(4,128)S(1)}, u32[]{:S(2)}, u32[]{:S(2)}) collective-permute-start(f32[3,4,4,128]{3,2,1,0:T(4,128)S(1)} %get-tuple-element.61), channel_id=1, source_target_pairs={{0,1},{1,0},{2,3},{3,2},{4,5},{5,4},{6,7},{7,6},{8,9},{9,8},{10,11... | collective-permute-start | bytes 73736 | tf_op jit(solution)/shard_map/ppermute | solution.py:566

commit v13 on v12

--- a/solution.py
+++ b/solution.py
@@ -239,7 +239,7 @@
 
 def up_kernel(
     idx, src0, gain0, ub0, src1, gain1, ub1, src2, shared, out,
-    flat, f3, w3, ga3, gb3, ua3, ub3, f4, w4, s4, e3, gain2, u2, wide2, cell1, ua1, ut1, wide1, wide0, ua0, ut0,
+    flat, f3, w3, ga3, gb3, ua3, ub3, f4, w4, s4, e3, gain2, u2, wide2, cell1, ua1, ut1, wide1, wide0, ua0, ut0, done, sems,
 ):
     ix, iy = idx[0], idx[1]
     lane = lanes(16)
@@ -514,20 +514,29 @@
         new = win0.relaxed(x + 3, ut0)
         for c in range(2):
             ua0[c, x + 3] = new[c]
-            out[c, x] = ua0[c, x + 3, pl.ds(3, 16), :]
-
-    repeat(0, 16, finish0, 16)
-
-
-def call(kernel, name, out_shape, scratch, *args, micros=2):
+            done[c, x] = ua0[c, x + 3, pl.ds(3, 16), :]
+
+    copies = []
+    for half in range(2):
+        repeat(8 * half, 8 * half + 8, finish0, 8)
+        rows = pl.ds(8 * half, 8)
+        copy = pltpu.make_async_copy(done.at[:, rows], out.at[:, rows], sems.at[half])
+        copy.start()
+        copies.append(copy)
+    for copy in copies:
+        copy.wait()
+
+
+def call(kernel, name, out_shape, scratch, *args, micros=2, sems=0):
     vmem = pl.BlockSpec(memory_space=pltpu.VMEM)
     return pl.pallas_call(
         kernel,
         name=name,
         out_shape=[jax.ShapeDtypeStruct(shape, F32) for shape in out_shape],
         in_specs=[pl.BlockSpec(memory_space=pltpu.SMEM)] + [vmem] * (len(args) - 1),
-        out_specs=[vmem] * len(out_shape),
-        scratch_shapes=[pltpu.VMEM(shape, F32) for shape in scratch],
+        out_specs=[pl.BlockSpec(memory_space=pl.ANY) if sems else vmem] * len(out_shape),
+        scratch_shapes=[pltpu.VMEM(shape, F32) for shape in scratch]
+        + ([pltpu.SemaphoreType.DMA((sems,))] if sems else []),
         cost_estimate=pl.CostEstimate(
             flops=0, bytes_accessed=micros * 3_500_000, transcendentals=0
         ),
@@ -620,7 +629,7 @@
         [(520, 128), wide, wide, wide, wide, wide, wide]
         + [(4, 16, 128), (4, 16, 128), (4, 16, 128), (5, 32, 128)]
         + [(2, 4, 16, 128), (2, 6, 16, 128), (2, 4, 40, 128)]
-        + [(2, 10, 16, 128), n1, n1, (2, 10, 40, 128), (2, 16, 40, 128), n0, n0],
+        + [(2, 10, 16, 128), n1, n1, (2, 10, 40, 128), (2, 16, 40, 128), n0, n0, (2, 16, 16, 128)],
         idx,
         src0,
         gain0,
@@ -631,6 +640,7 @@
         src2,
         flat,
         micros=10,
+        sems=2,
     )[0]
 
 

time: 69.2 us -> 69.3 us (level)
  no operation moved by 1% of the time
where the time goes in v13:
time: 69.3 us; the launch traced here: 69.2 us
  starting transfers between devices  30.3 us (44%)
  waiting for transfers between devices  25.1 us (36%)
  Pallas kernels  11.8 us (17%)
  other arithmetic  1.47 us (2%)
    all_to_all x1, starting transfers between devices, body(): flat = lax.all_to_all(part, ('gx', 'gy'), 0, 0).reshape(512, 128)  15.5 us
    pallas_call x3, Pallas kernels, call(): pl.pallas_call(kernel, name=name, out_shape=[jax.ShapeDtypeStruct(shape,...  11.8 us
    ppermute x6, starting transfers between devices, trade(): two = lax.ppermute(two, BOTH, partners(axis, 1))  11 us
    all_to_all x1, waiting for transfers between devices, body(): flat = lax.all_to_all(part, ('gx', 'gy'), 0, 0).reshape(512, 128)  10.3 us
    ppermute x6, waiting for transfers between devices, trade(): one = lax.ppermute(one, BOTH, partners(axis, 0))  9.96 us
    ppermute x6, waiting for transfers between devices, trade(): two = lax.ppermute(two, BOTH, partners(axis, 1))  4.76 us
    ppermute x6, starting transfers between devices, trade(): one = lax.ppermute(one, BOTH, partners(axis, 0))  3.84 us
  transfers between devices with their start and end apart: 13, of which 9 were waited for; matrix products, arithmetic and copies ran while one was open for 0% of the time, Pallas kernels for 0%

profile of v13, /device:TPU:1, one launch (start us, length us, event | category | flops | bytes accessed | tf_op | source)
XLA Modules:
  0.0 69.2 jit_solution(14106858487374103753)
XLA Ops:
  0.0 0.0 copy-start
  0.0 0.0 copy-start.1
  0.0 0.9 %fusion = f32[3,3,16,128]{3,2,1,0:T(8,128)S(1)} fusion(f32[1,16,16,128]{3,2,1,0:T(8,128)} %bitcast.23, f32[2,16,16,128]{3,2,1,0:T(8,128)} %param.2, pred[]{:T(512)S(6)} %eq.18), kind=kLoop, calls=%fused_computation.13 | loop fusion | flops 55296 | bytes 466945 | tf_op jit(solution)/shard_map/jit(_where)/select_n | solution.py:573
  0.9 3.1 %collective-permute-start.1 = (f32[3,3,16,128]{3,2,1,0:T(8,128)S(1)}, f32[3,3,16,128]{3,2,1,0:T(8,128)S(1)}, u32[]{:S(2)}, u32[]{:S(2)}) collective-permute-start(f32[3,3,16,128]{3,2,1,0:T(8,128)S(1)} %fusion), channel_id=1, source_target_pairs={{0,1},{1,0},{2,3},{3,2},{4,5},{5,4},{6,7},{7,6},{8,9},{9,8},{10,11... | collective-permute-start | bytes 221192 | tf_op jit(solution)/shard_map/ppermute | solution.py:574
  4.0 0.0 copy-done
  4.0 0.0 copy-done.1
  4.1 0.3 collective-permute-start
  4.4 0.1 pad.22.clone
  4.5 1.6 %collective-permute-done.1 = f32[3,3,16,128]{3,2,1,0:T(8,128)S(1)} collective-permute-done((f32[3,3,16,128]{3,2,1,0:T(8,128)S(1)}, f32[3,3,16,128]{3,2,1,0:T(8,128)S(1)}, u32[]{:S(2)}, u32[]{:S(2)}) %collective-permute-start.1) | collective-permute-done | bytes 73760 | tf_op jit(solution)/shard_map/ppermute | solution.py:574
  6.1 0.0 collective-permute-done
  6.1 0.1 select_bitcast_fusion
  6.2 2.6 %collective-permute-start.3 = (f32[9,22,128]{2,1,0:T(8,128)S(1)}, f32[9,22,128]{2,1,0:T(8,128)S(1)}, u32[]{:S(2)}, u32[]{:S(2)}) collective-permute-start(f32[9,22,128]{2,1,0:T(8,128)S(1)} %bitcast.29), channel_id=1, source_target_pairs={{0,16},{1,2},{2,1},{3,4},{4,3},{5,6},{6,5},{7,8},{8,7},{9,10},{10,... | collective-permute-start | bytes 304136 | tf_op jit(solution)/shard_map/ppermute | solution.py:574
  8.9 0.4 collective-permute-start.2
  9.3 0.1 pad_add_fusion.idx
  9.4 0.4 collective-permute-done.3
  9.8 3.9 %collective-permute-done.2 = f32[9,22,128]{2,1,0:T(8,128)S(1)} collective-permute-done((f32[9,22,128]{2,1,0:T(8,128)S(1)}, f32[9,22,128]{2,1,0:T(8,128)S(1)}, u32[]{:S(2)}, u32[]{:S(2)}) %collective-permute-start.2) | collective-permute-done | bytes 101408 | tf_op jit(solution)/shard_map/ppermute | solution.py:575
  13.7 0.1 copy_bitcast_fusion
  13.7 0.2 maximum_maximum_fusion.src.src0
  13.9 1.7 %down0.1 = (f32[3,4,8,128]{3,2,1,0:T(8,128)S(1)}, f32[2,22,24,128]{3,2,1,0:T(8,128)S(1)}, f32[2,22,24,128]{3,2,1,0:T(8,128)S(1)}) custom-call(s32[2]{0:T(128)S(1)} %pad_add_fusion.idx, f32[3,22,24,128]{3,2,1,0:T(8,128)S(1)} %maximum_maximum_fusion.src.src0), custom_call_target="tpu_custom_call" | custom-call | bytes 7000000 | tf_op jit(solution)/shard_map/down0/pallas_call | solution.py:532
  15.7 1.0 %collective-permute-start.5 = (f32[3,3,8,128]{3,2,1,0:T(8,128)S(1)}, f32[3,3,8,128]{3,2,1,0:T(8,128)S(1)}, u32[]{:S(2)}, u32[]{:S(2)}) collective-permute-start(f32[3,3,8,128]{3,2,1,0:T(8,128)S(1)} %get-tuple-element.62), channel_id=1, source_target_pairs={{0,1},{1,0},{2,3},{3,2},{4,5},{5,4},{6,7},{7,6},{8,9},{9,8},{10,11... | collective-permute-start | bytes 110600 | tf_op jit(solution)/shard_map/ppermute | solution.py:574
  16.7 0.6 collective-permute-start.4
  17.2 1.9 %collective-permute-done.5 = f32[3,3,8,128]{3,2,1,0:T(8,128)S(1)} collective-permute-done((f32[3,3,8,128]{3,2,1,0:T(8,128)S(1)}, f32[3,3,8,128]{3,2,1,0:T(8,128)S(1)}, u32[]{:S(2)}, u32[]{:S(2)}) %collective-permute-start.5) | collective-permute-done | bytes 36896 | tf_op jit(solution)/shard_map/ppermute | solution.py:574
  19.1 0.0 collective-permute-done.4
  19.2 1.5 %collective-permute-start.7 = (f32[3,10,8,128]{3,2,1,0:T(8,128)S(1)}, f32[3,10,8,128]{3,2,1,0:T(8,128)S(1)}, u32[]{:S(2)}, u32[]{:S(2)}) collective-permute-start(f32[3,10,8,128]{3,2,1,0:T(8,128)S(1)} %pad_maximum_fusion.5), channel_id=1, source_target_pairs={{0,16},{1,2},{2,1},{3,4},{4,3},{5,6},{6,5},{7,8},{8,7},{9,10},{10,... | collective-permute-start | bytes 368648 | tf_op jit(solution)/shard_map/ppermute | solution.py:574
  20.6 0.5 collective-permute-start.6
  21.1 0.5 collective-permute-done.7
  21.6 3.9 %collective-permute-done.6 = f32[3,10,8,128]{3,2,1,0:T(8,128)S(1)} collective-permute-done((f32[3,10,8,128]{3,2,1,0:T(8,128)S(1)}, f32[3,10,8,128]{3,2,1,0:T(8,128)S(1)}, u32[]{:S(2)}, u32[]{:S(2)}) %collective-permute-start.6) | collective-permute-done | bytes 122912 | tf_op jit(solution)/shard_map/ppermute | solution.py:575
  25.6 2.7 %down1.1 = (f32[64,8,128]{2,1,0:T(8,128)}, f32[3,2,8,128]{3,2,1,0:T(8,128)S(1)}, f32[2,10,24,128]{3,2,1,0:T(8,128)S(1)}, f32[2,12,24,128]{3,2,1,0:T(8,128)S(1)}) custom-call(s32[2]{0:T(128)S(1)} %pad_add_fusion.idx, f32[3,10,24,128]{3,2,1,0:T(8,128)S(1)} %pad_maximum_fusion.src.src1), custom_call_target="tpu_custom_call" | custom-call | bytes 7000000 | tf_op jit(solution)/shard_map/down1/pallas_call | solution.py:532
  28.3 0.6 collective-permute-start.9
  28.9 1.5 %collective-permute-start.8 = (f32[3,1,8,128]{3,2,1,0:T(8,128)S(1)}, f32[3,1,8,128]{3,2,1,0:T(8,128)S(1)}, u32[]{:S(2)}, u32[]{:S(2)}) collective-permute-start(f32[3,1,8,128]{3,2,1,0:T(8,128)S(1)} %get-tuple-element.67), channel_id=1, source_target_pairs={{0,16},{1,17},{2,18},{3,19},{4,20},{5,21},{6,22},{7,23},{8,24},{9,... | collective-permute-start | bytes 36872 | tf_op jit(solution)/shard_map/ppermute | solution.py:575
  30.4 15.5 %all-to-all-start = ((f32[256,2,128]{2,1,0:T(2,128)}), f32[256,2,128]{2,1,0:T(2,128)S(1)}, u32[]{:S(2)}, u32[]{:S(2)}) async-start(f32[256,2,128]{2,1,0:T(2,128)} %bitcast.12), calls=%async_computation | async-start | bytes 524288 | tf_op jit(solution)/shard_map/all_to_all | solution.py:618
  45.9 0.0 collective-permute-done.9
  45.9 0.0 collective-permute-done.8
  46.0 2.2 %collective-permute-start.11 = (f32[3,4,4,128]{3,2,1,0:T(4,128)S(1)}, f32[3,4,4,128]{3,2,1,0:T(4,128)S(1)}, u32[]{:S(2)}, u32[]{:S(2)}) collective-permute-start(f32[3,4,4,128]{3,2,1,0:T(4,128)S(1)} %get-tuple-element.60), channel_id=1, source_target_pairs={{0,16},{1,2},{2,1},{3,4},{4,3},{5,6},{6,5},{7,8},{8,7},{9,10},{10,... | collective-permute-start | bytes 73736 | tf_op jit(solution)/shard_map/ppermute | solution.py:574
  48.2 0.4 collective-permute-start.10
  48.6 0.4 collective-permute-done.11
  49.0 2.2 %collective-permute-done.10 = f32[3,4,4,128]{3,2,1,0:T(4,128)S(1)} collective-permute-done((f32[3,4,4,128]{3,2,1,0:T(4,128)S(1)}, f32[3,4,4,128]{3,2,1,0:T(4,128)S(1)}, u32[]{:S(2)}, u32[]{:S(2)}) %collective-permute-start.10) | collective-permute-done | bytes 24608 | tf_op jit(solution)/shard_map/ppermute | solution.py:575
  51.3 10.3 %all-to-all-done = f32[256,2,128]{2,1,0:T(2,128)S(1)} async-done(((f32[256,2,128]{2,1,0:T(2,128)}), f32[256,2,128]{2,1,0:T(2,128)S(1)}, u32[]{:S(2)}, u32[]{:S(2)}) %all-to-all-start) | async-done | bytes 262176 | tf_op jit(solution)/shard_map/all_to_all | solution.py:618
  61.6 7.4 %up.1 = f32[2,16,16,128]{3,2,1,0:T(8,128)} custom-call(s32[2]{0:T(128)S(1)} %pad_add_fusion.idx, f32[3,22,24,128]{3,2,1,0:T(8,128)S(1)} %maximum_maximum_fusion.src.src0, f32[2,22,24,128]{3,2,1,0:T(8,128)S(1)} %get-tuple-element.32.gain0, f32[2,22,24,128]{3,2,1,0:T(8,128)S(1)} %get-tuple-element.33.ub0, f32[3,10,24,128]{3,2,1,0:T(8,128)S(1)} %pad_maximum_fusion.src.src1, ...), custom_call_target="tpu_custom_call" | custom-call | bytes 35000000 | tf_op jit(solution)/shard_map/up/pallas_call | solution.py:532
  (18 shorter events, 0.3 us)
Async XLA Ops:
  0.0 4.0 %copy-start = (f32[2,16,16,128]{3,2,1,0:T(8,128)S(1)}, f32[2,16,16,128]{3,2,1,0:T(8,128)}, u32[]{:S(2)}) copy-start(f32[2,16,16,128]{3,2,1,0:T(8,128)} %param.2) | copy-start | bytes 786436
  0.0 4.0 %copy-start.1 = (f32[16,16,128]{2,1,0:T(8,128)S(1)}, f32[16,16,128]{2,1,0:T(8,128)}, u32[]{:S(2)}) copy-start(f32[16,16,128]{2,1,0:T(8,128)} %param.3) | copy-start | bytes 393220
  0.9 5.2 %collective-permute-start.1 = (f32[3,3,16,128]{3,2,1,0:T(8,128)S(1)}, f32[3,3,16,128]{3,2,1,0:T(8,128)S(1)}, u32[]{:S(2)}, u32[]{:S(2)}) collective-permute-start(f32[3,3,16,128]{3,2,1,0:T(8,128)S(1)} %fusion), channel_id=1, source_target_pairs={{0,1},{1,0},{2,3},{3,2},{4,5},{5,4},{6,7},{7,6},{8,9},{9,8},{10,11... | collective-permute-start | bytes 221192 | tf_op jit(solution)/shard_map/ppermute | solution.py:574
  4.1 2.0 %collective-permute-start = (f32[3,3,16,128]{3,2,1,0:T(8,128)S(1)}, f32[3,3,16,128]{3,2,1,0:T(8,128)S(1)}, u32[]{:S(2)}, u32[]{:S(2)}) collective-permute-start(f32[3,3,16,128]{3,2,1,0:T(8,128)S(1)} %fusion.1), channel_id=1, source_target_pairs={{0,16},{1,17},{2,18},{3,19},{4,20},{5,21},{6,22},{7,23},{8,24},{9,... | collective-permute-start | bytes 221192 | tf_op jit(solution)/shard_map/ppermute | solution.py:575
  6.2 3.6 %collective-permute-start.3 = (f32[9,22,128]{2,1,0:T(8,128)S(1)}, f32[9,22,128]{2,1,0:T(8,128)S(1)}, u32[]{:S(2)}, u32[]{:S(2)}) collective-permute-start(f32[9,22,128]{2,1,0:T(8,128)S(1)} %bitcast.29), channel_id=1, source_target_pairs={{0,16},{1,2},{2,1},{3,4},{4,3},{5,6},{6,5},{7,8},{8,7},{9,10},{10,... | collective-permute-start | bytes 304136 | tf_op jit(solution)/shard_map/ppermute | solution.py:574
  8.9 4.8 %collective-permute-start.2 = (f32[9,22,128]{2,1,0:T(8,128)S(1)}, f32[9,22,128]{2,1,0:T(8,128)S(1)}, u32[]{:S(2)}, u32[]{:S(2)}) collective-permute-start(f32[9,22,128]{2,1,0:T(8,128)S(1)} %bitcast.30), channel_id=1, source_target_pairs={{0,1},{1,0},{2,3},{3,2},{4,5},{5,4},{6,7},{7,6},{8,9},{9,8},{10,11... | collective-permute-start | bytes 304136 | tf_op jit(solution)/shard_map/ppermute | solution.py:575
  15.7 3.5 %collective-permute-start.5 = (f32[3,3,8,128]{3,2,1,0:T(8,128)S(1)}, f32[3,3,8,128]{3,2,1,0:T(8,128)S(1)}, u32[]{:S(2)}, u32[]{:S(2)}) collective-permute-start(f32[3,3,8,128]{3,2,1,0:T(8,128)S(1)} %get-tuple-element.62), channel_id=1, source_target_pairs={{0,1},{1,0},{2,3},{3,2},{4,5},{5,4},{6,7},{7,6},{8,9},{9,8},{10,11... | collective-permute-start | bytes 110600 | tf_op jit(solution)/shard_map/ppermute | solution.py:574
  16.7 2.5 %collective-permute-start.4 = (f32[3,3,8,128]{3,2,1,0:T(8,128)S(1)}, f32[3,3,8,128]{3,2,1,0:T(8,128)S(1)}, u32[]{:S(2)}, u32[]{:S(2)}) collective-permute-start(f32[3,3,8,128]{3,2,1,0:T(8,128)S(1)} %get-tuple-element.63), channel_id=1, source_target_pairs={{0,16},{1,17},{2,18},{3,19},{4,20},{5,21},{6,22},{7,23},{8,24},{9,... | collective-permute-start | bytes 110600 | tf_op jit(solution)/shard_map/ppermute | solution.py:575
  19.2 2.4 %collective-permute-start.7 = (f32[3,10,8,128]{3,2,1,0:T(8,128)S(1)}, f32[3,10,8,128]{3,2,1,0:T(8,128)S(1)}, u32[]{:S(2)}, u32[]{:S(2)}) collective-permute-start(f32[3,10,8,128]{3,2,1,0:T(8,128)S(1)} %pad_maximum_fusion.5), channel_id=1, source_target_pairs={{0,16},{1,2},{2,1},{3,4},{4,3},{5,6},{6,5},{7,8},{8,7},{9,10},{10,... | collective-permute-start | bytes 368648 | tf_op jit(solution)/shard_map/ppermute | solution.py:574
  20.6 4.9 %collective-permute-start.6 = (f32[3,10,8,128]{3,2,1,0:T(8,128)S(1)}, f32[3,10,8,128]{3,2,1,0:T(8,128)S(1)}, u32[]{:S(2)}, u32[]{:S(2)}) collective-permute-start(f32[3,10,8,128]{3,2,1,0:T(8,128)S(1)} %pad_maximum_fusion.5), channel_id=1, source_target_pairs={{0,1},{1,0},{2,3},{3,2},{4,5},{5,4},{6,7},{7,6},{8,9},{9,8},{10,11... | collective-permute-start | bytes 368648 | tf_op jit(solution)/shard_map/ppermute | solution.py:575
  28.3 17.6 %collective-permute-start.9 = (f32[3,1,8,128]{3,2,1,0:T(8,128)S(1)}, f32[3,1,8,128]{3,2,1,0:T(8,128)S(1)}, u32[]{:S(2)}, u32[]{:S(2)}) collective-permute-start(f32[3,1,8,128]{3,2,1,0:T(8,128)S(1)} %get-tuple-element.66), channel_id=1, source_target_pairs={{0,1},{1,0},{2,3},{3,2},{4,5},{5,4},{6,7},{7,6},{8,9},{9,8},{10,11... | collective-permute-start | bytes 36872 | tf_op jit(solution)/shard_map/ppermute | solution.py:574
  28.9 17.0 %collective-permute-start.8 = (f32[3,1,8,128]{3,2,1,0:T(8,128)S(1)}, f32[3,1,8,128]{3,2,1,0:T(8,128)S(1)}, u32[]{:S(2)}, u32[]{:S(2)}) collective-permute-start(f32[3,1,8,128]{3,2,1,0:T(8,128)S(1)} %get-tuple-element.67), channel_id=1, source_target_pairs={{0,16},{1,17},{2,18},{3,19},{4,20},{5,21},{6,22},{7,23},{8,24},{9,... | collective-permute-start | bytes 36872 | tf_op jit(solution)/shard_map/ppermute | solution.py:575
  30.4 31.2 %all-to-all-start = ((f32[256,2,128]{2,1,0:T(2,128)}), f32[256,2,128]{2,1,0:T(2,128)S(1)}, u32[]{:S(2)}, u32[]{:S(2)}) async-start(f32[256,2,128]{2,1,0:T(2,128)} %bitcast.12), calls=%async_computation | async-start | bytes 524288 | tf_op jit(solution)/shard_map/all_to_all | solution.py:618
  46.0 3.1 %collective-permute-start.11 = (f32[3,4,4,128]{3,2,1,0:T(4,128)S(1)}, f32[3,4,4,128]{3,2,1,0:T(4,128)S(1)}, u32[]{:S(2)}, u32[]{:S(2)}) collective-permute-start(f32[3,4,4,128]{3,2,1,0:T(4,128)S(1)} %get-tuple-element.60), channel_id=1, source_target_pairs={{0,16},{1,2},{2,1},{3,4},{4,3},{5,6},{6,5},{7,8},{8,7},{9,10},{10,... | collective-permute-start | bytes 73736 | tf_op jit(solution)/shard_map/ppermute | solution.py:574
  48.2 3.1 %collective-permute-start.10 = (f32[3,4,4,128]{3,2,1,0:T(4,128)S(1)}, f32[3,4,4,128]{3,2,1,0:T(4,128)S(1)}, u32[]{:S(2)}, u32[]{:S(2)}) collective-permute-start(f32[3,4,4,128]{3,2,1,0:T(4,128)S(1)} %get-tuple-element.61), channel_id=1, source_target_pairs={{0,1},{1,0},{2,3},{3,2},{4,5},{5,4},{6,7},{7,6},{8,9},{9,8},{10,11... | collective-permute-start | bytes 73736 | tf_op jit(solution)/shard_map/ppermute | solution.py:575
